TPU v7x, 32 devices: a whole 2x2x4 slice. The times are simulated.
32 devices in a mesh: lat: 4 (over y, x), lon: 8 (over z, core).
Axes of the slice: x: 2, y: 2, z: 4, core: 2. Of those that a mesh axis runs over, the one named last changes fastest.
Arguments:
- state: bfloat16 [32, 128, 256], P('lat', 'lon'), may hold values from -6 to 6
- weight_first: bfloat16 [9, 256, 256], replicated, may hold values from -0.125 to 0.125
- weight_second: bfloat16 [9, 256, 256], replicated, may hold values from -0.125 to 0.125
- obs_owner: int32 [4096, 1], P(('lat', 'lon')), may hold values from 0 to 31; in each aligned block of 128 rows (0 to 127, 128 to 255, ...) at most 6 rows name the same one
- obs_cell: int32 [4096, 32], P(('lat', 'lon')), may hold values from 0 to 110, as said below
- obs_level: int32 [4096, 32], P(('lat', 'lon')), may hold values from 0 to 255
- obs_count: int32 [4096], P(('lat', 'lon')), may hold values from 1 to 32
- obs_frac: float32 [4096, 2, 32], P(('lat', 'lon')), may hold values from 0 to 1
- obs_value: float32 [4096, 32], P(('lat', 'lon')), may hold values from -6 to 6
- obs_weight: float32 [4096, 32], P(('lat', 'lon')), may hold values from 0.1 to 1
Outputs:
- state_grad: float32 [32, 128, 256], P('lat', 'lon')
- grad_first: float32 [9, 256, 256], replicated
- grad_second: float32 [9, 256, 256], replicated
Inputs may be any that keep to these rules, and one draw needn't show every extreme that they name: `obs_owner`: in the blocks of one device no owner is named more than 6 times; some owner is named exactly 6 times. `obs_cell`: Row-major index over the owner's 8 x 16 tile; the cell's row is below 7 and its column below 15.
All inputs are finite; a program needn't handle non-finite values.
Results may differ from a plain program's by a relative error of at most 0.0039.
Values may be sent and summed in bfloat16 or wider, within the bound.
No kernel may reach another device: no remote copies, remote signals or barrier semaphores. Data moves between devices by JAX's collectives and lax.ppermute only.
A program may use at most 64 MiB of HBM per device.

v0:
```python
import math

import jax
import jax.numpy as jnp
from jax import lax
from jax.sharding import PartitionSpec as P


def with_halo(x, sides, width, wrap):
    for axis, dim in sides:
        count, length = (lax.axis_size(axis), x.shape[dim])
        up = [(i, (i + 1) % count) for i in range(count if wrap else count - 1)]
        down = [(j, i) for i, j in up]
        last = lax.slice_in_dim(x, length - width, length, axis=dim)
        first = lax.slice_in_dim(x, 0, width, axis=dim)
        before = lax.ppermute(last, axis, up)
        after = lax.ppermute(first, axis, down)
        x = jnp.concatenate([before, x, after], axis=dim)
    return x


def widen_tile(field):
    across = with_halo(field, (("lon", 1),), 1, True)
    return with_halo(across, (("lat", 0),), 1, False)


def conv_taps(padded, weight, rows, cols, flipped):
    total = jnp.zeros((rows * cols, weight.shape[2]), jnp.float32)
    for first_tap in range(3):
        for second_tap in range(3):
            if flipped:
                piece = padded[
                    2 - first_tap : 2 - first_tap + rows, 2 - second_tap : 2 - second_tap + cols
                ]
                total = total + lax.dot_general(
                    piece.reshape(rows * cols, -1),
                    weight[3 * first_tap + second_tap],
                    (((1,), (1,)), ((), ())),
                    preferred_element_type=jnp.float32,
                )
            else:
                piece = padded[first_tap : first_tap + rows, second_tap : second_tap + cols]
                total = total + jnp.dot(
                    piece.reshape(rows * cols, -1),
                    weight[3 * first_tap + second_tap],
                    preferred_element_type=jnp.float32,
                )
    return total.reshape(rows, cols, -1)


def tap_grads(padded, pullback, rows, cols):
    flat_pull = pullback.reshape(rows * cols, -1)
    result = []
    for first_tap in range(3):
        for second_tap in range(3):
            piece = padded[first_tap : first_tap + rows, second_tap : second_tap + cols].reshape(
                rows * cols, -1
            )
            result.append(
                lax.dot_general(
                    piece, flat_pull, (((0,), (0,)), ((), ())), preferred_element_type=jnp.float32
                )
            )
    return jnp.stack(result)


def route_blocks(obs_owner, obs_cell, obs_level, obs_count, obs_frac, obs_value, obs_weight):
    devices = lax.axis_size(("lat", "lon"))
    blocks, width = obs_value.shape
    slots = max(2, 3 * blocks // (2 * devices))
    owner = obs_owner[:, 0]
    order = lax.broadcasted_iota(jnp.int32, (blocks, blocks), 1) < lax.broadcasted_iota(
        jnp.int32, (blocks, blocks), 0
    )
    earlier = jnp.logical_and(owner[:, None] == owner[None, :], order)
    rank = jnp.sum(earlier.astype(jnp.int32), axis=1)
    target = owner * slots + rank
    valid = (lax.broadcasted_iota(jnp.int32, (blocks, width), 1) < obs_count[:, None]).astype(
        jnp.float32
    )
    packed = jnp.stack(
        [
            obs_frac[:, 0, :],
            obs_frac[:, 1, :],
            obs_value,
            obs_weight,
            obs_cell.astype(jnp.float32),
            obs_level.astype(jnp.float32),
            valid,
        ],
        axis=1,
    )
    outgoing = jnp.zeros((devices * slots, 7, width), jnp.float32).at[target].set(packed)
    return lax.all_to_all(outgoing, ("lat", "lon"), split_axis=0, concat_axis=0, tiled=True)


def observe(corrected, arrived, rows, cols, chans):
    fields = jnp.transpose(arrived, (1, 0, 2)).reshape(7, -1)
    row_total = fields.shape[1]
    span_rows = math.gcd(row_total, 1024)
    fields = jnp.transpose(fields.reshape(7, row_total // span_rows, span_rows), (1, 0, 2))
    grid = corrected.reshape(rows * cols, chans)
    cells = lax.broadcasted_iota(jnp.int32, (1, rows * cols), 1)
    levels = lax.broadcasted_iota(jnp.int32, (1, chans), 1)

    def advance(summed, portion):
        frac_lat = portion[0][:, None]
        frac_lon = portion[1][:, None]
        corner = portion[4].astype(jnp.int32)[:, None]
        level = portion[5].astype(jnp.int32)[:, None]
        weights = (1.0 - frac_lat) * (1.0 - frac_lon) * (cells == corner).astype(jnp.float32)
        weights = weights + (1.0 - frac_lat) * frac_lon * (cells == corner + 1).astype(jnp.float32)
        weights = weights + frac_lat * (1.0 - frac_lon) * (cells == corner + cols).astype(
            jnp.float32
        )
        weights = weights + frac_lat * frac_lon * (cells == corner + cols + 1).astype(jnp.float32)
        onehot = (levels == level).astype(jnp.float32)
        sampled = jnp.dot(
            weights, grid, precision=lax.Precision.HIGHEST, preferred_element_type=jnp.float32
        )
        predicted = jnp.sum(sampled * onehot, axis=1)
        misfit = portion[6] * portion[3] * (predicted - portion[2])
        summed = summed + lax.dot_general(
            weights,
            onehot * misfit[:, None],
            (((0,), (0,)), ((), ())),
            precision=lax.Precision.HIGHEST,
            preferred_element_type=jnp.float32,
        )
        return (summed, None)

    summed, unused = lax.scan(advance, jnp.zeros((rows * cols, chans), jnp.float32), fields)
    return summed.reshape(rows, cols, chans)


def per_device(
    state,
    weight_first,
    weight_second,
    obs_owner,
    obs_cell,
    obs_level,
    obs_count,
    obs_frac,
    obs_value,
    obs_weight,
):
    rows, cols, chans = state.shape
    wide_state = widen_tile(state)
    first = conv_taps(wide_state, weight_first, rows, cols, False)
    hidden = jax.nn.silu(first).astype(jnp.bfloat16)
    wide_hidden = widen_tile(hidden)
    corrected = state.astype(jnp.float32) + conv_taps(wide_hidden, weight_second, rows, cols, False)
    arrived = route_blocks(
        obs_owner, obs_cell, obs_level, obs_count, obs_frac, obs_value, obs_weight
    )
    adjoint = observe(corrected, arrived, rows, cols, chans)
    pullback = adjoint.astype(jnp.bfloat16)
    wide_pull = widen_tile(pullback)
    local_second = tap_grads(wide_hidden, pullback, rows, cols)
    back = conv_taps(wide_pull, weight_second, rows, cols, True)
    sig = jax.nn.sigmoid(first)
    pull_first = (back * sig * (1.0 + first * (1.0 - sig))).astype(jnp.bfloat16)
    wide_pull_first = widen_tile(pull_first)
    local_first = tap_grads(wide_state, pull_first, rows, cols)
    state_grad = adjoint + conv_taps(wide_pull_first, weight_first, rows, cols, True)
    grad_first, grad_second = lax.psum((local_first, local_second), ("lat", "lon"))
    return (state_grad, grad_first, grad_second)


def solution(mesh):
    placed = (
        P("lat", "lon", None),
        P(),
        P(),
        P(("lat", "lon"), None),
        P(("lat", "lon"), None),
        P(("lat", "lon"), None),
        P(("lat", "lon")),
        P(("lat", "lon"), None, None),
        P(("lat", "lon"), None),
        P(("lat", "lon"), None),
    )
    return jax.shard_map(
        per_device,
        mesh=mesh,
        in_specs=placed,
        out_specs=(P("lat", "lon", None), P(), P()),
        check_vma=False,
    )
```

profile of v0, /device:TPU:0, one launch (start us, length us, event | category | flops | bytes accessed | tf_op | source)
XLA Modules:
  0.0 293.9 jit_solution(10903405902182401793)
XLA Ops:
  8.5 4.1 %collective-permute-start.1 = (bf16[8,1,256]{2,1,0:T(2,128)(2,1)S(1)}, bf16[8,1,256]{2,1,0:T(2,128)(2,1)S(1)}, u32[]{:S(2)}, u32[]{:S(2)}) collective-permute-start(bf16[8,1,256]{2,1,0:T(2,128)(2,1)S(1)} %get-tuple-element.212), channel_id=1, source_target_pairs={{1,0},{2,1},{3,2},{4,3},{5,4},{6,5},{7,6},{0,7},{9,8},{10,9},{11,1... | collective-permute-start | bytes 12296 | tf_op jit(solution)/shard_map/ppermute | solution.py:17
  18.8 4.4 %scatter_fusion = f32[192,7,32]{2,1,0:T(8,128)S(1)} fusion(f32[192,7,32]{2,1,0:T(8,128)S(1)} %broadcast_in_dim.5, s32[128]{0:T(128)S(1)} %fusion.146, f32[128,7,32]{2,1,0:T(8,128)S(1)} %copy.19), kind=kCustom, calls=%fused_computation | custom fusion | bytes 344576 | tf_op jit(solution)/shard_map/scatter | solution.py:93
  23.1 1.1 reshape.394
  24.2 4.5 %all-to-all-start = ((f32[32,1,1344]{2,1,0:T(1,128)}), f32[32,1,1344]{2,1,0:T(1,128)S(1)}, u32[]{:S(2)}, u32[]{:S(2)}) async-start(f32[32,1,1344]{2,1,0:T(1,128)} %reshape.394), calls=%async_computation | async-start | bytes 360448 | tf_op jit(solution)/shard_map/all_to_all | solution.py:94
  29.0 3.7 %collective-permute-start.2 = (bf16[1,18,256]{2,1,0:T(8,128)(2,1)S(1)}, bf16[1,18,256]{2,1,0:T(8,128)(2,1)S(1)}, u32[]{:S(2)}, u32[]{:S(2)}) collective-permute-start(bf16[1,18,256]{2,1,0:T(8,128)(2,1)S(1)} %get-tuple-element.195), channel_id=1, source_target_pairs={{0,8},{8,16},{16,24},{1,9},{9,17},{17,25},{2,10},{10,18},{18,26},{... | collective-permute-start | bytes 27656 | tf_op jit(solution)/shard_map/ppermute | solution.py:16
  32.7 1.3 collective-permute-start.3
  34.1 4.2 %collective-permute-done.3 = bf16[1,18,256]{2,1,0:T(8,128)(2,1)S(1)} collective-permute-done((bf16[1,18,256]{2,1,0:T(8,128)(2,1)S(1)}, bf16[1,18,256]{2,1,0:T(8,128)(2,1)S(1)}, u32[]{:S(2)}, u32[]{:S(2)}) %collective-permute-start.3) | collective-permute-done | bytes 9248 | tf_op jit(solution)/shard_map/ppermute | solution.py:17
  40.0 3.5 %collective-permute-start.5 = (bf16[8,1,256]{2,1,0:T(2,128)(2,1)S(1)}, bf16[8,1,256]{2,1,0:T(2,128)(2,1)S(1)}, u32[]{:S(2)}, u32[]{:S(2)}) collective-permute-start(bf16[8,1,256]{2,1,0:T(2,128)(2,1)S(1)} %get-tuple-element.208), channel_id=1, source_target_pairs={{1,0},{2,1},{3,2},{4,3},{5,4},{6,5},{7,6},{0,7},{9,8},{10,9},{11,1... | collective-permute-start | bytes 12296 | tf_op jit(solution)/shard_map/ppermute | solution.py:17
  43.7 1.2 collective-permute-done.4
  45.0 4.3 %collective-permute-start.6 = (bf16[1,18,256]{2,1,0:T(8,128)(2,1)S(1)}, bf16[1,18,256]{2,1,0:T(8,128)(2,1)S(1)}, u32[]{:S(2)}, u32[]{:S(2)}) collective-permute-start(bf16[1,18,256]{2,1,0:T(8,128)(2,1)S(1)} %get-tuple-element.191), channel_id=1, source_target_pairs={{0,8},{8,16},{16,24},{1,9},{9,17},{17,25},{2,10},{10,18},{18,26},{... | collective-permute-start | bytes 27656 | tf_op jit(solution)/shard_map/ppermute | solution.py:16
  49.3 1.3 collective-permute-start.7
  50.6 4.2 %collective-permute-done.7 = bf16[1,18,256]{2,1,0:T(8,128)(2,1)S(1)} collective-permute-done((bf16[1,18,256]{2,1,0:T(8,128)(2,1)S(1)}, bf16[1,18,256]{2,1,0:T(8,128)(2,1)S(1)}, u32[]{:S(2)}, u32[]{:S(2)}) %collective-permute-start.7) | collective-permute-done | bytes 9248 | tf_op jit(solution)/shard_map/ppermute | solution.py:17
  57.6 1.7 reduce
  59.3 1.2 reshape.395
  60.6 1.0 copy.20
  61.5 1.4 reshape_reshape.3
  63.0 46.3 %while.14 = (s32[]{:T(128)}, f32[128,256]{1,0:T(8,128)}, f32[6,7,1024]{2,0,1:T(8,128)S(1)}, f32[128,256]{1,0:T(8,128)}, s32[]{:T(128)}, /*index=5*/s32[]{:T(128)}, s32[]{}, s32[]{}, s32[]{}, s32[]{}, /*index=10*/s32[]{}, s32[]{}) while((s32[]{:T(128)}, f32[128,256]{1,0:T(8,128)}, f32[6,7,1024]{2,0,1:T(8,128)S(1)}, ...), condition=%wide.region_4.5_spmd.clone.clone, body=%wide.region_2.4_spmd.clone.clone.sunk | while | flops 809579520 | bytes 585967 | solution.py:132
  63.1 3.9 %fusion.237 = f32[1024]{0:T(1024)S(1)} fusion(f32[128,256]{1,0:T(8,128)} %get-tuple-element.292, s32[1024]{0:T(1024)S(1)} %bitcast.403, f32[1024]{0:T(1024)S(1)} %get-tuple-element.256, s32[1024]{0:T(1024)S(1)} %get-tuple-element.258, f32[1024]{0:T(1024)S(1)} %get-tuple-element.259, s32[1024]{0:T(1024)S(1)} %get-tuple-element.260, ...), kind=kOutput, calls=%fused_computation.8.clone.1 | convolution fusion | flops 404880384 | bytes 172032 | tf_op jit(solution)/shard_map/while/body/eval_jaxpr/dot_general | solution.py:118
  67.0 2.9 %convolution_add_fusion.26 = f32[128,256]{1,0:T(8,128)} fusion(f32[1024]{0:T(1024)S(1)} %subtract_multiply_fusion.7, s32[1024]{0:T(1024)S(1)} %bitcast.404, f32[1024]{0:T(1024)S(1)} %get-tuple-element.256, s32[1024]{0:T(1024)S(1)} %get-tuple-element.258, f32[1024]{0:T(1024)S(1)} %get-tuple-element.259, s32[1024]{0:T(1024)S(1)} %get-tuple-element.260, ...), kind=kOutput, calls=%fused_computation.9.clone.1 | convolution fusion | flops 404684800 | bytes 303105 | tf_op jit(solution)/shard_map/while/body/eval_jaxpr/dot_general | solution.py:123
  70.0 3.9 %fusion.237 = f32[1024]{0:T(1024)S(1)} fusion(f32[128,256]{1,0:T(8,128)} %get-tuple-element.292, s32[1024]{0:T(1024)S(1)} %bitcast.403, f32[1024]{0:T(1024)S(1)} %get-tuple-element.256, s32[1024]{0:T(1024)S(1)} %get-tuple-element.258, f32[1024]{0:T(1024)S(1)} %get-tuple-element.259, s32[1024]{0:T(1024)S(1)} %get-tuple-element.260, ...), kind=kOutput, calls=%fused_computation.8.clone.1 | convolution fusion | flops 404880384 | bytes 172032 | tf_op jit(solution)/shard_map/while/body/eval_jaxpr/dot_general | solution.py:118
  74.0 3.8 %convolution_add_fusion.26 = f32[128,256]{1,0:T(8,128)} fusion(f32[1024]{0:T(1024)S(1)} %subtract_multiply_fusion.7, s32[1024]{0:T(1024)S(1)} %bitcast.404, f32[1024]{0:T(1024)S(1)} %get-tuple-element.256, s32[1024]{0:T(1024)S(1)} %get-tuple-element.258, f32[1024]{0:T(1024)S(1)} %get-tuple-element.259, s32[1024]{0:T(1024)S(1)} %get-tuple-element.260, ...), kind=kOutput, calls=%fused_computation.9.clone.1 | convolution fusion | flops 404684800 | bytes 303105 | tf_op jit(solution)/shard_map/while/body/eval_jaxpr/dot_general | solution.py:123
  77.9 3.9 %fusion.237 = f32[1024]{0:T(1024)S(1)} fusion(f32[128,256]{1,0:T(8,128)} %get-tuple-element.292, s32[1024]{0:T(1024)S(1)} %bitcast.403, f32[1024]{0:T(1024)S(1)} %get-tuple-element.256, s32[1024]{0:T(1024)S(1)} %get-tuple-element.258, f32[1024]{0:T(1024)S(1)} %get-tuple-element.259, s32[1024]{0:T(1024)S(1)} %get-tuple-element.260, ...), kind=kOutput, calls=%fused_computation.8.clone.1 | convolution fusion | flops 404880384 | bytes 172032 | tf_op jit(solution)/shard_map/while/body/eval_jaxpr/dot_general | solution.py:118
  81.8 3.8 %convolution_add_fusion.26 = f32[128,256]{1,0:T(8,128)} fusion(f32[1024]{0:T(1024)S(1)} %subtract_multiply_fusion.7, s32[1024]{0:T(1024)S(1)} %bitcast.404, f32[1024]{0:T(1024)S(1)} %get-tuple-element.256, s32[1024]{0:T(1024)S(1)} %get-tuple-element.258, f32[1024]{0:T(1024)S(1)} %get-tuple-element.259, s32[1024]{0:T(1024)S(1)} %get-tuple-element.260, ...), kind=kOutput, calls=%fused_computation.9.clone.1 | convolution fusion | flops 404684800 | bytes 303105 | tf_op jit(solution)/shard_map/while/body/eval_jaxpr/dot_general | solution.py:123
  85.7 3.9 %fusion.237 = f32[1024]{0:T(1024)S(1)} fusion(f32[128,256]{1,0:T(8,128)} %get-tuple-element.292, s32[1024]{0:T(1024)S(1)} %bitcast.403, f32[1024]{0:T(1024)S(1)} %get-tuple-element.256, s32[1024]{0:T(1024)S(1)} %get-tuple-element.258, f32[1024]{0:T(1024)S(1)} %get-tuple-element.259, s32[1024]{0:T(1024)S(1)} %get-tuple-element.260, ...), kind=kOutput, calls=%fused_computation.8.clone.1 | convolution fusion | flops 404880384 | bytes 172032 | tf_op jit(solution)/shard_map/while/body/eval_jaxpr/dot_general | solution.py:118
  89.7 3.8 %convolution_add_fusion.26 = f32[128,256]{1,0:T(8,128)} fusion(f32[1024]{0:T(1024)S(1)} %subtract_multiply_fusion.7, s32[1024]{0:T(1024)S(1)} %bitcast.404, f32[1024]{0:T(1024)S(1)} %get-tuple-element.256, s32[1024]{0:T(1024)S(1)} %get-tuple-element.258, f32[1024]{0:T(1024)S(1)} %get-tuple-element.259, s32[1024]{0:T(1024)S(1)} %get-tuple-element.260, ...), kind=kOutput, calls=%fused_computation.9.clone.1 | convolution fusion | flops 404684800 | bytes 303105 | tf_op jit(solution)/shard_map/while/body/eval_jaxpr/dot_general | solution.py:123
  93.6 3.9 %fusion.237 = f32[1024]{0:T(1024)S(1)} fusion(f32[128,256]{1,0:T(8,128)} %get-tuple-element.292, s32[1024]{0:T(1024)S(1)} %bitcast.403, f32[1024]{0:T(1024)S(1)} %get-tuple-element.256, s32[1024]{0:T(1024)S(1)} %get-tuple-element.258, f32[1024]{0:T(1024)S(1)} %get-tuple-element.259, s32[1024]{0:T(1024)S(1)} %get-tuple-element.260, ...), kind=kOutput, calls=%fused_computation.8.clone.1 | convolution fusion | flops 404880384 | bytes 172032 | tf_op jit(solution)/shard_map/while/body/eval_jaxpr/dot_general | solution.py:118
  97.5 3.8 %convolution_add_fusion.26 = f32[128,256]{1,0:T(8,128)} fusion(f32[1024]{0:T(1024)S(1)} %subtract_multiply_fusion.7, s32[1024]{0:T(1024)S(1)} %bitcast.404, f32[1024]{0:T(1024)S(1)} %get-tuple-element.256, s32[1024]{0:T(1024)S(1)} %get-tuple-element.258, f32[1024]{0:T(1024)S(1)} %get-tuple-element.259, s32[1024]{0:T(1024)S(1)} %get-tuple-element.260, ...), kind=kOutput, calls=%fused_computation.9.clone.1 | convolution fusion | flops 404684800 | bytes 303105 | tf_op jit(solution)/shard_map/while/body/eval_jaxpr/dot_general | solution.py:123
  101.5 3.9 %fusion.237 = f32[1024]{0:T(1024)S(1)} fusion(f32[128,256]{1,0:T(8,128)} %get-tuple-element.292, s32[1024]{0:T(1024)S(1)} %bitcast.403, f32[1024]{0:T(1024)S(1)} %get-tuple-element.256, s32[1024]{0:T(1024)S(1)} %get-tuple-element.258, f32[1024]{0:T(1024)S(1)} %get-tuple-element.259, s32[1024]{0:T(1024)S(1)} %get-tuple-element.260, ...), kind=kOutput, calls=%fused_computation.8.clone.1 | convolution fusion | flops 404880384 | bytes 172032 | tf_op jit(solution)/shard_map/while/body/eval_jaxpr/dot_general | solution.py:118
  105.4 3.8 %convolution_add_fusion.26 = f32[128,256]{1,0:T(8,128)} fusion(f32[1024]{0:T(1024)S(1)} %subtract_multiply_fusion.7, s32[1024]{0:T(1024)S(1)} %bitcast.404, f32[1024]{0:T(1024)S(1)} %get-tuple-element.256, s32[1024]{0:T(1024)S(1)} %get-tuple-element.258, f32[1024]{0:T(1024)S(1)} %get-tuple-element.259, s32[1024]{0:T(1024)S(1)} %get-tuple-element.260, ...), kind=kOutput, calls=%fused_computation.9.clone.1 | convolution fusion | flops 404684800 | bytes 303105 | tf_op jit(solution)/shard_map/while/body/eval_jaxpr/dot_general | solution.py:123
  109.2 0.9 convert_element_type.99
  110.5 3.5 %collective-permute-start.9 = (bf16[8,1,256]{2,1,0:T(2,128)(2,1)S(1)}, bf16[8,1,256]{2,1,0:T(2,128)(2,1)S(1)}, u32[]{:S(2)}, u32[]{:S(2)}) collective-permute-start(bf16[8,1,256]{2,1,0:T(2,128)(2,1)S(1)} %get-tuple-element.204), channel_id=1, source_target_pairs={{1,0},{2,1},{3,2},{4,3},{5,4},{6,5},{7,6},{0,7},{9,8},{10,9},{11,1... | collective-permute-start | bytes 12296 | tf_op jit(solution)/shard_map/ppermute | solution.py:17
  116.2 1.3 collective-permute-start.10
  117.5 4.5 %collective-permute-start.11 = (bf16[1,18,256]{2,1,0:T(8,128)(2,1)S(1)}, bf16[1,18,256]{2,1,0:T(8,128)(2,1)S(1)}, u32[]{:S(2)}, u32[]{:S(2)}) collective-permute-start(bf16[1,18,256]{2,1,0:T(8,128)(2,1)S(1)} %get-tuple-element.188), channel_id=1, source_target_pairs={{0,8},{8,16},{16,24},{1,9},{9,17},{17,25},{2,10},{10,18},{18,26},{... | collective-permute-start | bytes 27656 | tf_op jit(solution)/shard_map/ppermute | solution.py:16
  122.1 1.3 collective-permute-done.11
  126.6 3.5 %collective-permute-start.13 = (bf16[8,1,256]{2,1,0:T(2,128)(2,1)S(1)}, bf16[8,1,256]{2,1,0:T(2,128)(2,1)S(1)}, u32[]{:S(2)}, u32[]{:S(2)}) collective-permute-start(bf16[8,1,256]{2,1,0:T(2,128)(2,1)S(1)} %get-tuple-element.200), channel_id=1, source_target_pairs={{1,0},{2,1},{3,2},{4,3},{5,4},{6,5},{7,6},{0,7},{9,8},{10,9},{11,1... | collective-permute-start | bytes 12296 | tf_op jit(solution)/shard_map/ppermute | solution.py:17
  130.2 0.9 fusion.49
  131.1 0.9 fusion.48
  132.9 0.9 fusion.46
  133.8 0.9 fusion.45
  135.7 0.9 fusion.43
  136.6 0.9 fusion.42
  137.6 1.3 collective-permute-start.14
  138.9 4.9 %collective-permute-start.15 = (bf16[1,18,256]{2,1,0:T(8,128)(2,1)S(1)}, bf16[1,18,256]{2,1,0:T(8,128)(2,1)S(1)}, u32[]{:S(2)}, u32[]{:S(2)}) collective-permute-start(bf16[1,18,256]{2,1,0:T(8,128)(2,1)S(1)} %get-tuple-element.184), channel_id=1, source_target_pairs={{0,8},{8,16},{16,24},{1,9},{9,17},{17,25},{2,10},{10,18},{18,26},{... | collective-permute-start | bytes 27656 | tf_op jit(solution)/shard_map/ppermute | solution.py:16
  143.9 1.4 collective-permute-done.15
  146.8 1.8 fusion.59
  148.5 133.8 %all-reduce.3.cloned.1.call-done = (f32[9,256,256]{2,1,0:T(8,128)}, f32[9,256,256]{2,1,0:T(8,128)}) async-done(((f32[9,256,256]{2,1,0:T(8,128)}, f32[9,256,256]{2,1,0:T(8,128)}), (f32[9,256,256]{2,1,0:T(8,128)}, f32[9,256,256]{2,1,0:T(8,128)})) %all-reduce.3.cloned.1.call-update) | async-done | bytes 4718608 | tf_op jit(solution)/shard_map/psum | solution.py:167
  282.3 3.4 %copy.64 = f32[9,256,256]{2,1,0:T(8,128)} copy(f32[9,256,256]{2,1,0:T(8,128)} %get-tuple-element.302) | data formatting | bytes 4718592
  285.7 1.4 copy.65
  (167 shorter events, 21.6 us)
Async XLA Ops:
  8.0 21.0 %collective-permute-start = (bf16[8,1,256]{2,1,0:T(2,128)(2,1)S(1)}, bf16[8,1,256]{2,1,0:T(2,128)(2,1)S(1)}, u32[]{:S(2)}, u32[]{:S(2)}) collective-permute-start(bf16[8,1,256]{2,1,0:T(2,128)(2,1)S(1)} %get-tuple-element.211), channel_id=1, source_target_pairs={{0,1},{1,2},{2,3},{3,4},{4,5},{5,6},{6,7},{7,0},{8,9},{9,10},{10,1... | collective-permute-start | bytes 12296 | tf_op jit(solution)/shard_map/ppermute | solution.py:16
  8.5 20.5 %collective-permute-start.1 = (bf16[8,1,256]{2,1,0:T(2,128)(2,1)S(1)}, bf16[8,1,256]{2,1,0:T(2,128)(2,1)S(1)}, u32[]{:S(2)}, u32[]{:S(2)}) collective-permute-start(bf16[8,1,256]{2,1,0:T(2,128)(2,1)S(1)} %get-tuple-element.212), channel_id=1, source_target_pairs={{1,0},{2,1},{3,2},{4,3},{5,4},{6,5},{7,6},{0,7},{9,8},{10,9},{11,1... | collective-permute-start | bytes 12296 | tf_op jit(solution)/shard_map/ppermute | solution.py:17
  18.7 10.0 %copy-start.1 = (bf16[9,256,256]{2,1,0:T(8,128)(2,1)S(1)}, bf16[9,256,256]{2,1,0:T(8,128)(2,1)}, u32[]{:S(2)}) copy-start(bf16[9,256,256]{2,1,0:T(8,128)(2,1)} %param.13) | copy-start | bytes 3538948
  18.8 10.0 %copy-start.2 = (bf16[8,16,256]{2,1,0:T(8,128)(2,1)S(1)}, bf16[8,16,256]{2,1,0:T(8,128)(2,1)}, u32[]{:S(2)}) copy-start(bf16[8,16,256]{2,1,0:T(8,128)(2,1)} %param.12) | copy-start | bytes 196612
  24.2 32.8 %all-to-all-start = ((f32[32,1,1344]{2,1,0:T(1,128)}), f32[32,1,1344]{2,1,0:T(1,128)S(1)}, u32[]{:S(2)}, u32[]{:S(2)}) async-start(f32[32,1,1344]{2,1,0:T(1,128)} %reshape.394), calls=%async_computation | async-start | bytes 360448 | tf_op jit(solution)/shard_map/all_to_all | solution.py:94
  28.7 253.6 %all-reduce.3.cloned.1.call-start = ((), (), s32[]{:S(2)}) async-start(), calls=%async_computation.1 | async-start | bytes 9437184 | tf_op jit(solution)/shard_map/psum | solution.py:167
  29.0 5.1 %collective-permute-start.2 = (bf16[1,18,256]{2,1,0:T(8,128)(2,1)S(1)}, bf16[1,18,256]{2,1,0:T(8,128)(2,1)S(1)}, u32[]{:S(2)}, u32[]{:S(2)}) collective-permute-start(bf16[1,18,256]{2,1,0:T(8,128)(2,1)S(1)} %get-tuple-element.195), channel_id=1, source_target_pairs={{0,8},{8,16},{16,24},{1,9},{9,17},{17,25},{2,10},{10,18},{18,26},{... | collective-permute-start | bytes 27656 | tf_op jit(solution)/shard_map/ppermute | solution.py:16
  32.7 5.6 %collective-permute-start.3 = (bf16[1,18,256]{2,1,0:T(8,128)(2,1)S(1)}, bf16[1,18,256]{2,1,0:T(8,128)(2,1)S(1)}, u32[]{:S(2)}, u32[]{:S(2)}) collective-permute-start(bf16[1,18,256]{2,1,0:T(8,128)(2,1)S(1)} %get-tuple-element.196), channel_id=1, source_target_pairs={{8,0},{16,8},{24,16},{9,1},{17,9},{25,17},{10,2},{18,10},{26,18},{... | collective-permute-start | bytes 27656 | tf_op jit(solution)/shard_map/ppermute | solution.py:17
  34.0 5.2 %copy-start.11 = (bf16[8,16,256]{2,1,0:T(8,128)(2,1)}, bf16[8,16,256]{2,1,0:T(8,128)(2,1)S(1)}, u32[]{:S(2)}) copy-start(bf16[8,16,256]{2,1,0:T(8,128)(2,1)S(1)} %get-tuple-element.210) | copy-start | bytes 196612
  38.3 0.6 copy-start.7
  38.3 0.7 copy-start.9
  39.2 4.4 %copy-start = (bf16[9,256,256]{2,1,0:T(8,128)(2,1)S(1)}, bf16[9,256,256]{2,1,0:T(8,128)(2,1)}, u32[]{:S(2)}) copy-start(bf16[9,256,256]{2,1,0:T(8,128)(2,1)} %param.14) | copy-start | bytes 3538948
  40.0 5.0 %collective-permute-start.4 = (bf16[8,1,256]{2,1,0:T(2,128)(2,1)S(1)}, bf16[8,1,256]{2,1,0:T(2,128)(2,1)S(1)}, u32[]{:S(2)}, u32[]{:S(2)}) collective-permute-start(bf16[8,1,256]{2,1,0:T(2,128)(2,1)S(1)} %get-tuple-element.207), channel_id=1, source_target_pairs={{0,1},{1,2},{2,3},{3,4},{4,5},{5,6},{6,7},{7,0},{8,9},{9,10},{10,1... | collective-permute-start | bytes 12296 | tf_op jit(solution)/shard_map/ppermute | solution.py:16
  40.0 4.9 %collective-permute-start.5 = (bf16[8,1,256]{2,1,0:T(2,128)(2,1)S(1)}, bf16[8,1,256]{2,1,0:T(2,128)(2,1)S(1)}, u32[]{:S(2)}, u32[]{:S(2)}) collective-permute-start(bf16[8,1,256]{2,1,0:T(2,128)(2,1)S(1)} %get-tuple-element.208), channel_id=1, source_target_pairs={{1,0},{2,1},{3,2},{4,3},{5,4},{6,5},{7,6},{0,7},{9,8},{10,9},{11,1... | collective-permute-start | bytes 12296 | tf_op jit(solution)/shard_map/ppermute | solution.py:17
  45.0 5.7 %collective-permute-start.6 = (bf16[1,18,256]{2,1,0:T(8,128)(2,1)S(1)}, bf16[1,18,256]{2,1,0:T(8,128)(2,1)S(1)}, u32[]{:S(2)}, u32[]{:S(2)}) collective-permute-start(bf16[1,18,256]{2,1,0:T(8,128)(2,1)S(1)} %get-tuple-element.191), channel_id=1, source_target_pairs={{0,8},{8,16},{16,24},{1,9},{9,17},{17,25},{2,10},{10,18},{18,26},{... | collective-permute-start | bytes 27656 | tf_op jit(solution)/shard_map/ppermute | solution.py:16
  49.3 5.6 %collective-permute-start.7 = (bf16[1,18,256]{2,1,0:T(8,128)(2,1)S(1)}, bf16[1,18,256]{2,1,0:T(8,128)(2,1)S(1)}, u32[]{:S(2)}, u32[]{:S(2)}) collective-permute-start(bf16[1,18,256]{2,1,0:T(8,128)(2,1)S(1)} %get-tuple-element.192), channel_id=1, source_target_pairs={{8,0},{16,8},{24,16},{9,1},{17,9},{25,17},{10,2},{18,10},{26,18},{... | collective-permute-start | bytes 27656 | tf_op jit(solution)/shard_map/ppermute | solution.py:17
  50.6 5.1 %copy-start.15 = (bf16[8,16,256]{2,1,0:T(8,128)(2,1)}, bf16[8,16,256]{2,1,0:T(8,128)(2,1)S(1)}, u32[]{:S(2)}) copy-start(bf16[8,16,256]{2,1,0:T(8,128)(2,1)S(1)} %get-tuple-element.206) | copy-start | bytes 196612
  50.6 5.2 %copy-start.13 = (bf16[8,16,256]{2,1,0:T(8,128)(2,1)}, bf16[8,16,256]{2,1,0:T(8,128)(2,1)S(1)}, u32[]{:S(2)}) copy-start(bf16[8,16,256]{2,1,0:T(8,128)(2,1)S(1)} %get-tuple-element.205) | copy-start | bytes 196612
  54.9 0.8 copy-start.5
  63.0 47.2 %copy-start.6 = (bf16[9,18,256]{2,1,0:T(8,128)(2,1)S(1)}, bf16[9,18,256]{2,1,0:T(8,128)(2,1)}, u32[]{:S(2)}) copy-start(bf16[9,18,256]{2,1,0:T(8,128)(2,1)} %copy-done.5) | copy-start | bytes 248836
  110.2 4.3 %copy-start.16 = (bf16[8,16,256]{2,1,0:T(8,128)(2,1)S(1)}, bf16[8,16,256]{2,1,0:T(8,128)(2,1)}, u32[]{:S(2)}) copy-start(bf16[8,16,256]{2,1,0:T(8,128)(2,1)} %copy-done.15) | copy-start | bytes 196612
  110.4 5.7 %collective-permute-start.8 = (bf16[8,1,256]{2,1,0:T(2,128)(2,1)S(1)}, bf16[8,1,256]{2,1,0:T(2,128)(2,1)S(1)}, u32[]{:S(2)}, u32[]{:S(2)}) collective-permute-start(bf16[8,1,256]{2,1,0:T(2,128)(2,1)S(1)} %get-tuple-element.203), channel_id=1, source_target_pairs={{0,1},{1,2},{2,3},{3,4},{4,5},{5,6},{6,7},{7,0},{8,9},{9,10},{10,1... | collective-permute-start | bytes 12296 | tf_op jit(solution)/shard_map/ppermute | solution.py:16
  110.5 5.7 %collective-permute-start.9 = (bf16[8,1,256]{2,1,0:T(2,128)(2,1)S(1)}, bf16[8,1,256]{2,1,0:T(2,128)(2,1)S(1)}, u32[]{:S(2)}, u32[]{:S(2)}) collective-permute-start(bf16[8,1,256]{2,1,0:T(2,128)(2,1)S(1)} %get-tuple-element.204), channel_id=1, source_target_pairs={{1,0},{2,1},{3,2},{4,3},{5,4},{6,5},{7,6},{0,7},{9,8},{10,9},{11,1... | collective-permute-start | bytes 12296 | tf_op jit(solution)/shard_map/ppermute | solution.py:17
  114.2 0.8 copy-start.14
  115.9 8.0 %copy-start.4 = (f32[9,256,256]{2,1,0:T(8,128)}, f32[9,256,256]{2,1,0:T(8,128)S(1)}, u32[]{:S(2)}) copy-start(f32[9,256,256]{2,1,0:T(8,128)S(1)} %fusion.33) | copy-start | bytes 7077892
  116.2 5.9 %collective-permute-start.10 = (bf16[1,18,256]{2,1,0:T(8,128)(2,1)S(1)}, bf16[1,18,256]{2,1,0:T(8,128)(2,1)S(1)}, u32[]{:S(2)}, u32[]{:S(2)}) collective-permute-start(bf16[1,18,256]{2,1,0:T(8,128)(2,1)S(1)} %get-tuple-element.187), channel_id=1, source_target_pairs={{8,0},{16,8},{24,16},{9,1},{17,9},{25,17},{10,2},{18,10},{26,18},{... | collective-permute-start | bytes 27656 | tf_op jit(solution)/shard_map/ppermute | solution.py:17
  117.5 5.9 %collective-permute-start.11 = (bf16[1,18,256]{2,1,0:T(8,128)(2,1)S(1)}, bf16[1,18,256]{2,1,0:T(8,128)(2,1)S(1)}, u32[]{:S(2)}, u32[]{:S(2)}) collective-permute-start(bf16[1,18,256]{2,1,0:T(8,128)(2,1)S(1)} %get-tuple-element.188), channel_id=1, source_target_pairs={{0,8},{8,16},{16,24},{1,9},{9,17},{17,25},{2,10},{10,18},{18,26},{... | collective-permute-start | bytes 27656 | tf_op jit(solution)/shard_map/ppermute | solution.py:16
  124.8 0.9 copy-start.10
  125.7 6.3 %copy-start.12 = (bf16[8,16,256]{2,1,0:T(8,128)(2,1)S(1)}, bf16[8,16,256]{2,1,0:T(8,128)(2,1)}, u32[]{:S(2)}) copy-start(bf16[8,16,256]{2,1,0:T(8,128)(2,1)} %copy-done.11) | copy-start | bytes 196612
  126.6 10.9 %collective-permute-start.12 = (bf16[8,1,256]{2,1,0:T(2,128)(2,1)S(1)}, bf16[8,1,256]{2,1,0:T(2,128)(2,1)S(1)}, u32[]{:S(2)}, u32[]{:S(2)}) collective-permute-start(bf16[8,1,256]{2,1,0:T(2,128)(2,1)S(1)} %get-tuple-element.199), channel_id=1, source_target_pairs={{0,1},{1,2},{2,3},{3,4},{4,5},{5,6},{6,7},{7,0},{8,9},{9,10},{10,1... | collective-permute-start | bytes 12296 | tf_op jit(solution)/shard_map/ppermute | solution.py:16
  126.6 10.9 %collective-permute-start.13 = (bf16[8,1,256]{2,1,0:T(2,128)(2,1)S(1)}, bf16[8,1,256]{2,1,0:T(2,128)(2,1)S(1)}, u32[]{:S(2)}, u32[]{:S(2)}) collective-permute-start(bf16[8,1,256]{2,1,0:T(2,128)(2,1)S(1)} %get-tuple-element.200), channel_id=1, source_target_pairs={{1,0},{2,1},{3,2},{4,3},{5,4},{6,5},{7,6},{0,7},{9,8},{10,9},{11,1... | collective-permute-start | bytes 12296 | tf_op jit(solution)/shard_map/ppermute | solution.py:17
  132.0 2.8 copy-start.8
  137.6 6.3 %collective-permute-start.14 = (bf16[1,18,256]{2,1,0:T(8,128)(2,1)S(1)}, bf16[1,18,256]{2,1,0:T(8,128)(2,1)S(1)}, u32[]{:S(2)}, u32[]{:S(2)}) collective-permute-start(bf16[1,18,256]{2,1,0:T(8,128)(2,1)S(1)} %get-tuple-element.183), channel_id=1, source_target_pairs={{8,0},{16,8},{24,16},{9,1},{17,9},{25,17},{10,2},{18,10},{26,18},{... | collective-permute-start | bytes 27656 | tf_op jit(solution)/shard_map/ppermute | solution.py:17
  138.9 6.3 %collective-permute-start.15 = (bf16[1,18,256]{2,1,0:T(8,128)(2,1)S(1)}, bf16[1,18,256]{2,1,0:T(8,128)(2,1)S(1)}, u32[]{:S(2)}, u32[]{:S(2)}) collective-permute-start(bf16[1,18,256]{2,1,0:T(8,128)(2,1)S(1)} %get-tuple-element.184), channel_id=1, source_target_pairs={{0,8},{8,16},{16,24},{1,9},{9,17},{17,25},{2,10},{10,18},{18,26},{... | collective-permute-start | bytes 27656 | tf_op jit(solution)/shard_map/ppermute | solution.py:16
  282.3 3.4 %copy-start.3 = (f32[9,256,256]{2,1,0:T(8,128)S(1)}, f32[9,256,256]{2,1,0:T(8,128)}, u32[]{:S(2)}) copy-start(f32[9,256,256]{2,1,0:T(8,128)} %get-tuple-element.303) | copy-start | bytes 7077892
Sparse Core Ops, SparseCore 0:
  137.7 144.6 all-reduce.2
where the time goes:
time: 295 us; the launch traced here: 294 us
  waiting for transfers between devices  146 us (49%)
  matrix products  63.9 us (22%)
  starting transfers between devices  42.4 us (14%)
  local copies, waits for them, and re-layouts  18.4 us (6%)
  between operations  14.8 us (5%)
  other arithmetic  8 us (3%)
    psum x1, waiting for transfers between devices, per_device(): lax.psum((local_first, local_second), ('lat', 'lon'))  134 us
    dot_general x6, matrix products, advance(): jnp.dot(weights, grid, precision=lax.Precision.HIGHEST, preferred_element...  23.5 us
    dot_general x6, matrix products, advance(): lax.dot_general(weights, onehot * misfit[:, None], (((0,), (0,)), ((), ()...  22.2 us
    ppermute x8, starting transfers between devices, with_halo(): after = lax.ppermute(first, axis, down)  19.9 us
    ppermute x8, starting transfers between devices, with_halo(): before = lax.ppermute(last, axis, up)  18 us
    dot_general x18, matrix products, tap_grads(): lax.dot_general(piece, flat_pull, (((0,), (0,)), ((), ())), preferred_ele...  10.2 us
    unnamed x41, local copies, waits for them, and re-layouts  9.76 us
    ppermute x8, waiting for transfers between devices, with_halo(): after = lax.ppermute(first, axis, down)  8.42 us
  transfers between devices with their start and end apart: 18, of which 6 were waited for; matrix products, arithmetic and copies ran while one was open for 10% of the time, Pallas kernels for 0%

commit v1 on v0

v1 whole, which is shorter than its diff:
```python
import functools

import jax
import jax.numpy as jnp
from jax import lax
from jax.experimental import pallas as pl
from jax.experimental.pallas import tpu as pltpu
from jax.sharding import PartitionSpec as P

F32 = jnp.float32
BF16 = jnp.bfloat16
FIELDS = 5
VMEM_LIMIT = 60 * 1024 * 1024


def params(limit=VMEM_LIMIT):
    return pltpu.CompilerParams(vmem_limit_bytes=limit)


def vmem():
    return pl.BlockSpec(memory_space=pltpu.VMEM)


def iota(shape, dim, dtype=jnp.int32):
    return lax.broadcasted_iota(jnp.int32, shape, dim).astype(dtype)


def dot(x, y, precision=None):
    return jnp.dot(x, y, precision=precision, preferred_element_type=F32)


def dot_nt(x, y, precision=None):
    return lax.dot_general(
        x, y, (((1,), (1,)), ((), ())), precision=precision, preferred_element_type=F32
    )


def slot_layout(slots):
    full, rest = divmod(slots, 4)
    rows = full * FIELDS + (0 if rest == 0 else -(-FIELDS // 2))
    return full, rest, -(-rows // 8) * 8


def route_kernel(
    devices, slots, chans, owner_ref, count_ref, cell_ref, level_ref, frac_ref, value_ref,
    weight_ref, out_ref
):
    width, blocks = value_ref.shape
    owner = owner_ref[...].astype(F32)
    across = jnp.broadcast_to(owner, (blocks, blocks))
    down = across.T
    earlier = iota((blocks, blocks), 0) < iota((blocks, blocks), 1)
    hits = jnp.where(jnp.logical_and(across == down, earlier), 1.0, 0.0)
    rank = jnp.sum(hits, axis=0, keepdims=True)
    target = rank * float(devices) + owner
    places = iota((slots * devices, blocks), 0, F32) == target
    onehot = jnp.where(places, 1.0, 0.0)
    valid = iota((width, blocks), 0) < count_ref[...]
    fields = jnp.concatenate(
        [
            frac_ref[0],
            frac_ref[1],
            value_ref[...],
            jnp.where(valid, weight_ref[...], 0.0),
            (cell_ref[...] * chans + level_ref[...]).astype(F32),
        ],
        axis=0,
    )
    placed = dot_nt(onehot, fields, lax.Precision.HIGHEST)
    full, rest, rows = slot_layout(slots)
    out_ref[...] = jnp.zeros(out_ref.shape, F32)
    for slot in range(slots):
        for field in range(FIELDS):
            piece = placed[
                slot * devices : (slot + 1) * devices, field * width : (field + 1) * width
            ]
            if slot < 4 * full:
                row, lane = (slot // 4) * FIELDS + field, (slot % 4) * width
            else:
                row = full * FIELDS + field // 2
                lane = (field % 2) * 2 * width + (slot - 4 * full) * width
            out_ref[:, row, lane : lane + width] = piece


def route(devices, slots, chans, obs_owner, obs_cell, obs_level, obs_count, obs_frac, obs_value,
          obs_weight):
    blocks = obs_value.shape[0]
    rows = slot_layout(slots)[2]
    return pl.pallas_call(
        functools.partial(route_kernel, devices, slots, chans),
        out_shape=jax.ShapeDtypeStruct((devices, rows, 128), F32),
        in_specs=[vmem()] * 7,
        out_specs=vmem(),
        compiler_params=params(),
        name="route",
    )(
        obs_owner.reshape(1, blocks),
        obs_count.reshape(1, blocks),
        obs_cell.T,
        obs_level.T,
        jnp.transpose(obs_frac, (1, 2, 0)),
        obs_value.T,
        obs_weight.T,
    )


def silu_parts(first):
    sig = 1.0 / (1.0 + jnp.exp(-first))
    return sig, first * sig


def forward_kernel(slots, tiles, group, wide_ref, w1_ref, w2_ref, got_ref, adj_ref, pull_ref,
                   line_ref, shift_ref, hid_ref, obs_ref):
    rows, cols, chans = (wide_ref.shape[0] - 4, wide_ref.shape[1] - 4, wide_ref.shape[2])
    span = 32
    line_ref[:, 0 : cols + 4, :] = wide_ref[...].astype(F32)
    line_ref[:, cols + 4 :, :] = jnp.zeros(
        (rows + 4, line_ref.shape[1] - cols - 4, chans), F32
    )
    first = jnp.zeros(((rows + 2) * span, chans), F32)
    for b in range(3):
        shift_ref[...] = (
            line_ref[:, b : b + span, :].astype(BF16).reshape((rows + 4) * span, chans)
        )
        for a in range(3):
            first = first + dot(
                shift_ref[a * span : a * span + (rows + 2) * span, :], w1_ref[3 * a + b]
            )
    hidden = silu_parts(first)[1].astype(BF16).astype(F32).reshape(rows + 2, span, chans)
    lat = lax.axis_index("lat") * rows + iota((rows + 2, span, chans), 0) - 1
    hidden = jnp.where(jnp.logical_and(lat >= 0, lat < tiles * rows), hidden, 0.0)
    hid_ref[...] = hidden
    total = line_ref[2 : 2 + rows, 2 : 2 + cols, :].reshape(rows * cols, chans)
    for b in range(3):
        shift_ref[0 : (rows + 2) * cols, :] = (
            hid_ref[:, b : b + cols, :].astype(BF16).reshape((rows + 2) * cols, chans)
        )
        for a in range(3):
            total = total + dot(
                shift_ref[a * cols : a * cols + rows * cols, :], w2_ref[3 * a + b]
            )
    cells = rows * cols
    turned = total.T
    grid_high = turned.astype(BF16)
    grid_low = (turned - grid_high.astype(F32)).astype(BF16)
    grid_both = jnp.concatenate([grid_high, grid_low], axis=1)

    devices = got_ref.shape[0]
    full, rest, _ = slot_layout(slots)
    half = devices // 2
    for field in range(FIELDS):
        for part in range(full):
            obs_ref[field, part * devices : (part + 1) * devices, :] = got_ref[
                :, part * FIELDS + field, :
            ]
        if rest:
            tail = got_ref[:, full * FIELDS + field // 2, :]
            low, high = tail[:half], tail[half:]
            if field % 2 == 0:
                high = pltpu.roll(high, 64, 1)
            else:
                low = pltpu.roll(low, 64, 1)
            obs_ref[field, full * devices : full * devices + half, :] = jnp.where(
                iota((half, 128), 1) < 64, low, high
            )
    code = obs_ref[4].astype(jnp.int32)
    shift = chans.bit_length() - 1
    cell = lax.shift_right_logical(code, shift)
    obs_ref[4] = (code & (chans - 1)).astype(F32)
    obs_ref[0] = obs_ref[0] + lax.shift_right_logical(cell, 4).astype(F32)
    obs_ref[1] = obs_ref[1] + (cell & (cols - 1)).astype(F32)

    adj_ref[...] = jnp.zeros(adj_ref.shape, F32)
    count = obs_ref.shape[1] // group
    row_ids = iota((rows, 128), 0, F32)
    col_ids = iota((cols, 128), 0, F32)
    level_ids = iota((chans, 128), 0, F32)

    def step(index, carry):
        high, low, masks, marks = [], [], [], []
        for piece in range(group):
            at = index * group + piece
            mark = [obs_ref[field, pl.ds(at, 1), :] for field in range(FIELDS)]
            up = jnp.maximum(0.0, 1.0 - jnp.abs(row_ids - mark[0]))
            along = jnp.maximum(0.0, 1.0 - jnp.abs(col_ids - mark[1]))
            weights = (up[:, None, :] * along[None, :, :]).reshape(cells, 128)
            weights_high = weights.astype(BF16)
            high.append(weights_high)
            low.append((weights - weights_high.astype(F32)).astype(BF16))
            masks.append(level_ids == mark[4])
            marks.append(mark)
        high = jnp.concatenate(high, axis=1)
        low = jnp.concatenate(low, axis=1)
        sampled = dot(grid_both, jnp.concatenate([high, high], axis=0)) + dot(grid_high, low)
        hot_high, hot_low = [], []
        for piece in range(group):
            mine = sampled[:, piece * 128 : (piece + 1) * 128]
            predicted = jnp.sum(jnp.where(masks[piece], mine, 0.0), axis=0, keepdims=True)
            misfit = marks[piece][3] * (predicted - marks[piece][2])
            misfit_high = misfit.astype(BF16).astype(F32)
            hot_high.append(jnp.where(masks[piece], misfit_high, 0.0).astype(BF16))
            hot_low.append(jnp.where(masks[piece], misfit - misfit_high, 0.0).astype(BF16))
        hot_high = jnp.concatenate(hot_high, axis=1)
        hot_low = jnp.concatenate(hot_low, axis=1)
        adj_ref[...] += dot_nt(
            jnp.concatenate([high, high, low], axis=1),
            jnp.concatenate([hot_high, hot_low, hot_high], axis=1),
        )
        return carry

    lax.fori_loop(0, count, step, 0)
    pull_ref[...] = adj_ref[...].astype(BF16)


def forward(slots, tiles, wide, w1, w2, got):
    rows, cols, chans = (wide.shape[0] - 4, wide.shape[1] - 4, wide.shape[2])
    devices = got.shape[0]
    full, rest, _ = slot_layout(slots)
    groups = full * devices + (devices // 2 if rest else 0)
    group = 4
    return pl.pallas_call(
        functools.partial(forward_kernel, slots, tiles, group),
        out_shape=[
            jax.ShapeDtypeStruct((rows * cols, chans), F32),
            jax.ShapeDtypeStruct((rows * cols, chans), BF16),
        ],
        in_specs=[vmem()] * 4,
        out_specs=[vmem()] * 2,
        scratch_shapes=[
            pltpu.VMEM((rows + 4, 40, chans), F32),
            pltpu.VMEM(((rows + 4) * 32, chans), BF16),
            pltpu.VMEM((rows + 2, 32, chans), F32),
            pltpu.VMEM((FIELDS, groups, 128), F32),
        ],
        compiler_params=params(),
        name="forward",
    )(wide, w1, w2, got)


def spread_matrix(steps):
    lons = 16 * steps
    place = iota(((steps + 2) * 16, lons), 0)
    lon = (place & 15) * steps + lax.shift_right_logical(place, 4) - 1
    lon = jnp.where(lon < 0, lon + lons, jnp.where(lon >= lons, lon - lons, lon))
    return jnp.where(iota(((steps + 2) * 16, lons), 1) == lon, 1.0, 0.0).astype(BF16)


def spread(all_ref, pad_ref):
    bands, tiles, rows, group, chans = all_ref.shape
    steps = pad_ref.shape[1] - 2
    matrix = spread_matrix(steps)
    blank = jnp.zeros(pad_ref.shape[1:], BF16)
    pad_ref[0] = blank
    pad_ref[bands * rows + 1] = blank

    def place(band, carry):
        for row in range(rows):
            line = all_ref[band, :, row].reshape(tiles * group, chans)
            pad_ref[1 + band * rows + row] = (
                dot(matrix, line).astype(BF16).reshape(steps + 2, 16, chans)
            )
        return carry

    lax.fori_loop(0, bands, place, 0)


def conv_block(pad_ref, weight_ref, start, rows, flipped):
    steps = pad_ref.shape[1] - 2
    chans = pad_ref.shape[3]
    total = None
    for a in range(3):
        for b in range(3):
            da, db = (2 - a, 2 - b) if flipped else (a, b)
            piece = pad_ref[pl.ds(start + da, rows), db : db + steps]
            term = dot(piece.reshape(rows * steps * 16, chans), weight_ref[3 * a + b])
            total = term if total is None else total + term
    return total


def whole_kernel(block, all_ref, w1_ref, w2_ref, slope_ref, hidden_ref, state_ref, w2t_ref, pad_ref):
    lats = pad_ref.shape[0] - 2
    steps = pad_ref.shape[1] - 2
    chans = pad_ref.shape[3]
    size = block * steps * 16
    spread(all_ref, pad_ref)

    def step(index, carry):
        start = index * block
        first = conv_block(pad_ref, w1_ref, start, block, False)
        sig, hidden = silu_parts(first)
        at = pl.ds(pl.multiple_of(index * size, size), size)
        slope_ref[at, :] = sig * (1.0 + first * (1.0 - sig))
        hidden_ref[:, at] = hidden.astype(BF16).T
        centre = pad_ref[pl.ds(start + 1, block), 1 : 1 + steps].reshape(size, chans)
        state_ref[:, at] = centre.T
        return carry

    lax.fori_loop(0, lats // block, step, 0)
    for tap in range(9):
        w2t_ref[tap] = w2_ref[tap].T


def whole(state_all, w1, w2):
    bands, tiles, rows, group, chans = state_all.shape
    lats, lons = bands * rows, tiles * group
    steps = lons // 16
    block = 512 // lons
    return pl.pallas_call(
        functools.partial(whole_kernel, block),
        out_shape=[
            jax.ShapeDtypeStruct((lats * lons, chans), F32),
            jax.ShapeDtypeStruct((chans, lats * lons), BF16),
            jax.ShapeDtypeStruct((chans, lats * lons), BF16),
            jax.ShapeDtypeStruct((9, chans, chans), BF16),
        ],
        in_specs=[vmem()] * 3,
        out_specs=[vmem()] * 4,
        scratch_shapes=[pltpu.VMEM((lats + 2, steps + 2, 16, chans), BF16)],
        compiler_params=params(),
        name="whole",
    )(state_all, w1, w2)


def tap_sums(turned_ref, pad_ref, out_ref):
    lats = pad_ref.shape[0] - 2
    steps = pad_ref.shape[1] - 2
    chans = pad_ref.shape[3]
    per_row = steps * 16
    part = 4096 // per_row

    def step(tap, carry):
        a, b = tap // 3, tap % 3
        total = None
        for start in range(0, lats, part):
            piece = pad_ref[pl.ds(start + 2 - a, part), pl.ds(2 - b, steps)]
            term = dot(
                turned_ref[:, start * per_row : (start + part) * per_row],
                piece.reshape(part * per_row, chans),
            )
            total = term if total is None else total + term
        out_ref[tap] = total
        return carry

    lax.fori_loop(0, 9, step, 0)


def tail_kernel(block, all_ref, slope_hbm, hidden_hbm, state_hbm, w2t_ref, w1_ref, adj_ref,
                grad_ref, g1_ref, g2_ref, pull_ref, first_ref, near_ref, slope_ref, hidden_ref,
                state_ref, slope_sems, big_sems):
    lats = pull_ref.shape[0] - 2
    steps = pull_ref.shape[1] - 2
    chans = pull_ref.shape[3]
    lons = steps * 16
    size = block * lons
    count = lats // block
    rows = all_ref.shape[2]
    cols = all_ref.shape[3]
    hidden_copy = pltpu.make_async_copy(hidden_hbm, hidden_ref, big_sems.at[0])
    state_copy = pltpu.make_async_copy(state_hbm, state_ref, big_sems.at[1])

    def slope_copy(index, slot):
        at = pl.ds(pl.multiple_of(index * size, size), size)
        return pltpu.make_async_copy(slope_hbm.at[at, :], slope_ref.at[slot], slope_sems.at[slot])

    slope_copy(0, 0).start()
    hidden_copy.start()
    state_copy.start()
    spread(all_ref, pull_ref)
    blank = jnp.zeros(first_ref.shape[1:], BF16)
    first_ref[0] = blank
    first_ref[lats + 1] = blank

    def step(index, carry):
        start = index * block
        slot = index & 1

        @pl.when(index + 1 < count)
        def _():
            slope_copy(index + 1, 1 - slot).start()

        back = conv_block(pull_ref, w2t_ref, start, block, True)
        slope_copy(index, slot).wait()
        pull = (back * slope_ref[slot]).astype(BF16).astype(F32)
        pull = pull.reshape(block, steps, 16, chans)
        last, head = pull[:, steps - 1], pull[:, 0]
        before = jnp.concatenate([last[:, 15:], last[:, :15]], axis=1)
        after = jnp.concatenate([head[:, 1:], head[:, :1]], axis=1)
        to = pl.ds(1 + start, block)
        first_ref[to, 1 : 1 + steps] = pull.astype(BF16)
        first_ref[to, 0] = before.astype(BF16)
        first_ref[to, steps + 1] = after.astype(BF16)
        return carry

    lax.fori_loop(0, count, step, 0)
    hidden_copy.wait()
    tap_sums(hidden_ref, pull_ref, g2_ref)
    state_copy.wait()
    tap_sums(state_ref, first_ref, g1_ref)

    top = lax.axis_index("lat") * rows
    left = lax.axis_index("lon") * cols
    place = iota((3 * cols, lons), 0)
    shift = 1 - lax.shift_right_logical(place, cols.bit_length() - 1)
    lon = left + (place & (cols - 1)) + shift
    lon = jnp.where(lon < 0, lon + lons, jnp.where(lon >= lons, lon - lons, lon))
    column = iota((3 * cols, lons), 1)
    theirs = (column & 15) * steps + lax.shift_right_logical(column, 4)
    select = jnp.where(theirs == lon, 1.0, 0.0).astype(BF16)
    for row in range(rows + 2):
        line = first_ref[top + row, 1 : 1 + steps].reshape(lons, chans)
        near = dot(select, line).astype(BF16)
        for b in range(3):
            near_ref[b, row * cols : (row + 1) * cols, :] = near[b * cols : (b + 1) * cols]
    total = adj_ref[...]
    for a in range(3):
        for b in range(3):
            total = total + dot_nt(
                near_ref[b, (2 - a) * cols : (2 - a + rows) * cols, :], w1_ref[3 * a + b]
            )
    grad_ref[...] = total


def tail(pull_all, slope, hidden, state, w2t, w1, adjoint):
    bands, tiles, rows, group, chans = pull_all.shape
    lats, lons = bands * rows, tiles * group
    steps = lons // 16
    block = 512 // lons
    padded = pltpu.VMEM((lats + 2, steps + 2, 16, chans), BF16)
    return pl.pallas_call(
        functools.partial(tail_kernel, block),
        out_shape=[
            jax.ShapeDtypeStruct((rows * group, chans), F32),
            jax.ShapeDtypeStruct((9, chans, chans), F32),
            jax.ShapeDtypeStruct((9, chans, chans), F32),
        ],
        in_specs=[vmem()] + [pl.BlockSpec(memory_space=pl.ANY)] * 3 + [vmem()] * 3,
        out_specs=[vmem()] * 3,
        scratch_shapes=[
            padded,
            padded,
            pltpu.VMEM((3, (rows + 2) * group, chans), BF16),
            pltpu.VMEM((2, block * lons, chans), F32),
            pltpu.VMEM((chans, lats * lons), BF16),
            pltpu.VMEM((chans, lats * lons), BF16),
            pltpu.SemaphoreType.DMA((2,)),
            pltpu.SemaphoreType.DMA((2,)),
        ],
        compiler_params=params(),
        name="tail",
    )(pull_all, slope, hidden, state, w2t, w1, adjoint)


def with_halo(x, axis, dim, width, wrap):
    count, length = (lax.axis_size(axis), x.shape[dim])
    up = [(i, (i + 1) % count) for i in range(count if wrap else count - 1)]
    down = [(j, i) for i, j in up]
    last = lax.slice_in_dim(x, length - width, length, axis=dim)
    first = lax.slice_in_dim(x, 0, width, axis=dim)
    before = lax.ppermute(last, axis, up)
    after = lax.ppermute(first, axis, down)
    return jnp.concatenate([before, x, after], axis=dim)


def gather_tiles(x):
    bands, tiles = lax.axis_size("lat"), lax.axis_size("lon")
    everything = lax.all_gather(x, ("lat", "lon"), axis=0, tiled=False)
    return everything.reshape((bands, tiles) + x.shape)


def per_device(
    state, weight_first, weight_second, obs_owner, obs_cell, obs_level, obs_count, obs_frac,
    obs_value, obs_weight,
):
    rows, cols, chans = state.shape
    bands = lax.axis_size("lat")
    devices = lax.axis_size(("lat", "lon"))
    slots = max(2, 3 * obs_value.shape[0] // (2 * devices))
    outgoing = route(
        devices, slots, chans, obs_owner, obs_cell, obs_level, obs_count, obs_frac, obs_value,
        obs_weight,
    )
    got = lax.all_to_all(outgoing, ("lat", "lon"), split_axis=0, concat_axis=0, tiled=True)
    wide = with_halo(with_halo(state, "lon", 1, 2, True), "lat", 0, 2, False)
    state_all = gather_tiles(state)
    adjoint, pullback = forward(slots, bands, wide, weight_first, weight_second, got)
    pull_all = gather_tiles(pullback.reshape(rows, cols, chans))
    slope, hidden, turned, w2t = whole(state_all, weight_first, weight_second)
    grad, g1, g2 = tail(pull_all, slope, hidden, turned, w2t, weight_first, adjoint)
    return grad.reshape(rows, cols, chans), g1, g2


def solution(mesh):
    both = P(("lat", "lon"), None)
    placed = (
        P("lat", "lon", None),
        P(),
        P(),
        both,
        both,
        both,
        P(("lat", "lon")),
        P(("lat", "lon"), None, None),
        both,
        both,
    )
    return jax.shard_map(
        per_device,
        mesh=mesh,
        in_specs=placed,
        out_specs=(P("lat", "lon", None), P(), P()),
        check_vma=False,
    )
```

time: 295 us -> 162 us (0.55)
  waiting for transfers between devices: 146 us -> 73.9 us
  matrix products: 63.9 us -> 0 us
  Pallas kernels: 0 us -> 55.9 us
  starting transfers between devices: 42.4 us -> 14.2 us
  local copies, waits for them, and re-layouts: 18.4 us -> 1.45 us
  other arithmetic: 8 us -> 2.31 us
    psum x1 -> x0, waiting for transfers between devices: 134 us -> none  [per_device(): lax.psum((local_first, local_second), ('lat', 'lon'))]
    all_gather x0 -> x2, waiting for transfers between devices: none -> 68.8 us  [gather_tiles(): everything = lax.all_gather(x, ('lat', 'lon'), axis=0, tiled=False)]
    dot_general x66 -> x0, matrix products: 63.9 us -> none  [the longest x6 23.5 us: advance(): jnp.dot(weights, grid, precision=lax.Precision.HIGHEST, preferred_element...]
    pallas_call x0 -> x4, Pallas kernels: none -> 55.9 us  [the longest x1 25.6 us: tail(): pl.pallas_call(functools.partial(tail_kernel, block), out_shape=[jax.Shap...]
    ppermute x8 -> x2, starting transfers between devices: 19.9 us -> 5.39 us  [with_halo(): after = lax.ppermute(first, axis, down)]
    ppermute x8 -> x2, starting transfers between devices: 18 us -> 4.21 us  [with_halo(): before = lax.ppermute(last, axis, up)]
    unnamed x41 -> x2, local copies, waits for them, and re-layouts: 9.76 us -> 0.66 us
    scatter x1 -> x0, local copies, waits for them, and re-layouts: 4.36 us -> none  [route_blocks(): jnp.zeros((devices * slots, 7, width), jnp.float32).at[target].set(packed)]
  transfers between devices with their start and end apart: 18 -> 7, of which waited for: 6 -> 4; matrix products, arithmetic and copies ran while one was open for 10% -> 2% of each run, Pallas kernels for 0% -> 19%
where the time goes in v1:
time: 162 us
  waiting for transfers between devices  73.9 us (46%)
  Pallas kernels  55.9 us (35%)
  starting transfers between devices  14.2 us (9%)
  between operations  14.1 us (9%)
  other arithmetic  2.31 us (1%)
    all_gather x2, waiting for transfers between devices, gather_tiles(): everything = lax.all_gather(x, ('lat', 'lon'), axis=0, tiled=False)  68.8 us
    pallas_call x1, Pallas kernels, tail(): pl.pallas_call(functools.partial(tail_kernel, block), out_shape=[jax.Shap...  25.6 us
    pallas_call x1, Pallas kernels, whole(): pl.pallas_call(functools.partial(whole_kernel, block), out_shape=[jax.Sha...  14.8 us
    pallas_call x1, Pallas kernels, forward(): pl.pallas_call(functools.partial(forward_kernel, slots, tiles, group), ou...  12.8 us
    ppermute x2, starting transfers between devices, with_halo(): after = lax.ppermute(first, axis, down)  5.39 us
    all_to_all x1, starting transfers between devices, per_device(): lax.all_to_all(outgoing, ('lat', 'lon'), split_axis=0, concat_axis=0, til...  4.49 us
    ppermute x2, waiting for transfers between devices, with_halo(): after = lax.ppermute(first, axis, down)  4.22 us
    ppermute x2, starting transfers between devices, with_halo(): before = lax.ppermute(last, axis, up)  4.21 us
  transfers between devices with their start and end apart: 7, of which 4 were waited for; matrix products, arithmetic and copies ran while one was open for 2% of the time, Pallas kernels for 19%

profile of v1, /device:TPU:0, one launch (start us, length us, event | category | flops | bytes accessed | tf_op | source)
XLA Modules:
  0.0 161.8 jit_solution(3711478181249880214)
XLA Ops:
  7.2 0.0 all-gather.6.cloned.1.call-start
  7.2 0.7 all-gather.6.cloned.1.call-update
  7.9 0.8 fusion
  8.7 0.5 collective-permute-start
  9.2 4.1 %collective-permute-start.1 = (bf16[8,2,256]{2,1,0:T(2,128)(2,1)S(1)}, bf16[8,2,256]{2,1,0:T(2,128)(2,1)S(1)}, u32[]{:S(2)}, u32[]{:S(2)}) collective-permute-start(bf16[8,2,256]{2,1,0:T(2,128)(2,1)S(1)} %get-tuple-element.24), channel_id=1, source_target_pairs={{1,0},{2,1},{3,2},{4,3},{5,4},{6,5},{7,6},{0,7},{9,8},{10,9},{11,1... | collective-permute-start | bytes 24584 | tf_op jit(solution)/shard_map/ppermute | solution.py:460
  13.3 2.7 %route.1 = f32[32,8,128]{2,1,0:T(8,128)} custom-call(s32[1,128]{1,0:T(1,128)} %bitcast.19, s32[1,128]{1,0:T(1,128)} %bitcast.20, s32[32,128]{1,0:T(8,128)} %bitcast.15, s32[32,128]{1,0:T(8,128)} %bitcast.16, f32[2,32,128]{2,1,0:T(8,128)} %bitcast.14, f32[32,128]{1,0:T(8,128)} %bitcast.17, f32[32,128]{1,0:T(8,128)} %bitcast.18), custom_call_target="tpu_custom_call" | custom-call | tf_op jit(solution)/shard_map/route/pallas_call | solution.py:89
  16.0 4.5 %all-to-all-start = ((f32[32,8,128]{2,1,0:T(8,128)}), f32[32,8,128]{2,1,0:T(8,128)S(1)}, u32[]{:S(2)}, u32[]{:S(2)}) async-start(f32[32,8,128]{2,1,0:T(8,128)} %route.1), calls=%async_computation | async-start | bytes 262144 | tf_op jit(solution)/shard_map/all_to_all | solution.py:482
  20.5 0.0 all-gather.4.cloned.1.call-start
  20.6 0.0 collective-permute-done
  20.6 0.0 collective-permute-done.1
  20.6 0.8 pad_maximum_fusion.3
  21.4 3.7 %collective-permute-start.2 = (bf16[2,20,256]{2,1,0:T(8,128)(2,1)S(1)}, bf16[2,20,256]{2,1,0:T(8,128)(2,1)S(1)}, u32[]{:S(2)}, u32[]{:S(2)}) collective-permute-start(bf16[2,20,256]{2,1,0:T(8,128)(2,1)S(1)} %get-tuple-element.21), channel_id=1, source_target_pairs={{0,8},{8,16},{16,24},{1,9},{9,17},{17,25},{2,10},{10,18},{18,26},{... | collective-permute-start | bytes 61448 | tf_op jit(solution)/shard_map/ppermute | solution.py:459
  25.1 1.3 collective-permute-start.3
  26.4 0.2 collective-permute-done.2
  26.6 4.2 %collective-permute-done.3 = bf16[2,20,256]{2,1,0:T(8,128)(2,1)S(1)} collective-permute-done((bf16[2,20,256]{2,1,0:T(8,128)(2,1)S(1)}, bf16[2,20,256]{2,1,0:T(8,128)(2,1)S(1)}, u32[]{:S(2)}, u32[]{:S(2)}) %collective-permute-start.3) | collective-permute-done | bytes 20512 | tf_op jit(solution)/shard_map/ppermute | solution.py:460
  30.8 1.5 pad_maximum_fusion.wide_ref
  32.3 0.0 all-to-all-done.got_ref
  32.3 0.0 copy-start
  32.3 0.7 copy-done
  33.0 12.8 %forward.1 = (f32[128,256]{1,0:T(8,128)}, bf16[128,256]{1,0:T(8,128)(2,1)}) custom-call(bf16[12,20,256]{2,1,0:T(8,128)(2,1)} %pad_maximum_fusion.wide_ref, bf16[9,256,256]{2,1,0:T(8,128)(2,1)} %w1_ref.5, bf16[9,256,256]{2,1,0:T(8,128)(2,1)} %w2_ref.3, f32[32,8,128]{2,1,0:T(8,128)} %copy-done), custom_call_target="tpu_custom_call" | custom-call | tf_op jit(solution)/shard_map/forward/pallas_call | solution.py:221
  45.8 0.0 all-gather.4.cloned.1.call-update
  45.8 24.7 %all-gather.6.cloned.1.call-done = bf16[256,16,256]{2,1,0:T(8,128)(2,1)} async-done(((bf16[8,16,256]{2,1,0:T(8,128)(2,1)}), bf16[256,16,256]{2,1,0:T(8,128)(2,1)}) %all-gather.6.cloned.1.call-update) | async-done | bytes 2097168 | tf_op jit(solution)/shard_map/all_gather | solution.py:466
  70.5 14.8 %whole.1 = (f32[4096,256]{1,0:T(8,128)}, bf16[256,4096]{1,0:T(8,128)(2,1)}, bf16[256,4096]{1,0:T(8,128)(2,1)}, bf16[9,256,256]{2,1,0:T(8,128)(2,1)}) custom-call(bf16[4,8,8,16,256]{4,3,2,1,0:T(8,128)(2,1)} %bitcast.12, bf16[9,256,256]{2,1,0:T(8,128)(2,1)} %w1_ref.5, bf16[9,256,256]{2,1,0:T(8,128)(2,1)} %w2_ref.3), custom_call_target="tpu_custom_call" | custom-call | tf_op jit(solution)/shard_map/whole/pallas_call | solution.py:308
  85.3 44.1 %all-gather.4.cloned.1.call-done = bf16[32,8,16,256]{3,2,1,0:T(8,128)(2,1)} async-done(((bf16[1,8,16,256]{3,2,1,0:T(8,128)(2,1)}), bf16[32,8,16,256]{3,2,1,0:T(8,128)(2,1)}) %all-gather.4.cloned.1.call-update) | async-done | bytes 2097168 | tf_op jit(solution)/shard_map/all_gather | solution.py:466
  129.4 25.6 %tail.1 = (f32[128,256]{1,0:T(8,128)}, f32[9,256,256]{2,1,0:T(8,128)}, f32[9,256,256]{2,1,0:T(8,128)}) custom-call(bf16[4,8,8,16,256]{4,3,2,1,0:T(8,128)(2,1)} %bitcast.11, f32[4096,256]{1,0:T(8,128)} %get-tuple-element.13.slope_hbm, bf16[256,4096]{1,0:T(8,128)(2,1)} %get-tuple-element.14.hidden_hbm, bf16[256,4096]{1,0:T(8,128)(2,1)} %get-tuple-element.15.state_hbm, ...), custom_call_target="tpu_custom_call" | custom-call | tf_op jit(solution)/shard_map/tail/pallas_call | solution.py:429
Async XLA Ops:
  7.2 63.3 %all-gather.6.cloned.1.call-start = ((), (), s32[]{:S(2)}) async-start(), calls=%async_computation.2 | async-start | bytes 2162688 | tf_op jit(solution)/shard_map/all_gather | solution.py:466
  8.7 11.9 %collective-permute-start = (bf16[8,2,256]{2,1,0:T(2,128)(2,1)S(1)}, bf16[8,2,256]{2,1,0:T(2,128)(2,1)S(1)}, u32[]{:S(2)}, u32[]{:S(2)}) collective-permute-start(bf16[8,2,256]{2,1,0:T(2,128)(2,1)S(1)} %get-tuple-element.23), channel_id=1, source_target_pairs={{0,1},{1,2},{2,3},{3,4},{4,5},{5,6},{6,7},{7,0},{8,9},{9,10},{10,1... | collective-permute-start | bytes 24584 | tf_op jit(solution)/shard_map/ppermute | solution.py:459
  9.2 11.4 %collective-permute-start.1 = (bf16[8,2,256]{2,1,0:T(2,128)(2,1)S(1)}, bf16[8,2,256]{2,1,0:T(2,128)(2,1)S(1)}, u32[]{:S(2)}, u32[]{:S(2)}) collective-permute-start(bf16[8,2,256]{2,1,0:T(2,128)(2,1)S(1)} %get-tuple-element.24), channel_id=1, source_target_pairs={{1,0},{2,1},{3,2},{4,3},{5,4},{6,5},{7,6},{0,7},{9,8},{10,9},{11,1... | collective-permute-start | bytes 24584 | tf_op jit(solution)/shard_map/ppermute | solution.py:460
  16.0 16.3 %all-to-all-start = ((f32[32,8,128]{2,1,0:T(8,128)}), f32[32,8,128]{2,1,0:T(8,128)S(1)}, u32[]{:S(2)}, u32[]{:S(2)}) async-start(f32[32,8,128]{2,1,0:T(8,128)} %route.1), calls=%async_computation | async-start | bytes 262144 | tf_op jit(solution)/shard_map/all_to_all | solution.py:482
  20.5 108.9 %all-gather.4.cloned.1.call-start = ((), (), s32[]{:S(2)}) async-start(), calls=%async_computation.1 | async-start | bytes 2162688 | tf_op jit(solution)/shard_map/all_gather | solution.py:466
  21.4 5.2 %collective-permute-start.2 = (bf16[2,20,256]{2,1,0:T(8,128)(2,1)S(1)}, bf16[2,20,256]{2,1,0:T(8,128)(2,1)S(1)}, u32[]{:S(2)}, u32[]{:S(2)}) collective-permute-start(bf16[2,20,256]{2,1,0:T(8,128)(2,1)S(1)} %get-tuple-element.21), channel_id=1, source_target_pairs={{0,8},{8,16},{16,24},{1,9},{9,17},{17,25},{2,10},{10,18},{18,26},{... | collective-permute-start | bytes 61448 | tf_op jit(solution)/shard_map/ppermute | solution.py:459
  25.1 5.7 %collective-permute-start.3 = (bf16[2,20,256]{2,1,0:T(8,128)(2,1)S(1)}, bf16[2,20,256]{2,1,0:T(8,128)(2,1)S(1)}, u32[]{:S(2)}, u32[]{:S(2)}) collective-permute-start(bf16[2,20,256]{2,1,0:T(8,128)(2,1)S(1)} %get-tuple-element.22), channel_id=1, source_target_pairs={{8,0},{16,8},{24,16},{9,1},{17,9},{25,17},{10,2},{18,10},{26,18},{... | collective-permute-start | bytes 61448 | tf_op jit(solution)/shard_map/ppermute | solution.py:460
  32.3 0.7 copy-start
Sparse Core Ops, SparseCore 0:
  11.0 59.4 all-gather.5
  74.0 55.3 all-gather.3

commit v2 on v1

--- a/solution.py
+++ b/solution.py
@@ -110,7 +110,7 @@
 
 
 def forward_kernel(slots, tiles, group, wide_ref, w1_ref, w2_ref, got_ref, adj_ref, pull_ref,
-                   line_ref, shift_ref, hid_ref, obs_ref):
+                   line_ref, shift_ref, hid_ref, obs_ref, sum_ref):
     rows, cols, chans = (wide_ref.shape[0] - 4, wide_ref.shape[1] - 4, wide_ref.shape[2])
     span = 32
     line_ref[:, 0 : cols + 4, :] = wide_ref[...].astype(F32)
@@ -170,7 +170,7 @@
     obs_ref[0] = obs_ref[0] + lax.shift_right_logical(cell, 4).astype(F32)
     obs_ref[1] = obs_ref[1] + (cell & (cols - 1)).astype(F32)
 
-    adj_ref[...] = jnp.zeros(adj_ref.shape, F32)
+    sum_ref[...] = jnp.zeros(sum_ref.shape, F32)
     count = obs_ref.shape[1] // group
     row_ids = iota((rows, 128), 0, F32)
     col_ids = iota((cols, 128), 0, F32)
@@ -202,14 +202,14 @@
             hot_low.append(jnp.where(masks[piece], misfit - misfit_high, 0.0).astype(BF16))
         hot_high = jnp.concatenate(hot_high, axis=1)
         hot_low = jnp.concatenate(hot_low, axis=1)
-        adj_ref[...] += dot_nt(
-            jnp.concatenate([high, high, low], axis=1),
-            jnp.concatenate([hot_high, hot_low, hot_high], axis=1),
-        )
+        mixed = dot_nt(jnp.concatenate([hot_high, hot_low], axis=0), high)
+        sum_ref[...] += mixed[:chans] + (mixed[chans:] + dot_nt(hot_high, low))
         return carry
 
     lax.fori_loop(0, count, step, 0)
-    pull_ref[...] = adj_ref[...].astype(BF16)
+    adjoint = sum_ref[...].T
+    adj_ref[...] = adjoint
+    pull_ref[...] = adjoint.astype(BF16)
 
 
 def forward(slots, tiles, wide, w1, w2, got):
@@ -231,33 +231,38 @@
             pltpu.VMEM(((rows + 4) * 32, chans), BF16),
             pltpu.VMEM((rows + 2, 32, chans), F32),
             pltpu.VMEM((FIELDS, groups, 128), F32),
+            pltpu.VMEM((chans, rows * cols), F32),
         ],
         compiler_params=params(),
         name="forward",
     )(wide, w1, w2, got)
 
 
-def spread_matrix(steps):
+def spread_matrix(steps, tiles, split):
     lons = 16 * steps
     place = iota(((steps + 2) * 16, lons), 0)
     lon = (place & 15) * steps + lax.shift_right_logical(place, 4) - 1
     lon = jnp.where(lon < 0, lon + lons, jnp.where(lon >= lons, lon - lons, lon))
-    return jnp.where(iota(((steps + 2) * 16, lons), 1) == lon, 1.0, 0.0).astype(BF16)
-
-
-def spread(all_ref, pad_ref):
-    bands, tiles, rows, group, chans = all_ref.shape
+    column = iota(((steps + 2) * 16, lons), 1)
+    if split:
+        half = tiles // 2
+        chunk = lax.shift_right_logical(column, 4)
+        core = lax.shift_right_logical(chunk, half.bit_length() - 1)
+        column = (2 * (chunk & (half - 1)) + core) * 16 + (column & 15)
+    return jnp.where(column == lon, 1.0, 0.0).astype(BF16)
+
+
+def spread(line_of, bands, rows, matrix, pad_ref):
     steps = pad_ref.shape[1] - 2
-    matrix = spread_matrix(steps)
     blank = jnp.zeros(pad_ref.shape[1:], BF16)
     pad_ref[0] = blank
     pad_ref[bands * rows + 1] = blank
 
     def place(band, carry):
         for row in range(rows):
-            line = all_ref[band, :, row].reshape(tiles * group, chans)
+            line = line_of(band, row)
             pad_ref[1 + band * rows + row] = (
-                dot(matrix, line).astype(BF16).reshape(steps + 2, 16, chans)
+                dot(matrix, line).astype(BF16).reshape(steps + 2, 16, line.shape[1])
             )
         return carry
 
@@ -267,14 +272,13 @@
 def conv_block(pad_ref, weight_ref, start, rows, flipped):
     steps = pad_ref.shape[1] - 2
     chans = pad_ref.shape[3]
-    total = None
+    pieces = []
     for a in range(3):
         for b in range(3):
             da, db = (2 - a, 2 - b) if flipped else (a, b)
             piece = pad_ref[pl.ds(start + da, rows), db : db + steps]
-            term = dot(piece.reshape(rows * steps * 16, chans), weight_ref[3 * a + b])
-            total = term if total is None else total + term
-    return total
+            pieces.append(piece.reshape(rows * steps * 16, chans))
+    return dot(jnp.concatenate(pieces, axis=1), weight_ref[...].reshape(9 * chans, chans))
 
 
 def whole_kernel(block, all_ref, w1_ref, w2_ref, slope_ref, hidden_ref, state_ref, w2t_ref, pad_ref):
@@ -282,7 +286,11 @@
     steps = pad_ref.shape[1] - 2
     chans = pad_ref.shape[3]
     size = block * steps * 16
-    spread(all_ref, pad_ref)
+    bands, tiles, rows, group, _ = all_ref.shape
+    spread(
+        lambda band, row: all_ref[band, :, row].reshape(tiles * group, chans),
+        bands, rows, spread_matrix(steps, tiles, False), pad_ref,
+    )
 
     def step(index, carry):
         start = index * block
@@ -321,7 +329,7 @@
     )(state_all, w1, w2)
 
 
-def tap_sums(turned_ref, pad_ref, out_ref):
+def tap_sums(turned_ref, pad_ref, sum_ref, out_ref, sem):
     lats = pad_ref.shape[0] - 2
     steps = pad_ref.shape[1] - 2
     chans = pad_ref.shape[3]
@@ -338,23 +346,27 @@
                 piece.reshape(part * per_row, chans),
             )
             total = term if total is None else total + term
-        out_ref[tap] = total
+        sum_ref[tap] = total
+        pltpu.make_async_copy(sum_ref.at[tap], out_ref.at[tap], sem.at[tap]).start()
         return carry
 
     lax.fori_loop(0, 9, step, 0)
 
 
-def tail_kernel(block, all_ref, slope_hbm, hidden_hbm, state_hbm, w2t_ref, w1_ref, adj_ref,
-                grad_ref, g1_ref, g2_ref, pull_ref, first_ref, near_ref, slope_ref, hidden_ref,
-                state_ref, slope_sems, big_sems):
+def tail_kernel(block, mine_hbm, other_hbm, slope_hbm, hidden_hbm, state_hbm, w2t_ref, w1_ref,
+                adj_ref, grad_ref, g1_hbm, g2_hbm, all_ref, pull_ref, first_ref, near_ref,
+                slope_ref, hidden_ref, state_ref, g1_ref, g2_ref, slope_sems, big_sems,
+                g1_sems, g2_sems):
     lats = pull_ref.shape[0] - 2
     steps = pull_ref.shape[1] - 2
     chans = pull_ref.shape[3]
     lons = steps * 16
     size = block * lons
     count = lats // block
-    rows = all_ref.shape[2]
-    cols = all_ref.shape[3]
+    _, bands, half, rows, cols, _ = all_ref.shape
+    core = lax.axis_index("lon") & 1
+    mine_copy = pltpu.make_async_copy(mine_hbm, all_ref.at[core], big_sems.at[2])
+    other_copy = pltpu.make_async_copy(other_hbm, all_ref.at[1 - core], big_sems.at[3])
     hidden_copy = pltpu.make_async_copy(hidden_hbm, hidden_ref, big_sems.at[0])
     state_copy = pltpu.make_async_copy(state_hbm, state_ref, big_sems.at[1])
 
@@ -362,13 +374,21 @@
         at = pl.ds(pl.multiple_of(index * size, size), size)
         return pltpu.make_async_copy(slope_hbm.at[at, :], slope_ref.at[slot], slope_sems.at[slot])
 
+    mine_copy.start()
+    other_copy.start()
     slope_copy(0, 0).start()
     hidden_copy.start()
     state_copy.start()
-    spread(all_ref, pull_ref)
     blank = jnp.zeros(first_ref.shape[1:], BF16)
     first_ref[0] = blank
     first_ref[lats + 1] = blank
+    matrix = spread_matrix(steps, 2 * half, True)
+    mine_copy.wait()
+    other_copy.wait()
+    spread(
+        lambda band, row: all_ref[:, band, :, row].reshape(lons, chans),
+        bands, rows, matrix, pull_ref,
+    )
 
     def step(index, carry):
         start = index * block
@@ -391,11 +411,11 @@
         first_ref[to, steps + 1] = after.astype(BF16)
         return carry
 
+    hidden_copy.wait()
+    tap_sums(hidden_ref, pull_ref, g2_ref, g2_hbm, g2_sems)
     lax.fori_loop(0, count, step, 0)
-    hidden_copy.wait()
-    tap_sums(hidden_ref, pull_ref, g2_ref)
     state_copy.wait()
-    tap_sums(state_ref, first_ref, g1_ref)
+    tap_sums(state_ref, first_ref, g1_ref, g1_hbm, g1_sems)
 
     top = lax.axis_index("lat") * rows
     left = lax.axis_index("lon") * cols
@@ -418,14 +438,18 @@
                 near_ref[b, (2 - a) * cols : (2 - a + rows) * cols, :], w1_ref[3 * a + b]
             )
     grad_ref[...] = total
-
-
-def tail(pull_all, slope, hidden, state, w2t, w1, adjoint):
-    bands, tiles, rows, group, chans = pull_all.shape
-    lats, lons = bands * rows, tiles * group
+    for tap in range(9):
+        pltpu.make_async_copy(g2_ref.at[tap], g2_hbm.at[tap], g2_sems.at[tap]).wait()
+        pltpu.make_async_copy(g1_ref.at[tap], g1_hbm.at[tap], g1_sems.at[tap]).wait()
+
+
+def tail(mine, other, slope, hidden, state, w2t, w1, adjoint):
+    bands, half, rows, group, chans = mine.shape
+    lats, lons = bands * rows, 2 * half * group
     steps = lons // 16
     block = 512 // lons
     padded = pltpu.VMEM((lats + 2, steps + 2, 16, chans), BF16)
+    anywhere = pl.BlockSpec(memory_space=pl.ANY)
     return pl.pallas_call(
         functools.partial(tail_kernel, block),
         out_shape=[
@@ -433,21 +457,26 @@
             jax.ShapeDtypeStruct((9, chans, chans), F32),
             jax.ShapeDtypeStruct((9, chans, chans), F32),
         ],
-        in_specs=[vmem()] + [pl.BlockSpec(memory_space=pl.ANY)] * 3 + [vmem()] * 3,
-        out_specs=[vmem()] * 3,
+        in_specs=[anywhere] * 5 + [vmem()] * 3,
+        out_specs=[vmem(), anywhere, anywhere],
         scratch_shapes=[
+            pltpu.VMEM((2,) + mine.shape, BF16),
             padded,
             padded,
             pltpu.VMEM((3, (rows + 2) * group, chans), BF16),
             pltpu.VMEM((2, block * lons, chans), F32),
             pltpu.VMEM((chans, lats * lons), BF16),
             pltpu.VMEM((chans, lats * lons), BF16),
+            pltpu.VMEM((9, chans, chans), F32),
+            pltpu.VMEM((9, chans, chans), F32),
             pltpu.SemaphoreType.DMA((2,)),
-            pltpu.SemaphoreType.DMA((2,)),
+            pltpu.SemaphoreType.DMA((4,)),
+            pltpu.SemaphoreType.DMA((9,)),
+            pltpu.SemaphoreType.DMA((9,)),
         ],
         compiler_params=params(),
         name="tail",
-    )(pull_all, slope, hidden, state, w2t, w1, adjoint)
+    )(mine, other, slope, hidden, state, w2t, w1, adjoint)
 
 
 def with_halo(x, axis, dim, width, wrap):
@@ -461,10 +490,20 @@
     return jnp.concatenate([before, x, after], axis=dim)
 
 
+def gather_state(x):
+    return lax.all_gather(lax.all_gather(x, "lon"), "lat")
+
+
 def gather_tiles(x):
     bands, tiles = lax.axis_size("lat"), lax.axis_size("lon")
-    everything = lax.all_gather(x, ("lat", "lon"), axis=0, tiled=False)
-    return everything.reshape((bands, tiles) + x.shape)
+    half = tiles // 2
+    same = [[2 * q + core for q in range(half)] for core in range(2)]
+    copies = jnp.broadcast_to(x[None], (half,) + x.shape)
+    line = lax.all_to_all(copies, "lon", 0, 0, axis_index_groups=same, tiled=True)
+    copies = jnp.broadcast_to(line[None], (bands,) + line.shape)
+    mine = lax.all_to_all(copies, "lat", 0, 0, tiled=True)
+    other = lax.ppermute(mine, "lon", [(i, i ^ 1) for i in range(tiles)])
+    return mine, other
 
 
 def per_device(
@@ -481,11 +520,11 @@
     )
     got = lax.all_to_all(outgoing, ("lat", "lon"), split_axis=0, concat_axis=0, tiled=True)
     wide = with_halo(with_halo(state, "lon", 1, 2, True), "lat", 0, 2, False)
-    state_all = gather_tiles(state)
+    state_all = gather_state(state)
     adjoint, pullback = forward(slots, bands, wide, weight_first, weight_second, got)
-    pull_all = gather_tiles(pullback.reshape(rows, cols, chans))
+    mine, other = gather_tiles(pullback.reshape(rows, cols, chans))
     slope, hidden, turned, w2t = whole(state_all, weight_first, weight_second)
-    grad, g1, g2 = tail(pull_all, slope, hidden, turned, w2t, weight_first, adjoint)
+    grad, g1, g2 = tail(mine, other, slope, hidden, turned, w2t, weight_first, adjoint)
     return grad.reshape(rows, cols, chans), g1, g2
 
 

time: 162 us -> 137 us (0.85)
  waiting for transfers between devices: 73.9 us -> 4.45 us
  blocking collectives: 0 us -> 44.2 us
  local copies, waits for them, and re-layouts: 1.45 us -> 3.38 us
  starting transfers between devices: 14.2 us -> 12.3 us
    all_gather x2 -> x1, waiting for transfers between devices: 68.8 us -> 0.01 us  [gather_state(): return lax.all_gather(lax.all_gather(x, 'lon'), 'lat')]
    all_to_all x0 -> x2, blocking collectives: none -> 26.4 us  [the longest x1 14.4 us: gather_tiles(): mine = lax.all_to_all(copies, 'lat', 0, 0, tiled=True)]
    all_gather x0 -> x1, blocking collectives: none -> 17.8 us  [gather_state(): return lax.all_gather(lax.all_gather(x, 'lon'), 'lat')]
  transfers between devices with their start and end apart: 7 -> 7, of which waited for: 4 -> 2; matrix products, arithmetic and copies ran while one was open for 2% -> 3% of each run, Pallas kernels for 19% -> 22%
where the time goes in v2:
time: 137 us
  Pallas kernels  56 us (41%)
  blocking collectives  44.2 us (32%)
  between operations  14.1 us (10%)
  starting transfers between devices  12.3 us (9%)
  waiting for transfers between devices  4.45 us (3%)
  local copies, waits for them, and re-layouts  3.38 us (2%)
  other arithmetic  2.31 us (2%)
    pallas_call x1, Pallas kernels, tail(): pl.pallas_call(functools.partial(tail_kernel, block), out_shape=[jax.Shap...  26 us
    all_gather x1, blocking collectives, gather_state(): return lax.all_gather(lax.all_gather(x, 'lon'), 'lat')  17.8 us
    pallas_call x1, Pallas kernels, whole(): pl.pallas_call(functools.partial(whole_kernel, block), out_shape=[jax.Sha...  15.1 us
    all_to_all x1, blocking collectives, gather_tiles(): mine = lax.all_to_all(copies, 'lat', 0, 0, tiled=True)  14.4 us
    pallas_call x1, Pallas kernels, forward(): pl.pallas_call(functools.partial(forward_kernel, slots, tiles, group), ou...  12.2 us
    all_to_all x1, blocking collectives, gather_tiles(): lax.all_to_all(copies, 'lon', 0, 0, axis_index_groups=same, tiled=True)  11.9 us
    ppermute x2, starting transfers between devices, with_halo(): after = lax.ppermute(first, axis, down)  4.49 us
    ppermute x2, waiting for transfers between devices, with_halo(): after = lax.ppermute(first, axis, down)  4.22 us
  transfers between devices with their start and end apart: 7, of which 2 were waited for; matrix products, arithmetic and copies ran while one was open for 3% of the time, Pallas kernels for 22%

profile of v2, /device:TPU:0, one launch (start us, length us, event | category | flops | bytes accessed | tf_op | source)
XLA Modules:
  0.0 136.8 jit_solution(1186149863181320865)
XLA Ops:
  7.2 0.0 all-gather.4.cloned.1.call-start
  7.2 17.8 %all-gather = bf16[64,16,256]{2,1,0:T(8,128)(2,1)} all-gather(bf16[8,16,256]{2,1,0:T(8,128)(2,1)} %param.10), channel_id=2, replica_groups=mesh['lat'=4,'lon'=8] {'lon'}, dimensions={0}, use_global_device_ids=true | all-gather | bytes 589824 | tf_op jit(solution)/shard_map/all_gather | solution.py:494
  25.0 0.0 all-gather.4.cloned.1.call-update
  25.0 0.8 fusion
  25.8 0.4 collective-permute-start
  26.2 3.2 %collective-permute-start.1 = (bf16[8,2,256]{2,1,0:T(2,128)(2,1)S(1)}, bf16[8,2,256]{2,1,0:T(2,128)(2,1)S(1)}, u32[]{:S(2)}, u32[]{:S(2)}) collective-permute-start(bf16[8,2,256]{2,1,0:T(2,128)(2,1)S(1)} %get-tuple-element.24), channel_id=1, source_target_pairs={{1,0},{2,1},{3,2},{4,3},{5,4},{6,5},{7,6},{0,7},{9,8},{10,9},{11,1... | collective-permute-start | bytes 24584 | tf_op jit(solution)/shard_map/ppermute | solution.py:489
  29.4 2.7 %route.1 = f32[32,8,128]{2,1,0:T(8,128)} custom-call(s32[1,128]{1,0:T(1,128)} %bitcast.19, s32[1,128]{1,0:T(1,128)} %bitcast.20, s32[32,128]{1,0:T(8,128)} %bitcast.15, s32[32,128]{1,0:T(8,128)} %bitcast.16, f32[2,32,128]{2,1,0:T(8,128)} %bitcast.14, f32[32,128]{1,0:T(8,128)} %bitcast.17, f32[32,128]{1,0:T(8,128)} %bitcast.18), custom_call_target="tpu_custom_call" | custom-call | tf_op jit(solution)/shard_map/route/pallas_call | solution.py:89
  32.1 3.7 %all-to-all-start = ((f32[32,8,128]{2,1,0:T(8,128)}), f32[32,8,128]{2,1,0:T(8,128)S(1)}, u32[]{:S(2)}, u32[]{:S(2)}) async-start(f32[32,8,128]{2,1,0:T(8,128)} %route.1), calls=%async_computation | async-start | bytes 262144 | tf_op jit(solution)/shard_map/all_to_all | solution.py:521
  35.9 0.0 collective-permute-done
  35.9 0.0 collective-permute-done.1
  35.9 0.8 pad_maximum_fusion.3
  36.7 3.7 %collective-permute-start.2 = (bf16[2,20,256]{2,1,0:T(8,128)(2,1)S(1)}, bf16[2,20,256]{2,1,0:T(8,128)(2,1)S(1)}, u32[]{:S(2)}, u32[]{:S(2)}) collective-permute-start(bf16[2,20,256]{2,1,0:T(8,128)(2,1)S(1)} %get-tuple-element.21), channel_id=1, source_target_pairs={{0,8},{8,16},{16,24},{1,9},{9,17},{17,25},{2,10},{10,18},{18,26},{... | collective-permute-start | bytes 61448 | tf_op jit(solution)/shard_map/ppermute | solution.py:488
  40.3 1.3 collective-permute-start.3
  41.6 0.2 collective-permute-done.2
  41.8 4.2 %collective-permute-done.3 = bf16[2,20,256]{2,1,0:T(8,128)(2,1)S(1)} collective-permute-done((bf16[2,20,256]{2,1,0:T(8,128)(2,1)S(1)}, bf16[2,20,256]{2,1,0:T(8,128)(2,1)S(1)}, u32[]{:S(2)}, u32[]{:S(2)}) %collective-permute-start.3) | collective-permute-done | bytes 20512 | tf_op jit(solution)/shard_map/ppermute | solution.py:489
  46.1 1.5 %pad_maximum_fusion.wide_ref = bf16[12,20,256]{2,1,0:T(8,128)(2,1)} fusion(bf16[2,20,256]{2,1,0:T(8,128)(2,1)S(1)} %collective-permute-done.3, bf16[8,2,256]{2,1,0:T(2,128)(2,1)S(1)} %collective-permute-done.1, bf16[8,16,256]{2,1,0:T(8,128)(2,1)} %param.10, bf16[8,2,256]{2,1,0:T(2,128)(2,1)S(1)} %collective-permute-done, ...), kind=kLoop, calls=%fused_computation | loop fusion | flops 614400 | bytes 245760 | tf_op jit(solution)/shard_map/concatenate | solution.py:490
  47.6 0.0 all-to-all-done.got_ref
  47.6 0.0 copy-start.2
  47.6 0.7 copy-done.2
  48.3 12.2 %forward.1 = (f32[128,256]{1,0:T(8,128)}, bf16[128,256]{1,0:T(8,128)(2,1)}) custom-call(bf16[12,20,256]{2,1,0:T(8,128)(2,1)} %pad_maximum_fusion.wide_ref, bf16[9,256,256]{2,1,0:T(8,128)(2,1)} %w1_ref.5, bf16[9,256,256]{2,1,0:T(8,128)(2,1)} %w2_ref.3, f32[32,8,128]{2,1,0:T(8,128)} %copy-done.2), custom_call_target="tpu_custom_call" | custom-call | tf_op jit(solution)/shard_map/forward/pallas_call | solution.py:221
  60.5 0.9 broadcast_in_dim.14
  61.3 11.9 %all_to_all.15 = bf16[4,8,16,256]{3,2,1,0:T(8,128)(2,1)S(1)} all-to-all(bf16[4,8,16,256]{3,2,1,0:T(8,128)(2,1)S(1)} %broadcast_in_dim.14), channel_id=1, replica_groups={{0,2,4,6},{1,3,5,7},{8,10,12,14},{9,11,13,15},{16,18,20,22},{17,19,21,2..., dimensions={0} | all-to-all | bytes 524288 | tf_op jit(solution)/shard_map/all_to_all | solution.py:502
  73.3 0.1 broadcast_in_dim.15
  73.4 14.4 %all_to_all.16.mine_hbm = bf16[4,4,8,16,256]{4,3,2,1,0:T(8,128)(2,1)S(1)} all-to-all(bf16[4,4,8,16,256]{4,3,2,1,0:T(8,128)(2,1)S(1)} %broadcast_in_dim.15), channel_id=1, replica_groups=mesh['lat'=4,'lon'=8] {'lat'}, dimensions={0} | all-to-all | bytes 2097152 | tf_op jit(solution)/shard_map/all_to_all | solution.py:504
  87.8 0.0 copy-start
  87.8 0.0 collective-permute-start.4
  87.8 0.0 all-gather.4.cloned.1.call-done
  87.8 15.1 %whole.1 = (f32[4096,256]{1,0:T(8,128)}, bf16[256,4096]{1,0:T(8,128)(2,1)}, bf16[256,4096]{1,0:T(8,128)(2,1)}, bf16[9,256,256]{2,1,0:T(8,128)(2,1)}) custom-call(bf16[4,8,8,16,256]{4,3,2,1,0:T(8,128)(2,1)} %bitcast.11, bf16[9,256,256]{2,1,0:T(8,128)(2,1)} %w1_ref.5, bf16[9,256,256]{2,1,0:T(8,128)(2,1)} %w2_ref.3), custom_call_target="tpu_custom_call" | custom-call | tf_op jit(solution)/shard_map/whole/pallas_call | solution.py:316
  102.9 0.0 copy-done
  102.9 0.0 collective-permute-done.4.other_hbm
  102.9 0.0 copy-start.1
  103.0 1.0 copy-done.1
  103.9 26.0 %tail.1 = (f32[128,256]{1,0:T(8,128)}, f32[9,256,256]{2,1,0:T(8,128)}, f32[9,256,256]{2,1,0:T(8,128)}) custom-call(bf16[4,4,8,16,256]{4,3,2,1,0:T(8,128)(2,1)} %copy-done, bf16[4,4,8,16,256]{4,3,2,1,0:T(8,128)(2,1)} %copy-done.1, f32[4096,256]{1,0:T(8,128)} %get-tuple-element.13.slope_hbm, bf16[256,4096]{1,0:T(8,128)(2,1)} %get-tuple-element.14.hidden_hbm, ...), custom_call_target="tpu_custom_call" | custom-call | tf_op jit(solution)/shard_map/tail/pallas_call | solution.py:453
Async XLA Ops:
  7.2 80.7 %all-gather.4.cloned.1.call-start = ((), (), s32[]{:S(2)}) async-start(), calls=%async_computation.3 | async-start | bytes 2621440 | tf_op jit(solution)/shard_map/all_gather | solution.py:494
  25.8 10.0 %collective-permute-start = (bf16[8,2,256]{2,1,0:T(2,128)(2,1)S(1)}, bf16[8,2,256]{2,1,0:T(2,128)(2,1)S(1)}, u32[]{:S(2)}, u32[]{:S(2)}) collective-permute-start(bf16[8,2,256]{2,1,0:T(2,128)(2,1)S(1)} %get-tuple-element.23), channel_id=1, source_target_pairs={{0,1},{1,2},{2,3},{3,4},{4,5},{5,6},{6,7},{7,0},{8,9},{9,10},{10,1... | collective-permute-start | bytes 24584 | tf_op jit(solution)/shard_map/ppermute | solution.py:488
  26.2 9.7 %collective-permute-start.1 = (bf16[8,2,256]{2,1,0:T(2,128)(2,1)S(1)}, bf16[8,2,256]{2,1,0:T(2,128)(2,1)S(1)}, u32[]{:S(2)}, u32[]{:S(2)}) collective-permute-start(bf16[8,2,256]{2,1,0:T(2,128)(2,1)S(1)} %get-tuple-element.24), channel_id=1, source_target_pairs={{1,0},{2,1},{3,2},{4,3},{5,4},{6,5},{7,6},{0,7},{9,8},{10,9},{11,1... | collective-permute-start | bytes 24584 | tf_op jit(solution)/shard_map/ppermute | solution.py:489
  32.1 15.5 %all-to-all-start = ((f32[32,8,128]{2,1,0:T(8,128)}), f32[32,8,128]{2,1,0:T(8,128)S(1)}, u32[]{:S(2)}, u32[]{:S(2)}) async-start(f32[32,8,128]{2,1,0:T(8,128)} %route.1), calls=%async_computation | async-start | bytes 262144 | tf_op jit(solution)/shard_map/all_to_all | solution.py:521
  36.7 5.2 %collective-permute-start.2 = (bf16[2,20,256]{2,1,0:T(8,128)(2,1)S(1)}, bf16[2,20,256]{2,1,0:T(8,128)(2,1)S(1)}, u32[]{:S(2)}, u32[]{:S(2)}) collective-permute-start(bf16[2,20,256]{2,1,0:T(8,128)(2,1)S(1)} %get-tuple-element.21), channel_id=1, source_target_pairs={{0,8},{8,16},{16,24},{1,9},{9,17},{17,25},{2,10},{10,18},{18,26},{... | collective-permute-start | bytes 61448 | tf_op jit(solution)/shard_map/ppermute | solution.py:488
  40.3 5.7 %collective-permute-start.3 = (bf16[2,20,256]{2,1,0:T(8,128)(2,1)S(1)}, bf16[2,20,256]{2,1,0:T(8,128)(2,1)S(1)}, u32[]{:S(2)}, u32[]{:S(2)}) collective-permute-start(bf16[2,20,256]{2,1,0:T(8,128)(2,1)S(1)} %get-tuple-element.22), channel_id=1, source_target_pairs={{8,0},{16,8},{24,16},{9,1},{17,9},{25,17},{10,2},{18,10},{26,18},{... | collective-permute-start | bytes 61448 | tf_op jit(solution)/shard_map/ppermute | solution.py:489
  47.6 0.7 copy-start.2
  87.8 15.1 %copy-start = (bf16[4,4,8,16,256]{4,3,2,1,0:T(8,128)(2,1)}, bf16[4,4,8,16,256]{4,3,2,1,0:T(8,128)(2,1)S(1)}, u32[]{:S(2)}) copy-start(bf16[4,4,8,16,256]{4,3,2,1,0:T(8,128)(2,1)S(1)} %all_to_all.16.mine_hbm) | copy-start | bytes 3145732
  87.8 15.1 %collective-permute-start.4 = (bf16[4,4,8,16,256]{4,3,2,1,0:T(8,128)(2,1)S(1)}, bf16[4,4,8,16,256]{4,3,2,1,0:T(8,128)(2,1)S(1)}, u32[]{:S(2)}, u32[]{:S(2)}) collective-permute-start(bf16[4,4,8,16,256]{4,3,2,1,0:T(8,128)(2,1)S(1)} %all_to_all.16.mine_hbm), channel_id=1, source_target_pairs={{0,1},{1,0},{2,3},{3,2},{4,5},{5,4},{6,7},{7,6},{8,9},{9,8},{10,11... | collective-permute-start | bytes 3145736 | tf_op jit(solution)/shard_map/ppermute | solution.py:505
  102.9 1.0 copy-start.1
Sparse Core Ops, SparseCore 0:
  25.1 37.9 all-gather.3

commit v3 on v0

--- a/solution.py
+++ b/solution.py
@@ -1,9 +1,445 @@
+import functools
 import math
 
 import jax
 import jax.numpy as jnp
 from jax import lax
+from jax.experimental import pallas as pl
+from jax.experimental.pallas import tpu as pltpu
 from jax.sharding import PartitionSpec as P
+
+F32 = jnp.float32
+BF16 = jnp.bfloat16
+FIELDS = 5
+WHOLE_CELLS = 4096
+VMEM_LIMIT = 60 * 1024 * 1024
+
+
+def params(limit=VMEM_LIMIT):
+    return pltpu.CompilerParams(vmem_limit_bytes=limit)
+
+
+def vmem():
+    return pl.BlockSpec(memory_space=pltpu.VMEM)
+
+
+def iota(shape, dim, dtype=jnp.int32):
+    return lax.broadcasted_iota(jnp.int32, shape, dim).astype(dtype)
+
+
+def dot(x, y, precision=None):
+    return jnp.dot(x, y, precision=precision, preferred_element_type=F32)
+
+
+def dot_nt(x, y, precision=None):
+    return lax.dot_general(
+        x, y, (((1,), (1,)), ((), ())), precision=precision, preferred_element_type=F32
+    )
+
+
+def slot_layout(slots):
+    full, rest = divmod(slots, 4)
+    rows = full * FIELDS + (0 if rest == 0 else -(-FIELDS // 2))
+    return full, rest, -(-rows // 8) * 8
+
+
+def route_kernel(
+    devices, slots, chans, owner_ref, count_ref, cell_ref, level_ref, frac_ref, value_ref,
+    weight_ref, out_ref
+):
+    width, blocks = value_ref.shape
+    owner = owner_ref[...].astype(F32)
+    across = jnp.broadcast_to(owner, (blocks, blocks))
+    down = across.T
+    earlier = iota((blocks, blocks), 0) < iota((blocks, blocks), 1)
+    hits = jnp.where(jnp.logical_and(across == down, earlier), 1.0, 0.0)
+    rank = jnp.sum(hits, axis=0, keepdims=True)
+    target = rank * float(devices) + owner
+    places = iota((slots * devices, blocks), 0, F32) == target
+    onehot = jnp.where(places, 1.0, 0.0)
+    valid = iota((width, blocks), 0) < count_ref[...]
+    fields = jnp.concatenate(
+        [
+            frac_ref[0],
+            frac_ref[1],
+            value_ref[...],
+            jnp.where(valid, weight_ref[...], 0.0),
+            (cell_ref[...] * chans + level_ref[...]).astype(F32),
+        ],
+        axis=0,
+    )
+    placed = dot_nt(onehot, fields, lax.Precision.HIGHEST)
+    full, rest, rows = slot_layout(slots)
+    out_ref[...] = jnp.zeros(out_ref.shape, F32)
+    for slot in range(slots):
+        for field in range(FIELDS):
+            piece = placed[
+                slot * devices : (slot + 1) * devices, field * width : (field + 1) * width
+            ]
+            if slot < 4 * full:
+                row, lane = (slot // 4) * FIELDS + field, (slot % 4) * width
+            else:
+                row = full * FIELDS + field // 2
+                lane = (field % 2) * 2 * width + (slot - 4 * full) * width
+            out_ref[:, row, lane : lane + width] = piece
+
+
+def route(devices, slots, chans, obs_owner, obs_cell, obs_level, obs_count, obs_frac, obs_value,
+          obs_weight):
+    blocks = obs_value.shape[0]
+    rows = slot_layout(slots)[2]
+    return pl.pallas_call(
+        functools.partial(route_kernel, devices, slots, chans),
+        out_shape=jax.ShapeDtypeStruct((devices, rows, 128), F32),
+        in_specs=[vmem()] * 7,
+        out_specs=vmem(),
+        compiler_params=params(),
+        name="route",
+    )(
+        obs_owner.reshape(1, blocks),
+        obs_count.reshape(1, blocks),
+        obs_cell.T,
+        obs_level.T,
+        jnp.transpose(obs_frac, (1, 2, 0)),
+        obs_value.T,
+        obs_weight.T,
+    )
+
+
+def silu_parts(first):
+    sig = 1.0 / (1.0 + jnp.exp(-first))
+    return sig, first * sig
+
+
+def forward_kernel(slots, tiles, group, parts, *refs):
+    piece_refs, (w1_ref, w2_ref, got_ref, adj_ref, pull_ref) = refs[:9], refs[9:14]
+    line_ref, shift_ref, hid_ref, obs_ref, sum_ref = refs[14:]
+    rows, cols, chans = piece_refs[4].shape
+    span = 32
+    heights, widths = (2, rows, 2), (2, cols, 2)
+    for place in range(9):
+        down, over = place // 3, place % 3
+        y, x = (0, 2, 2 + rows)[down], (0, 2, 2 + cols)[over]
+        line_ref[y : y + heights[down], x : x + widths[over], :] = piece_refs[place][...].astype(F32)
+    line_ref[:, cols + 4 :, :] = jnp.zeros(
+        (rows + 4, line_ref.shape[1] - cols - 4, chans), F32
+    )
+    first = jnp.zeros(((rows + 2) * span, chans), F32)
+    for b in range(3):
+        shift_ref[...] = (
+            line_ref[:, b : b + span, :].astype(BF16).reshape((rows + 4) * span, chans)
+        )
+        for a in range(3):
+            first = first + dot(
+                shift_ref[a * span : a * span + (rows + 2) * span, :], w1_ref[3 * a + b]
+            )
+    hidden = silu_parts(first)[1].astype(BF16).astype(F32).reshape(rows + 2, span, chans)
+    lat = lax.axis_index("lat") * rows + iota((rows + 2, span, chans), 0) - 1
+    hidden = jnp.where(jnp.logical_and(lat >= 0, lat < tiles * rows), hidden, 0.0)
+    hid_ref[...] = hidden
+    total = line_ref[2 : 2 + rows, 2 : 2 + cols, :].reshape(rows * cols, chans)
+    for b in range(3):
+        shift_ref[0 : (rows + 2) * cols, :] = (
+            hid_ref[:, b : b + cols, :].astype(BF16).reshape((rows + 2) * cols, chans)
+        )
+        for a in range(3):
+            total = total + dot(
+                shift_ref[a * cols : a * cols + rows * cols, :], w2_ref[3 * a + b]
+            )
+    cells = rows * cols
+    turned = total.T
+    grid_high = turned.astype(BF16)
+    grid_low = (turned - grid_high.astype(F32)).astype(BF16)
+    grid_both = jnp.concatenate([grid_high, grid_low], axis=1)
+
+    devices = got_ref.shape[0]
+    full, rest, _ = slot_layout(slots)
+    half = devices // 2
+    for field in range(FIELDS):
+        for part in range(full):
+            obs_ref[field, part * devices : (part + 1) * devices, :] = got_ref[
+                :, part * FIELDS + field, :
+            ]
+        if rest:
+            tail = got_ref[:, full * FIELDS + field // 2, :]
+            low, high = tail[:half], tail[half:]
+            if field % 2 == 0:
+                high = pltpu.roll(high, 64, 1)
+            else:
+                low = pltpu.roll(low, 64, 1)
+            obs_ref[field, full * devices : full * devices + half, :] = jnp.where(
+                iota((half, 128), 1) < 64, low, high
+            )
+    code = obs_ref[4].astype(jnp.int32)
+    shift = chans.bit_length() - 1
+    cell = lax.shift_right_logical(code, shift)
+    obs_ref[4] = (code & (chans - 1)).astype(F32)
+    obs_ref[0] = obs_ref[0] + lax.shift_right_logical(cell, 4).astype(F32)
+    obs_ref[1] = obs_ref[1] + (cell & (cols - 1)).astype(F32)
+
+    sum_ref[...] = jnp.zeros(sum_ref.shape, F32)
+    count = obs_ref.shape[1] // (group * parts)
+    row_ids = iota((rows, 128), 0, F32)
+    col_ids = iota((cols, 128), 0, F32)
+    level_ids = iota((chans, 128), 0, F32)
+
+    def add_group(start):
+        high, low, masks, marks = [], [], [], []
+        for piece in range(group):
+            mark = [obs_ref[field, pl.ds(start + piece, 1), :] for field in range(FIELDS)]
+            up = jnp.maximum(0.0, 1.0 - jnp.abs(row_ids - mark[0]))
+            along = jnp.maximum(0.0, 1.0 - jnp.abs(col_ids - mark[1]))
+            weights = (up[:, None, :] * along[None, :, :]).reshape(cells, 128)
+            weights_high = weights.astype(BF16)
+            high.append(weights_high)
+            low.append((weights - weights_high.astype(F32)).astype(BF16))
+            masks.append(level_ids == mark[4])
+            marks.append(mark)
+        high = jnp.concatenate(high, axis=1)
+        low = jnp.concatenate(low, axis=1)
+        sampled = dot(grid_both, jnp.concatenate([high, high], axis=0)) + dot(grid_high, low)
+        hot_high, hot_low = [], []
+        for piece in range(group):
+            mine = sampled[:, piece * 128 : (piece + 1) * 128]
+            predicted = jnp.sum(jnp.where(masks[piece], mine, 0.0), axis=0, keepdims=True)
+            misfit = marks[piece][3] * (predicted - marks[piece][2])
+            misfit_high = misfit.astype(BF16).astype(F32)
+            hot_high.append(jnp.where(masks[piece], misfit_high, 0.0).astype(BF16))
+            hot_low.append(jnp.where(masks[piece], misfit - misfit_high, 0.0).astype(BF16))
+        hot_high = jnp.concatenate(hot_high, axis=1)
+        hot_low = jnp.concatenate(hot_low, axis=1)
+        mixed = dot_nt(jnp.concatenate([hot_high, hot_low], axis=0), high)
+        return mixed[:chans] + (mixed[chans:] + dot_nt(hot_high, low))
+
+    def step(index, carry):
+        total = sum_ref[...]
+        for part in range(parts):
+            total = total + add_group((index * parts + part) * group)
+        sum_ref[...] = total
+        return carry
+
+    lax.fori_loop(0, count, step, 0)
+    adjoint = sum_ref[...].T
+    adj_ref[...] = adjoint
+    pull_ref[...] = adjoint.astype(BF16)
+
+
+def forward(slots, tiles, pieces, w1, w2, got):
+    rows, cols, chans = pieces[4].shape
+    devices = got.shape[0]
+    full, rest, _ = slot_layout(slots)
+    groups = full * devices + (devices // 2 if rest else 0)
+    return pl.pallas_call(
+        functools.partial(forward_kernel, slots, tiles, 2, 4),
+        out_shape=[
+            jax.ShapeDtypeStruct((rows * cols, chans), F32),
+            jax.ShapeDtypeStruct((rows * cols, chans), BF16),
+        ],
+        in_specs=[vmem()] * 12,
+        out_specs=[vmem()] * 2,
+        scratch_shapes=[
+            pltpu.VMEM((rows + 4, 40, chans), F32),
+            pltpu.VMEM(((rows + 4) * 32, chans), BF16),
+            pltpu.VMEM((rows + 2, 32, chans), F32),
+            pltpu.VMEM((FIELDS, groups, 128), F32),
+            pltpu.VMEM((chans, rows * cols), F32),
+        ],
+        compiler_params=params(),
+        name="forward",
+    )(*pieces, w1, w2, got)
+
+
+def spread_matrix(steps, tiles, split):
+    lons = 16 * steps
+    place = iota(((steps + 2) * 16, lons), 0)
+    lon = (place & 15) * steps + lax.shift_right_logical(place, 4) - 1
+    lon = jnp.where(lon < 0, lon + lons, jnp.where(lon >= lons, lon - lons, lon))
+    column = iota(((steps + 2) * 16, lons), 1)
+    if split:
+        half = tiles // 2
+        chunk = lax.shift_right_logical(column, 4)
+        core = lax.shift_right_logical(chunk, half.bit_length() - 1)
+        column = (2 * (chunk & (half - 1)) + core) * 16 + (column & 15)
+    return jnp.where(column == lon, 1.0, 0.0).astype(BF16)
+
+
+def spread(line_of, bands, rows, matrix, pad_ref):
+    steps = pad_ref.shape[1] - 2
+    blank = jnp.zeros(pad_ref.shape[1:], BF16)
+    pad_ref[0] = blank
+    pad_ref[bands * rows + 1] = blank
+
+    def place(band, carry):
+        for row in range(rows):
+            line = line_of(band, row)
+            pad_ref[1 + band * rows + row] = (
+                dot(matrix, line).astype(BF16).reshape(steps + 2, 16, line.shape[1])
+            )
+        return carry
+
+    lax.fori_loop(0, bands, place, 0)
+
+
+def spread_state_kernel(all_ref, pad_ref):
+    bands, tiles, rows, group, chans = all_ref.shape
+    matrix = spread_matrix(pad_ref.shape[1] - 2, tiles, False)
+    spread(
+        lambda band, row: all_ref[band, :, row].reshape(tiles * group, chans),
+        bands, rows, matrix, pad_ref,
+    )
+
+
+def spread_state(state_all):
+    bands, tiles, rows, group, chans = state_all.shape
+    return pl.pallas_call(
+        spread_state_kernel,
+        out_shape=jax.ShapeDtypeStruct((bands * rows + 2, tiles * group // 16 + 2, 16, chans), BF16),
+        in_specs=[vmem()],
+        out_specs=vmem(),
+        compiler_params=params(),
+        name="spread_state",
+    )(state_all)
+
+
+def spread_pull_kernel(mine_hbm, other_hbm, pad_ref, plain_ref, all_ref, sems):
+    _, bands, half, rows, cols, chans = all_ref.shape
+    steps = plain_ref.shape[1]
+    core = lax.axis_index("lon") & 1
+    copies = [
+        pltpu.make_async_copy(mine_hbm, all_ref.at[core], sems.at[0]),
+        pltpu.make_async_copy(other_hbm, all_ref.at[1 - core], sems.at[1]),
+    ]
+    for copy in copies:
+        copy.start()
+    matrix = spread_matrix(steps, 2 * half, True)
+    for copy in copies:
+        copy.wait()
+    spread(
+        lambda band, row: all_ref[:, band, :, row].reshape(steps * 16, chans),
+        bands, rows, matrix, pad_ref,
+    )
+    plain_ref[...] = pad_ref[1 : bands * rows + 1, 1 : steps + 1]
+
+
+def spread_pull(mine, other):
+    bands, half, rows, group, chans = mine.shape
+    lats, steps = bands * rows, 2 * half * group // 16
+    return pl.pallas_call(
+        spread_pull_kernel,
+        out_shape=[
+            jax.ShapeDtypeStruct((lats + 2, steps + 2, 16, chans), BF16),
+            jax.ShapeDtypeStruct((lats, steps, 16, chans), BF16),
+        ],
+        in_specs=[pl.BlockSpec(memory_space=pl.ANY)] * 2,
+        out_specs=[vmem()] * 2,
+        scratch_shapes=[pltpu.VMEM((2,) + mine.shape, BF16), pltpu.SemaphoreType.DMA((2,))],
+        compiler_params=params(),
+        name="spread_pull",
+    )(mine, other)
+
+
+def pad_kernel(plain_ref, pad_ref):
+    lats, steps, group, chans = plain_ref.shape
+    blank = jnp.zeros(pad_ref.shape[1:], BF16)
+    pad_ref[0] = blank
+    pad_ref[lats + 1] = blank
+
+    def step(lat, carry):
+        pad_ref[lat + 1, 1 : steps + 1] = plain_ref[lat]
+        last = plain_ref[lat, steps - 1].astype(F32)
+        head = plain_ref[lat, 0].astype(F32)
+        pad_ref[lat + 1, 0] = jnp.concatenate([last[15:], last[:15]], axis=0).astype(BF16)
+        pad_ref[lat + 1, steps + 1] = jnp.concatenate([head[1:], head[:1]], axis=0).astype(BF16)
+        return carry
+
+    lax.fori_loop(0, lats, step, 0, unroll=4)
+
+
+def pad(plain):
+    lats, steps, group, chans = plain.shape
+    return pl.pallas_call(
+        pad_kernel,
+        out_shape=jax.ShapeDtypeStruct((lats + 2, steps + 2, group, chans), BF16),
+        in_specs=[vmem()],
+        out_specs=vmem(),
+        compiler_params=params(),
+        name="pad",
+    )(plain)
+
+
+def conv(padded, weight):
+    chans = weight.shape[1]
+    return lax.conv_general_dilated(
+        padded, weight.reshape(3, 3, chans, -1), (1, 1), "VALID",
+        dimension_numbers=("HWNC", "HWIO", "HWNC"), preferred_element_type=F32,
+    )
+
+
+def convt(padded, weight):
+    chans = weight.shape[1]
+    return lax.conv_general_dilated(
+        padded, lax.rev(weight.reshape(3, 3, chans, -1), (0, 1)), (1, 1), "VALID",
+        dimension_numbers=("HWNC", "HWOI", "HWNC"), preferred_element_type=F32,
+    )
+
+
+def tap_grads(padded, pull):
+    chans = pull.shape[3]
+    grads = lax.conv_general_dilated(
+        padded, pull, (1, 1), "VALID",
+        dimension_numbers=("HWCN", "HWIO", "HWNC"), preferred_element_type=F32,
+    )
+    return grads.reshape(9, -1, chans)
+
+
+def local_kernel(rows, cols, pull_hbm, w1_ref, adj_ref, grad_ref, pull_ref, near_ref, sem):
+    lats, steps, _, chans = pull_hbm.shape
+    lons = steps * 16
+    top = lax.axis_index("lat") * rows - 1
+    begin = jnp.clip(top, 0, lats - rows - 2)
+    copy = pltpu.make_async_copy(pull_hbm.at[pl.ds(begin, rows + 2)], pull_ref, sem)
+    copy.start()
+    left = lax.axis_index("lon") * cols
+    place = iota((3 * cols, lons), 0)
+    shift = 1 - lax.shift_right_logical(place, cols.bit_length() - 1)
+    lon = left + (place & (cols - 1)) + shift
+    lon = jnp.where(lon < 0, lon + lons, jnp.where(lon >= lons, lon - lons, lon))
+    column = iota((3 * cols, lons), 1)
+    theirs = (column & 15) * steps + lax.shift_right_logical(column, 4)
+    select = jnp.where(theirs == lon, 1.0, 0.0)
+    copy.wait()
+    for row in range(rows + 2):
+        lat = top + row
+        inside = jnp.logical_and(lat >= 0, lat < lats)
+        line = pull_ref[jnp.clip(lat - begin, 0, rows + 1)].reshape(lons, chans)
+        chosen = jnp.where(inside, select, 0.0).astype(BF16)
+        near = dot(chosen, line).astype(BF16)
+        for b in range(3):
+            near_ref[b, row * cols : (row + 1) * cols, :] = near[b * cols : (b + 1) * cols]
+    total = adj_ref[...]
+    for a in range(3):
+        for b in range(3):
+            total = total + dot_nt(
+                near_ref[b, (2 - a) * cols : (2 - a + rows) * cols, :], w1_ref[3 * a + b]
+            )
+    grad_ref[...] = total
+
+
+def local_grad(rows, cols, pull, w1, adjoint):
+    lats, steps, _, chans = pull.shape
+    return pl.pallas_call(
+        functools.partial(local_kernel, rows, cols),
+        out_shape=jax.ShapeDtypeStruct((rows * cols, chans), F32),
+        in_specs=[pl.BlockSpec(memory_space=pl.ANY), vmem(), vmem()],
+        out_specs=vmem(),
+        scratch_shapes=[
+            pltpu.VMEM((rows + 2, steps, 16, chans), BF16),
+            pltpu.VMEM((3, (rows + 2) * cols, chans), BF16),
+            pltpu.SemaphoreType.DMA,
+        ],
+        compiler_params=params(),
+        name="local_grad",
+    )(pull, w1, adjoint)
 
 
 def with_halo(x, sides, width, wrap):
@@ -24,7 +460,7 @@
     return with_halo(across, (("lat", 0),), 1, False)
 
 
-def conv_taps(padded, weight, rows, cols, flipped):
+def tile_conv(padded, weight, rows, cols, flipped):
     total = jnp.zeros((rows * cols, weight.shape[2]), jnp.float32)
     for first_tap in range(3):
         for second_tap in range(3):
@@ -48,7 +484,7 @@
     return total.reshape(rows, cols, -1)
 
 
-def tap_grads(padded, pullback, rows, cols):
+def tile_grads(padded, pullback, rows, cols):
     flat_pull = pullback.reshape(rows * cols, -1)
     result = []
     for first_tap in range(3):
@@ -133,7 +569,7 @@
     return summed.reshape(rows, cols, chans)
 
 
-def per_device(
+def by_tiles(
     state,
     weight_first,
     weight_second,
@@ -147,39 +583,119 @@
 ):
     rows, cols, chans = state.shape
     wide_state = widen_tile(state)
-    first = conv_taps(wide_state, weight_first, rows, cols, False)
+    first = tile_conv(wide_state, weight_first, rows, cols, False)
     hidden = jax.nn.silu(first).astype(jnp.bfloat16)
     wide_hidden = widen_tile(hidden)
-    corrected = state.astype(jnp.float32) + conv_taps(wide_hidden, weight_second, rows, cols, False)
+    corrected = state.astype(jnp.float32) + tile_conv(wide_hidden, weight_second, rows, cols, False)
     arrived = route_blocks(
         obs_owner, obs_cell, obs_level, obs_count, obs_frac, obs_value, obs_weight
     )
     adjoint = observe(corrected, arrived, rows, cols, chans)
     pullback = adjoint.astype(jnp.bfloat16)
     wide_pull = widen_tile(pullback)
-    local_second = tap_grads(wide_hidden, pullback, rows, cols)
-    back = conv_taps(wide_pull, weight_second, rows, cols, True)
+    local_second = tile_grads(wide_hidden, pullback, rows, cols)
+    back = tile_conv(wide_pull, weight_second, rows, cols, True)
     sig = jax.nn.sigmoid(first)
     pull_first = (back * sig * (1.0 + first * (1.0 - sig))).astype(jnp.bfloat16)
     wide_pull_first = widen_tile(pull_first)
-    local_first = tap_grads(wide_state, pull_first, rows, cols)
-    state_grad = adjoint + conv_taps(wide_pull_first, weight_first, rows, cols, True)
+    local_first = tile_grads(wide_state, pull_first, rows, cols)
+    state_grad = adjoint + tile_conv(wide_pull_first, weight_first, rows, cols, True)
     grad_first, grad_second = lax.psum((local_first, local_second), ("lat", "lon"))
     return (state_grad, grad_first, grad_second)
 
 
+def halo_pieces(x):
+    bands, tiles = lax.axis_size("lat"), lax.axis_size("lon")
+    rows, cols, _ = x.shape
+    pieces = []
+    for dy in (-1, 0, 1):
+        for dx in (-1, 0, 1):
+            if dy == 0 and dx == 0:
+                pieces.append(x)
+                continue
+            block = x
+            if dy:
+                block = block[rows - 2 :] if dy < 0 else block[:2]
+            if dx:
+                block = block[:, cols - 2 :] if dx < 0 else block[:, :2]
+            pairs = []
+            for lat in range(bands):
+                for lon in range(tiles):
+                    from_lat, from_lon = lat + dy, (lon + dx) % tiles
+                    if 0 <= from_lat < bands:
+                        pairs.append((from_lat * tiles + from_lon, lat * tiles + lon))
+            pieces.append(lax.ppermute(block, ("lat", "lon"), pairs))
+    return pieces
+
+
+def gather_state(x):
+    bands, tiles = lax.axis_size("lat"), lax.axis_size("lon")
+    return lax.all_gather(x, ("lat", "lon")).reshape((bands, tiles) + x.shape)
+
+
+def gather_tiles(x):
+    bands, tiles = lax.axis_size("lat"), lax.axis_size("lon")
+    half = tiles // 2
+    same = [[2 * q + core for q in range(half)] for core in range(2)]
+    copies = jnp.broadcast_to(x[None], (half,) + x.shape)
+    line = lax.all_to_all(copies, "lon", 0, 0, axis_index_groups=same, tiled=True)
+    copies = jnp.broadcast_to(line[None], (bands,) + line.shape)
+    mine = lax.all_to_all(copies, "lat", 0, 0, tiled=True)
+    other = lax.ppermute(mine, "lon", [(i, i ^ 1) for i in range(tiles)])
+    return mine, other
+
+
+def per_device(
+    state, weight_first, weight_second, obs_owner, obs_cell, obs_level, obs_count, obs_frac,
+    obs_value, obs_weight,
+):
+    rows, cols, chans = state.shape
+    bands = lax.axis_size("lat")
+    devices = lax.axis_size(("lat", "lon"))
+    if devices * rows * cols > WHOLE_CELLS:
+        return by_tiles(
+            state, weight_first, weight_second, obs_owner, obs_cell, obs_level, obs_count,
+            obs_frac, obs_value, obs_weight,
+        )
+    slots = max(2, 3 * obs_value.shape[0] // (2 * devices))
+    state_all = gather_state(state)
+    pieces = halo_pieces(state)
+    outgoing = route(
+        devices, slots, chans, obs_owner, obs_cell, obs_level, obs_count, obs_frac, obs_value,
+        obs_weight,
+    )
+    got = lax.all_to_all(outgoing, ("lat", "lon"), split_axis=0, concat_axis=0, tiled=True)
+    adjoint, pullback = forward(slots, bands, pieces, weight_first, weight_second, got)
+    mine, other = gather_tiles(pullback.reshape(rows, cols, chans))
+
+    wide_state = spread_state(state_all)
+    first = conv(wide_state, weight_first)
+    sig = jax.nn.sigmoid(first)
+    hidden = (first * sig).astype(BF16)
+    slope = sig * (1.0 + first * (1.0 - sig))
+    wide_hidden = pad(hidden)
+
+    wide_pull, pull = spread_pull(mine, other)
+    g2 = tap_grads(wide_hidden, pull)
+    pull_first = (convt(wide_pull, weight_second) * slope).astype(BF16)
+    g1 = tap_grads(wide_state, pull_first)
+    grad = local_grad(rows, cols, pull_first, weight_first, adjoint)
+    return grad.reshape(rows, cols, chans), g1, g2
+
+
 def solution(mesh):
+    both = P(("lat", "lon"), None)
     placed = (
         P("lat", "lon", None),
         P(),
         P(),
-        P(("lat", "lon"), None),
-        P(("lat", "lon"), None),
-        P(("lat", "lon"), None),
+        both,
+        both,
+        both,
         P(("lat", "lon")),
         P(("lat", "lon"), None, None),
-        P(("lat", "lon"), None),
-        P(("lat", "lon"), None),
+        both,
+        both,
     )
     return jax.shard_map(
         per_device,

time: 295 us -> 151 us (0.51)
  waiting for transfers between devices: 146 us -> 13.2 us
  matrix products: 63.9 us -> 29.3 us
  Pallas kernels: 0 us -> 31.9 us
  blocking collectives: 0 us -> 30.4 us
  starting transfers between devices: 42.4 us -> 25.3 us
  local copies, waits for them, and re-layouts: 18.4 us -> 5.48 us
  other arithmetic: 8 us -> 0 us
    psum x1 -> x0, waiting for transfers between devices: 134 us -> none  [per_device(): lax.psum((local_first, local_second), ('lat', 'lon'))]
    dot_general x66 -> x0, matrix products: 63.9 us -> none  [the longest x6 23.5 us: advance(): jnp.dot(weights, grid, precision=lax.Precision.HIGHEST, preferred_element...]
    pallas_call x0 -> x6, Pallas kernels: none -> 31.9 us  [the longest x1 12.3 us: forward(): pl.pallas_call(functools.partial(forward_kernel, slots, tiles, 2, 4), out...]
    all_to_all x0 -> x2, blocking collectives: none -> 30.4 us  [the longest x1 15.4 us: gather_tiles(): mine = lax.all_to_all(copies, 'lat', 0, 0, tiled=True)]
    conv_general_dilated x0 -> x4, matrix products: none -> 29.3 us  [the longest x2 14.4 us: tap_grads(): lax.conv_general_dilated(padded, pull, (1, 1), 'VALID', dimension_numbers...]
    ppermute x16 -> x9, starting transfers between devices: 37.9 us -> 17.1 us  [the longest x8 17.1 us: halo_pieces(): pieces.append(lax.ppermute(block, ('lat', 'lon'), pairs))]
    unnamed x41 -> x34, local copies, waits for them, and re-layouts: 9.76 us -> 2.23 us
    scatter x1 -> x0, local copies, waits for them, and re-layouts: 4.36 us -> none  [route_blocks(): jnp.zeros((devices * slots, 7, width), jnp.float32).at[target].set(packed)]
  transfers between devices with their start and end apart: 18 -> 11, of which waited for: 6 -> 4; matrix products, arithmetic and copies ran while one was open for 10% -> 2% of each run, Pallas kernels for 0% -> 13%
where the time goes in v3:
time: 151 us; the launch traced here: 150 us
  Pallas kernels  31.9 us (21%)
  blocking collectives  30.4 us (20%)
  matrix products  29.3 us (19%)
  starting transfers between devices  25.3 us (17%)
  between operations  14.3 us (9%)
  waiting for transfers between devices  13.2 us (9%)
  local copies, waits for them, and re-layouts  5.48 us (4%)
    ppermute x8, starting transfers between devices, halo_pieces(): pieces.append(lax.ppermute(block, ('lat', 'lon'), pairs))  17.1 us
    all_to_all x1, blocking collectives, gather_tiles(): mine = lax.all_to_all(copies, 'lat', 0, 0, tiled=True)  15.4 us
    all_to_all x1, blocking collectives, gather_tiles(): lax.all_to_all(copies, 'lon', 0, 0, axis_index_groups=same, tiled=True)  15 us
    conv_general_dilated x2, matrix products, tap_grads(): lax.conv_general_dilated(padded, pull, (1, 1), 'VALID', dimension_numbers...  14.4 us
    pallas_call x1, Pallas kernels, forward(): pl.pallas_call(functools.partial(forward_kernel, slots, tiles, 2, 4), out...  12.3 us
    ppermute x8, waiting for transfers between devices, halo_pieces(): pieces.append(lax.ppermute(block, ('lat', 'lon'), pairs))  9.81 us
    conv_general_dilated x1, matrix products, conv(): lax.conv_general_dilated(padded, weight.reshape(3, 3, chans, -1), (1, 1),...  8.33 us
    all_to_all x1, starting transfers between devices, per_device(): lax.all_to_all(outgoing, ('lat', 'lon'), split_axis=0, concat_axis=0, til...  8.16 us
  transfers between devices with their start and end apart: 11, of which 4 were waited for; matrix products, arithmetic and copies ran while one was open for 2% of the time, Pallas kernels for 13%

profile of v3, /device:TPU:0, one launch (start us, length us, event | category | flops | bytes accessed | tf_op | source)
XLA Modules:
  0.0 149.7 jit_solution(2677725449870187651)
XLA Ops:
  7.2 0.0 all-gather.3.cloned.1.call-start
  7.2 0.7 all-gather.3.cloned.1.call-update
  7.9 0.8 fusion
  8.7 1.3 collective-permute-start.7
  10.0 2.7 %route.1 = f32[32,8,128]{2,1,0:T(8,128)} custom-call(s32[1,128]{1,0:T(1,128)} %bitcast.32, s32[1,128]{1,0:T(1,128)} %bitcast.33, s32[32,128]{1,0:T(8,128)} %bitcast.28, s32[32,128]{1,0:T(8,128)} %bitcast.29, f32[2,32,128]{2,1,0:T(8,128)} %bitcast.27, f32[32,128]{1,0:T(8,128)} %bitcast.30, f32[32,128]{1,0:T(8,128)} %bitcast.31), custom_call_target="tpu_custom_call" | custom-call | tf_op jit(solution)/shard_map/route/pallas_call | solution.py:91
  12.7 8.2 %all-to-all-start = ((f32[32,8,128]{2,1,0:T(8,128)}), f32[32,8,128]{2,1,0:T(8,128)S(1)}, u32[]{:S(2)}, u32[]{:S(2)}) async-start(f32[32,8,128]{2,1,0:T(8,128)} %route.1), calls=%async_computation | async-start | bytes 262144 | tf_op jit(solution)/shard_map/all_to_all | solution.py:667
  20.9 0.7 fusion.1
  21.6 1.3 collective-permute-start.6
  22.9 4.5 %collective-permute-start.1 = (bf16[2,16,256]{2,1,0:T(8,128)(2,1)S(1)}, bf16[2,16,256]{2,1,0:T(8,128)(2,1)S(1)}, u32[]{:S(2)}, u32[]{:S(2)}) collective-permute-start(bf16[2,16,256]{2,1,0:T(8,128)(2,1)S(1)} %get-tuple-element.16), channel_id=1, source_target_pairs={{0,8},{1,9},{2,10},{3,11},{4,12},{5,13},{6,14},{7,15},{8,16},{9,17... | collective-permute-start | bytes 49160 | tf_op jit(solution)/shard_map/ppermute | solution.py:627
  27.4 0.8 fusion.2
  28.2 2.9 %collective-permute-start.4 = (bf16[8,2,256]{2,1,0:T(2,128)(2,1)S(1)}, bf16[8,2,256]{2,1,0:T(2,128)(2,1)S(1)}, u32[]{:S(2)}, u32[]{:S(2)}) collective-permute-start(bf16[8,2,256]{2,1,0:T(2,128)(2,1)S(1)} %get-tuple-element.17), channel_id=1, source_target_pairs={{1,0},{2,1},{3,2},{4,3},{5,4},{6,5},{7,6},{0,7},{9,8},{10,9},{11,1... | collective-permute-start | bytes 24584 | tf_op jit(solution)/shard_map/ppermute | solution.py:627
  31.1 0.0 collective-permute-start.3
  31.1 0.0 collective-permute-done.7.refs_8_
  31.1 1.3 collective-permute-start.5
  32.4 7.2 %collective-permute-done.5.refs_6_ = bf16[2,2,256]{2,1,0:T(2,128)(2,1)S(1)} collective-permute-done((bf16[2,2,256]{2,1,0:T(2,128)(2,1)S(1)}, bf16[2,2,256]{2,1,0:T(2,128)(2,1)S(1)}, u32[]{:S(2)}, u32[]{:S(2)}) %collective-permute-start.5) | collective-permute-done | bytes 2080 | tf_op jit(solution)/shard_map/ppermute | solution.py:627
  39.6 4.5 %collective-permute-start.2 = (bf16[2,2,256]{2,1,0:T(2,128)(2,1)S(1)}, bf16[2,2,256]{2,1,0:T(2,128)(2,1)S(1)}, u32[]{:S(2)}, u32[]{:S(2)}) collective-permute-start(bf16[2,2,256]{2,1,0:T(2,128)(2,1)S(1)} %get-tuple-element.13), channel_id=1, source_target_pairs={{1,8},{2,9},{3,10},{4,11},{5,12},{6,13},{7,14},{0,15},{9,16},{10,1... | collective-permute-start | bytes 6152 | tf_op jit(solution)/shard_map/ppermute | solution.py:627
  44.2 1.3 collective-permute-done.2.refs_2_
  45.5 1.3 collective-permute-start
  46.7 1.3 collective-permute-done.refs_0_
  48.0 0.0 collective-permute-done.4.refs_5_
  48.0 0.0 collective-permute-done.3.refs_3_
  48.1 0.0 collective-permute-done.6.refs_7_
  48.1 0.0 collective-permute-done.1.refs_1_
  48.1 0.0 copy-start.8
  48.1 0.0 all-to-all-done.refs_11_
  48.1 0.5 copy-done.14
  48.6 0.0 copy-done.9
  48.6 0.0 copy-done.10
  48.6 0.0 copy-done.7
  48.7 0.0 copy-done.8
  48.7 0.7 copy-done.6
  49.4 12.3 %forward.1 = (f32[128,256]{1,0:T(8,128)}, bf16[128,256]{1,0:T(8,128)(2,1)}) custom-call(bf16[2,2,256]{2,1,0:T(2,128)(2,1)} %copy-done.14, bf16[2,16,256]{2,1,0:T(8,128)(2,1)} %copy-done.8, bf16[2,2,256]{2,1,0:T(2,128)(2,1)} %copy-done.13, bf16[8,2,256]{2,1,0:T(2,128)(2,1)} %copy-done.10, bf16[8,16,256]{2,1,0:T(8,128)(2,1)} %refs_4_.1, ...), custom_call_target="tpu_custom_call" | custom-call | tf_op jit(solution)/shard_map/forward/pallas_call | solution.py:232
  61.7 0.9 broadcast_in_dim.14
  62.6 15.0 %all_to_all.15 = bf16[4,8,16,256]{3,2,1,0:T(8,128)(2,1)S(1)} all-to-all(bf16[4,8,16,256]{3,2,1,0:T(8,128)(2,1)S(1)} %broadcast_in_dim.14), channel_id=1, replica_groups={{0,2,4,6},{1,3,5,7},{8,10,12,14},{9,11,13,15},{16,18,20,22},{17,19,21,2..., dimensions={0} | all-to-all | bytes 524288 | tf_op jit(solution)/shard_map/all_to_all | solution.py:641
  77.5 0.1 broadcast_in_dim.15
  77.6 15.4 %all_to_all.16.mine_hbm = bf16[4,4,8,16,256]{4,3,2,1,0:T(8,128)(2,1)S(1)} all-to-all(bf16[4,4,8,16,256]{4,3,2,1,0:T(8,128)(2,1)S(1)} %broadcast_in_dim.15), channel_id=1, replica_groups=mesh['lat'=4,'lon'=8] {'lat'}, dimensions={0} | all-to-all | bytes 2097152 | tf_op jit(solution)/shard_map/all_to_all | solution.py:643
  93.0 2.7 %collective-permute-done.8.other_hbm = bf16[4,4,8,16,256]{4,3,2,1,0:T(8,128)(2,1)S(1)} collective-permute-done((bf16[4,4,8,16,256]{4,3,2,1,0:T(8,128)(2,1)S(1)}, bf16[4,4,8,16,256]{4,3,2,1,0:T(8,128)(2,1)S(1)}, u32[]{:S(2)}, u32[]{:S(2)}) %collective-permute-start.8) | collective-permute-done | bytes 1048608 | tf_op jit(solution)/shard_map/ppermute | solution.py:644
  95.7 1.0 copy-done.5
  96.7 5.1 %spread_pull.1 = (bf16[34,10,16,256]{3,2,1,0:T(8,128)(2,1)}, bf16[32,8,16,256]{3,2,1,0:T(8,128)(2,1)}) custom-call(bf16[4,4,8,16,256]{4,3,2,1,0:T(8,128)(2,1)} %copy-done.1, bf16[4,4,8,16,256]{4,3,2,1,0:T(8,128)(2,1)} %copy-done.5), custom_call_target="tpu_custom_call" | custom-call | tf_op jit(solution)/shard_map/spread_pull/pallas_call | solution.py:327
  101.8 0.0 copy-start
  101.8 0.0 all-gather.3.cloned.1.call-done
  101.8 4.6 %spread_state.1 = bf16[34,10,16,256]{3,2,1,0:T(8,128)(2,1)} custom-call(bf16[4,8,8,16,256]{4,3,2,1,0:T(8,128)(2,1)} %bitcast.23), custom_call_target="tpu_custom_call" | custom-call | tf_op jit(solution)/shard_map/spread_state/pallas_call | solution.py:294
  106.4 8.3 %multiply_convert_fusion = (bf16[32,8,16,256]{3,2,1,0:T(8,128)(2,1)}, f32[32,8,16,256]{3,2,1,0:T(8,128)S(1)}) fusion(bf16[34,10,16,256]{3,2,1,0:T(8,128)(2,1)} %spread_state.1, bf16[3,3,256,256]{3,2,1,0:T(8,128)(2,1)S(1)} %bitcast.22), kind=kOutput, calls=%fused_computation | convolution fusion | flops 4837081088 | bytes 10256384 | tf_op jit(solution)/shard_map/conv_general_dilated | solution.py:372
  114.8 6.5 %multiply_convert_fusion.1.pull_hbm = bf16[32,8,16,256]{3,2,1,0:T(8,128)(2,1)S(1)} fusion(f32[32,8,16,256]{3,2,1,0:T(8,128)S(1)} %get-tuple-element.20, bf16[34,10,16,256]{3,2,1,0:T(8,128)(2,1)S(1)} %copy-done.15, bf16[3,3,256,256]{3,2,1,0:T(8,128)(2,1)S(1)} %bitcast.24), kind=kOutput, calls=%fused_computation.1 | convolution fusion | flops 4841275392 | bytes 10256384 | tf_op jit(solution)/shard_map/conv_general_dilated | solution.py:380
  121.3 6.8 %fusion.3 = f32[3,3,256,256]{3,2,1,0:T(8,128)} fusion(bf16[34,10,16,256]{3,2,1,0:T(8,128)(2,1)S(1)} %copy-done.2, bf16[32,8,16,256]{3,2,1,0:T(8,128)(2,1)S(1)} %multiply_convert_fusion.1.pull_hbm), kind=kOutput, calls=%fused_computation.6 | convolution fusion | flops 4831838208 | bytes 7241728 | tf_op jit(solution)/shard_map/conv_general_dilated | solution.py:388
  128.1 3.6 %local_grad.1 = f32[128,256]{1,0:T(8,128)} custom-call(bf16[32,8,16,256]{3,2,1,0:T(8,128)(2,1)} %copy-done.3, bf16[9,256,256]{2,1,0:T(8,128)(2,1)} %w1_ref.1, f32[128,256]{1,0:T(8,128)} %get-tuple-element.9.adj_ref), custom_call_target="tpu_custom_call" | custom-call | tf_op jit(solution)/shard_map/local_grad/pallas_call | solution.py:430
  131.7 3.5 %pad.1 = bf16[34,10,16,256]{3,2,1,0:T(8,128)(2,1)} custom-call(bf16[32,8,16,256]{3,2,1,0:T(8,128)(2,1)} %get-tuple-element.19.plain_ref), custom_call_target="tpu_custom_call" | custom-call | tf_op jit(solution)/shard_map/pad/pallas_call | solution.py:360
  135.2 7.7 %fusion.4 = f32[3,3,256,256]{3,2,1,0:T(8,128)} fusion(bf16[34,10,16,256]{3,2,1,0:T(8,128)(2,1)} %pad.1, bf16[32,8,16,256]{3,2,1,0:T(8,128)(2,1)S(1)} %copy-done.16), kind=kOutput, calls=%fused_computation.7 | convolution fusion | flops 4831838208 | bytes 7241728 | tf_op jit(solution)/shard_map/conv_general_dilated | solution.py:388
  (26 shorter events, 0.0 us)
Async XLA Ops:
  7.2 94.7 %all-gather.3.cloned.1.call-start = ((), (), s32[]{:S(2)}) async-start(), calls=%async_computation.3 | async-start | bytes 2162688 | tf_op jit(solution)/shard_map/all_gather | solution.py:633
  8.7 22.4 %collective-permute-start.7 = (bf16[2,2,256]{2,1,0:T(2,128)(2,1)S(1)}, bf16[2,2,256]{2,1,0:T(2,128)(2,1)S(1)}, u32[]{:S(2)}, u32[]{:S(2)}) collective-permute-start(bf16[2,2,256]{2,1,0:T(2,128)(2,1)S(1)} %get-tuple-element.11), channel_id=1, source_target_pairs={{9,0},{10,1},{11,2},{12,3},{13,4},{14,5},{15,6},{8,7},{17,8},{18,9... | collective-permute-start | bytes 6152 | tf_op jit(solution)/shard_map/ppermute | solution.py:627
  12.7 35.4 %all-to-all-start = ((f32[32,8,128]{2,1,0:T(8,128)}), f32[32,8,128]{2,1,0:T(8,128)S(1)}, u32[]{:S(2)}, u32[]{:S(2)}) async-start(f32[32,8,128]{2,1,0:T(8,128)} %route.1), calls=%async_computation | async-start | bytes 262144 | tf_op jit(solution)/shard_map/all_to_all | solution.py:667
  21.6 26.5 %collective-permute-start.6 = (bf16[2,16,256]{2,1,0:T(8,128)(2,1)S(1)}, bf16[2,16,256]{2,1,0:T(8,128)(2,1)S(1)}, u32[]{:S(2)}, u32[]{:S(2)}) collective-permute-start(bf16[2,16,256]{2,1,0:T(8,128)(2,1)S(1)} %get-tuple-element.15), channel_id=1, source_target_pairs={{8,0},{9,1},{10,2},{11,3},{12,4},{13,5},{14,6},{15,7},{16,8},{17,9... | collective-permute-start | bytes 49160 | tf_op jit(solution)/shard_map/ppermute | solution.py:627
  22.9 25.2 %collective-permute-start.1 = (bf16[2,16,256]{2,1,0:T(8,128)(2,1)S(1)}, bf16[2,16,256]{2,1,0:T(8,128)(2,1)S(1)}, u32[]{:S(2)}, u32[]{:S(2)}) collective-permute-start(bf16[2,16,256]{2,1,0:T(8,128)(2,1)S(1)} %get-tuple-element.16), channel_id=1, source_target_pairs={{0,8},{1,9},{2,10},{3,11},{4,12},{5,13},{6,14},{7,15},{8,16},{9,17... | collective-permute-start | bytes 49160 | tf_op jit(solution)/shard_map/ppermute | solution.py:627
  28.2 19.8 %collective-permute-start.4 = (bf16[8,2,256]{2,1,0:T(2,128)(2,1)S(1)}, bf16[8,2,256]{2,1,0:T(2,128)(2,1)S(1)}, u32[]{:S(2)}, u32[]{:S(2)}) collective-permute-start(bf16[8,2,256]{2,1,0:T(2,128)(2,1)S(1)} %get-tuple-element.17), channel_id=1, source_target_pairs={{1,0},{2,1},{3,2},{4,3},{5,4},{6,5},{7,6},{0,7},{9,8},{10,9},{11,1... | collective-permute-start | bytes 24584 | tf_op jit(solution)/shard_map/ppermute | solution.py:627
  31.1 16.9 %collective-permute-start.3 = (bf16[8,2,256]{2,1,0:T(2,128)(2,1)S(1)}, bf16[8,2,256]{2,1,0:T(2,128)(2,1)S(1)}, u32[]{:S(2)}, u32[]{:S(2)}) collective-permute-start(bf16[8,2,256]{2,1,0:T(2,128)(2,1)S(1)} %get-tuple-element.18), channel_id=1, source_target_pairs={{7,0},{0,1},{1,2},{2,3},{3,4},{4,5},{5,6},{6,7},{15,8},{8,9},{9,10... | collective-permute-start | bytes 24584 | tf_op jit(solution)/shard_map/ppermute | solution.py:627
  31.1 17.0 %copy-start.11 = (bf16[2,2,256]{2,1,0:T(2,128)(2,1)}, bf16[2,2,256]{2,1,0:T(2,128)(2,1)S(1)}, u32[]{:S(2)}) copy-start(bf16[2,2,256]{2,1,0:T(2,128)(2,1)S(1)} %collective-permute-done.7.refs_8_) | copy-start | bytes 6148
  31.1 8.5 %collective-permute-start.5 = (bf16[2,2,256]{2,1,0:T(2,128)(2,1)S(1)}, bf16[2,2,256]{2,1,0:T(2,128)(2,1)S(1)}, u32[]{:S(2)}, u32[]{:S(2)}) collective-permute-start(bf16[2,2,256]{2,1,0:T(2,128)(2,1)S(1)} %get-tuple-element.12), channel_id=1, source_target_pairs={{15,0},{8,1},{9,2},{10,3},{11,4},{12,5},{13,6},{14,7},{23,8},{16,9... | collective-permute-start | bytes 6152 | tf_op jit(solution)/shard_map/ppermute | solution.py:627
  39.6 8.5 %copy-start.12 = (bf16[2,2,256]{2,1,0:T(2,128)(2,1)}, bf16[2,2,256]{2,1,0:T(2,128)(2,1)S(1)}, u32[]{:S(2)}) copy-start(bf16[2,2,256]{2,1,0:T(2,128)(2,1)S(1)} %collective-permute-done.5.refs_6_) | copy-start | bytes 6148
  39.6 5.8 %collective-permute-start.2 = (bf16[2,2,256]{2,1,0:T(2,128)(2,1)S(1)}, bf16[2,2,256]{2,1,0:T(2,128)(2,1)S(1)}, u32[]{:S(2)}, u32[]{:S(2)}) collective-permute-start(bf16[2,2,256]{2,1,0:T(2,128)(2,1)S(1)} %get-tuple-element.13), channel_id=1, source_target_pairs={{1,8},{2,9},{3,10},{4,11},{5,12},{6,13},{7,14},{0,15},{9,16},{10,1... | collective-permute-start | bytes 6152 | tf_op jit(solution)/shard_map/ppermute | solution.py:627
  45.5 2.7 %copy-start.13 = (bf16[2,2,256]{2,1,0:T(2,128)(2,1)}, bf16[2,2,256]{2,1,0:T(2,128)(2,1)S(1)}, u32[]{:S(2)}) copy-start(bf16[2,2,256]{2,1,0:T(2,128)(2,1)S(1)} %collective-permute-done.2.refs_2_) | copy-start | bytes 6148
  45.5 2.6 %collective-permute-start = (bf16[2,2,256]{2,1,0:T(2,128)(2,1)S(1)}, bf16[2,2,256]{2,1,0:T(2,128)(2,1)S(1)}, u32[]{:S(2)}, u32[]{:S(2)}) collective-permute-start(bf16[2,2,256]{2,1,0:T(2,128)(2,1)S(1)} %get-tuple-element.14), channel_id=1, source_target_pairs={{7,8},{0,9},{1,10},{2,11},{3,12},{4,13},{5,14},{6,15},{15,16},{8,1... | collective-permute-start | bytes 6152 | tf_op jit(solution)/shard_map/ppermute | solution.py:627
  48.0 0.6 copy-start.14
  48.0 0.6 copy-start.9
  48.1 0.6 copy-start.10
  48.1 0.6 copy-start.7
  48.1 0.6 copy-start.8
  48.7 0.7 copy-start.6
  93.0 2.7 %copy-start.1 = (bf16[4,4,8,16,256]{4,3,2,1,0:T(8,128)(2,1)}, bf16[4,4,8,16,256]{4,3,2,1,0:T(8,128)(2,1)S(1)}, u32[]{:S(2)}) copy-start(bf16[4,4,8,16,256]{4,3,2,1,0:T(8,128)(2,1)S(1)} %all_to_all.16.mine_hbm) | copy-start | bytes 3145732
  93.0 2.7 %collective-permute-start.8 = (bf16[4,4,8,16,256]{4,3,2,1,0:T(8,128)(2,1)S(1)}, bf16[4,4,8,16,256]{4,3,2,1,0:T(8,128)(2,1)S(1)}, u32[]{:S(2)}, u32[]{:S(2)}) collective-permute-start(bf16[4,4,8,16,256]{4,3,2,1,0:T(8,128)(2,1)S(1)} %all_to_all.16.mine_hbm), channel_id=1, source_target_pairs={{0,1},{1,0},{2,3},{3,2},{4,5},{5,4},{6,7},{7,6},{8,9},{9,8},{10,11... | collective-permute-start | bytes 3145736 | tf_op jit(solution)/shard_map/ppermute | solution.py:644
  95.7 1.0 copy-start.5
  101.8 4.6 %copy-start = (bf16[9,256,256]{2,1,0:T(8,128)(2,1)S(1)}, bf16[9,256,256]{2,1,0:T(8,128)(2,1)}, u32[]{:S(2)}) copy-start(bf16[9,256,256]{2,1,0:T(8,128)(2,1)} %w1_ref.1) | copy-start | bytes 3538948
  106.4 8.3 %copy-start.4 = (bf16[9,256,256]{2,1,0:T(8,128)(2,1)S(1)}, bf16[9,256,256]{2,1,0:T(8,128)(2,1)}, u32[]{:S(2)}) copy-start(bf16[9,256,256]{2,1,0:T(8,128)(2,1)} %refs_10_.1) | copy-start | bytes 3538948
  106.4 8.3 %copy-start.15 = (bf16[34,10,16,256]{3,2,1,0:T(8,128)(2,1)S(1)}, bf16[34,10,16,256]{3,2,1,0:T(8,128)(2,1)}, u32[]{:S(2)}) copy-start(bf16[34,10,16,256]{3,2,1,0:T(8,128)(2,1)} %get-tuple-element.8) | copy-start | bytes 8355844
  114.8 6.5 %copy-start.2 = (bf16[34,10,16,256]{3,2,1,0:T(8,128)(2,1)S(1)}, bf16[34,10,16,256]{3,2,1,0:T(8,128)(2,1)}, u32[]{:S(2)}) copy-start(bf16[34,10,16,256]{3,2,1,0:T(8,128)(2,1)} %spread_state.1) | copy-start | bytes 8355844
  121.3 6.8 %copy-start.3 = (bf16[32,8,16,256]{3,2,1,0:T(8,128)(2,1)}, bf16[32,8,16,256]{3,2,1,0:T(8,128)(2,1)S(1)}, u32[]{:S(2)}) copy-start(bf16[32,8,16,256]{3,2,1,0:T(8,128)(2,1)S(1)} %multiply_convert_fusion.1.pull_hbm) | copy-start | bytes 6291460
  131.7 3.5 %copy-start.16 = (bf16[32,8,16,256]{3,2,1,0:T(8,128)(2,1)S(1)}, bf16[32,8,16,256]{3,2,1,0:T(8,128)(2,1)}, u32[]{:S(2)}) copy-start(bf16[32,8,16,256]{3,2,1,0:T(8,128)(2,1)} %get-tuple-element.10) | copy-start | bytes 6291460
Sparse Core Ops, SparseCore 0:
  11.0 59.2 all-gather.2

commit v4 on v3

--- a/solution.py
+++ b/solution.py
@@ -11,12 +11,17 @@
 F32 = jnp.float32
 BF16 = jnp.bfloat16
 FIELDS = 5
+SPAN = 32
 WHOLE_CELLS = 4096
 VMEM_LIMIT = 60 * 1024 * 1024
 
 
 def params(limit=VMEM_LIMIT):
     return pltpu.CompilerParams(vmem_limit_bytes=limit)
+
+
+def cost(flops, moved):
+    return pl.CostEstimate(flops=int(flops), bytes_accessed=int(moved), transcendentals=0)
 
 
 def vmem():
@@ -111,16 +116,21 @@
     return sig, first * sig
 
 
-def forward_kernel(slots, tiles, group, parts, *refs):
-    piece_refs, (w1_ref, w2_ref, got_ref, adj_ref, pull_ref) = refs[:9], refs[9:14]
-    line_ref, shift_ref, hid_ref, obs_ref, sum_ref = refs[14:]
-    rows, cols, chans = piece_refs[4].shape
-    span = 32
-    heights, widths = (2, rows, 2), (2, cols, 2)
-    for place in range(9):
-        down, over = place // 3, place % 3
-        y, x = (0, 2, 2 + rows)[down], (0, 2, 2 + cols)[over]
-        line_ref[y : y + heights[down], x : x + widths[over], :] = piece_refs[place][...].astype(F32)
+def inside_grid(rows, shape, bands):
+    lat = lax.axis_index("lat") * rows + iota(shape, 0) - 1
+    return jnp.logical_and(lat >= 0, lat < bands * rows)
+
+
+def forward_kernel(slots, bands, group, parts, tile_ref, north_ref, south_ref, west_ref, east_ref,
+                   w1_ref, w2_ref, got_ref, adj_ref, pull_ref, slope_ref, line_ref, shift_ref,
+                   hid_ref, obs_ref, sum_ref):
+    rows, cols, chans = tile_ref.shape
+    span = hid_ref.shape[1]
+    line_ref[0:2, 2 : 2 + cols, :] = north_ref[...].astype(F32)
+    line_ref[2 : 2 + rows, 2 : 2 + cols, :] = tile_ref[...].astype(F32)
+    line_ref[2 + rows :, 2 : 2 + cols, :] = south_ref[...].astype(F32)
+    line_ref[:, 0:2, :] = west_ref[...].astype(F32)
+    line_ref[:, 2 + cols : 4 + cols, :] = east_ref[...].astype(F32)
     line_ref[:, cols + 4 :, :] = jnp.zeros(
         (rows + 4, line_ref.shape[1] - cols - 4, chans), F32
     )
@@ -133,9 +143,10 @@
             first = first + dot(
                 shift_ref[a * span : a * span + (rows + 2) * span, :], w1_ref[3 * a + b]
             )
-    hidden = silu_parts(first)[1].astype(BF16).astype(F32).reshape(rows + 2, span, chans)
-    lat = lax.axis_index("lat") * rows + iota((rows + 2, span, chans), 0) - 1
-    hidden = jnp.where(jnp.logical_and(lat >= 0, lat < tiles * rows), hidden, 0.0)
+    sig, hidden = silu_parts(first)
+    slope_ref[...] = sig * (1.0 + first * (1.0 - sig))
+    hidden = hidden.astype(BF16).astype(F32).reshape(rows + 2, span, chans)
+    hidden = jnp.where(inside_grid(rows, hidden.shape, bands), hidden, 0.0)
     hid_ref[...] = hidden
     total = line_ref[2 : 2 + rows, 2 : 2 + cols, :].reshape(rows * cols, chans)
     for b in range(3):
@@ -208,8 +219,10 @@
             hot_low.append(jnp.where(masks[piece], misfit - misfit_high, 0.0).astype(BF16))
         hot_high = jnp.concatenate(hot_high, axis=1)
         hot_low = jnp.concatenate(hot_low, axis=1)
-        mixed = dot_nt(jnp.concatenate([hot_high, hot_low], axis=0), high)
-        return mixed[:chans] + (mixed[chans:] + dot_nt(hot_high, low))
+        mixed = dot_nt(
+            jnp.concatenate([hot_high, hot_low], axis=0), jnp.concatenate([high, low], axis=0)
+        )
+        return mixed[:chans, :cells] + (mixed[chans:, :cells] + mixed[:chans, cells:])
 
     def step(index, carry):
         total = sum_ref[...]
@@ -224,27 +237,29 @@
     pull_ref[...] = adjoint.astype(BF16)
 
 
-def forward(slots, tiles, pieces, w1, w2, got):
-    rows, cols, chans = pieces[4].shape
+def forward(slots, bands, pieces, w1, w2, got):
+    rows, cols, chans = pieces[0].shape
     devices = got.shape[0]
     full, rest, _ = slot_layout(slots)
     groups = full * devices + (devices // 2 if rest else 0)
     return pl.pallas_call(
-        functools.partial(forward_kernel, slots, tiles, 2, 4),
+        functools.partial(forward_kernel, slots, bands, 2, 4),
         out_shape=[
             jax.ShapeDtypeStruct((rows * cols, chans), F32),
             jax.ShapeDtypeStruct((rows * cols, chans), BF16),
+            jax.ShapeDtypeStruct(((rows + 2) * SPAN, chans), F32),
         ],
-        in_specs=[vmem()] * 12,
-        out_specs=[vmem()] * 2,
+        in_specs=[vmem()] * 8,
+        out_specs=[vmem()] * 3,
         scratch_shapes=[
-            pltpu.VMEM((rows + 4, 40, chans), F32),
-            pltpu.VMEM(((rows + 4) * 32, chans), BF16),
-            pltpu.VMEM((rows + 2, 32, chans), F32),
+            pltpu.VMEM((rows + 4, SPAN + 8, chans), F32),
+            pltpu.VMEM(((rows + 4) * SPAN, chans), BF16),
+            pltpu.VMEM((rows + 2, SPAN, chans), F32),
             pltpu.VMEM((FIELDS, groups, 128), F32),
             pltpu.VMEM((chans, rows * cols), F32),
         ],
         compiler_params=params(),
+        cost_estimate=cost(4e9, 4e6),
         name="forward",
     )(*pieces, w1, w2, got)
 
@@ -263,183 +278,257 @@
     return jnp.where(column == lon, 1.0, 0.0).astype(BF16)
 
 
-def spread(line_of, bands, rows, matrix, pad_ref):
+def spread(line_of, start, lats, matrix, pad_ref):
     steps = pad_ref.shape[1] - 2
-    blank = jnp.zeros(pad_ref.shape[1:], BF16)
-    pad_ref[0] = blank
-    pad_ref[bands * rows + 1] = blank
-
-    def place(band, carry):
-        for row in range(rows):
-            line = line_of(band, row)
-            pad_ref[1 + band * rows + row] = (
-                dot(matrix, line).astype(BF16).reshape(steps + 2, 16, line.shape[1])
+    for row in range(pad_ref.shape[0]):
+        lat = start + row
+        inside = jnp.logical_and(lat >= 0, lat < lats)
+        line = line_of(jnp.clip(lat, 0, lats - 1))
+        chosen = jnp.where(inside, matrix, 0.0).astype(BF16)
+        pad_ref[row] = dot(chosen, line).astype(BF16).reshape(steps + 2, 16, line.shape[1])
+
+
+def conv_block(pad_ref, weight_ref, start, rows, flipped):
+    steps = pad_ref.shape[1] - 2
+    chans = pad_ref.shape[3]
+    pieces = []
+    for a in range(3):
+        for b in range(3):
+            da, db = (2 - a, 2 - b) if flipped else (a, b)
+            piece = pad_ref[pl.ds(start + da, rows), db : db + steps]
+            pieces.append(piece.reshape(rows * steps * 16, chans))
+    return dot(jnp.concatenate(pieces, axis=1), weight_ref[...].reshape(9 * chans, chans))
+
+
+def whole_kernel(block, all_ref, w1_ref, w2_ref, slope_ref, hidden_ref, state_ref, w2t_ref, pad_ref):
+    bands, tiles, rows, group, chans = all_ref.shape
+    lats, lons = bands * rows, tiles * group
+    steps = lons // 16
+    size = block * lons
+    mine = pad_ref.shape[0] - 4
+    base = (lax.axis_index("lon") & 1) * mine
+    spread(
+        lambda lat: all_ref[lat // rows, :, lat % rows].reshape(lons, chans),
+        base - 2, lats, spread_matrix(steps, tiles, False).astype(F32), pad_ref,
+    )
+
+    def step(index, carry):
+        start = index * block
+        first = conv_block(pad_ref, w1_ref, start, block, False)
+        sig, hidden = silu_parts(first)
+        at = pl.ds(pl.multiple_of(index * size, size), size)
+        slope_ref[at, :] = sig * (1.0 + first * (1.0 - sig))
+        lat = base - 1 + start + lax.shift_right_logical(
+            iota((size, chans), 0), lons.bit_length() - 1
+        )
+        hidden = jnp.where(jnp.logical_and(lat >= 0, lat < lats), hidden, 0.0)
+        hidden_ref[:, at] = hidden.astype(BF16).T
+        centre = pad_ref[pl.ds(start + 1, block), 1 : 1 + steps].reshape(size, chans)
+        state_ref[:, at] = centre.T
+        return carry
+
+    lax.fori_loop(0, (mine + 2) // block, step, 0)
+    for tap in range(9):
+        w2t_ref[tap] = w2_ref[tap].T
+
+
+def whole(state_all, w1, w2):
+    bands, tiles, rows, group, chans = state_all.shape
+    lats, lons = bands * rows, tiles * group
+    mine = lats // 2
+    steps = lons // 16
+    cells = (mine + 2) * lons
+    return pl.pallas_call(
+        functools.partial(whole_kernel, 3),
+        out_shape=[
+            jax.ShapeDtypeStruct((cells, chans), F32),
+            jax.ShapeDtypeStruct((chans, cells), BF16),
+            jax.ShapeDtypeStruct((chans, cells), BF16),
+            jax.ShapeDtypeStruct((9, chans, chans), BF16),
+        ],
+        in_specs=[vmem()] * 3,
+        out_specs=[vmem()] * 4,
+        scratch_shapes=[pltpu.VMEM((mine + 4, steps + 2, 16, chans), BF16)],
+        compiler_params=params(),
+        cost_estimate=cost(6e9, 10e6),
+        name="whole",
+    )(state_all, w1, w2)
+
+
+def tap_sums(turned_ref, pad_ref, first_row, rows, sum_ref, out_ref, sem):
+    steps = pad_ref.shape[1] - 2
+    chans = pad_ref.shape[3]
+    lons = steps * 16
+
+    def step(tap, carry):
+        a, b = tap // 3, tap % 3
+        piece = pad_ref[first_row : first_row + rows, pl.ds(2 - b, steps)]
+        at = pl.ds(pl.multiple_of(a * lons, lons), rows * lons)
+        sum_ref[tap] = dot(turned_ref[:, at], piece.reshape(rows * lons, chans))
+        pltpu.make_async_copy(sum_ref.at[tap], out_ref.at[tap], sem.at[tap]).start()
+        return carry
+
+    lax.fori_loop(0, 9, step, 0)
+
+
+def tail_kernel(block, mine_hbm, other_hbm, slope_hbm, hidden_hbm, state_hbm, w2t_ref, g1_hbm,
+                g2_hbm, all_ref, pull_ref, first_ref, slope_ref, hidden_ref, state_ref, g1_ref,
+                g2_ref, big_sems, g1_sems, g2_sems):
+    steps = pull_ref.shape[1] - 2
+    chans = pull_ref.shape[3]
+    lons = steps * 16
+    size = block * lons
+    _, bands, half, rows, cols, _ = all_ref.shape
+    lats = bands * rows
+    mine = lats // 2
+    core = lax.axis_index("lon") & 1
+    base = core * mine
+    mine_copy = pltpu.make_async_copy(mine_hbm, all_ref.at[core], big_sems.at[0])
+    other_copy = pltpu.make_async_copy(other_hbm, all_ref.at[1 - core], big_sems.at[1])
+    hidden_copy = pltpu.make_async_copy(hidden_hbm, hidden_ref, big_sems.at[2])
+    slope_copy = pltpu.make_async_copy(
+        slope_hbm.at[pl.ds(lons, mine * lons), :], slope_ref, big_sems.at[3]
+    )
+    state_copy = pltpu.make_async_copy(state_hbm, state_ref, big_sems.at[4])
+    mine_copy.start()
+    other_copy.start()
+    hidden_copy.start()
+    slope_copy.start()
+    state_copy.start()
+    matrix = spread_matrix(steps, 2 * half, True).astype(F32)
+    mine_copy.wait()
+    other_copy.wait()
+    spread(
+        lambda lat: all_ref[:, lat // rows, :, lat % rows].reshape(lons, chans),
+        base - 1, lats, matrix, pull_ref,
+    )
+    hidden_copy.wait()
+    tap_sums(hidden_ref, pull_ref, 1, mine, g2_ref, g2_hbm, g2_sems)
+    slope_copy.wait()
+
+    def step(index, carry):
+        start = index * block
+        back = conv_block(pull_ref, w2t_ref, start, block, True)
+        at = pl.ds(pl.multiple_of(index * size, size), size)
+        pull = (back * slope_ref[at, :]).astype(BF16).astype(F32)
+        pull = pull.reshape(block, steps, 16, chans)
+        last, head = pull[:, steps - 1], pull[:, 0]
+        before = jnp.concatenate([last[:, 15:], last[:, :15]], axis=1)
+        after = jnp.concatenate([head[:, 1:], head[:, :1]], axis=1)
+        to = pl.ds(start, block)
+        first_ref[to, 1 : 1 + steps] = pull.astype(BF16)
+        first_ref[to, 0] = before.astype(BF16)
+        first_ref[to, steps + 1] = after.astype(BF16)
+        return carry
+
+    lax.fori_loop(0, mine // block, step, 0)
+    state_copy.wait()
+    tap_sums(state_ref, first_ref, 0, mine, g1_ref, g1_hbm, g1_sems)
+    for tap in range(9):
+        pltpu.make_async_copy(g2_ref.at[tap], g2_hbm.at[tap], g2_sems.at[tap]).wait()
+        pltpu.make_async_copy(g1_ref.at[tap], g1_hbm.at[tap], g1_sems.at[tap]).wait()
+
+
+def tail(mine, other, slope, hidden, state, w2t):
+    bands, half, rows, group, chans = mine.shape
+    lats, lons = bands * rows, 2 * half * group
+    steps = lons // 16
+    ours = lats // 2
+    anywhere = pl.BlockSpec(memory_space=pl.ANY)
+    return pl.pallas_call(
+        functools.partial(tail_kernel, 4),
+        out_shape=[jax.ShapeDtypeStruct((9, chans, chans), F32)] * 2,
+        in_specs=[anywhere] * 5 + [vmem()],
+        out_specs=[anywhere] * 2,
+        scratch_shapes=[
+            pltpu.VMEM((2,) + mine.shape, BF16),
+            pltpu.VMEM((ours + 2, steps + 2, 16, chans), BF16),
+            pltpu.VMEM((ours, steps + 2, 16, chans), BF16),
+            pltpu.VMEM((ours * lons, chans), F32),
+            pltpu.VMEM(hidden.shape, BF16),
+            pltpu.VMEM(state.shape, BF16),
+            pltpu.VMEM((9, chans, chans), F32),
+            pltpu.VMEM((9, chans, chans), F32),
+            pltpu.SemaphoreType.DMA((5,)),
+            pltpu.SemaphoreType.DMA((9,)),
+            pltpu.SemaphoreType.DMA((9,)),
+        ],
+        compiler_params=params(),
+        cost_estimate=cost(10e9, 15e6),
+        name="tail",
+    )(mine, other, slope, hidden, state, w2t)
+
+
+def local_kernel(mine_hbm, other_hbm, slope_ref, adj_ref, w1_ref, w2_ref, grad_ref, near_ref,
+                 line_ref, shift_ref, pull_ref, sems):
+    bands, half, rows, cols, chans = mine_hbm.shape
+    span = pull_ref.shape[1]
+    lat, lon = lax.axis_index("lat"), lax.axis_index("lon")
+    west = lax.shift_right_logical((lon + 2 * half - 1) & (2 * half - 1), 1)
+    east = lax.shift_right_logical((lon + 1) & (2 * half - 1), 1)
+    here = lax.shift_right_logical(lon, 1)
+    copies = []
+    for down in range(3):
+        band = jnp.clip(lat + down - 1, 0, bands - 1)
+        for over, (source, q) in enumerate(((other_hbm, west), (mine_hbm, here), (other_hbm, east))):
+            copy = pltpu.make_async_copy(
+                source.at[band, q], near_ref.at[down, over], sems.at[down, over]
             )
-        return carry
-
-    lax.fori_loop(0, bands, place, 0)
-
-
-def spread_state_kernel(all_ref, pad_ref):
-    bands, tiles, rows, group, chans = all_ref.shape
-    matrix = spread_matrix(pad_ref.shape[1] - 2, tiles, False)
-    spread(
-        lambda band, row: all_ref[band, :, row].reshape(tiles * group, chans),
-        bands, rows, matrix, pad_ref,
-    )
-
-
-def spread_state(state_all):
-    bands, tiles, rows, group, chans = state_all.shape
-    return pl.pallas_call(
-        spread_state_kernel,
-        out_shape=jax.ShapeDtypeStruct((bands * rows + 2, tiles * group // 16 + 2, 16, chans), BF16),
-        in_specs=[vmem()],
-        out_specs=vmem(),
-        compiler_params=params(),
-        name="spread_state",
-    )(state_all)
-
-
-def spread_pull_kernel(mine_hbm, other_hbm, pad_ref, plain_ref, all_ref, sems):
-    _, bands, half, rows, cols, chans = all_ref.shape
-    steps = plain_ref.shape[1]
-    core = lax.axis_index("lon") & 1
-    copies = [
-        pltpu.make_async_copy(mine_hbm, all_ref.at[core], sems.at[0]),
-        pltpu.make_async_copy(other_hbm, all_ref.at[1 - core], sems.at[1]),
-    ]
-    for copy in copies:
-        copy.start()
-    matrix = spread_matrix(steps, 2 * half, True)
+            copy.start()
+            copies.append(copy)
+    line_ref[:, cols + 4 :, :] = jnp.zeros(
+        (rows + 4, line_ref.shape[1] - cols - 4, chans), F32
+    )
     for copy in copies:
         copy.wait()
-    spread(
-        lambda band, row: all_ref[:, band, :, row].reshape(steps * 16, chans),
-        bands, rows, matrix, pad_ref,
-    )
-    plain_ref[...] = pad_ref[1 : bands * rows + 1, 1 : steps + 1]
-
-
-def spread_pull(mine, other):
-    bands, half, rows, group, chans = mine.shape
-    lats, steps = bands * rows, 2 * half * group // 16
+    for down, (y, height, first) in enumerate(((0, 2, rows - 2), (2, rows, 0), (2 + rows, 2, 0))):
+        band = lat + down - 1
+        for over, (x, width, left) in enumerate(((0, 2, cols - 2), (2, cols, 0), (2 + cols, 2, 0))):
+            part = near_ref[down, over].astype(F32)[
+                first : first + height, left : left + width
+            ]
+            if down != 1:
+                part = jnp.where(jnp.logical_and(band >= 0, band < bands), part, 0.0)
+            line_ref[y : y + height, x : x + width, :] = part
+    back = jnp.zeros(((rows + 2) * span, chans), F32)
+    for b in range(3):
+        shift_ref[...] = (
+            line_ref[:, 2 - b : 2 - b + span, :].astype(BF16).reshape((rows + 4) * span, chans)
+        )
+        for a in range(3):
+            piece = shift_ref[(2 - a) * span : (2 - a) * span + (rows + 2) * span, :]
+            back = back + dot_nt(piece, w2_ref[3 * a + b])
+    pull = (back * slope_ref[...]).reshape(rows + 2, span, chans)
+    pull_ref[...] = jnp.where(inside_grid(rows, pull.shape, bands), pull, 0.0)
+    total = adj_ref[...]
+    for b in range(3):
+        shift_ref[0 : (rows + 2) * cols, :] = (
+            pull_ref[:, 2 - b : 2 - b + cols, :].astype(BF16).reshape((rows + 2) * cols, chans)
+        )
+        for a in range(3):
+            piece = shift_ref[(2 - a) * cols : (2 - a) * cols + rows * cols, :]
+            total = total + dot_nt(piece, w1_ref[3 * a + b])
+    grad_ref[...] = total
+
+
+def local_grad(mine, other, slope, adjoint, w1, w2):
+    bands, half, rows, cols, chans = mine.shape
     return pl.pallas_call(
-        spread_pull_kernel,
-        out_shape=[
-            jax.ShapeDtypeStruct((lats + 2, steps + 2, 16, chans), BF16),
-            jax.ShapeDtypeStruct((lats, steps, 16, chans), BF16),
-        ],
-        in_specs=[pl.BlockSpec(memory_space=pl.ANY)] * 2,
-        out_specs=[vmem()] * 2,
-        scratch_shapes=[pltpu.VMEM((2,) + mine.shape, BF16), pltpu.SemaphoreType.DMA((2,))],
-        compiler_params=params(),
-        name="spread_pull",
-    )(mine, other)
-
-
-def pad_kernel(plain_ref, pad_ref):
-    lats, steps, group, chans = plain_ref.shape
-    blank = jnp.zeros(pad_ref.shape[1:], BF16)
-    pad_ref[0] = blank
-    pad_ref[lats + 1] = blank
-
-    def step(lat, carry):
-        pad_ref[lat + 1, 1 : steps + 1] = plain_ref[lat]
-        last = plain_ref[lat, steps - 1].astype(F32)
-        head = plain_ref[lat, 0].astype(F32)
-        pad_ref[lat + 1, 0] = jnp.concatenate([last[15:], last[:15]], axis=0).astype(BF16)
-        pad_ref[lat + 1, steps + 1] = jnp.concatenate([head[1:], head[:1]], axis=0).astype(BF16)
-        return carry
-
-    lax.fori_loop(0, lats, step, 0, unroll=4)
-
-
-def pad(plain):
-    lats, steps, group, chans = plain.shape
-    return pl.pallas_call(
-        pad_kernel,
-        out_shape=jax.ShapeDtypeStruct((lats + 2, steps + 2, group, chans), BF16),
-        in_specs=[vmem()],
-        out_specs=vmem(),
-        compiler_params=params(),
-        name="pad",
-    )(plain)
-
-
-def conv(padded, weight):
-    chans = weight.shape[1]
-    return lax.conv_general_dilated(
-        padded, weight.reshape(3, 3, chans, -1), (1, 1), "VALID",
-        dimension_numbers=("HWNC", "HWIO", "HWNC"), preferred_element_type=F32,
-    )
-
-
-def convt(padded, weight):
-    chans = weight.shape[1]
-    return lax.conv_general_dilated(
-        padded, lax.rev(weight.reshape(3, 3, chans, -1), (0, 1)), (1, 1), "VALID",
-        dimension_numbers=("HWNC", "HWOI", "HWNC"), preferred_element_type=F32,
-    )
-
-
-def tap_grads(padded, pull):
-    chans = pull.shape[3]
-    grads = lax.conv_general_dilated(
-        padded, pull, (1, 1), "VALID",
-        dimension_numbers=("HWCN", "HWIO", "HWNC"), preferred_element_type=F32,
-    )
-    return grads.reshape(9, -1, chans)
-
-
-def local_kernel(rows, cols, pull_hbm, w1_ref, adj_ref, grad_ref, pull_ref, near_ref, sem):
-    lats, steps, _, chans = pull_hbm.shape
-    lons = steps * 16
-    top = lax.axis_index("lat") * rows - 1
-    begin = jnp.clip(top, 0, lats - rows - 2)
-    copy = pltpu.make_async_copy(pull_hbm.at[pl.ds(begin, rows + 2)], pull_ref, sem)
-    copy.start()
-    left = lax.axis_index("lon") * cols
-    place = iota((3 * cols, lons), 0)
-    shift = 1 - lax.shift_right_logical(place, cols.bit_length() - 1)
-    lon = left + (place & (cols - 1)) + shift
-    lon = jnp.where(lon < 0, lon + lons, jnp.where(lon >= lons, lon - lons, lon))
-    column = iota((3 * cols, lons), 1)
-    theirs = (column & 15) * steps + lax.shift_right_logical(column, 4)
-    select = jnp.where(theirs == lon, 1.0, 0.0)
-    copy.wait()
-    for row in range(rows + 2):
-        lat = top + row
-        inside = jnp.logical_and(lat >= 0, lat < lats)
-        line = pull_ref[jnp.clip(lat - begin, 0, rows + 1)].reshape(lons, chans)
-        chosen = jnp.where(inside, select, 0.0).astype(BF16)
-        near = dot(chosen, line).astype(BF16)
-        for b in range(3):
-            near_ref[b, row * cols : (row + 1) * cols, :] = near[b * cols : (b + 1) * cols]
-    total = adj_ref[...]
-    for a in range(3):
-        for b in range(3):
-            total = total + dot_nt(
-                near_ref[b, (2 - a) * cols : (2 - a + rows) * cols, :], w1_ref[3 * a + b]
-            )
-    grad_ref[...] = total
-
-
-def local_grad(rows, cols, pull, w1, adjoint):
-    lats, steps, _, chans = pull.shape
-    return pl.pallas_call(
-        functools.partial(local_kernel, rows, cols),
+        local_kernel,
         out_shape=jax.ShapeDtypeStruct((rows * cols, chans), F32),
-        in_specs=[pl.BlockSpec(memory_space=pl.ANY), vmem(), vmem()],
+        in_specs=[pl.BlockSpec(memory_space=pl.ANY)] * 2 + [vmem()] * 4,
         out_specs=vmem(),
         scratch_shapes=[
-            pltpu.VMEM((rows + 2, steps, 16, chans), BF16),
-            pltpu.VMEM((3, (rows + 2) * cols, chans), BF16),
-            pltpu.SemaphoreType.DMA,
+            pltpu.VMEM((3, 3, rows, cols, chans), BF16),
+            pltpu.VMEM((rows + 4, SPAN + 8, chans), F32),
+            pltpu.VMEM(((rows + 4) * SPAN, chans), BF16),
+            pltpu.VMEM((rows + 2, SPAN, chans), F32),
+            pltpu.SemaphoreType.DMA((3, 3)),
         ],
         compiler_params=params(),
+        cost_estimate=cost(3e9, 4e6),
         name="local_grad",
-    )(pull, w1, adjoint)
+    )(mine, other, slope, adjoint, w1, w2)
 
 
 def with_halo(x, sides, width, wrap):
@@ -607,25 +696,13 @@
 def halo_pieces(x):
     bands, tiles = lax.axis_size("lat"), lax.axis_size("lon")
     rows, cols, _ = x.shape
-    pieces = []
-    for dy in (-1, 0, 1):
-        for dx in (-1, 0, 1):
-            if dy == 0 and dx == 0:
-                pieces.append(x)
-                continue
-            block = x
-            if dy:
-                block = block[rows - 2 :] if dy < 0 else block[:2]
-            if dx:
-                block = block[:, cols - 2 :] if dx < 0 else block[:, :2]
-            pairs = []
-            for lat in range(bands):
-                for lon in range(tiles):
-                    from_lat, from_lon = lat + dy, (lon + dx) % tiles
-                    if 0 <= from_lat < bands:
-                        pairs.append((from_lat * tiles + from_lon, lat * tiles + lon))
-            pieces.append(lax.ppermute(block, ("lat", "lon"), pairs))
-    return pieces
+    north = lax.ppermute(x[rows - 2 :], "lat", [(i, i + 1) for i in range(bands - 1)])
+    south = lax.ppermute(x[:2], "lat", [(i + 1, i) for i in range(bands - 1)])
+    last = jnp.concatenate([p[:, cols - 2 :] for p in (north, x, south)], axis=0)
+    first = jnp.concatenate([p[:, :2] for p in (north, x, south)], axis=0)
+    west = lax.ppermute(last, "lon", [(i, (i + 1) % tiles) for i in range(tiles)])
+    east = lax.ppermute(first, "lon", [((i + 1) % tiles, i) for i in range(tiles)])
+    return x, north, south, west, east
 
 
 def gather_state(x):
@@ -665,21 +742,16 @@
         obs_weight,
     )
     got = lax.all_to_all(outgoing, ("lat", "lon"), split_axis=0, concat_axis=0, tiled=True)
-    adjoint, pullback = forward(slots, bands, pieces, weight_first, weight_second, got)
+    adjoint, pullback, near_slope = forward(
+        slots, bands, pieces, weight_first, weight_second, got
+    )
     mine, other = gather_tiles(pullback.reshape(rows, cols, chans))
-
-    wide_state = spread_state(state_all)
-    first = conv(wide_state, weight_first)
-    sig = jax.nn.sigmoid(first)
-    hidden = (first * sig).astype(BF16)
-    slope = sig * (1.0 + first * (1.0 - sig))
-    wide_hidden = pad(hidden)
-
-    wide_pull, pull = spread_pull(mine, other)
-    g2 = tap_grads(wide_hidden, pull)
-    pull_first = (convt(wide_pull, weight_second) * slope).astype(BF16)
-    g1 = tap_grads(wide_state, pull_first)
-    grad = local_grad(rows, cols, pull_first, weight_first, adjoint)
+    slope, hidden, turned, w2t = whole(state_all, weight_first, weight_second)
+    sums = tail(mine, other, slope, hidden, turned, w2t)
+    swap = [(i, i ^ 1) for i in range(lax.axis_size("lon"))]
+    theirs = [lax.ppermute(part, "lon", swap) for part in sums]
+    grad = local_grad(mine, other, near_slope, adjoint, weight_first, weight_second)
+    g1, g2 = [part + their for part, their in zip(sums, theirs)]
     return grad.reshape(rows, cols, chans), g1, g2
 
 

time: 151 us -> 122 us (0.81)
  matrix products: 29.3 us -> 0 us
  Pallas kernels: 31.9 us -> 44.9 us
  waiting for transfers between devices: 13.2 us -> 4.51 us
  starting transfers between devices: 25.3 us -> 17.3 us
  other arithmetic: 0 us -> 6.95 us
    conv_general_dilated x4 -> x0, matrix products: 29.3 us -> none  [the longest x2 14.4 us: tap_grads(): lax.conv_general_dilated(padded, pull, (1, 1), 'VALID', dimension_numbers...]
    pallas_call x5 -> x4, Pallas kernels: 29.1 us -> 42.2 us  [the longest x1 15.6 us: tail(): pl.pallas_call(functools.partial(tail_kernel, 4), out_shape=[jax.ShapeDty...]
    ppermute x8 -> x6, waiting for transfers between devices: 9.81 us -> 2.57 us  [the longest x1 2.56 us: halo_pieces(): lax.ppermute(last, 'lon', [(i, (i + 1) % tiles) for i in range(tiles)])]
    add x0 -> x2, other arithmetic: none -> 6.9 us  [per_device(): g1, g2 = [part + their for part, their in zip(sums, theirs)]]
    ppermute x8 -> x6, starting transfers between devices: 17.1 us -> 11 us  [the longest x1 5.47 us: halo_pieces(): lax.ppermute(x[rows - 2:], 'lat', [(i, i + 1) for i in range(bands - 1)])]
    ppermute x1, waiting for transfers between devices: 2.66 us -> 0.01 us  [gather_tiles(): other = lax.ppermute(mine, 'lon', [(i, i ^ 1) for i in range(tiles)])]
    all_to_all x1, blocking collectives: 15 us -> 12.3 us  [gather_tiles(): lax.all_to_all(copies, 'lon', 0, 0, axis_index_groups=same, tiled=True)]
    all_to_all x1, blocking collectives: 15.4 us -> 17.3 us  [gather_tiles(): mine = lax.all_to_all(copies, 'lat', 0, 0, tiled=True)]
  transfers between devices with their start and end apart: 11 -> 9, of which waited for: 4 -> 2; matrix products, arithmetic and copies ran while one was open for 2% -> 5% of each run, Pallas kernels for 13% -> 24%
where the time goes in v4:
time: 122 us
  Pallas kernels  44.9 us (37%)
  blocking collectives  29.6 us (24%)
  starting transfers between devices  17.3 us (14%)
  between operations  14.2 us (12%)
  other arithmetic  6.95 us (6%)
  waiting for transfers between devices  4.51 us (4%)
  local copies, waits for them, and re-layouts  4.24 us (3%)
    all_to_all x1, blocking collectives, gather_tiles(): mine = lax.all_to_all(copies, 'lat', 0, 0, tiled=True)  17.3 us
    pallas_call x1, Pallas kernels, tail(): pl.pallas_call(functools.partial(tail_kernel, 4), out_shape=[jax.ShapeDty...  15.6 us
    all_to_all x1, blocking collectives, gather_tiles(): lax.all_to_all(copies, 'lon', 0, 0, axis_index_groups=same, tiled=True)  12.3 us
    pallas_call x1, Pallas kernels, forward(): pl.pallas_call(functools.partial(forward_kernel, slots, bands, 2, 4), out...  10.7 us
    pallas_call x1, Pallas kernels, whole(): pl.pallas_call(functools.partial(whole_kernel, 3), out_shape=[jax.ShapeDt...  10.6 us
    add x2, other arithmetic, per_device(): g1, g2 = [part + their for part, their in zip(sums, theirs)]  6.9 us
    all_to_all x1, starting transfers between devices, per_device(): lax.all_to_all(outgoing, ('lat', 'lon'), split_axis=0, concat_axis=0, til...  6.32 us
    ppermute x1, starting transfers between devices, halo_pieces(): lax.ppermute(x[rows - 2:], 'lat', [(i, i + 1) for i in range(bands - 1)])  5.47 us
  transfers between devices with their start and end apart: 9, of which 2 were waited for; matrix products, arithmetic and copies ran while one was open for 5% of the time, Pallas kernels for 24%

profile of v4, /device:TPU:0, one launch (start us, length us, event | category | flops | bytes accessed | tf_op | source)
XLA Modules:
  0.0 121.7 jit_solution(13743416875435735023)
XLA Ops:
  7.2 0.0 all-gather.3.cloned.1.call-start
  7.2 0.7 all-gather.3.cloned.1.call-update
  7.9 0.7 fusion.1
  8.6 1.3 %collective-permute-start.1 = (bf16[2,16,256]{2,1,0:T(8,128)(2,1)S(1)}, bf16[2,16,256]{2,1,0:T(8,128)(2,1)S(1)}, u32[]{:S(2)}, u32[]{:S(2)}) collective-permute-start(bf16[2,16,256]{2,1,0:T(8,128)(2,1)S(1)} %get-tuple-element.23), channel_id=1, source_target_pairs={{8,0},{16,8},{24,16},{9,1},{17,9},{25,17},{10,2},{18,10},{26,18},{... | collective-permute-start | bytes 49160 | tf_op jit(solution)/shard_map/ppermute | solution.py:700
  9.9 5.5 %collective-permute-start = (bf16[2,16,256]{2,1,0:T(8,128)(2,1)S(1)}, bf16[2,16,256]{2,1,0:T(8,128)(2,1)S(1)}, u32[]{:S(2)}, u32[]{:S(2)}) collective-permute-start(bf16[2,16,256]{2,1,0:T(8,128)(2,1)S(1)} %get-tuple-element.24), channel_id=1, source_target_pairs={{0,8},{8,16},{16,24},{1,9},{9,17},{17,25},{2,10},{10,18},{18,26},{... | collective-permute-start | bytes 49160 | tf_op jit(solution)/shard_map/ppermute | solution.py:699
  15.4 2.7 %route.1 = f32[32,8,128]{2,1,0:T(8,128)} custom-call(s32[1,128]{1,0:T(1,128)} %bitcast.16, s32[1,128]{1,0:T(1,128)} %bitcast.17, s32[32,128]{1,0:T(8,128)} %bitcast.12, s32[32,128]{1,0:T(8,128)} %bitcast.13, f32[2,32,128]{2,1,0:T(8,128)} %bitcast.11, f32[32,128]{1,0:T(8,128)} %bitcast.14, f32[32,128]{1,0:T(8,128)} %bitcast.15), custom_call_target="tpu_custom_call" | custom-call | tf_op jit(solution)/shard_map/route/pallas_call | solution.py:96
  18.1 6.3 %all-to-all-start = ((f32[32,8,128]{2,1,0:T(8,128)}), f32[32,8,128]{2,1,0:T(8,128)S(1)}, u32[]{:S(2)}, u32[]{:S(2)}) async-start(f32[32,8,128]{2,1,0:T(8,128)} %route.1), calls=%async_computation | async-start | bytes 262144 | tf_op jit(solution)/shard_map/all_to_all | solution.py:744
  24.5 0.8 fusion
  25.3 0.0 collective-permute-done.1.south_ref
  25.3 0.0 copy-start.4
  25.3 0.0 collective-permute-done.north_ref
  25.3 0.0 copy-start.5
  25.4 0.3 collective-permute-start.2
  25.7 3.3 %collective-permute-start.3 = (bf16[12,2,256]{2,1,0:T(2,128)(2,1)S(1)}, bf16[12,2,256]{2,1,0:T(2,128)(2,1)S(1)}, u32[]{:S(2)}, u32[]{:S(2)}) collective-permute-start(bf16[12,2,256]{2,1,0:T(2,128)(2,1)S(1)} %pad_maximum_fusion.1), channel_id=1, source_target_pairs={{1,0},{2,1},{3,2},{4,3},{5,4},{6,5},{7,6},{0,7},{9,8},{10,9},{11,1... | collective-permute-start | bytes 36872 | tf_op jit(solution)/shard_map/ppermute | solution.py:704
  29.0 2.6 %collective-permute-done.2.west_ref = bf16[12,2,256]{2,1,0:T(2,128)(2,1)S(1)} collective-permute-done((bf16[12,2,256]{2,1,0:T(2,128)(2,1)S(1)}, bf16[12,2,256]{2,1,0:T(2,128)(2,1)S(1)}, u32[]{:S(2)}, u32[]{:S(2)}) %collective-permute-start.2) | collective-permute-done | bytes 12320 | tf_op jit(solution)/shard_map/ppermute | solution.py:703
  31.6 0.0 copy-start.7
  31.6 0.0 collective-permute-done.3.east_ref
  31.6 0.0 copy-start.8
  31.6 1.2 %all-to-all-done.got_ref = f32[32,8,128]{2,1,0:T(8,128)S(1)} async-done(((f32[32,8,128]{2,1,0:T(8,128)}), f32[32,8,128]{2,1,0:T(8,128)S(1)}, u32[]{:S(2)}, u32[]{:S(2)}) %all-to-all-start) | async-done | bytes 131104 | tf_op jit(solution)/shard_map/all_to_all | solution.py:744
  32.8 0.0 copy-done.4
  32.9 0.0 copy-done.5
  32.9 0.0 copy-done.7
  32.9 0.0 copy-done.8
  32.9 0.0 copy-start.3
  32.9 0.6 copy-done.3
  33.5 10.7 %forward.1 = (f32[128,256]{1,0:T(8,128)}, bf16[128,256]{1,0:T(8,128)(2,1)}, f32[320,256]{1,0:T(8,128)}) custom-call(bf16[8,16,256]{2,1,0:T(8,128)(2,1)} %tile_ref.1, bf16[2,16,256]{2,1,0:T(8,128)(2,1)} %copy-done.5, bf16[2,16,256]{2,1,0:T(8,128)(2,1)} %copy-done.4, bf16[12,2,256]{2,1,0:T(2,128)(2,1)} %copy-done.7, bf16[12,2,256]{2,1,0:T(2,128)(2,1)} %copy-done.8, ...), custom_call_target="tpu_custom_call" | custom-call | flops 4000000000 | bytes 4000000 | tf_op jit(solution)/shard_map/forward/pallas_call | solution.py:245
  44.3 0.9 broadcast_in_dim.14
  45.1 12.3 %all_to_all.15 = bf16[4,8,16,256]{3,2,1,0:T(8,128)(2,1)S(1)} all-to-all(bf16[4,8,16,256]{3,2,1,0:T(8,128)(2,1)S(1)} %broadcast_in_dim.14), channel_id=1, replica_groups={{0,2,4,6},{1,3,5,7},{8,10,12,14},{9,11,13,15},{16,18,20,22},{17,19,21,2..., dimensions={0} | all-to-all | bytes 524288 | tf_op jit(solution)/shard_map/all_to_all | solution.py:718
  57.4 0.1 broadcast_in_dim.15
  57.5 17.3 %all_to_all.16.mine_hbm = bf16[4,4,8,16,256]{4,3,2,1,0:T(8,128)(2,1)S(1)} all-to-all(bf16[4,4,8,16,256]{4,3,2,1,0:T(8,128)(2,1)S(1)} %broadcast_in_dim.15), channel_id=1, replica_groups=mesh['lat'=4,'lon'=8] {'lat'}, dimensions={0} | all-to-all | bytes 2097152 | tf_op jit(solution)/shard_map/all_to_all | solution.py:720
  74.8 0.0 copy-start.2
  74.8 0.0 collective-permute-start.4
  74.9 0.0 all-gather.3.cloned.1.call-done
  74.9 10.6 %whole.1 = (f32[2304,256]{1,0:T(8,128)}, bf16[256,2304]{1,0:T(8,128)(2,1)}, bf16[256,2304]{1,0:T(8,128)(2,1)}, bf16[9,256,256]{2,1,0:T(8,128)(2,1)}) custom-call(bf16[4,8,8,16,256]{4,3,2,1,0:T(8,128)(2,1)} %bitcast.18, bf16[9,256,256]{2,1,0:T(8,128)(2,1)} %w1_ref.5, bf16[9,256,256]{2,1,0:T(8,128)(2,1)} %w2_ref.5), custom_call_target="tpu_custom_call" | custom-call | flops 6000000000 | bytes 10000000 | tf_op jit(solution)/shard_map/whole/pallas_call | solution.py:341
  85.4 0.0 copy-done.2
  85.4 0.0 collective-permute-done.4.other_hbm
  85.4 1.1 copy-done.6
  86.5 15.6 %tail.1 = (f32[9,256,256]{2,1,0:T(8,128)}, f32[9,256,256]{2,1,0:T(8,128)}) custom-call(bf16[4,4,8,16,256]{4,3,2,1,0:T(8,128)(2,1)} %copy-done.2, bf16[4,4,8,16,256]{4,3,2,1,0:T(8,128)(2,1)} %copy-done.6, f32[2304,256]{1,0:T(8,128)} %get-tuple-element.15.slope_hbm, bf16[256,2304]{1,0:T(8,128)(2,1)} %get-tuple-element.16.hidden_hbm, ...), custom_call_target="tpu_custom_call" | custom-call | flops 10000000000 | bytes 15000000 | tf_op jit(solution)/shard_map/tail/pallas_call | solution.py:438
  102.0 0.2 collective-permute-start.5
  102.2 0.4 collective-permute-start.6
  102.6 5.3 %local_grad.1 = f32[128,256]{1,0:T(8,128)} custom-call(bf16[4,4,8,16,256]{4,3,2,1,0:T(8,128)(2,1)} %copy-done.2, bf16[4,4,8,16,256]{4,3,2,1,0:T(8,128)(2,1)} %copy-done.6, f32[320,256]{1,0:T(8,128)} %get-tuple-element.13.slope_ref, f32[128,256]{1,0:T(8,128)} %get-tuple-element.14.adj_ref, bf16[9,256,256]{2,1,0:T(8,128)(2,1)} %w1_ref.5, ...), custom_call_target="tpu_custom_call" | custom-call | flops 3000000000 | bytes 4000000 | tf_op jit(solution)/shard_map/local_grad/pallas_call | solution.py:516
  107.9 0.0 copy-start
  108.0 0.0 collective-permute-done.5
  108.0 0.0 copy-done.1
  108.0 3.5 %add.6 = f32[9,256,256]{2,1,0:T(8,128)} add(f32[9,256,256]{2,1,0:T(8,128)S(1)} %copy-done.1, f32[9,256,256]{2,1,0:T(8,128)} %collective-permute-done.5) | non-fusion elementwise | flops 589824 | bytes 7077888 | tf_op jit(solution)/shard_map/add | solution.py:754
  111.5 0.0 collective-permute-done.6
  111.5 0.0 copy-done
  111.5 3.4 %add.7 = f32[9,256,256]{2,1,0:T(8,128)} add(f32[9,256,256]{2,1,0:T(8,128)S(1)} %copy-done, f32[9,256,256]{2,1,0:T(8,128)} %collective-permute-done.6) | non-fusion elementwise | flops 589824 | bytes 7077888 | tf_op jit(solution)/shard_map/add | solution.py:754
  (6 shorter events, 0.1 us)
Async XLA Ops:
  7.2 67.7 %all-gather.3.cloned.1.call-start = ((), (), s32[]{:S(2)}) async-start(), calls=%async_computation.3 | async-start | bytes 2162688 | tf_op jit(solution)/shard_map/all_gather | solution.py:710
  8.6 16.6 %collective-permute-start.1 = (bf16[2,16,256]{2,1,0:T(8,128)(2,1)S(1)}, bf16[2,16,256]{2,1,0:T(8,128)(2,1)S(1)}, u32[]{:S(2)}, u32[]{:S(2)}) collective-permute-start(bf16[2,16,256]{2,1,0:T(8,128)(2,1)S(1)} %get-tuple-element.23), channel_id=1, source_target_pairs={{8,0},{16,8},{24,16},{9,1},{17,9},{25,17},{10,2},{18,10},{26,18},{... | collective-permute-start | bytes 49160 | tf_op jit(solution)/shard_map/ppermute | solution.py:700
  9.9 15.4 %collective-permute-start = (bf16[2,16,256]{2,1,0:T(8,128)(2,1)S(1)}, bf16[2,16,256]{2,1,0:T(8,128)(2,1)S(1)}, u32[]{:S(2)}, u32[]{:S(2)}) collective-permute-start(bf16[2,16,256]{2,1,0:T(8,128)(2,1)S(1)} %get-tuple-element.24), channel_id=1, source_target_pairs={{0,8},{8,16},{16,24},{1,9},{9,17},{17,25},{2,10},{10,18},{18,26},{... | collective-permute-start | bytes 49160 | tf_op jit(solution)/shard_map/ppermute | solution.py:699
  18.1 14.7 %all-to-all-start = ((f32[32,8,128]{2,1,0:T(8,128)}), f32[32,8,128]{2,1,0:T(8,128)S(1)}, u32[]{:S(2)}, u32[]{:S(2)}) async-start(f32[32,8,128]{2,1,0:T(8,128)} %route.1), calls=%async_computation | async-start | bytes 262144 | tf_op jit(solution)/shard_map/all_to_all | solution.py:744
  25.3 7.6 %copy-start.4 = (bf16[2,16,256]{2,1,0:T(8,128)(2,1)}, bf16[2,16,256]{2,1,0:T(8,128)(2,1)S(1)}, u32[]{:S(2)}) copy-start(bf16[2,16,256]{2,1,0:T(8,128)(2,1)S(1)} %collective-permute-done.1.south_ref) | copy-start | bytes 49156
  25.3 7.6 %copy-start.5 = (bf16[2,16,256]{2,1,0:T(8,128)(2,1)}, bf16[2,16,256]{2,1,0:T(8,128)(2,1)S(1)}, u32[]{:S(2)}) copy-start(bf16[2,16,256]{2,1,0:T(8,128)(2,1)S(1)} %collective-permute-done.north_ref) | copy-start | bytes 49156
  25.4 6.2 %collective-permute-start.2 = (bf16[12,2,256]{2,1,0:T(2,128)(2,1)S(1)}, bf16[12,2,256]{2,1,0:T(2,128)(2,1)S(1)}, u32[]{:S(2)}, u32[]{:S(2)}) collective-permute-start(bf16[12,2,256]{2,1,0:T(2,128)(2,1)S(1)} %pad_maximum_fusion), channel_id=1, source_target_pairs={{0,1},{1,2},{2,3},{3,4},{4,5},{5,6},{6,7},{7,0},{8,9},{9,10},{10,1... | collective-permute-start | bytes 36872 | tf_op jit(solution)/shard_map/ppermute | solution.py:703
  25.7 5.9 %collective-permute-start.3 = (bf16[12,2,256]{2,1,0:T(2,128)(2,1)S(1)}, bf16[12,2,256]{2,1,0:T(2,128)(2,1)S(1)}, u32[]{:S(2)}, u32[]{:S(2)}) collective-permute-start(bf16[12,2,256]{2,1,0:T(2,128)(2,1)S(1)} %pad_maximum_fusion.1), channel_id=1, source_target_pairs={{1,0},{2,1},{3,2},{4,3},{5,4},{6,5},{7,6},{0,7},{9,8},{10,9},{11,1... | collective-permute-start | bytes 36872 | tf_op jit(solution)/shard_map/ppermute | solution.py:704
  31.6 1.3 %copy-start.7 = (bf16[12,2,256]{2,1,0:T(2,128)(2,1)}, bf16[12,2,256]{2,1,0:T(2,128)(2,1)S(1)}, u32[]{:S(2)}) copy-start(bf16[12,2,256]{2,1,0:T(2,128)(2,1)S(1)} %collective-permute-done.2.west_ref) | copy-start | bytes 36868
  31.6 1.3 %copy-start.8 = (bf16[12,2,256]{2,1,0:T(2,128)(2,1)}, bf16[12,2,256]{2,1,0:T(2,128)(2,1)S(1)}, u32[]{:S(2)}) copy-start(bf16[12,2,256]{2,1,0:T(2,128)(2,1)S(1)} %collective-permute-done.3.east_ref) | copy-start | bytes 36868
  32.9 0.7 copy-start.3
  74.8 10.6 %copy-start.2 = (bf16[4,4,8,16,256]{4,3,2,1,0:T(8,128)(2,1)}, bf16[4,4,8,16,256]{4,3,2,1,0:T(8,128)(2,1)S(1)}, u32[]{:S(2)}) copy-start(bf16[4,4,8,16,256]{4,3,2,1,0:T(8,128)(2,1)S(1)} %all_to_all.16.mine_hbm) | copy-start | bytes 3145732
  74.8 10.6 %collective-permute-start.4 = (bf16[4,4,8,16,256]{4,3,2,1,0:T(8,128)(2,1)S(1)}, bf16[4,4,8,16,256]{4,3,2,1,0:T(8,128)(2,1)S(1)}, u32[]{:S(2)}, u32[]{:S(2)}) collective-permute-start(bf16[4,4,8,16,256]{4,3,2,1,0:T(8,128)(2,1)S(1)} %all_to_all.16.mine_hbm), channel_id=1, source_target_pairs={{0,1},{1,0},{2,3},{3,2},{4,5},{5,4},{6,7},{7,6},{8,9},{9,8},{10,11... | collective-permute-start | bytes 3145736 | tf_op jit(solution)/shard_map/ppermute | solution.py:721
  85.4 1.1 copy-start.6
  102.0 5.9 %collective-permute-start.5 = (f32[9,256,256]{2,1,0:T(8,128)}, f32[9,256,256]{2,1,0:T(8,128)}, u32[]{:S(2)}, u32[]{:S(2)}) collective-permute-start(f32[9,256,256]{2,1,0:T(8,128)} %get-tuple-element.19), channel_id=1, source_target_pairs={{0,1},{1,0},{2,3},{3,2},{4,5},{5,4},{6,7},{7,6},{8,9},{9,8},{10,11... | collective-permute-start | bytes 7077896 | tf_op jit(solution)/shard_map/ppermute | solution.py:752
  102.2 9.3 %collective-permute-start.6 = (f32[9,256,256]{2,1,0:T(8,128)}, f32[9,256,256]{2,1,0:T(8,128)}, u32[]{:S(2)}, u32[]{:S(2)}) collective-permute-start(f32[9,256,256]{2,1,0:T(8,128)} %get-tuple-element.20), channel_id=1, source_target_pairs={{0,1},{1,0},{2,3},{3,2},{4,5},{5,4},{6,7},{7,6},{8,9},{9,8},{10,11... | collective-permute-start | bytes 7077896 | tf_op jit(solution)/shard_map/ppermute | solution.py:752
  102.6 5.3 %copy-start.1 = (f32[9,256,256]{2,1,0:T(8,128)S(1)}, f32[9,256,256]{2,1,0:T(8,128)}, u32[]{:S(2)}) copy-start(f32[9,256,256]{2,1,0:T(8,128)} %get-tuple-element.19) | copy-start | bytes 7077892
  107.9 3.6 %copy-start = (f32[9,256,256]{2,1,0:T(8,128)S(1)}, f32[9,256,256]{2,1,0:T(8,128)}, u32[]{:S(2)}) copy-start(f32[9,256,256]{2,1,0:T(8,128)} %get-tuple-element.20) | copy-start | bytes 7077892
Sparse Core Ops, SparseCore 0:
  11.0 59.5 all-gather.2

commit v5 on v4

--- a/solution.py
+++ b/solution.py
@@ -264,18 +264,17 @@
     )(*pieces, w1, w2, got)
 
 
-def spread_matrix(steps, tiles, split):
+def spread_matrix(steps, tiles):
     lons = 16 * steps
+    half = tiles // 2
     place = iota(((steps + 2) * 16, lons), 0)
     lon = (place & 15) * steps + lax.shift_right_logical(place, 4) - 1
     lon = jnp.where(lon < 0, lon + lons, jnp.where(lon >= lons, lon - lons, lon))
     column = iota(((steps + 2) * 16, lons), 1)
-    if split:
-        half = tiles // 2
-        chunk = lax.shift_right_logical(column, 4)
-        core = lax.shift_right_logical(chunk, half.bit_length() - 1)
-        column = (2 * (chunk & (half - 1)) + core) * 16 + (column & 15)
-    return jnp.where(column == lon, 1.0, 0.0).astype(BF16)
+    chunk = lax.shift_right_logical(column, 4)
+    core = lax.shift_right_logical(chunk, half.bit_length() - 1)
+    column = (2 * (chunk & (half - 1)) + core) * 16 + (column & 15)
+    return jnp.where(column == lon, 1.0, 0.0)
 
 
 def spread(line_of, start, lats, matrix, pad_ref):
@@ -300,16 +299,27 @@
     return dot(jnp.concatenate(pieces, axis=1), weight_ref[...].reshape(9 * chans, chans))
 
 
-def whole_kernel(block, all_ref, w1_ref, w2_ref, slope_ref, hidden_ref, state_ref, w2t_ref, pad_ref):
-    bands, tiles, rows, group, chans = all_ref.shape
-    lats, lons = bands * rows, tiles * group
+def whole_kernel(block, mine_hbm, other_hbm, w1_ref, w2_ref, slope_ref, hidden_ref, state_ref,
+                 w2t_ref, pad_ref, all_ref, sems):
+    _, bands, half, rows, group, chans = all_ref.shape
+    lats, lons = bands * rows, 2 * half * group
     steps = lons // 16
     size = block * lons
     mine = pad_ref.shape[0] - 4
-    base = (lax.axis_index("lon") & 1) * mine
+    core = lax.axis_index("lon") & 1
+    base = core * mine
+    mine_copy = pltpu.make_async_copy(mine_hbm, all_ref.at[core], sems.at[0])
+    other_copy = pltpu.make_async_copy(other_hbm, all_ref.at[1 - core], sems.at[1])
+    mine_copy.start()
+    other_copy.start()
+    matrix = spread_matrix(steps, 2 * half)
+    for tap in range(9):
+        w2t_ref[tap] = w2_ref[tap].T
+    mine_copy.wait()
+    other_copy.wait()
     spread(
-        lambda lat: all_ref[lat // rows, :, lat % rows].reshape(lons, chans),
-        base - 2, lats, spread_matrix(steps, tiles, False).astype(F32), pad_ref,
+        lambda lat: all_ref[:, lat // rows, :, lat % rows].reshape(lons, chans),
+        base - 2, lats, matrix, pad_ref,
     )
 
     def step(index, carry):
@@ -328,13 +338,11 @@
         return carry
 
     lax.fori_loop(0, (mine + 2) // block, step, 0)
-    for tap in range(9):
-        w2t_ref[tap] = w2_ref[tap].T
-
-
-def whole(state_all, w1, w2):
-    bands, tiles, rows, group, chans = state_all.shape
-    lats, lons = bands * rows, tiles * group
+
+
+def whole(state_mine, state_other, w1, w2):
+    bands, half, rows, group, chans = state_mine.shape
+    lats, lons = bands * rows, 2 * half * group
     mine = lats // 2
     steps = lons // 16
     cells = (mine + 2) * lons
@@ -346,13 +354,17 @@
             jax.ShapeDtypeStruct((chans, cells), BF16),
             jax.ShapeDtypeStruct((9, chans, chans), BF16),
         ],
-        in_specs=[vmem()] * 3,
+        in_specs=[pl.BlockSpec(memory_space=pl.ANY)] * 2 + [vmem()] * 2,
         out_specs=[vmem()] * 4,
-        scratch_shapes=[pltpu.VMEM((mine + 4, steps + 2, 16, chans), BF16)],
+        scratch_shapes=[
+            pltpu.VMEM((mine + 4, steps + 2, 16, chans), BF16),
+            pltpu.VMEM((2,) + state_mine.shape, BF16),
+            pltpu.SemaphoreType.DMA((2,)),
+        ],
         compiler_params=params(),
         cost_estimate=cost(6e9, 10e6),
         name="whole",
-    )(state_all, w1, w2)
+    )(state_mine, state_other, w1, w2)
 
 
 def tap_sums(turned_ref, pad_ref, first_row, rows, sum_ref, out_ref, sem):
@@ -395,7 +407,7 @@
     hidden_copy.start()
     slope_copy.start()
     state_copy.start()
-    matrix = spread_matrix(steps, 2 * half, True).astype(F32)
+    matrix = spread_matrix(steps, 2 * half)
     mine_copy.wait()
     other_copy.wait()
     spread(
@@ -531,6 +543,25 @@
     )(mine, other, slope, adjoint, w1, w2)
 
 
+def add_kernel(a1_ref, a2_ref, b1_ref, b2_ref, o1_ref, o2_ref):
+    o1_ref[...] = a1_ref[...] + b1_ref[...]
+    o2_ref[...] = a2_ref[...] + b2_ref[...]
+
+
+def add_pairs(ours, theirs):
+    shape = ours[0].shape
+    block = pl.BlockSpec((1,) + shape[1:], lambda tap: (tap, 0, 0))
+    return pl.pallas_call(
+        add_kernel,
+        grid=(shape[0],),
+        out_shape=[jax.ShapeDtypeStruct(shape, F32)] * 2,
+        in_specs=[block] * 4,
+        out_specs=[block] * 2,
+        compiler_params=params(),
+        name="add_pairs",
+    )(*ours, *theirs)
+
+
 def with_halo(x, sides, width, wrap):
     for axis, dim in sides:
         count, length = (lax.axis_size(axis), x.shape[dim])
@@ -693,31 +724,24 @@
     return (state_grad, grad_first, grad_second)
 
 
-def halo_pieces(x):
+def halo_pieces(x, after):
     bands, tiles = lax.axis_size("lat"), lax.axis_size("lon")
     rows, cols, _ = x.shape
     north = lax.ppermute(x[rows - 2 :], "lat", [(i, i + 1) for i in range(bands - 1)])
     south = lax.ppermute(x[:2], "lat", [(i + 1, i) for i in range(bands - 1)])
     last = jnp.concatenate([p[:, cols - 2 :] for p in (north, x, south)], axis=0)
     first = jnp.concatenate([p[:, :2] for p in (north, x, south)], axis=0)
+    last, first, after = lax.optimization_barrier((last, first, after))
     west = lax.ppermute(last, "lon", [(i, (i + 1) % tiles) for i in range(tiles)])
     east = lax.ppermute(first, "lon", [((i + 1) % tiles, i) for i in range(tiles)])
-    return x, north, south, west, east
-
-
-def gather_state(x):
-    bands, tiles = lax.axis_size("lat"), lax.axis_size("lon")
-    return lax.all_gather(x, ("lat", "lon")).reshape((bands, tiles) + x.shape)
+    return (x, north, south, west, east), after
 
 
 def gather_tiles(x):
     bands, tiles = lax.axis_size("lat"), lax.axis_size("lon")
-    half = tiles // 2
-    same = [[2 * q + core for q in range(half)] for core in range(2)]
-    copies = jnp.broadcast_to(x[None], (half,) + x.shape)
-    line = lax.all_to_all(copies, "lon", 0, 0, axis_index_groups=same, tiled=True)
-    copies = jnp.broadcast_to(line[None], (bands,) + line.shape)
-    mine = lax.all_to_all(copies, "lat", 0, 0, tiled=True)
+    same = [[device for device in range(bands * tiles) if device % 2 == core] for core in range(2)]
+    mine = lax.all_gather(x, ("lat", "lon"), axis_index_groups=same)
+    mine = mine.reshape((bands, tiles // 2) + x.shape)
     other = lax.ppermute(mine, "lon", [(i, i ^ 1) for i in range(tiles)])
     return mine, other
 
@@ -735,23 +759,25 @@
             obs_frac, obs_value, obs_weight,
         )
     slots = max(2, 3 * obs_value.shape[0] // (2 * devices))
-    state_all = gather_state(state)
-    pieces = halo_pieces(state)
+    state_mine, state_other = gather_tiles(state)
     outgoing = route(
         devices, slots, chans, obs_owner, obs_cell, obs_level, obs_count, obs_frac, obs_value,
         obs_weight,
     )
+    pieces, outgoing = halo_pieces(state, outgoing)
     got = lax.all_to_all(outgoing, ("lat", "lon"), split_axis=0, concat_axis=0, tiled=True)
     adjoint, pullback, near_slope = forward(
         slots, bands, pieces, weight_first, weight_second, got
     )
     mine, other = gather_tiles(pullback.reshape(rows, cols, chans))
-    slope, hidden, turned, w2t = whole(state_all, weight_first, weight_second)
+    slope, hidden, turned, w2t = whole(
+        state_mine, state_other, weight_first, weight_second
+    )
     sums = tail(mine, other, slope, hidden, turned, w2t)
     swap = [(i, i ^ 1) for i in range(lax.axis_size("lon"))]
     theirs = [lax.ppermute(part, "lon", swap) for part in sums]
     grad = local_grad(mine, other, near_slope, adjoint, weight_first, weight_second)
-    g1, g2 = [part + their for part, their in zip(sums, theirs)]
+    g1, g2 = add_pairs(sums, theirs)
     return grad.reshape(rows, cols, chans), g1, g2
 
 

time: 122 us -> 180 us (1.48)
  waiting for transfers between devices: 4.51 us -> 89.4 us
  blocking collectives: 29.6 us -> 0 us
  Pallas kernels: 44.9 us -> 53.8 us
  other arithmetic: 6.95 us -> 0.04 us
    all_gather x1 -> x2, waiting for transfers between devices: 0.01 us -> 81.5 us  [gather_tiles(): mine = lax.all_gather(x, ('lat', 'lon'), axis_index_groups=same)]
    all_to_all x2 -> x0, blocking collectives: 29.6 us -> none  [the longest x1 17.3 us: gather_tiles(): mine = lax.all_to_all(copies, 'lat', 0, 0, tiled=True)]
    pallas_call x0 -> x1, Pallas kernels: none -> 8.86 us  [add_pairs(): pl.pallas_call(add_kernel, grid=(shape[0],), out_shape=[jax.ShapeDtypeStr...]
    add x2 -> x0, other arithmetic: 6.9 us -> none  [per_device(): g1, g2 = [part + their for part, their in zip(sums, theirs)]]
    ppermute x2, waiting for transfers between devices: 0.01 us -> 2.61 us  [per_device(): theirs = [lax.ppermute(part, 'lon', swap) for part in sums]]
  transfers between devices with their start and end apart: 9 -> 11, of which waited for: 2 -> 6; matrix products, arithmetic and copies ran while one was open for 5% -> 1% of each run, Pallas kernels for 24% -> 16%
where the time goes in v5:
time: 180 us
  waiting for transfers between devices  89.4 us (50%)
  Pallas kernels  53.8 us (30%)
  starting transfers between devices  17.4 us (10%)
  between operations  14.2 us (8%)
  local copies, waits for them, and re-layouts  4.8 us (3%)
    all_gather x2, waiting for transfers between devices, gather_tiles(): mine = lax.all_gather(x, ('lat', 'lon'), axis_index_groups=same)  81.5 us
    pallas_call x1, Pallas kernels, tail(): pl.pallas_call(functools.partial(tail_kernel, 4), out_shape=[jax.ShapeDty...  15.6 us
    pallas_call x1, Pallas kernels, whole(): pl.pallas_call(functools.partial(whole_kernel, 3), out_shape=[jax.ShapeDt...  10.7 us
    pallas_call x1, Pallas kernels, forward(): pl.pallas_call(functools.partial(forward_kernel, slots, bands, 2, 4), out...  10.7 us
    pallas_call x1, Pallas kernels, add_pairs(): pl.pallas_call(add_kernel, grid=(shape[0],), out_shape=[jax.ShapeDtypeStr...  8.86 us
    all_to_all x1, starting transfers between devices, per_device(): lax.all_to_all(outgoing, ('lat', 'lon'), split_axis=0, concat_axis=0, til...  6.33 us
    ppermute x1, starting transfers between devices, halo_pieces(): lax.ppermute(x[rows - 2:], 'lat', [(i, i + 1) for i in range(bands - 1)])  5.47 us
    pallas_call x1, Pallas kernels, local_grad(): pl.pallas_call(local_kernel, out_shape=jax.ShapeDtypeStruct((rows * cols,...  5.18 us
  transfers between devices with their start and end apart: 11, of which 6 were waited for; matrix products, arithmetic and copies ran while one was open for 1% of the time, Pallas kernels for 16%

profile of v5, /device:TPU:0, one launch (start us, length us, event | category | flops | bytes accessed | tf_op | source)
XLA Modules:
  0.0 179.6 jit_solution(7866648670194370274)
XLA Ops:
  7.2 0.0 all-gather.6.cloned.1.call-start
  7.2 0.7 all-gather.6.cloned.1.call-update
  7.9 0.7 fusion.1
  8.6 1.3 collective-permute-start.1
  9.9 5.5 %collective-permute-start = (bf16[2,16,256]{2,1,0:T(8,128)(2,1)S(1)}, bf16[2,16,256]{2,1,0:T(8,128)(2,1)S(1)}, u32[]{:S(2)}, u32[]{:S(2)}) collective-permute-start(bf16[2,16,256]{2,1,0:T(8,128)(2,1)S(1)} %get-tuple-element.34), channel_id=1, source_target_pairs={{0,8},{8,16},{16,24},{1,9},{9,17},{17,25},{2,10},{10,18},{18,26},{... | collective-permute-start | bytes 49160 | tf_op jit(solution)/shard_map/ppermute | solution.py:730
  15.4 0.8 fusion
  16.2 2.7 %route.1 = f32[32,8,128]{2,1,0:T(8,128)} custom-call(s32[1,128]{1,0:T(1,128)} %bitcast.17, s32[1,128]{1,0:T(1,128)} %bitcast.18, s32[32,128]{1,0:T(8,128)} %bitcast.13, s32[32,128]{1,0:T(8,128)} %bitcast.14, f32[2,32,128]{2,1,0:T(8,128)} %bitcast.12, f32[32,128]{1,0:T(8,128)} %bitcast.15, f32[32,128]{1,0:T(8,128)} %bitcast.16), custom_call_target="tpu_custom_call" | custom-call | tf_op jit(solution)/shard_map/route/pallas_call | solution.py:96
  18.9 0.0 collective-permute-done.1.south_ref
  18.9 0.0 copy-start.2
  18.9 0.0 collective-permute-done.north_ref
  19.0 0.0 copy-start.3
  19.0 6.3 %all-to-all-start = ((f32[32,8,128]{2,1,0:T(8,128)}), f32[32,8,128]{2,1,0:T(8,128)S(1)}, u32[]{:S(2)}, u32[]{:S(2)}) async-start(f32[32,8,128]{2,1,0:T(8,128)} %route.1), calls=%async_computation | async-start | bytes 262144 | tf_op jit(solution)/shard_map/all_to_all | solution.py:768
  25.4 0.0 all-gather.4.cloned.1.call-start
  25.4 0.3 collective-permute-start.2
  25.7 3.3 %collective-permute-start.3 = (bf16[12,2,256]{2,1,0:T(2,128)(2,1)S(1)}, bf16[12,2,256]{2,1,0:T(2,128)(2,1)S(1)}, u32[]{:S(2)}, u32[]{:S(2)}) collective-permute-start(bf16[12,2,256]{2,1,0:T(2,128)(2,1)S(1)} %get-tuple-element.18), channel_id=1, source_target_pairs={{1,0},{2,1},{3,2},{4,3},{5,4},{6,5},{7,6},{0,7},{9,8},{10,9},{11,1... | collective-permute-start | bytes 36872 | tf_op jit(solution)/shard_map/ppermute | solution.py:736
  29.0 3.5 %collective-permute-done.2.west_ref = bf16[12,2,256]{2,1,0:T(2,128)(2,1)S(1)} collective-permute-done((bf16[12,2,256]{2,1,0:T(2,128)(2,1)S(1)}, bf16[12,2,256]{2,1,0:T(2,128)(2,1)S(1)}, u32[]{:S(2)}, u32[]{:S(2)}) %collective-permute-start.2) | collective-permute-done | bytes 12320 | tf_op jit(solution)/shard_map/ppermute | solution.py:735
  32.5 0.0 copy-start.6
  32.5 0.0 collective-permute-done.3.east_ref
  32.5 0.0 copy-start.7
  32.5 1.0 all-to-all-done.got_ref
  33.5 0.0 copy-done.2
  33.5 0.0 copy-done.3
  33.5 0.0 copy-done.6
  33.6 0.0 copy-done.7
  33.6 0.0 copy-start.1
  33.6 0.6 copy-done.1
  34.2 10.7 %forward.1 = (f32[128,256]{1,0:T(8,128)}, bf16[128,256]{1,0:T(8,128)(2,1)}, f32[320,256]{1,0:T(8,128)}) custom-call(bf16[8,16,256]{2,1,0:T(8,128)(2,1)} %tile_ref.1, bf16[2,16,256]{2,1,0:T(8,128)(2,1)} %copy-done.3, bf16[2,16,256]{2,1,0:T(8,128)(2,1)} %copy-done.2, bf16[12,2,256]{2,1,0:T(2,128)(2,1)} %copy-done.6, bf16[12,2,256]{2,1,0:T(2,128)(2,1)} %copy-done.7, ...), custom_call_target="tpu_custom_call" | custom-call | flops 4000000000 | bytes 4000000 | tf_op jit(solution)/shard_map/forward/pallas_call | solution.py:245
  44.9 0.0 all-gather.4.cloned.1.call-update
  45.0 24.0 %all-gather.6.cloned.1.call-done = bf16[128,16,256]{2,1,0:T(8,128)(2,1)} async-done(((bf16[8,16,256]{2,1,0:T(8,128)(2,1)}), bf16[128,16,256]{2,1,0:T(8,128)(2,1)}) %all-gather.6.cloned.1.call-update) | async-done | bytes 1048592 | tf_op jit(solution)/shard_map/all_gather | solution.py:743
  69.0 0.0 collective-permute-start.5
  69.0 57.5 %all-gather.4.cloned.1.call-done = bf16[16,8,16,256]{3,2,1,0:T(8,128)(2,1)} async-done(((bf16[1,8,16,256]{3,2,1,0:T(8,128)(2,1)}), bf16[16,8,16,256]{3,2,1,0:T(8,128)(2,1)}) %all-gather.4.cloned.1.call-update) | async-done | bytes 1048592 | tf_op jit(solution)/shard_map/all_gather | solution.py:743
  126.5 0.0 collective-permute-start.4
  126.5 0.0 collective-permute-done.5.other_hbm
  126.5 0.0 copy-start.5
  126.5 1.0 copy-done.5
  127.5 10.7 %whole.1 = (f32[2304,256]{1,0:T(8,128)}, bf16[256,2304]{1,0:T(8,128)(2,1)}, bf16[256,2304]{1,0:T(8,128)(2,1)}, bf16[9,256,256]{2,1,0:T(8,128)(2,1)}) custom-call(bf16[4,4,8,16,256]{4,3,2,1,0:T(8,128)(2,1)} %bitcast.20, bf16[4,4,8,16,256]{4,3,2,1,0:T(8,128)(2,1)} %copy-done.5, bf16[9,256,256]{2,1,0:T(8,128)(2,1)} %w1_ref.5, bf16[9,256,256]{2,1,0:T(8,128)(2,1)} %w2_ref.5), custom_call_target="tpu_custom_call" | custom-call | flops 6000000000 | bytes 10000000 | tf_op jit(solution)/shard_map/whole/pallas_call | solution.py:349
  138.2 0.0 collective-permute-done.4.other_hbm
  138.2 0.0 copy-start.4
  138.2 1.1 copy-done.4
  139.3 15.6 %tail.1 = (f32[9,256,256]{2,1,0:T(8,128)}, f32[9,256,256]{2,1,0:T(8,128)}) custom-call(bf16[4,4,8,16,256]{4,3,2,1,0:T(8,128)(2,1)} %bitcast.22, bf16[4,4,8,16,256]{4,3,2,1,0:T(8,128)(2,1)} %copy-done.4, f32[2304,256]{1,0:T(8,128)} %get-tuple-element.23.slope_hbm, bf16[256,2304]{1,0:T(8,128)(2,1)} %get-tuple-element.24.hidden_hbm, ...), custom_call_target="tpu_custom_call" | custom-call | flops 10000000000 | bytes 15000000 | tf_op jit(solution)/shard_map/tail/pallas_call | solution.py:450
  154.9 0.6 collective-permute-start.6
  155.4 0.1 collective-permute-start.7
  155.5 5.2 %local_grad.1 = f32[128,256]{1,0:T(8,128)} custom-call(bf16[4,4,8,16,256]{4,3,2,1,0:T(8,128)(2,1)} %bitcast.23, bf16[4,4,8,16,256]{4,3,2,1,0:T(8,128)(2,1)} %copy-done.4, f32[320,256]{1,0:T(8,128)} %get-tuple-element.21.slope_ref, f32[128,256]{1,0:T(8,128)} %get-tuple-element.22.adj_ref, bf16[9,256,256]{2,1,0:T(8,128)(2,1)} %w1_ref.5, ...), custom_call_target="tpu_custom_call" | custom-call | flops 3000000000 | bytes 4000000 | tf_op jit(solution)/shard_map/local_grad/pallas_call | solution.py:528
  160.7 1.7 collective-permute-done.6.b1_ref
  162.4 0.0 copy-start
  162.4 0.9 collective-permute-done.7.b2_ref
  163.3 0.5 copy-done
  163.9 8.9 %add_pairs.1 = (f32[9,256,256]{2,1,0:T(8,128)}, f32[9,256,256]{2,1,0:T(8,128)}) custom-call(f32[9,256,256]{2,1,0:T(8,128)} %get-tuple-element.27.a1_ref, f32[9,256,256]{2,1,0:T(8,128)} %get-tuple-element.28.a2_ref, f32[9,256,256]{2,1,0:T(8,128)} %copy-done, f32[9,256,256]{2,1,0:T(8,128)} %collective-permute-done.7.b2_ref), custom_call_target="tpu_custom_call" | custom-call | tf_op jit(solution)/shard_map/add_pairs/pallas_call | solution.py:554
  (3 shorter events, 0.1 us)
Async XLA Ops:
  7.2 61.8 %all-gather.6.cloned.1.call-start = ((), (), s32[]{:S(2)}) async-start(), calls=%async_computation.2 | async-start | bytes 1114112 | tf_op jit(solution)/shard_map/all_gather | solution.py:743
  8.6 10.3 %collective-permute-start.1 = (bf16[2,16,256]{2,1,0:T(8,128)(2,1)S(1)}, bf16[2,16,256]{2,1,0:T(8,128)(2,1)S(1)}, u32[]{:S(2)}, u32[]{:S(2)}) collective-permute-start(bf16[2,16,256]{2,1,0:T(8,128)(2,1)S(1)} %get-tuple-element.33), channel_id=1, source_target_pairs={{8,0},{16,8},{24,16},{9,1},{17,9},{25,17},{10,2},{18,10},{26,18},{... | collective-permute-start | bytes 49160 | tf_op jit(solution)/shard_map/ppermute | solution.py:731
  9.9 9.0 %collective-permute-start = (bf16[2,16,256]{2,1,0:T(8,128)(2,1)S(1)}, bf16[2,16,256]{2,1,0:T(8,128)(2,1)S(1)}, u32[]{:S(2)}, u32[]{:S(2)}) collective-permute-start(bf16[2,16,256]{2,1,0:T(8,128)(2,1)S(1)} %get-tuple-element.34), channel_id=1, source_target_pairs={{0,8},{8,16},{16,24},{1,9},{9,17},{17,25},{2,10},{10,18},{18,26},{... | collective-permute-start | bytes 49160 | tf_op jit(solution)/shard_map/ppermute | solution.py:730
  18.9 14.6 %copy-start.2 = (bf16[2,16,256]{2,1,0:T(8,128)(2,1)}, bf16[2,16,256]{2,1,0:T(8,128)(2,1)S(1)}, u32[]{:S(2)}) copy-start(bf16[2,16,256]{2,1,0:T(8,128)(2,1)S(1)} %collective-permute-done.1.south_ref) | copy-start | bytes 49156
  19.0 14.6 %copy-start.3 = (bf16[2,16,256]{2,1,0:T(8,128)(2,1)}, bf16[2,16,256]{2,1,0:T(8,128)(2,1)S(1)}, u32[]{:S(2)}) copy-start(bf16[2,16,256]{2,1,0:T(8,128)(2,1)S(1)} %collective-permute-done.north_ref) | copy-start | bytes 49156
  19.0 14.5 %all-to-all-start = ((f32[32,8,128]{2,1,0:T(8,128)}), f32[32,8,128]{2,1,0:T(8,128)S(1)}, u32[]{:S(2)}, u32[]{:S(2)}) async-start(f32[32,8,128]{2,1,0:T(8,128)} %route.1), calls=%async_computation | async-start | bytes 262144 | tf_op jit(solution)/shard_map/all_to_all | solution.py:768
  25.4 101.1 %all-gather.4.cloned.1.call-start = ((), (), s32[]{:S(2)}) async-start(), calls=%async_computation.1 | async-start | bytes 1114112 | tf_op jit(solution)/shard_map/all_gather | solution.py:743
  25.4 7.1 %collective-permute-start.2 = (bf16[12,2,256]{2,1,0:T(2,128)(2,1)S(1)}, bf16[12,2,256]{2,1,0:T(2,128)(2,1)S(1)}, u32[]{:S(2)}, u32[]{:S(2)}) collective-permute-start(bf16[12,2,256]{2,1,0:T(2,128)(2,1)S(1)} %get-tuple-element.17), channel_id=1, source_target_pairs={{0,1},{1,2},{2,3},{3,4},{4,5},{5,6},{6,7},{7,0},{8,9},{9,10},{10,1... | collective-permute-start | bytes 36872 | tf_op jit(solution)/shard_map/ppermute | solution.py:735
  25.7 6.8 %collective-permute-start.3 = (bf16[12,2,256]{2,1,0:T(2,128)(2,1)S(1)}, bf16[12,2,256]{2,1,0:T(2,128)(2,1)S(1)}, u32[]{:S(2)}, u32[]{:S(2)}) collective-permute-start(bf16[12,2,256]{2,1,0:T(2,128)(2,1)S(1)} %get-tuple-element.18), channel_id=1, source_target_pairs={{1,0},{2,1},{3,2},{4,3},{5,4},{6,5},{7,6},{0,7},{9,8},{10,9},{11,1... | collective-permute-start | bytes 36872 | tf_op jit(solution)/shard_map/ppermute | solution.py:736
  32.5 1.1 copy-start.6
  32.5 1.1 copy-start.7
  33.6 0.7 copy-start.1
  69.0 57.5 %collective-permute-start.5 = (bf16[4,4,8,16,256]{4,3,2,1,0:T(8,128)(2,1)}, bf16[4,4,8,16,256]{4,3,2,1,0:T(8,128)(2,1)S(1)}, u32[]{:S(2)}, u32[]{:S(2)}) collective-permute-start(bf16[4,4,8,16,256]{4,3,2,1,0:T(8,128)(2,1)} %bitcast.19), channel_id=1, source_target_pairs={{0,1},{1,0},{2,3},{3,2},{4,5},{5,4},{6,7},{7,6},{8,9},{9,8},{10,11... | collective-permute-start | bytes 3145736 | tf_op jit(solution)/shard_map/ppermute | solution.py:745
  126.5 11.7 %collective-permute-start.4 = (bf16[4,4,8,16,256]{4,3,2,1,0:T(8,128)(2,1)}, bf16[4,4,8,16,256]{4,3,2,1,0:T(8,128)(2,1)S(1)}, u32[]{:S(2)}, u32[]{:S(2)}) collective-permute-start(bf16[4,4,8,16,256]{4,3,2,1,0:T(8,128)(2,1)} %bitcast.21), channel_id=1, source_target_pairs={{0,1},{1,0},{2,3},{3,2},{4,5},{5,4},{6,7},{7,6},{8,9},{9,8},{10,11... | collective-permute-start | bytes 3145736 | tf_op jit(solution)/shard_map/ppermute | solution.py:745
  126.5 1.0 copy-start.5
  138.2 1.1 copy-start.4
  154.9 7.5 %collective-permute-start.6 = (f32[9,256,256]{2,1,0:T(8,128)}, f32[9,256,256]{2,1,0:T(8,128)S(1)}, u32[]{:S(2)}, u32[]{:S(2)}) collective-permute-start(f32[9,256,256]{2,1,0:T(8,128)} %get-tuple-element.27.a1_ref), channel_id=1, source_target_pairs={{0,1},{1,0},{2,3},{3,2},{4,5},{5,4},{6,7},{7,6},{8,9},{9,8},{10,11... | collective-permute-start | bytes 7077896 | tf_op jit(solution)/shard_map/ppermute | solution.py:778
  155.4 7.9 %collective-permute-start.7 = (f32[9,256,256]{2,1,0:T(8,128)}, f32[9,256,256]{2,1,0:T(8,128)}, u32[]{:S(2)}, u32[]{:S(2)}) collective-permute-start(f32[9,256,256]{2,1,0:T(8,128)} %get-tuple-element.28.a2_ref), channel_id=1, source_target_pairs={{0,1},{1,0},{2,3},{3,2},{4,5},{5,4},{6,7},{7,6},{8,9},{9,8},{10,11... | collective-permute-start | bytes 7077896 | tf_op jit(solution)/shard_map/ppermute | solution.py:778
  162.4 1.5 copy-start
Sparse Core Ops, SparseCore 0:
  10.7 58.1 all-gather.5
  72.3 54.1 all-gather.3

commit v6 on v4

--- a/solution.py
+++ b/solution.py
@@ -13,11 +13,10 @@
 FIELDS = 5
 SPAN = 32
 WHOLE_CELLS = 4096
-VMEM_LIMIT = 60 * 1024 * 1024
-
-
-def params(limit=VMEM_LIMIT):
-    return pltpu.CompilerParams(vmem_limit_bytes=limit)
+
+
+def params(mebibytes):
+    return pltpu.CompilerParams(vmem_limit_bytes=mebibytes * 1024 * 1024)
 
 
 def cost(flops, moved):
@@ -26,6 +25,10 @@
 
 def vmem():
     return pl.BlockSpec(memory_space=pltpu.VMEM)
+
+
+def anywhere():
+    return pl.BlockSpec(memory_space=pl.ANY)
 
 
 def iota(shape, dim, dtype=jnp.int32):
@@ -98,7 +101,7 @@
         out_shape=jax.ShapeDtypeStruct((devices, rows, 128), F32),
         in_specs=[vmem()] * 7,
         out_specs=vmem(),
-        compiler_params=params(),
+        compiler_params=params(16),
         name="route",
     )(
         obs_owner.reshape(1, blocks),
@@ -121,19 +124,68 @@
     return jnp.logical_and(lat >= 0, lat < bands * rows)
 
 
-def forward_kernel(slots, bands, group, parts, tile_ref, north_ref, south_ref, west_ref, east_ref,
-                   w1_ref, w2_ref, got_ref, adj_ref, pull_ref, slope_ref, line_ref, shift_ref,
-                   hid_ref, obs_ref, sum_ref):
-    rows, cols, chans = tile_ref.shape
-    span = hid_ref.shape[1]
-    line_ref[0:2, 2 : 2 + cols, :] = north_ref[...].astype(F32)
-    line_ref[2 : 2 + rows, 2 : 2 + cols, :] = tile_ref[...].astype(F32)
-    line_ref[2 + rows :, 2 : 2 + cols, :] = south_ref[...].astype(F32)
-    line_ref[:, 0:2, :] = west_ref[...].astype(F32)
-    line_ref[:, 2 + cols : 4 + cols, :] = east_ref[...].astype(F32)
+def band_copies(bands, piece_refs, all_ref, sems):
+    core = lax.axis_index("lon") & 1
+    lat = lax.axis_index("lat")
+    copies = []
+    for offset in range(bands):
+        band = (lat + bands - offset) % bands
+        for side in range(2):
+            copies.append(
+                pltpu.make_async_copy(
+                    piece_refs[2 * offset + side],
+                    all_ref.at[core if side == 0 else 1 - core, band],
+                    sems.at[offset, side],
+                )
+            )
+    return copies
+
+
+def nearby_copies(bands, piece_refs, near_ref, sems):
+    half = piece_refs[0].shape[0]
+    lon = lax.axis_index("lon")
+    west = lax.shift_right_logical((lon + 2 * half - 1) & (2 * half - 1), 1)
+    east = lax.shift_right_logical((lon + 1) & (2 * half - 1), 1)
+    here = lax.shift_right_logical(lon, 1)
+    copies = []
+    for down, offset in enumerate((1, 0, bands - 1)):
+        mine, other = piece_refs[2 * offset], piece_refs[2 * offset + 1]
+        for over, (source, q) in enumerate(((other, west), (mine, here), (other, east))):
+            copies.append(
+                pltpu.make_async_copy(source.at[q], near_ref.at[down, over], sems.at[down, over])
+            )
+    return copies
+
+
+def fill_line(bands, near_ref, line_ref):
+    rows, cols, chans = near_ref.shape[2:]
+    lat = lax.axis_index("lat")
+    for down, (y, height, first) in enumerate(((0, 2, rows - 2), (2, rows, 0), (2 + rows, 2, 0))):
+        band = lat + down - 1
+        for over, (x, width, left) in enumerate(((0, 2, cols - 2), (2, cols, 0), (2 + cols, 2, 0))):
+            part = near_ref[down, over].astype(F32)[
+                first : first + height, left : left + width
+            ]
+            if down != 1:
+                part = jnp.where(jnp.logical_and(band >= 0, band < bands), part, 0.0)
+            line_ref[y : y + height, x : x + width, :] = part
     line_ref[:, cols + 4 :, :] = jnp.zeros(
         (rows + 4, line_ref.shape[1] - cols - 4, chans), F32
     )
+
+
+def forward_kernel(slots, bands, group, parts, *refs):
+    piece_refs, refs = refs[: 2 * bands], refs[2 * bands :]
+    w1_ref, w2_ref, got_ref, adj_ref, pull_ref, slope_ref = refs[:6]
+    line_ref, shift_ref, hid_ref, obs_ref, sum_ref, near_ref, sems = refs[6:]
+    rows, cols, chans = near_ref.shape[2:]
+    span = hid_ref.shape[1]
+    copies = nearby_copies(bands, piece_refs, near_ref, sems)
+    for copy in copies:
+        copy.start()
+    for copy in copies:
+        copy.wait()
+    fill_line(bands, near_ref, line_ref)
     first = jnp.zeros(((rows + 2) * span, chans), F32)
     for b in range(3):
         shift_ref[...] = (
@@ -238,7 +290,7 @@
 
 
 def forward(slots, bands, pieces, w1, w2, got):
-    rows, cols, chans = pieces[0].shape
+    half, rows, cols, chans = pieces[0].shape
     devices = got.shape[0]
     full, rest, _ = slot_layout(slots)
     groups = full * devices + (devices // 2 if rest else 0)
@@ -249,7 +301,7 @@
             jax.ShapeDtypeStruct((rows * cols, chans), BF16),
             jax.ShapeDtypeStruct(((rows + 2) * SPAN, chans), F32),
         ],
-        in_specs=[vmem()] * 8,
+        in_specs=[anywhere()] * len(pieces) + [vmem()] * 3,
         out_specs=[vmem()] * 3,
         scratch_shapes=[
             pltpu.VMEM((rows + 4, SPAN + 8, chans), F32),
@@ -257,25 +309,26 @@
             pltpu.VMEM((rows + 2, SPAN, chans), F32),
             pltpu.VMEM((FIELDS, groups, 128), F32),
             pltpu.VMEM((chans, rows * cols), F32),
+            pltpu.VMEM((3, 3, rows, cols, chans), BF16),
+            pltpu.SemaphoreType.DMA((3, 3)),
         ],
-        compiler_params=params(),
+        compiler_params=params(24),
         cost_estimate=cost(4e9, 4e6),
         name="forward",
     )(*pieces, w1, w2, got)
 
 
-def spread_matrix(steps, tiles, split):
+def spread_matrix(steps, tiles):
     lons = 16 * steps
+    half = tiles // 2
     place = iota(((steps + 2) * 16, lons), 0)
     lon = (place & 15) * steps + lax.shift_right_logical(place, 4) - 1
     lon = jnp.where(lon < 0, lon + lons, jnp.where(lon >= lons, lon - lons, lon))
     column = iota(((steps + 2) * 16, lons), 1)
-    if split:
-        half = tiles // 2
-        chunk = lax.shift_right_logical(column, 4)
-        core = lax.shift_right_logical(chunk, half.bit_length() - 1)
-        column = (2 * (chunk & (half - 1)) + core) * 16 + (column & 15)
-    return jnp.where(column == lon, 1.0, 0.0).astype(BF16)
+    chunk = lax.shift_right_logical(column, 4)
+    core = lax.shift_right_logical(chunk, half.bit_length() - 1)
+    column = (2 * (chunk & (half - 1)) + core) * 16 + (column & 15)
+    return jnp.where(column == lon, 1.0, 0.0)
 
 
 def spread(line_of, start, lats, matrix, pad_ref):
@@ -300,16 +353,27 @@
     return dot(jnp.concatenate(pieces, axis=1), weight_ref[...].reshape(9 * chans, chans))
 
 
-def whole_kernel(block, all_ref, w1_ref, w2_ref, slope_ref, hidden_ref, state_ref, w2t_ref, pad_ref):
-    bands, tiles, rows, group, chans = all_ref.shape
-    lats, lons = bands * rows, tiles * group
+def whole_kernel(block, *refs):
+    bands = refs[-2].shape[1]
+    piece_refs, refs = refs[: 2 * bands], refs[2 * bands :]
+    w1_ref, w2_ref, slope_ref, hidden_ref, state_ref, w2t_ref, pad_ref, all_ref, sems = refs
+    _, _, half, rows, group, chans = all_ref.shape
+    lats, lons = bands * rows, 2 * half * group
     steps = lons // 16
     size = block * lons
     mine = pad_ref.shape[0] - 4
     base = (lax.axis_index("lon") & 1) * mine
+    copies = band_copies(bands, piece_refs, all_ref, sems)
+    for copy in copies:
+        copy.start()
+    matrix = spread_matrix(steps, 2 * half)
+    for tap in range(9):
+        w2t_ref[tap] = w2_ref[tap].T
+    for copy in copies:
+        copy.wait()
     spread(
-        lambda lat: all_ref[lat // rows, :, lat % rows].reshape(lons, chans),
-        base - 2, lats, spread_matrix(steps, tiles, False).astype(F32), pad_ref,
+        lambda lat: all_ref[:, lat // rows, :, lat % rows].reshape(lons, chans),
+        base - 2, lats, matrix, pad_ref,
     )
 
     def step(index, carry):
@@ -328,13 +392,11 @@
         return carry
 
     lax.fori_loop(0, (mine + 2) // block, step, 0)
-    for tap in range(9):
-        w2t_ref[tap] = w2_ref[tap].T
-
-
-def whole(state_all, w1, w2):
-    bands, tiles, rows, group, chans = state_all.shape
-    lats, lons = bands * rows, tiles * group
+
+
+def whole(bands, pieces, w1, w2):
+    half, rows, group, chans = pieces[0].shape
+    lats, lons = bands * rows, 2 * half * group
     mine = lats // 2
     steps = lons // 16
     cells = (mine + 2) * lons
@@ -346,13 +408,17 @@
             jax.ShapeDtypeStruct((chans, cells), BF16),
             jax.ShapeDtypeStruct((9, chans, chans), BF16),
         ],
-        in_specs=[vmem()] * 3,
+        in_specs=[anywhere()] * len(pieces) + [vmem()] * 2,
         out_specs=[vmem()] * 4,
-        scratch_shapes=[pltpu.VMEM((mine + 4, steps + 2, 16, chans), BF16)],
-        compiler_params=params(),
+        scratch_shapes=[
+            pltpu.VMEM((mine + 4, steps + 2, 16, chans), BF16),
+            pltpu.VMEM((2, bands) + pieces[0].shape, BF16),
+            pltpu.SemaphoreType.DMA((bands, 2)),
+        ],
+        compiler_params=params(28),
         cost_estimate=cost(6e9, 10e6),
         name="whole",
-    )(state_all, w1, w2)
+    )(*pieces, w1, w2)
 
 
 def tap_sums(turned_ref, pad_ref, first_row, rows, sum_ref, out_ref, sem):
@@ -371,9 +437,12 @@
     lax.fori_loop(0, 9, step, 0)
 
 
-def tail_kernel(block, mine_hbm, other_hbm, slope_hbm, hidden_hbm, state_hbm, w2t_ref, g1_hbm,
-                g2_hbm, all_ref, pull_ref, first_ref, slope_ref, hidden_ref, state_ref, g1_ref,
-                g2_ref, big_sems, g1_sems, g2_sems):
+def tail_kernel(block, *refs):
+    bands = (len(refs) - 18) // 2
+    piece_refs, refs = refs[: 2 * bands], refs[2 * bands :]
+    slope_hbm, hidden_hbm, state_hbm, w2t_ref, g1_hbm, g2_hbm = refs[:6]
+    all_ref, pull_ref, first_ref, slope_ref, hidden_ref, state_ref, g1_ref, g2_ref = refs[6:14]
+    piece_sems, big_sems, g1_sems, g2_sems = refs[14:]
     steps = pull_ref.shape[1] - 2
     chans = pull_ref.shape[3]
     lons = steps * 16
@@ -381,23 +450,21 @@
     _, bands, half, rows, cols, _ = all_ref.shape
     lats = bands * rows
     mine = lats // 2
-    core = lax.axis_index("lon") & 1
-    base = core * mine
-    mine_copy = pltpu.make_async_copy(mine_hbm, all_ref.at[core], big_sems.at[0])
-    other_copy = pltpu.make_async_copy(other_hbm, all_ref.at[1 - core], big_sems.at[1])
-    hidden_copy = pltpu.make_async_copy(hidden_hbm, hidden_ref, big_sems.at[2])
+    base = (lax.axis_index("lon") & 1) * mine
+    copies = band_copies(bands, piece_refs, all_ref, piece_sems)
+    hidden_copy = pltpu.make_async_copy(hidden_hbm, hidden_ref, big_sems.at[0])
     slope_copy = pltpu.make_async_copy(
-        slope_hbm.at[pl.ds(lons, mine * lons), :], slope_ref, big_sems.at[3]
-    )
-    state_copy = pltpu.make_async_copy(state_hbm, state_ref, big_sems.at[4])
-    mine_copy.start()
-    other_copy.start()
+        slope_hbm.at[pl.ds(lons, mine * lons), :], slope_ref, big_sems.at[1]
+    )
+    state_copy = pltpu.make_async_copy(state_hbm, state_ref, big_sems.at[2])
+    for copy in copies:
+        copy.start()
     hidden_copy.start()
     slope_copy.start()
     state_copy.start()
-    matrix = spread_matrix(steps, 2 * half, True).astype(F32)
-    mine_copy.wait()
-    other_copy.wait()
+    matrix = spread_matrix(steps, 2 * half)
+    for copy in copies:
+        copy.wait()
     spread(
         lambda lat: all_ref[:, lat // rows, :, lat % rows].reshape(lons, chans),
         base - 1, lats, matrix, pull_ref,
@@ -429,19 +496,18 @@
         pltpu.make_async_copy(g1_ref.at[tap], g1_hbm.at[tap], g1_sems.at[tap]).wait()
 
 
-def tail(mine, other, slope, hidden, state, w2t):
-    bands, half, rows, group, chans = mine.shape
+def tail(bands, pieces, slope, hidden, state, w2t):
+    half, rows, group, chans = pieces[0].shape
     lats, lons = bands * rows, 2 * half * group
     steps = lons // 16
     ours = lats // 2
-    anywhere = pl.BlockSpec(memory_space=pl.ANY)
     return pl.pallas_call(
         functools.partial(tail_kernel, 4),
         out_shape=[jax.ShapeDtypeStruct((9, chans, chans), F32)] * 2,
-        in_specs=[anywhere] * 5 + [vmem()],
-        out_specs=[anywhere] * 2,
+        in_specs=[anywhere()] * (len(pieces) + 3) + [vmem()],
+        out_specs=[anywhere()] * 2,
         scratch_shapes=[
-            pltpu.VMEM((2,) + mine.shape, BF16),
+            pltpu.VMEM((2, bands) + pieces[0].shape, BF16),
             pltpu.VMEM((ours + 2, steps + 2, 16, chans), BF16),
             pltpu.VMEM((ours, steps + 2, 16, chans), BF16),
             pltpu.VMEM((ours * lons, chans), F32),
@@ -449,47 +515,29 @@
             pltpu.VMEM(state.shape, BF16),
             pltpu.VMEM((9, chans, chans), F32),
             pltpu.VMEM((9, chans, chans), F32),
-            pltpu.SemaphoreType.DMA((5,)),
+            pltpu.SemaphoreType.DMA((bands, 2)),
+            pltpu.SemaphoreType.DMA((3,)),
             pltpu.SemaphoreType.DMA((9,)),
             pltpu.SemaphoreType.DMA((9,)),
         ],
-        compiler_params=params(),
+        compiler_params=params(36),
         cost_estimate=cost(10e9, 15e6),
         name="tail",
-    )(mine, other, slope, hidden, state, w2t)
-
-
-def local_kernel(mine_hbm, other_hbm, slope_ref, adj_ref, w1_ref, w2_ref, grad_ref, near_ref,
-                 line_ref, shift_ref, pull_ref, sems):
-    bands, half, rows, cols, chans = mine_hbm.shape
+    )(*pieces, slope, hidden, state, w2t)
+
+
+def local_kernel(bands, *refs):
+    piece_refs, refs = refs[: 2 * bands], refs[2 * bands :]
+    slope_ref, adj_ref, w1_ref, w2_ref, grad_ref = refs[:5]
+    near_ref, line_ref, shift_ref, pull_ref, sems = refs[5:]
+    rows, cols, chans = near_ref.shape[2:]
     span = pull_ref.shape[1]
-    lat, lon = lax.axis_index("lat"), lax.axis_index("lon")
-    west = lax.shift_right_logical((lon + 2 * half - 1) & (2 * half - 1), 1)
-    east = lax.shift_right_logical((lon + 1) & (2 * half - 1), 1)
-    here = lax.shift_right_logical(lon, 1)
-    copies = []
-    for down in range(3):
-        band = jnp.clip(lat + down - 1, 0, bands - 1)
-        for over, (source, q) in enumerate(((other_hbm, west), (mine_hbm, here), (other_hbm, east))):
-            copy = pltpu.make_async_copy(
-                source.at[band, q], near_ref.at[down, over], sems.at[down, over]
-            )
-            copy.start()
-            copies.append(copy)
-    line_ref[:, cols + 4 :, :] = jnp.zeros(
-        (rows + 4, line_ref.shape[1] - cols - 4, chans), F32
-    )
+    copies = nearby_copies(bands, piece_refs, near_ref, sems)
+    for copy in copies:
+        copy.start()
     for copy in copies:
         copy.wait()
-    for down, (y, height, first) in enumerate(((0, 2, rows - 2), (2, rows, 0), (2 + rows, 2, 0))):
-        band = lat + down - 1
-        for over, (x, width, left) in enumerate(((0, 2, cols - 2), (2, cols, 0), (2 + cols, 2, 0))):
-            part = near_ref[down, over].astype(F32)[
-                first : first + height, left : left + width
-            ]
-            if down != 1:
-                part = jnp.where(jnp.logical_and(band >= 0, band < bands), part, 0.0)
-            line_ref[y : y + height, x : x + width, :] = part
+    fill_line(bands, near_ref, line_ref)
     back = jnp.zeros(((rows + 2) * span, chans), F32)
     for b in range(3):
         shift_ref[...] = (
@@ -511,12 +559,12 @@
     grad_ref[...] = total
 
 
-def local_grad(mine, other, slope, adjoint, w1, w2):
-    bands, half, rows, cols, chans = mine.shape
+def local_grad(bands, pieces, slope, adjoint, w1, w2):
+    half, rows, cols, chans = pieces[0].shape
     return pl.pallas_call(
-        local_kernel,
+        functools.partial(local_kernel, bands),
         out_shape=jax.ShapeDtypeStruct((rows * cols, chans), F32),
-        in_specs=[pl.BlockSpec(memory_space=pl.ANY)] * 2 + [vmem()] * 4,
+        in_specs=[anywhere()] * len(pieces) + [vmem()] * 4,
         out_specs=vmem(),
         scratch_shapes=[
             pltpu.VMEM((3, 3, rows, cols, chans), BF16),
@@ -525,10 +573,10 @@
             pltpu.VMEM((rows + 2, SPAN, chans), F32),
             pltpu.SemaphoreType.DMA((3, 3)),
         ],
-        compiler_params=params(),
+        compiler_params=params(16),
         cost_estimate=cost(3e9, 4e6),
         name="local_grad",
-    )(mine, other, slope, adjoint, w1, w2)
+    )(*pieces, slope, adjoint, w1, w2)
 
 
 def with_halo(x, sides, width, wrap):
@@ -693,33 +741,20 @@
     return (state_grad, grad_first, grad_second)
 
 
-def halo_pieces(x):
-    bands, tiles = lax.axis_size("lat"), lax.axis_size("lon")
-    rows, cols, _ = x.shape
-    north = lax.ppermute(x[rows - 2 :], "lat", [(i, i + 1) for i in range(bands - 1)])
-    south = lax.ppermute(x[:2], "lat", [(i + 1, i) for i in range(bands - 1)])
-    last = jnp.concatenate([p[:, cols - 2 :] for p in (north, x, south)], axis=0)
-    first = jnp.concatenate([p[:, :2] for p in (north, x, south)], axis=0)
-    west = lax.ppermute(last, "lon", [(i, (i + 1) % tiles) for i in range(tiles)])
-    east = lax.ppermute(first, "lon", [((i + 1) % tiles, i) for i in range(tiles)])
-    return x, north, south, west, east
-
-
-def gather_state(x):
-    bands, tiles = lax.axis_size("lat"), lax.axis_size("lon")
-    return lax.all_gather(x, ("lat", "lon")).reshape((bands, tiles) + x.shape)
-
-
 def gather_tiles(x):
     bands, tiles = lax.axis_size("lat"), lax.axis_size("lon")
     half = tiles // 2
     same = [[2 * q + core for q in range(half)] for core in range(2)]
+    swap = [(i, i ^ 1) for i in range(tiles)]
     copies = jnp.broadcast_to(x[None], (half,) + x.shape)
     line = lax.all_to_all(copies, "lon", 0, 0, axis_index_groups=same, tiled=True)
-    copies = jnp.broadcast_to(line[None], (bands,) + line.shape)
-    mine = lax.all_to_all(copies, "lat", 0, 0, tiled=True)
-    other = lax.ppermute(mine, "lon", [(i, i ^ 1) for i in range(tiles)])
-    return mine, other
+    mine = [line]
+    for step in range(1, bands):
+        mine.append(lax.ppermute(line, "lat", [(i, (i + step) % bands) for i in range(bands)]))
+    pieces = []
+    for part in mine:
+        pieces += [part, lax.ppermute(part, "lon", swap)]
+    return pieces
 
 
 def per_device(
@@ -735,22 +770,21 @@
             obs_frac, obs_value, obs_weight,
         )
     slots = max(2, 3 * obs_value.shape[0] // (2 * devices))
-    state_all = gather_state(state)
-    pieces = halo_pieces(state)
+    state_pieces = gather_tiles(state)
     outgoing = route(
         devices, slots, chans, obs_owner, obs_cell, obs_level, obs_count, obs_frac, obs_value,
         obs_weight,
     )
     got = lax.all_to_all(outgoing, ("lat", "lon"), split_axis=0, concat_axis=0, tiled=True)
     adjoint, pullback, near_slope = forward(
-        slots, bands, pieces, weight_first, weight_second, got
-    )
-    mine, other = gather_tiles(pullback.reshape(rows, cols, chans))
-    slope, hidden, turned, w2t = whole(state_all, weight_first, weight_second)
-    sums = tail(mine, other, slope, hidden, turned, w2t)
+        slots, bands, state_pieces, weight_first, weight_second, got
+    )
+    pull_pieces = gather_tiles(pullback.reshape(rows, cols, chans))
+    slope, hidden, turned, w2t = whole(bands, state_pieces, weight_first, weight_second)
+    sums = tail(bands, pull_pieces, slope, hidden, turned, w2t)
     swap = [(i, i ^ 1) for i in range(lax.axis_size("lon"))]
     theirs = [lax.ppermute(part, "lon", swap) for part in sums]
-    grad = local_grad(mine, other, near_slope, adjoint, weight_first, weight_second)
+    grad = local_grad(bands, pull_pieces, near_slope, adjoint, weight_first, weight_second)
     g1, g2 = [part + their for part, their in zip(sums, theirs)]
     return grad.reshape(rows, cols, chans), g1, g2
 

time: 122 us -> 115 us (0.943)
  waiting for transfers between devices: 4.51 us -> 22.9 us
  between operations: 14.2 us -> 0.75 us
  Pallas kernels: 44.9 us -> 32.7 us
  starting transfers between devices: 17.3 us -> 7.71 us
  blocking collectives: 29.6 us -> 38.6 us
  local copies, waits for them, and re-layouts: 4.24 us -> 8.35 us
  other arithmetic: 6.95 us -> 3.42 us
    ppermute x5 -> x14, waiting for transfers between devices: 2.57 us -> 20.2 us  [the longest x6 20.2 us: gather_tiles(): lax.ppermute(line, 'lat', [(i, (i + step) % bands) for i in range(bands)])]
    all_to_all x1 -> x2, blocking collectives: 12.3 us -> 27 us  [gather_tiles(): lax.all_to_all(copies, 'lon', 0, 0, axis_index_groups=same, tiled=True)]
    all_to_all x1 -> x0, starting transfers between devices: 6.32 us -> none  [per_device(): lax.all_to_all(outgoing, ('lat', 'lon'), split_axis=0, concat_axis=0, til...]
    unnamed x18 -> x22, local copies, waits for them, and re-layouts: 1.74 us -> 7.48 us
    all_to_all x1, blocking collectives: 17.3 us -> 11.6 us  [per_device(): lax.all_to_all(outgoing, ('lat', 'lon'), split_axis=0, concat_axis=0, til...]
    pallas_call x1, Pallas kernels: 10.6 us -> 5.99 us  [whole(): pl.pallas_call(functools.partial(whole_kernel, 3), out_shape=[jax.ShapeDt...]
    add x2, other arithmetic: 6.9 us -> 3.42 us  [per_device(): g1, g2 = [part + their for part, their in zip(sums, theirs)]]
    ppermute x5 -> x14, starting transfers between devices: 10.4 us -> 7.13 us  [the longest x6 6.1 us: gather_tiles(): lax.ppermute(line, 'lat', [(i, (i + step) % bands) for i in range(bands)])]
  transfers between devices with their start and end apart: 9 -> 16, of which waited for: 2 -> 6; matrix products, arithmetic and copies ran while one was open for 5% -> 1% of each run, Pallas kernels for 24% -> 9%
where the time goes in v6:
time: 115 us; the launch traced here: 114 us
  blocking collectives  38.6 us (34%)
  Pallas kernels  32.7 us (28%)
  waiting for transfers between devices  22.9 us (20%)
  local copies, waits for them, and re-layouts  8.35 us (7%)
  starting transfers between devices  7.71 us (7%)
  other arithmetic  3.42 us (3%)
    all_to_all x2, blocking collectives, gather_tiles(): lax.all_to_all(copies, 'lon', 0, 0, axis_index_groups=same, tiled=True)  27 us
    ppermute x6, waiting for transfers between devices, gather_tiles(): lax.ppermute(line, 'lat', [(i, (i + step) % bands) for i in range(bands)])  20.2 us
    pallas_call x1, Pallas kernels, tail(): pl.pallas_call(functools.partial(tail_kernel, 4), out_shape=[jax.ShapeDty...  13.4 us
    all_to_all x1, blocking collectives, per_device(): lax.all_to_all(outgoing, ('lat', 'lon'), split_axis=0, concat_axis=0, til...  11.6 us
    pallas_call x1, Pallas kernels, forward(): pl.pallas_call(functools.partial(forward_kernel, slots, bands, 2, 4), out...  9.05 us
    unnamed x22, local copies, waits for them, and re-layouts  7.48 us
    ppermute x6, starting transfers between devices, gather_tiles(): lax.ppermute(line, 'lat', [(i, (i + step) % bands) for i in range(bands)])  6.1 us
    pallas_call x1, Pallas kernels, whole(): pl.pallas_call(functools.partial(whole_kernel, 3), out_shape=[jax.ShapeDt...  5.99 us
  transfers between devices with their start and end apart: 16, of which 6 were waited for; matrix products, arithmetic and copies ran while one was open for 1% of the time, Pallas kernels for 9%

profile of v6, /device:TPU:0, one launch (start us, length us, event | category | flops | bytes accessed | tf_op | source)
XLA Modules:
  0.0 114.5 jit_solution(6174932357548045343)
XLA Ops:
  0.6 0.9 broadcast_in_dim.6
  1.5 15.0 %all_to_all.15.refs_0_ = bf16[4,8,16,256]{3,2,1,0:T(8,128)(2,1)S(1)} all-to-all(bf16[4,8,16,256]{3,2,1,0:T(8,128)(2,1)S(1)} %broadcast_in_dim.6), channel_id=1, replica_groups={{0,2,4,6},{1,3,5,7},{8,10,12,14},{9,11,13,15},{16,18,20,22},{17,19,21,2..., dimensions={0} | all-to-all | bytes 524288 | tf_op jit(solution)/shard_map/all_to_all | solution.py:750
  16.5 2.4 %collective-permute-start.5 = (bf16[4,8,16,256]{3,2,1,0:T(8,128)(2,1)S(1)}, bf16[4,8,16,256]{3,2,1,0:T(8,128)(2,1)S(1)}, u32[]{:S(2)}, u32[]{:S(2)}) collective-permute-start(bf16[4,8,16,256]{3,2,1,0:T(8,128)(2,1)S(1)} %all_to_all.15.refs_0_), channel_id=1, source_target_pairs={{0,24},{8,0},{16,8},{24,16},{1,25},{9,1},{17,9},{25,17},{2,26},{10... | collective-permute-start | bytes 786440 | tf_op jit(solution)/shard_map/ppermute | solution.py:753
  18.9 0.5 collective-permute-start.3
  19.4 0.6 collective-permute-start.1
  20.0 0.0 collective-permute-start
  20.0 5.6 %collective-permute-done.5.refs_6_ = bf16[4,8,16,256]{3,2,1,0:T(8,128)(2,1)S(1)} collective-permute-done((bf16[4,8,16,256]{3,2,1,0:T(8,128)(2,1)S(1)}, bf16[4,8,16,256]{3,2,1,0:T(8,128)(2,1)S(1)}, u32[]{:S(2)}, u32[]{:S(2)}) %collective-permute-start.5) | collective-permute-done | bytes 262176 | tf_op jit(solution)/shard_map/ppermute | solution.py:753
  25.6 4.4 %collective-permute-done.3.refs_4_ = bf16[4,8,16,256]{3,2,1,0:T(8,128)(2,1)S(1)} collective-permute-done((bf16[4,8,16,256]{3,2,1,0:T(8,128)(2,1)S(1)}, bf16[4,8,16,256]{3,2,1,0:T(8,128)(2,1)S(1)}, u32[]{:S(2)}, u32[]{:S(2)}) %collective-permute-start.3) | collective-permute-done | bytes 262176 | tf_op jit(solution)/shard_map/ppermute | solution.py:753
  30.0 0.0 collective-permute-start.4
  30.0 0.0 collective-permute-done.1.refs_2_
  30.0 0.5 collective-permute-start.2
  30.6 0.8 copy-done
  31.3 0.7 copy-done.1
  32.0 0.7 copy-done.2
  32.8 0.7 copy-done.3
  33.5 0.7 copy-done.4
  34.2 0.7 copy-done.5
  34.8 0.7 copy-done.6
  35.5 1.2 %route.1 = f32[32,8,128]{2,1,0:T(8,128)S(1)} custom-call(s32[1,128]{1,0:T(1,128)S(1)} %bitcast.15, s32[1,128]{1,0:T(1,128)S(1)} %bitcast.16, s32[32,128]{1,0:T(8,128)S(1)} %bitcast.11, s32[32,128]{1,0:T(8,128)S(1)} %bitcast.12, f32[2,32,128]{2,1,0:T(8,128)S(1)} %bitcast.10, f32[32,128]{1,0:T(8,128)S(1)} %bitcast.13, f32[32,128]{1,0:T(8,128)S(1)} %bitcast.14), custom_call_target="tpu_custom_call" | custom-call | tf_op jit(solution)/shard_map/route/pallas_call | solution.py:99
  36.7 11.6 %all_to_all.16.refs_10_ = f32[32,8,128]{2,1,0:T(8,128)S(1)} all-to-all(f32[32,8,128]{2,1,0:T(8,128)S(1)} %route.1), channel_id=1, replica_groups=mesh['lat'=4,'lon'=8] {'lat','lon'}, dimensions={0} | all-to-all | bytes 262144 | tf_op jit(solution)/shard_map/all_to_all | solution.py:778
  48.3 0.0 collective-permute-done.refs_1_
  48.3 0.0 collective-permute-done.6.refs_7_
  48.3 0.0 collective-permute-done.4.refs_5_
  48.4 0.0 copy-start.7
  48.4 1.3 %copy-done.7 = bf16[9,256,256]{2,1,0:T(8,128)(2,1)S(1)} copy-done((bf16[9,256,256]{2,1,0:T(8,128)(2,1)S(1)}, bf16[9,256,256]{2,1,0:T(8,128)(2,1)}, u32[]{:S(2)}) %copy-start.7) | copy-done | bytes 1179672
  49.6 1.3 %copy-done.9 = bf16[9,256,256]{2,1,0:T(8,128)(2,1)S(1)} copy-done((bf16[9,256,256]{2,1,0:T(8,128)(2,1)S(1)}, bf16[9,256,256]{2,1,0:T(8,128)(2,1)}, u32[]{:S(2)}) %copy-start.9) | copy-done | bytes 1179672
  50.9 9.0 %forward.1 = (f32[128,256]{1,0:T(8,128)S(1)}, bf16[128,256]{1,0:T(8,128)(2,1)S(1)}, f32[320,256]{1,0:T(8,128)S(1)}) custom-call(bf16[4,8,16,256]{3,2,1,0:T(8,128)(2,1)S(1)} %all_to_all.15.refs_0_, bf16[4,8,16,256]{3,2,1,0:T(8,128)(2,1)S(1)} %collective-permute-done.refs_1_, bf16[4,8,16,256]{3,2,1,0:T(8,128)(2,1)S(1)} %collective-permute-done.1.refs_2_, ...), custom_call_target="tpu_custom_call" | custom-call | flops 4000000000 | bytes 4000000 | tf_op jit(solution)/shard_map/forward/pallas_call | solution.py:297
  60.0 12.0 %all_to_all.17.refs_0_ = bf16[4,8,16,256]{3,2,1,0:T(8,128)(2,1)S(1)} all-to-all(bf16[4,8,16,256]{3,2,1,0:T(8,128)(2,1)S(1)} %broadcast_in_dim.15), channel_id=1, replica_groups={{0,2,4,6},{1,3,5,7},{8,10,12,14},{9,11,13,15},{16,18,20,22},{17,19,21,2..., dimensions={0} | all-to-all | bytes 524288 | tf_op jit(solution)/shard_map/all_to_all | solution.py:750
  72.0 0.6 collective-permute-start.12
  72.6 1.0 collective-permute-start.10
  73.5 1.0 collective-permute-start.8
  74.6 0.0 collective-permute-start.7
  74.6 6.7 %collective-permute-done.12.refs_6_ = bf16[4,8,16,256]{3,2,1,0:T(8,128)(2,1)S(1)} collective-permute-done((bf16[4,8,16,256]{3,2,1,0:T(8,128)(2,1)S(1)}, bf16[4,8,16,256]{3,2,1,0:T(8,128)(2,1)S(1)}, u32[]{:S(2)}, u32[]{:S(2)}) %collective-permute-start.12) | collective-permute-done | bytes 262176 | tf_op jit(solution)/shard_map/ppermute | solution.py:753
  81.2 0.0 collective-permute-start.13
  81.2 3.5 %collective-permute-done.10.refs_4_ = bf16[4,8,16,256]{3,2,1,0:T(8,128)(2,1)S(1)} collective-permute-done((bf16[4,8,16,256]{3,2,1,0:T(8,128)(2,1)S(1)}, bf16[4,8,16,256]{3,2,1,0:T(8,128)(2,1)S(1)}, u32[]{:S(2)}, u32[]{:S(2)}) %collective-permute-start.10) | collective-permute-done | bytes 262176 | tf_op jit(solution)/shard_map/ppermute | solution.py:753
  84.7 0.0 collective-permute-start.11
  84.7 0.0 collective-permute-done.8.refs_2_
  84.8 0.5 collective-permute-start.9
  85.3 6.0 %whole.1 = (f32[2304,256]{1,0:T(8,128)S(1)}, bf16[256,2304]{1,0:T(8,128)(2,1)S(1)}, bf16[256,2304]{1,0:T(8,128)(2,1)S(1)}, bf16[9,256,256]{2,1,0:T(8,128)(2,1)S(1)}) custom-call(bf16[4,8,16,256]{3,2,1,0:T(8,128)(2,1)S(1)} %all_to_all.15.refs_0_, bf16[4,8,16,256]{3,2,1,0:T(8,128)(2,1)S(1)} %collective-permute-done.refs_1_, ...), custom_call_target="tpu_custom_call" | custom-call | flops 6000000000 | bytes 10000000 | tf_op jit(solution)/shard_map/whole/pallas_call | solution.py:403
  91.3 0.0 collective-permute-done.13.refs_7_
  91.3 13.4 %tail.1 = (f32[9,256,256]{2,1,0:T(8,128)S(1)}, f32[9,256,256]{2,1,0:T(8,128)S(1)}) custom-call(bf16[4,8,16,256]{3,2,1,0:T(8,128)(2,1)S(1)} %all_to_all.17.refs_0_, bf16[4,8,16,256]{3,2,1,0:T(8,128)(2,1)S(1)} %collective-permute-done.7.refs_1_, bf16[4,8,16,256]{3,2,1,0:T(8,128)(2,1)S(1)} %collective-permute-done.8.refs_2_, ...), custom_call_target="tpu_custom_call" | custom-call | flops 10000000000 | bytes 15000000 | tf_op jit(solution)/shard_map/tail/pallas_call | solution.py:504
  104.8 0.1 collective-permute-start.14
  104.9 0.5 collective-permute-start.15
  105.3 3.0 %local_grad.1 = f32[128,256]{1,0:T(8,128)} custom-call(bf16[4,8,16,256]{3,2,1,0:T(8,128)(2,1)S(1)} %all_to_all.17.refs_0_, bf16[4,8,16,256]{3,2,1,0:T(8,128)(2,1)S(1)} %collective-permute-done.7.refs_1_, bf16[4,8,16,256]{3,2,1,0:T(8,128)(2,1)S(1)} %collective-permute-done.8.refs_2_, bf16[4,8,16,256]{3,2,1,0:T(8,128)(2,1)S(1)} %collective-permute-done.9.refs_3_, ...), custom_call_target="tpu_custom_call" | custom-call | flops 3000000000 | bytes 4000000 | tf_op jit(solution)/shard_map/local_grad/pallas_call | solution.py:564
  108.4 1.0 collective-permute-done.14
  109.4 1.7 %add.6 = f32[9,256,256]{2,1,0:T(8,128)} add(f32[9,256,256]{2,1,0:T(8,128)S(1)} %get-tuple-element.19, f32[9,256,256]{2,1,0:T(8,128)S(1)} %collective-permute-done.14) | non-fusion elementwise | flops 589824 | bytes 7077888 | tf_op jit(solution)/shard_map/add | solution.py:788
  111.1 1.7 %collective-permute-done.15 = f32[9,256,256]{2,1,0:T(8,128)S(1)} collective-permute-done((f32[9,256,256]{2,1,0:T(8,128)S(1)}, f32[9,256,256]{2,1,0:T(8,128)S(1)}, u32[]{:S(2)}, u32[]{:S(2)}) %collective-permute-start.15) | collective-permute-done | bytes 2359328 | tf_op jit(solution)/shard_map/ppermute | solution.py:786
  112.7 1.7 %add.7 = f32[9,256,256]{2,1,0:T(8,128)} add(f32[9,256,256]{2,1,0:T(8,128)S(1)} %get-tuple-element.20, f32[9,256,256]{2,1,0:T(8,128)S(1)} %collective-permute-done.15) | non-fusion elementwise | flops 589824 | bytes 7077888 | tf_op jit(solution)/shard_map/add | solution.py:788
  (18 shorter events, 0.1 us)
Async XLA Ops:
  16.5 9.1 %collective-permute-start.5 = (bf16[4,8,16,256]{3,2,1,0:T(8,128)(2,1)S(1)}, bf16[4,8,16,256]{3,2,1,0:T(8,128)(2,1)S(1)}, u32[]{:S(2)}, u32[]{:S(2)}) collective-permute-start(bf16[4,8,16,256]{3,2,1,0:T(8,128)(2,1)S(1)} %all_to_all.15.refs_0_), channel_id=1, source_target_pairs={{0,24},{8,0},{16,8},{24,16},{1,25},{9,1},{17,9},{25,17},{2,26},{10... | collective-permute-start | bytes 786440 | tf_op jit(solution)/shard_map/ppermute | solution.py:753
  18.9 11.1 %collective-permute-start.3 = (bf16[4,8,16,256]{3,2,1,0:T(8,128)(2,1)S(1)}, bf16[4,8,16,256]{3,2,1,0:T(8,128)(2,1)S(1)}, u32[]{:S(2)}, u32[]{:S(2)}) collective-permute-start(bf16[4,8,16,256]{3,2,1,0:T(8,128)(2,1)S(1)} %all_to_all.15.refs_0_), channel_id=1, source_target_pairs={{0,16},{8,24},{16,0},{24,8},{1,17},{9,25},{17,1},{25,9},{2,18},{10... | collective-permute-start | bytes 786440 | tf_op jit(solution)/shard_map/ppermute | solution.py:753
  19.4 10.6 %collective-permute-start.1 = (bf16[4,8,16,256]{3,2,1,0:T(8,128)(2,1)S(1)}, bf16[4,8,16,256]{3,2,1,0:T(8,128)(2,1)S(1)}, u32[]{:S(2)}, u32[]{:S(2)}) collective-permute-start(bf16[4,8,16,256]{3,2,1,0:T(8,128)(2,1)S(1)} %all_to_all.15.refs_0_), channel_id=1, source_target_pairs={{0,8},{8,16},{16,24},{24,0},{1,9},{9,17},{17,25},{25,1},{2,10},{10... | collective-permute-start | bytes 786440 | tf_op jit(solution)/shard_map/ppermute | solution.py:753
  20.0 28.3 %collective-permute-start = (bf16[4,8,16,256]{3,2,1,0:T(8,128)(2,1)S(1)}, bf16[4,8,16,256]{3,2,1,0:T(8,128)(2,1)S(1)}, u32[]{:S(2)}, u32[]{:S(2)}) collective-permute-start(bf16[4,8,16,256]{3,2,1,0:T(8,128)(2,1)S(1)} %all_to_all.15.refs_0_), channel_id=1, source_target_pairs={{0,1},{1,0},{2,3},{3,2},{4,5},{5,4},{6,7},{7,6},{8,9},{9,8},{10,11... | collective-permute-start | bytes 786440 | tf_op jit(solution)/shard_map/ppermute | solution.py:756
  25.6 22.7 %collective-permute-start.6 = (bf16[4,8,16,256]{3,2,1,0:T(8,128)(2,1)S(1)}, bf16[4,8,16,256]{3,2,1,0:T(8,128)(2,1)S(1)}, u32[]{:S(2)}, u32[]{:S(2)}) collective-permute-start(bf16[4,8,16,256]{3,2,1,0:T(8,128)(2,1)S(1)} %collective-permute-done.5.refs_6_), channel_id=1, source_target_pairs={{0,1},{1,0},{2,3},{3,2},{4,5},{5,4},{6,7},{7,6},{8,9},{9,8},{10,11... | collective-permute-start | bytes 786440 | tf_op jit(solution)/shard_map/ppermute | solution.py:756
  30.0 18.3 %collective-permute-start.4 = (bf16[4,8,16,256]{3,2,1,0:T(8,128)(2,1)S(1)}, bf16[4,8,16,256]{3,2,1,0:T(8,128)(2,1)S(1)}, u32[]{:S(2)}, u32[]{:S(2)}) collective-permute-start(bf16[4,8,16,256]{3,2,1,0:T(8,128)(2,1)S(1)} %collective-permute-done.3.refs_4_), channel_id=1, source_target_pairs={{0,1},{1,0},{2,3},{3,2},{4,5},{5,4},{6,7},{7,6},{8,9},{9,8},{10,11... | collective-permute-start | bytes 786440 | tf_op jit(solution)/shard_map/ppermute | solution.py:756
  30.0 18.3 %collective-permute-start.2 = (bf16[4,8,16,256]{3,2,1,0:T(8,128)(2,1)S(1)}, bf16[4,8,16,256]{3,2,1,0:T(8,128)(2,1)S(1)}, u32[]{:S(2)}, u32[]{:S(2)}) collective-permute-start(bf16[4,8,16,256]{3,2,1,0:T(8,128)(2,1)S(1)} %collective-permute-done.1.refs_2_), channel_id=1, source_target_pairs={{0,1},{1,0},{2,3},{3,2},{4,5},{5,4},{6,7},{7,6},{8,9},{9,8},{10,11... | collective-permute-start | bytes 786440 | tf_op jit(solution)/shard_map/ppermute | solution.py:756
  30.6 0.8 copy-start
  31.3 0.7 copy-start.1
  32.0 0.7 copy-start.2
  32.8 0.7 copy-start.3
  33.5 0.7 copy-start.4
  34.2 0.7 copy-start.5
  34.8 0.7 copy-start.6
  48.4 1.3 %copy-start.7 = (bf16[9,256,256]{2,1,0:T(8,128)(2,1)S(1)}, bf16[9,256,256]{2,1,0:T(8,128)(2,1)}, u32[]{:S(2)}) copy-start(bf16[9,256,256]{2,1,0:T(8,128)(2,1)} %refs_8_.3) | copy-start | bytes 3538948
  49.6 1.3 %copy-start.9 = (bf16[9,256,256]{2,1,0:T(8,128)(2,1)S(1)}, bf16[9,256,256]{2,1,0:T(8,128)(2,1)}, u32[]{:S(2)}) copy-start(bf16[9,256,256]{2,1,0:T(8,128)(2,1)} %refs_9_.3) | copy-start | bytes 3538948
  50.9 34.4 %copy-start.8 = (bf16[9,256,256]{2,1,0:T(8,128)(2,1)S(1)}, bf16[9,256,256]{2,1,0:T(8,128)(2,1)}, u32[]{:S(2)}) copy-start(bf16[9,256,256]{2,1,0:T(8,128)(2,1)} %refs_8_.3) | copy-start | bytes 3538948
  50.9 34.4 %copy-start.10 = (bf16[9,256,256]{2,1,0:T(8,128)(2,1)S(1)}, bf16[9,256,256]{2,1,0:T(8,128)(2,1)}, u32[]{:S(2)}) copy-start(bf16[9,256,256]{2,1,0:T(8,128)(2,1)} %refs_9_.3) | copy-start | bytes 3538948
  72.0 9.2 %collective-permute-start.12 = (bf16[4,8,16,256]{3,2,1,0:T(8,128)(2,1)S(1)}, bf16[4,8,16,256]{3,2,1,0:T(8,128)(2,1)S(1)}, u32[]{:S(2)}, u32[]{:S(2)}) collective-permute-start(bf16[4,8,16,256]{3,2,1,0:T(8,128)(2,1)S(1)} %all_to_all.17.refs_0_), channel_id=1, source_target_pairs={{0,24},{8,0},{16,8},{24,16},{1,25},{9,1},{17,9},{25,17},{2,26},{10... | collective-permute-start | bytes 786440 | tf_op jit(solution)/shard_map/ppermute | solution.py:753
  72.6 12.2 %collective-permute-start.10 = (bf16[4,8,16,256]{3,2,1,0:T(8,128)(2,1)S(1)}, bf16[4,8,16,256]{3,2,1,0:T(8,128)(2,1)S(1)}, u32[]{:S(2)}, u32[]{:S(2)}) collective-permute-start(bf16[4,8,16,256]{3,2,1,0:T(8,128)(2,1)S(1)} %all_to_all.17.refs_0_), channel_id=1, source_target_pairs={{0,16},{8,24},{16,0},{24,8},{1,17},{9,25},{17,1},{25,9},{2,18},{10... | collective-permute-start | bytes 786440 | tf_op jit(solution)/shard_map/ppermute | solution.py:753
  73.5 11.2 %collective-permute-start.8 = (bf16[4,8,16,256]{3,2,1,0:T(8,128)(2,1)S(1)}, bf16[4,8,16,256]{3,2,1,0:T(8,128)(2,1)S(1)}, u32[]{:S(2)}, u32[]{:S(2)}) collective-permute-start(bf16[4,8,16,256]{3,2,1,0:T(8,128)(2,1)S(1)} %all_to_all.17.refs_0_), channel_id=1, source_target_pairs={{0,8},{8,16},{16,24},{24,0},{1,9},{9,17},{17,25},{25,1},{2,10},{10... | collective-permute-start | bytes 786440 | tf_op jit(solution)/shard_map/ppermute | solution.py:753
  74.6 16.7 %collective-permute-start.7 = (bf16[4,8,16,256]{3,2,1,0:T(8,128)(2,1)S(1)}, bf16[4,8,16,256]{3,2,1,0:T(8,128)(2,1)S(1)}, u32[]{:S(2)}, u32[]{:S(2)}) collective-permute-start(bf16[4,8,16,256]{3,2,1,0:T(8,128)(2,1)S(1)} %all_to_all.17.refs_0_), channel_id=1, source_target_pairs={{0,1},{1,0},{2,3},{3,2},{4,5},{5,4},{6,7},{7,6},{8,9},{9,8},{10,11... | collective-permute-start | bytes 786440 | tf_op jit(solution)/shard_map/ppermute | solution.py:756
  81.2 10.0 %collective-permute-start.13 = (bf16[4,8,16,256]{3,2,1,0:T(8,128)(2,1)S(1)}, bf16[4,8,16,256]{3,2,1,0:T(8,128)(2,1)S(1)}, u32[]{:S(2)}, u32[]{:S(2)}) collective-permute-start(bf16[4,8,16,256]{3,2,1,0:T(8,128)(2,1)S(1)} %collective-permute-done.12.refs_6_), channel_id=1, source_target_pairs={{0,1},{1,0},{2,3},{3,2},{4,5},{5,4},{6,7},{7,6},{8,9},{9,8},{10,11... | collective-permute-start | bytes 786440 | tf_op jit(solution)/shard_map/ppermute | solution.py:756
  84.7 6.5 %collective-permute-start.11 = (bf16[4,8,16,256]{3,2,1,0:T(8,128)(2,1)S(1)}, bf16[4,8,16,256]{3,2,1,0:T(8,128)(2,1)S(1)}, u32[]{:S(2)}, u32[]{:S(2)}) collective-permute-start(bf16[4,8,16,256]{3,2,1,0:T(8,128)(2,1)S(1)} %collective-permute-done.10.refs_4_), channel_id=1, source_target_pairs={{0,1},{1,0},{2,3},{3,2},{4,5},{5,4},{6,7},{7,6},{8,9},{9,8},{10,11... | collective-permute-start | bytes 786440 | tf_op jit(solution)/shard_map/ppermute | solution.py:756
  84.8 6.6 %collective-permute-start.9 = (bf16[4,8,16,256]{3,2,1,0:T(8,128)(2,1)S(1)}, bf16[4,8,16,256]{3,2,1,0:T(8,128)(2,1)S(1)}, u32[]{:S(2)}, u32[]{:S(2)}) collective-permute-start(bf16[4,8,16,256]{3,2,1,0:T(8,128)(2,1)S(1)} %collective-permute-done.8.refs_2_), channel_id=1, source_target_pairs={{0,1},{1,0},{2,3},{3,2},{4,5},{5,4},{6,7},{7,6},{8,9},{9,8},{10,11... | collective-permute-start | bytes 786440 | tf_op jit(solution)/shard_map/ppermute | solution.py:756
  104.8 4.6 %collective-permute-start.14 = (f32[9,256,256]{2,1,0:T(8,128)S(1)}, f32[9,256,256]{2,1,0:T(8,128)S(1)}, u32[]{:S(2)}, u32[]{:S(2)}) collective-permute-start(f32[9,256,256]{2,1,0:T(8,128)S(1)} %get-tuple-element.19), channel_id=1, source_target_pairs={{0,1},{1,0},{2,3},{3,2},{4,5},{5,4},{6,7},{7,6},{8,9},{9,8},{10,11... | collective-permute-start | bytes 7077896 | tf_op jit(solution)/shard_map/ppermute | solution.py:786
  104.9 7.9 %collective-permute-start.15 = (f32[9,256,256]{2,1,0:T(8,128)S(1)}, f32[9,256,256]{2,1,0:T(8,128)S(1)}, u32[]{:S(2)}, u32[]{:S(2)}) collective-permute-start(f32[9,256,256]{2,1,0:T(8,128)S(1)} %get-tuple-element.20), channel_id=1, source_target_pairs={{0,1},{1,0},{2,3},{3,2},{4,5},{5,4},{6,7},{7,6},{8,9},{9,8},{10,11... | collective-permute-start | bytes 7077896 | tf_op jit(solution)/shard_map/ppermute | solution.py:786

commit v7 on v6

--- a/solution.py
+++ b/solution.py
@@ -174,18 +174,19 @@
     )
 
 
-def forward_kernel(slots, bands, group, parts, *refs):
-    piece_refs, refs = refs[: 2 * bands], refs[2 * bands :]
-    w1_ref, w2_ref, got_ref, adj_ref, pull_ref, slope_ref = refs[:6]
-    line_ref, shift_ref, hid_ref, obs_ref, sum_ref, near_ref, sems = refs[6:]
-    rows, cols, chans = near_ref.shape[2:]
+def forward_kernel(slots, bands, group, parts, tile_ref, north_ref, south_ref, west_ref, east_ref,
+                   w1_ref, w2_ref, got_ref, adj_ref, pull_ref, slope_ref, line_ref, shift_ref,
+                   hid_ref, obs_ref, sum_ref):
+    rows, cols, chans = tile_ref.shape
     span = hid_ref.shape[1]
-    copies = nearby_copies(bands, piece_refs, near_ref, sems)
-    for copy in copies:
-        copy.start()
-    for copy in copies:
-        copy.wait()
-    fill_line(bands, near_ref, line_ref)
+    line_ref[0:2, 2 : 2 + cols, :] = north_ref[...].astype(F32)
+    line_ref[2 : 2 + rows, 2 : 2 + cols, :] = tile_ref[...].astype(F32)
+    line_ref[2 + rows :, 2 : 2 + cols, :] = south_ref[...].astype(F32)
+    line_ref[:, 0:2, :] = west_ref[...].astype(F32)
+    line_ref[:, 2 + cols : 4 + cols, :] = east_ref[...].astype(F32)
+    line_ref[:, cols + 4 :, :] = jnp.zeros(
+        (rows + 4, line_ref.shape[1] - cols - 4, chans), F32
+    )
     first = jnp.zeros(((rows + 2) * span, chans), F32)
     for b in range(3):
         shift_ref[...] = (
@@ -290,7 +291,7 @@
 
 
 def forward(slots, bands, pieces, w1, w2, got):
-    half, rows, cols, chans = pieces[0].shape
+    rows, cols, chans = pieces[0].shape
     devices = got.shape[0]
     full, rest, _ = slot_layout(slots)
     groups = full * devices + (devices // 2 if rest else 0)
@@ -301,7 +302,7 @@
             jax.ShapeDtypeStruct((rows * cols, chans), BF16),
             jax.ShapeDtypeStruct(((rows + 2) * SPAN, chans), F32),
         ],
-        in_specs=[anywhere()] * len(pieces) + [vmem()] * 3,
+        in_specs=[vmem()] * 8,
         out_specs=[vmem()] * 3,
         scratch_shapes=[
             pltpu.VMEM((rows + 4, SPAN + 8, chans), F32),
@@ -309,8 +310,6 @@
             pltpu.VMEM((rows + 2, SPAN, chans), F32),
             pltpu.VMEM((FIELDS, groups, 128), F32),
             pltpu.VMEM((chans, rows * cols), F32),
-            pltpu.VMEM((3, 3, rows, cols, chans), BF16),
-            pltpu.SemaphoreType.DMA((3, 3)),
         ],
         compiler_params=params(24),
         cost_estimate=cost(4e9, 4e6),
@@ -741,19 +740,39 @@
     return (state_grad, grad_first, grad_second)
 
 
-def gather_tiles(x):
+def halo_pieces(x):
     bands, tiles = lax.axis_size("lat"), lax.axis_size("lon")
+    rows, cols, _ = x.shape
+    north = lax.ppermute(x[rows - 2 :], "lat", [(i, i + 1) for i in range(bands - 1)])
+    south = lax.ppermute(x[:2], "lat", [(i + 1, i) for i in range(bands - 1)])
+    last = jnp.concatenate([p[:, cols - 2 :] for p in (north, x, south)], axis=0)
+    first = jnp.concatenate([p[:, :2] for p in (north, x, south)], axis=0)
+    west = lax.ppermute(last, "lon", [(i, (i + 1) % tiles) for i in range(tiles)])
+    east = lax.ppermute(first, "lon", [((i + 1) % tiles, i) for i in range(tiles)])
+    return x, north, south, west, east
+
+
+def gather_line(x):
+    tiles = lax.axis_size("lon")
     half = tiles // 2
     same = [[2 * q + core for q in range(half)] for core in range(2)]
-    swap = [(i, i ^ 1) for i in range(tiles)]
     copies = jnp.broadcast_to(x[None], (half,) + x.shape)
-    line = lax.all_to_all(copies, "lon", 0, 0, axis_index_groups=same, tiled=True)
-    mine = [line]
-    for step in range(1, bands):
-        mine.append(lax.ppermute(line, "lat", [(i, (i + step) % bands) for i in range(bands)]))
+    return lax.all_to_all(copies, "lon", 0, 0, axis_index_groups=same, tiled=True)
+
+
+def gather_bands(line):
+    bands = lax.axis_size("lat")
+    return [line] + [
+        lax.ppermute(line, "lat", [(i, (i + step) % bands) for i in range(bands)])
+        for step in range(1, bands)
+    ]
+
+
+def with_other_core(lines):
+    swap = [(i, i ^ 1) for i in range(lax.axis_size("lon"))]
     pieces = []
-    for part in mine:
-        pieces += [part, lax.ppermute(part, "lon", swap)]
+    for line in lines:
+        pieces += [line, lax.ppermute(line, "lon", swap)]
     return pieces
 
 
@@ -770,17 +789,26 @@
             obs_frac, obs_value, obs_weight,
         )
     slots = max(2, 3 * obs_value.shape[0] // (2 * devices))
-    state_pieces = gather_tiles(state)
     outgoing = route(
         devices, slots, chans, obs_owner, obs_cell, obs_level, obs_count, obs_frac, obs_value,
         obs_weight,
     )
+    pieces = halo_pieces(state)
     got = lax.all_to_all(outgoing, ("lat", "lon"), split_axis=0, concat_axis=0, tiled=True)
+    pieces, got, sent = lax.optimization_barrier((pieces, got, state))
+    line = gather_line(sent)
+    line, pieces, got = lax.optimization_barrier((line, pieces, got))
+    state_lines = gather_bands(line)
     adjoint, pullback, near_slope = forward(
-        slots, bands, state_pieces, weight_first, weight_second, got
-    )
-    pull_pieces = gather_tiles(pullback.reshape(rows, cols, chans))
-    slope, hidden, turned, w2t = whole(bands, state_pieces, weight_first, weight_second)
+        slots, bands, pieces, weight_first, weight_second, got
+    )
+    state_lines, pullback = lax.optimization_barrier((state_lines, pullback))
+    state_pieces = with_other_core(state_lines)
+    pull_lines = gather_bands(gather_line(pullback.reshape(rows, cols, chans)))
+    firsts = whole(bands, state_pieces, weight_first, weight_second)
+    pull_lines, firsts = lax.optimization_barrier((pull_lines, firsts))
+    slope, hidden, turned, w2t = firsts
+    pull_pieces = with_other_core(pull_lines)
     sums = tail(bands, pull_pieces, slope, hidden, turned, w2t)
     swap = [(i, i ^ 1) for i in range(lax.axis_size("lon"))]
     theirs = [lax.ppermute(part, "lon", swap) for part in sums]

time: 115 us -> 110 us (0.957)
  blocking collectives: 38.6 us -> 12.1 us
  starting transfers between devices: 7.71 us -> 30.5 us
  waiting for transfers between devices: 22.9 us -> 15.3 us
  local copies, waits for them, and re-layouts: 8.35 us -> 13.8 us
    all_to_all x3 -> x1, blocking collectives: 38.6 us -> 12.1 us  [gather_line(): lax.all_to_all(copies, 'lon', 0, 0, axis_index_groups=same, tiled=True)]
    ppermute x14 -> x18, waiting for transfers between devices: 20.2 us -> 3.72 us  [the longest x1 2.05 us: halo_pieces(): lax.ppermute(last, 'lon', [(i, (i + 1) % tiles) for i in range(tiles)])]
    ppermute x14 -> x18, starting transfers between devices: 7.13 us -> 19.5 us  [the longest x6 7.56 us: gather_bands(): lax.ppermute(line, 'lat', [(i, (i + step) % bands) for i in range(bands)])]
    all_to_all x0 -> x2, starting transfers between devices: none -> 10.4 us  [the longest x1 7 us: per_device(): lax.all_to_all(outgoing, ('lat', 'lon'), split_axis=0, concat_axis=0, til...]
    all_to_all x0 -> x2, waiting for transfers between devices: none -> 8.96 us  [the longest x1 7.4 us: gather_line(): lax.all_to_all(copies, 'lon', 0, 0, axis_index_groups=same, tiled=True)]
    unnamed x22 -> x32, local copies, waits for them, and re-layouts: 7.48 us -> 10.7 us
    slice x0 -> x4, local copies, waits for them, and re-layouts: none -> 1.55 us  [the longest x3 0.81 us: halo_pieces(): first = jnp.concatenate([p[:, :2] for p in (north, x, south)], axis=0)]
  transfers between devices with their start and end apart: 16 -> 22, of which waited for: 6 -> 9; matrix products, arithmetic and copies ran while one was open for 1% -> 2% of each run, Pallas kernels for 9% -> 18%
where the time goes in v7:
time: 110 us; the launch traced here: 109 us
  Pallas kernels  33.2 us (30%)
  starting transfers between devices  30.5 us (28%)
  waiting for transfers between devices  15.3 us (14%)
  local copies, waits for them, and re-layouts  13.8 us (13%)
  blocking collectives  12.1 us (11%)
  other arithmetic  3.47 us (3%)
    pallas_call x1, Pallas kernels, tail(): pl.pallas_call(functools.partial(tail_kernel, 4), out_shape=[jax.ShapeDty...  13.4 us
    all_to_all x1, blocking collectives, gather_line(): lax.all_to_all(copies, 'lon', 0, 0, axis_index_groups=same, tiled=True)  12.1 us
    unnamed x32, local copies, waits for them, and re-layouts  10.7 us
    pallas_call x1, Pallas kernels, forward(): pl.pallas_call(functools.partial(forward_kernel, slots, bands, 2, 4), out...  8.22 us
    ppermute x6, starting transfers between devices, gather_bands(): lax.ppermute(line, 'lat', [(i, (i + step) % bands) for i in range(bands)])  7.56 us
    all_to_all x1, waiting for transfers between devices, gather_line(): lax.all_to_all(copies, 'lon', 0, 0, axis_index_groups=same, tiled=True)  7.4 us
    all_to_all x1, starting transfers between devices, per_device(): lax.all_to_all(outgoing, ('lat', 'lon'), split_axis=0, concat_axis=0, til...  7 us
    pallas_call x1, Pallas kernels, whole(): pl.pallas_call(functools.partial(whole_kernel, 3), out_shape=[jax.ShapeDt...  6.69 us
  transfers between devices with their start and end apart: 22, of which 9 were waited for; matrix products, arithmetic and copies ran while one was open for 2% of the time, Pallas kernels for 18%

profile of v7, /device:TPU:0, one launch (start us, length us, event | category | flops | bytes accessed | tf_op | source)
XLA Modules:
  0.0 109.3 jit_solution(11057057579359624494)
XLA Ops:
  0.6 0.7 fusion.1
  1.4 4.8 %collective-permute-start = (bf16[2,16,256]{2,1,0:T(8,128)(2,1)S(1)}, bf16[2,16,256]{2,1,0:T(8,128)(2,1)S(1)}, u32[]{:S(2)}, u32[]{:S(2)}) collective-permute-start(bf16[2,16,256]{2,1,0:T(8,128)(2,1)S(1)} %get-tuple-element.78), channel_id=1, source_target_pairs={{0,8},{8,16},{16,24},{1,9},{9,17},{17,25},{2,10},{10,18},{18,26},{... | collective-permute-start | bytes 49160 | tf_op jit(solution)/shard_map/ppermute | solution.py:746
  6.2 1.3 %collective-permute-start.1 = (bf16[2,16,256]{2,1,0:T(8,128)(2,1)S(1)}, bf16[2,16,256]{2,1,0:T(8,128)(2,1)S(1)}, u32[]{:S(2)}, u32[]{:S(2)}) collective-permute-start(bf16[2,16,256]{2,1,0:T(8,128)(2,1)S(1)} %get-tuple-element.77), channel_id=1, source_target_pairs={{8,0},{16,8},{24,16},{9,1},{17,9},{25,17},{10,2},{18,10},{26,18},{... | collective-permute-start | bytes 49160 | tf_op jit(solution)/shard_map/ppermute | solution.py:747
  7.5 0.7 copy-done.1
  8.3 0.7 copy-done.2
  9.0 0.7 copy-done.3
  9.7 0.7 copy-done.4
  10.4 0.7 copy-done.5
  11.1 0.7 copy-done.6
  11.8 0.7 copy-done.7
  12.5 1.9 %route.1 = f32[32,8,128]{2,1,0:T(8,128)} custom-call(s32[1,128]{1,0:T(1,128)S(1)} %bitcast.15, s32[1,128]{1,0:T(1,128)S(1)} %bitcast.16, s32[32,128]{1,0:T(8,128)S(1)} %bitcast.11, s32[32,128]{1,0:T(8,128)S(1)} %bitcast.12, f32[2,32,128]{2,1,0:T(8,128)S(1)} %bitcast.10, f32[32,128]{1,0:T(8,128)S(1)} %bitcast.13, f32[32,128]{1,0:T(8,128)S(1)} %bitcast.14), custom_call_target="tpu_custom_call" | custom-call | tf_op jit(solution)/shard_map/route/pallas_call | solution.py:99
  14.3 7.0 %all-to-all-start = ((f32[32,8,128]{2,1,0:T(8,128)}), f32[32,8,128]{2,1,0:T(8,128)S(1)}, u32[]{:S(2)}, u32[]{:S(2)}) async-start(f32[32,8,128]{2,1,0:T(8,128)} %route.1), calls=%async_computation | async-start | bytes 262144 | tf_op jit(solution)/shard_map/all_to_all | solution.py:797
  21.3 0.8 fusion
  22.6 3.3 %collective-permute-start.3 = (bf16[12,2,256]{2,1,0:T(2,128)(2,1)S(1)}, bf16[12,2,256]{2,1,0:T(2,128)(2,1)S(1)}, u32[]{:S(2)}, u32[]{:S(2)}) collective-permute-start(bf16[12,2,256]{2,1,0:T(2,128)(2,1)S(1)} %pad_maximum_fusion.1), channel_id=1, source_target_pairs={{1,0},{2,1},{3,2},{4,3},{5,4},{6,5},{7,6},{0,7},{9,8},{10,9},{11,1... | collective-permute-start | bytes 36872 | tf_op jit(solution)/shard_map/ppermute | solution.py:751
  25.9 2.0 %collective-permute-done.2.west_ref = bf16[12,2,256]{2,1,0:T(2,128)(2,1)S(1)} collective-permute-done((bf16[12,2,256]{2,1,0:T(2,128)(2,1)S(1)}, bf16[12,2,256]{2,1,0:T(2,128)(2,1)S(1)}, u32[]{:S(2)}, u32[]{:S(2)}) %collective-permute-start.2) | collective-permute-done | bytes 12320 | tf_op jit(solution)/shard_map/ppermute | solution.py:750
  27.9 1.6 %all-to-all-done.got_ref = f32[32,8,128]{2,1,0:T(8,128)S(1)} async-done(((f32[32,8,128]{2,1,0:T(8,128)}), f32[32,8,128]{2,1,0:T(8,128)S(1)}, u32[]{:S(2)}, u32[]{:S(2)}) %all-to-all-start) | async-done | bytes 131104 | tf_op jit(solution)/shard_map/all_to_all | solution.py:797
  29.5 0.9 broadcast_in_dim.6
  30.4 12.1 %all_to_all.15.refs_0_ = bf16[4,8,16,256]{3,2,1,0:T(8,128)(2,1)S(1)} all-to-all(bf16[4,8,16,256]{3,2,1,0:T(8,128)(2,1)S(1)} %broadcast_in_dim.6), channel_id=1, replica_groups={{0,2,4,6},{1,3,5,7},{8,10,12,14},{9,11,13,15},{16,18,20,22},{17,19,21,2..., dimensions={0} | all-to-all | bytes 524288 | tf_op jit(solution)/shard_map/all_to_all | solution.py:760
  42.5 1.4 %collective-permute-start.4 = (bf16[4,8,16,256]{3,2,1,0:T(8,128)(2,1)S(1)}, bf16[4,8,16,256]{3,2,1,0:T(8,128)(2,1)S(1)}, u32[]{:S(2)}, u32[]{:S(2)}) collective-permute-start(bf16[4,8,16,256]{3,2,1,0:T(8,128)(2,1)S(1)} %all_to_all.15.refs_0_), channel_id=1, source_target_pairs={{0,8},{8,16},{16,24},{24,0},{1,9},{9,17},{17,25},{25,1},{2,10},{10... | collective-permute-start | bytes 786440 | tf_op jit(solution)/shard_map/ppermute | solution.py:766
  44.0 2.9 %collective-permute-start.6 = (bf16[4,8,16,256]{3,2,1,0:T(8,128)(2,1)S(1)}, bf16[4,8,16,256]{3,2,1,0:T(8,128)(2,1)S(1)}, u32[]{:S(2)}, u32[]{:S(2)}) collective-permute-start(bf16[4,8,16,256]{3,2,1,0:T(8,128)(2,1)S(1)} %all_to_all.15.refs_0_), channel_id=1, source_target_pairs={{0,24},{8,0},{16,8},{24,16},{1,25},{9,1},{17,9},{25,17},{2,26},{10... | collective-permute-start | bytes 786440 | tf_op jit(solution)/shard_map/ppermute | solution.py:766
  46.9 0.8 copy-done
  47.7 1.3 %copy-done.8 = bf16[9,256,256]{2,1,0:T(8,128)(2,1)S(1)} copy-done((bf16[9,256,256]{2,1,0:T(8,128)(2,1)S(1)}, bf16[9,256,256]{2,1,0:T(8,128)(2,1)}, u32[]{:S(2)}) %copy-start.8) | copy-done | bytes 1179672
  49.0 1.3 %copy-done.10 = bf16[9,256,256]{2,1,0:T(8,128)(2,1)S(1)} copy-done((bf16[9,256,256]{2,1,0:T(8,128)(2,1)S(1)}, bf16[9,256,256]{2,1,0:T(8,128)(2,1)}, u32[]{:S(2)}) %copy-start.10) | copy-done | bytes 1179672
  50.3 8.2 %forward.1 = (f32[128,256]{1,0:T(8,128)S(1)}, bf16[128,256]{1,0:T(8,128)(2,1)S(1)}, f32[320,256]{1,0:T(8,128)S(1)}) custom-call(bf16[8,16,256]{2,1,0:T(8,128)(2,1)S(1)} %copy-done, bf16[2,16,256]{2,1,0:T(8,128)(2,1)S(1)} %collective-permute-done.north_ref, bf16[2,16,256]{2,1,0:T(8,128)(2,1)S(1)} %collective-permute-done.1.south_ref, ...), custom_call_target="tpu_custom_call" | custom-call | flops 4000000000 | bytes 4000000 | tf_op jit(solution)/shard_map/forward/pallas_call | solution.py:298
  58.5 0.7 copy-done.14
  59.2 0.7 copy-done.12
  59.9 0.7 broadcast_in_dim.15
  60.7 3.4 %all-to-all-start.2 = ((bf16[4,8,16,256]{3,2,1,0:T(8,128)(2,1)}), bf16[4,8,16,256]{3,2,1,0:T(8,128)(2,1)S(1)}, u32[]{:S(2)}, u32[]{:S(2)}) async-start(bf16[4,8,16,256]{3,2,1,0:T(8,128)(2,1)} %broadcast_in_dim.15), calls=%async_computation.2 | async-start | bytes 524288 | tf_op jit(solution)/shard_map/all_to_all | solution.py:760
  64.2 0.5 collective-permute-start.11
  64.7 0.4 collective-permute-start.13
  65.2 7.4 %all-to-all-done.2.refs_0_ = bf16[4,8,16,256]{3,2,1,0:T(8,128)(2,1)S(1)} async-done(((bf16[4,8,16,256]{3,2,1,0:T(8,128)(2,1)}), bf16[4,8,16,256]{3,2,1,0:T(8,128)(2,1)S(1)}, u32[]{:S(2)}, u32[]{:S(2)}) %all-to-all-start.2) | async-done | bytes 262176 | tf_op jit(solution)/shard_map/all_to_all | solution.py:760
  72.6 1.1 %collective-permute-start.8 = (bf16[4,8,16,256]{3,2,1,0:T(8,128)(2,1)S(1)}, bf16[4,8,16,256]{3,2,1,0:T(8,128)(2,1)S(1)}, u32[]{:S(2)}, u32[]{:S(2)}) collective-permute-start(bf16[4,8,16,256]{3,2,1,0:T(8,128)(2,1)S(1)} %all-to-all-done.2.refs_0_), channel_id=1, source_target_pairs={{0,16},{8,24},{16,0},{24,8},{1,17},{9,25},{17,1},{25,9},{2,18},{10... | collective-permute-start | bytes 786440 | tf_op jit(solution)/shard_map/ppermute | solution.py:766
  73.7 2.1 %collective-permute-start.9 = (bf16[4,8,16,256]{3,2,1,0:T(8,128)(2,1)S(1)}, bf16[4,8,16,256]{3,2,1,0:T(8,128)(2,1)S(1)}, u32[]{:S(2)}, u32[]{:S(2)}) collective-permute-start(bf16[4,8,16,256]{3,2,1,0:T(8,128)(2,1)S(1)} %all-to-all-done.2.refs_0_), channel_id=1, source_target_pairs={{0,24},{8,0},{16,8},{24,16},{1,25},{9,1},{17,9},{25,17},{2,26},{10... | collective-permute-start | bytes 786440 | tf_op jit(solution)/shard_map/ppermute | solution.py:766
  75.8 0.9 copy-done.13
  76.8 6.7 %whole.1 = (f32[2304,256]{1,0:T(8,128)S(1)}, bf16[256,2304]{1,0:T(8,128)(2,1)S(1)}, bf16[256,2304]{1,0:T(8,128)(2,1)S(1)}, bf16[9,256,256]{2,1,0:T(8,128)(2,1)S(1)}) custom-call(bf16[4,8,16,256]{3,2,1,0:T(8,128)(2,1)S(1)} %all_to_all.15.refs_0_, bf16[4,8,16,256]{3,2,1,0:T(8,128)(2,1)} %collective-permute-done.10.refs_1_, ...), custom_call_target="tpu_custom_call" | custom-call | flops 6000000000 | bytes 10000000 | tf_op jit(solution)/shard_map/whole/pallas_call | solution.py:402
  83.6 0.5 collective-permute-start.15
  84.2 0.4 collective-permute-start.17
  84.6 0.5 collective-permute-done.14.refs_1_
  85.1 0.4 collective-permute-done.15.refs_3_
  85.5 0.4 collective-permute-done.16.refs_5_
  85.8 0.4 collective-permute-done.17.refs_7_
  86.2 13.4 %tail.1 = (f32[9,256,256]{2,1,0:T(8,128)S(1)}, f32[9,256,256]{2,1,0:T(8,128)S(1)}) custom-call(bf16[4,8,16,256]{3,2,1,0:T(8,128)(2,1)S(1)} %all-to-all-done.2.refs_0_, bf16[4,8,16,256]{3,2,1,0:T(8,128)(2,1)S(1)} %collective-permute-done.14.refs_1_, bf16[4,8,16,256]{3,2,1,0:T(8,128)(2,1)S(1)} %collective-permute-done.7.refs_2_, ...), custom_call_target="tpu_custom_call" | custom-call | flops 10000000000 | bytes 15000000 | tf_op jit(solution)/shard_map/tail/pallas_call | solution.py:503
  99.9 0.4 collective-permute-start.19
  100.2 3.0 %local_grad.1 = f32[128,256]{1,0:T(8,128)} custom-call(bf16[4,8,16,256]{3,2,1,0:T(8,128)(2,1)S(1)} %all-to-all-done.2.refs_0_, bf16[4,8,16,256]{3,2,1,0:T(8,128)(2,1)S(1)} %collective-permute-done.14.refs_1_, bf16[4,8,16,256]{3,2,1,0:T(8,128)(2,1)S(1)} %collective-permute-done.7.refs_2_, bf16[4,8,16,256]{3,2,1,0:T(8,128)(2,1)S(1)} %collective-permute-done.15.refs_3_, ...), custom_call_target="tpu_custom_call" | custom-call | flops 3000000000 | bytes 4000000 | tf_op jit(solution)/shard_map/local_grad/pallas_call | solution.py:563
  103.3 1.0 collective-permute-done.18
  104.2 1.7 %add.6 = f32[9,256,256]{2,1,0:T(8,128)} add(f32[9,256,256]{2,1,0:T(8,128)S(1)} %get-tuple-element.73, f32[9,256,256]{2,1,0:T(8,128)S(1)} %collective-permute-done.18) | non-fusion elementwise | flops 589824 | bytes 7077888 | tf_op jit(solution)/shard_map/add | solution.py:816
  106.0 1.7 %collective-permute-done.19 = f32[9,256,256]{2,1,0:T(8,128)S(1)} collective-permute-done((f32[9,256,256]{2,1,0:T(8,128)S(1)}, f32[9,256,256]{2,1,0:T(8,128)S(1)}, u32[]{:S(2)}, u32[]{:S(2)}) %collective-permute-start.19) | collective-permute-done | bytes 2359328 | tf_op jit(solution)/shard_map/ppermute | solution.py:814
  107.6 1.7 %add.7 = f32[9,256,256]{2,1,0:T(8,128)} add(f32[9,256,256]{2,1,0:T(8,128)S(1)} %get-tuple-element.74, f32[9,256,256]{2,1,0:T(8,128)S(1)} %collective-permute-done.19) | non-fusion elementwise | flops 589824 | bytes 7077888 | tf_op jit(solution)/shard_map/add | solution.py:816
  (44 shorter events, 1.0 us)
Async XLA Ops:
  1.4 20.8 %collective-permute-start = (bf16[2,16,256]{2,1,0:T(8,128)(2,1)S(1)}, bf16[2,16,256]{2,1,0:T(8,128)(2,1)S(1)}, u32[]{:S(2)}, u32[]{:S(2)}) collective-permute-start(bf16[2,16,256]{2,1,0:T(8,128)(2,1)S(1)} %get-tuple-element.78), channel_id=1, source_target_pairs={{0,8},{8,16},{16,24},{1,9},{9,17},{17,25},{2,10},{10,18},{18,26},{... | collective-permute-start | bytes 49160 | tf_op jit(solution)/shard_map/ppermute | solution.py:746
  6.2 15.9 %collective-permute-start.1 = (bf16[2,16,256]{2,1,0:T(8,128)(2,1)S(1)}, bf16[2,16,256]{2,1,0:T(8,128)(2,1)S(1)}, u32[]{:S(2)}, u32[]{:S(2)}) collective-permute-start(bf16[2,16,256]{2,1,0:T(8,128)(2,1)S(1)} %get-tuple-element.77), channel_id=1, source_target_pairs={{8,0},{16,8},{24,16},{9,1},{17,9},{25,17},{10,2},{18,10},{26,18},{... | collective-permute-start | bytes 49160 | tf_op jit(solution)/shard_map/ppermute | solution.py:747
  7.5 0.8 copy-start.1
  8.3 0.7 copy-start.2
  9.0 0.7 copy-start.3
  9.7 0.7 copy-start.4
  10.4 0.7 copy-start.5
  11.1 0.7 copy-start.6
  11.8 0.7 copy-start.7
  14.3 15.2 %all-to-all-start = ((f32[32,8,128]{2,1,0:T(8,128)}), f32[32,8,128]{2,1,0:T(8,128)S(1)}, u32[]{:S(2)}, u32[]{:S(2)}) async-start(f32[32,8,128]{2,1,0:T(8,128)} %route.1), calls=%async_computation | async-start | bytes 262144 | tf_op jit(solution)/shard_map/all_to_all | solution.py:797
  22.2 5.7 %collective-permute-start.2 = (bf16[12,2,256]{2,1,0:T(2,128)(2,1)S(1)}, bf16[12,2,256]{2,1,0:T(2,128)(2,1)S(1)}, u32[]{:S(2)}, u32[]{:S(2)}) collective-permute-start(bf16[12,2,256]{2,1,0:T(2,128)(2,1)S(1)} %pad_maximum_fusion), channel_id=1, source_target_pairs={{0,1},{1,2},{2,3},{3,4},{4,5},{5,6},{6,7},{7,0},{8,9},{9,10},{10,1... | collective-permute-start | bytes 36872 | tf_op jit(solution)/shard_map/ppermute | solution.py:750
  22.6 5.4 %collective-permute-start.3 = (bf16[12,2,256]{2,1,0:T(2,128)(2,1)S(1)}, bf16[12,2,256]{2,1,0:T(2,128)(2,1)S(1)}, u32[]{:S(2)}, u32[]{:S(2)}) collective-permute-start(bf16[12,2,256]{2,1,0:T(2,128)(2,1)S(1)} %pad_maximum_fusion.1), channel_id=1, source_target_pairs={{1,0},{2,1},{3,2},{4,3},{5,4},{6,5},{7,6},{0,7},{9,8},{10,9},{11,1... | collective-permute-start | bytes 36872 | tf_op jit(solution)/shard_map/ppermute | solution.py:751
  42.5 16.7 %collective-permute-start.4 = (bf16[4,8,16,256]{3,2,1,0:T(8,128)(2,1)S(1)}, bf16[4,8,16,256]{3,2,1,0:T(8,128)(2,1)S(1)}, u32[]{:S(2)}, u32[]{:S(2)}) collective-permute-start(bf16[4,8,16,256]{3,2,1,0:T(8,128)(2,1)S(1)} %all_to_all.15.refs_0_), channel_id=1, source_target_pairs={{0,8},{8,16},{16,24},{24,0},{1,9},{9,17},{17,25},{25,1},{2,10},{10... | collective-permute-start | bytes 786440 | tf_op jit(solution)/shard_map/ppermute | solution.py:766
  44.0 15.3 %collective-permute-start.5 = (bf16[4,8,16,256]{3,2,1,0:T(8,128)(2,1)S(1)}, bf16[4,8,16,256]{3,2,1,0:T(8,128)(2,1)S(1)}, u32[]{:S(2)}, u32[]{:S(2)}) collective-permute-start(bf16[4,8,16,256]{3,2,1,0:T(8,128)(2,1)S(1)} %all_to_all.15.refs_0_), channel_id=1, source_target_pairs={{0,16},{8,24},{16,0},{24,8},{1,17},{9,25},{17,1},{25,9},{2,18},{10... | collective-permute-start | bytes 786440 | tf_op jit(solution)/shard_map/ppermute | solution.py:766
  44.0 15.3 %collective-permute-start.6 = (bf16[4,8,16,256]{3,2,1,0:T(8,128)(2,1)S(1)}, bf16[4,8,16,256]{3,2,1,0:T(8,128)(2,1)S(1)}, u32[]{:S(2)}, u32[]{:S(2)}) collective-permute-start(bf16[4,8,16,256]{3,2,1,0:T(8,128)(2,1)S(1)} %all_to_all.15.refs_0_), channel_id=1, source_target_pairs={{0,24},{8,0},{16,8},{24,16},{1,25},{9,1},{17,9},{25,17},{2,26},{10... | collective-permute-start | bytes 786440 | tf_op jit(solution)/shard_map/ppermute | solution.py:766
  46.9 0.8 copy-start
  47.7 1.3 %copy-start.8 = (bf16[9,256,256]{2,1,0:T(8,128)(2,1)S(1)}, bf16[9,256,256]{2,1,0:T(8,128)(2,1)}, u32[]{:S(2)}) copy-start(bf16[9,256,256]{2,1,0:T(8,128)(2,1)} %refs_10_.1) | copy-start | bytes 3538948
  49.0 1.3 %copy-start.10 = (bf16[9,256,256]{2,1,0:T(8,128)(2,1)S(1)}, bf16[9,256,256]{2,1,0:T(8,128)(2,1)}, u32[]{:S(2)}) copy-start(bf16[9,256,256]{2,1,0:T(8,128)(2,1)} %refs_11_.1) | copy-start | bytes 3538948
  50.3 25.5 %copy-start.9 = (bf16[9,256,256]{2,1,0:T(8,128)(2,1)S(1)}, bf16[9,256,256]{2,1,0:T(8,128)(2,1)}, u32[]{:S(2)}) copy-start(bf16[9,256,256]{2,1,0:T(8,128)(2,1)} %refs_10_.1) | copy-start | bytes 3538948
  50.3 25.5 %copy-start.11 = (bf16[9,256,256]{2,1,0:T(8,128)(2,1)S(1)}, bf16[9,256,256]{2,1,0:T(8,128)(2,1)}, u32[]{:S(2)}) copy-start(bf16[9,256,256]{2,1,0:T(8,128)(2,1)} %refs_11_.1) | copy-start | bytes 3538948
  58.5 0.7 copy-start.14
  59.2 0.7 copy-start.12
  60.7 11.9 %all-to-all-start.2 = ((bf16[4,8,16,256]{3,2,1,0:T(8,128)(2,1)}), bf16[4,8,16,256]{3,2,1,0:T(8,128)(2,1)S(1)}, u32[]{:S(2)}, u32[]{:S(2)}) async-start(bf16[4,8,16,256]{3,2,1,0:T(8,128)(2,1)} %broadcast_in_dim.15), calls=%async_computation.2 | async-start | bytes 524288 | tf_op jit(solution)/shard_map/all_to_all | solution.py:760
  64.1 8.5 %collective-permute-start.10 = (bf16[4,8,16,256]{3,2,1,0:T(8,128)(2,1)S(1)}, bf16[4,8,16,256]{3,2,1,0:T(8,128)(2,1)}, u32[]{:S(2)}, u32[]{:S(2)}) collective-permute-start(bf16[4,8,16,256]{3,2,1,0:T(8,128)(2,1)S(1)} %all_to_all.15.refs_0_), channel_id=1, source_target_pairs={{0,1},{1,0},{2,3},{3,2},{4,5},{5,4},{6,7},{7,6},{8,9},{9,8},{10,11... | collective-permute-start | bytes 786440 | tf_op jit(solution)/shard_map/ppermute | solution.py:775
  64.2 9.6 %collective-permute-start.11 = (bf16[4,8,16,256]{3,2,1,0:T(8,128)(2,1)S(1)}, bf16[4,8,16,256]{3,2,1,0:T(8,128)(2,1)}, u32[]{:S(2)}, u32[]{:S(2)}) collective-permute-start(bf16[4,8,16,256]{3,2,1,0:T(8,128)(2,1)S(1)} %collective-permute-done.4.refs_2_), channel_id=1, source_target_pairs={{0,1},{1,0},{2,3},{3,2},{4,5},{5,4},{6,7},{7,6},{8,9},{9,8},{10,11... | collective-permute-start | bytes 786440 | tf_op jit(solution)/shard_map/ppermute | solution.py:775
  64.7 11.1 %collective-permute-start.12 = (bf16[4,8,16,256]{3,2,1,0:T(8,128)(2,1)S(1)}, bf16[4,8,16,256]{3,2,1,0:T(8,128)(2,1)}, u32[]{:S(2)}, u32[]{:S(2)}) collective-permute-start(bf16[4,8,16,256]{3,2,1,0:T(8,128)(2,1)S(1)} %collective-permute-done.5.refs_4_), channel_id=1, source_target_pairs={{0,1},{1,0},{2,3},{3,2},{4,5},{5,4},{6,7},{7,6},{8,9},{9,8},{10,11... | collective-permute-start | bytes 786440 | tf_op jit(solution)/shard_map/ppermute | solution.py:775
  64.7 11.1 %collective-permute-start.13 = (bf16[4,8,16,256]{3,2,1,0:T(8,128)(2,1)}, bf16[4,8,16,256]{3,2,1,0:T(8,128)(2,1)}, u32[]{:S(2)}, u32[]{:S(2)}) collective-permute-start(bf16[4,8,16,256]{3,2,1,0:T(8,128)(2,1)} %copy-done.12), channel_id=1, source_target_pairs={{0,1},{1,0},{2,3},{3,2},{4,5},{5,4},{6,7},{7,6},{8,9},{9,8},{10,11... | collective-permute-start | bytes 786440 | tf_op jit(solution)/shard_map/ppermute | solution.py:775
  72.6 10.9 %collective-permute-start.7 = (bf16[4,8,16,256]{3,2,1,0:T(8,128)(2,1)S(1)}, bf16[4,8,16,256]{3,2,1,0:T(8,128)(2,1)S(1)}, u32[]{:S(2)}, u32[]{:S(2)}) collective-permute-start(bf16[4,8,16,256]{3,2,1,0:T(8,128)(2,1)S(1)} %all-to-all-done.2.refs_0_), channel_id=1, source_target_pairs={{0,8},{8,16},{16,24},{24,0},{1,9},{9,17},{17,25},{25,1},{2,10},{10... | collective-permute-start | bytes 786440 | tf_op jit(solution)/shard_map/ppermute | solution.py:766
  72.6 10.9 %collective-permute-start.8 = (bf16[4,8,16,256]{3,2,1,0:T(8,128)(2,1)S(1)}, bf16[4,8,16,256]{3,2,1,0:T(8,128)(2,1)S(1)}, u32[]{:S(2)}, u32[]{:S(2)}) collective-permute-start(bf16[4,8,16,256]{3,2,1,0:T(8,128)(2,1)S(1)} %all-to-all-done.2.refs_0_), channel_id=1, source_target_pairs={{0,16},{8,24},{16,0},{24,8},{1,17},{9,25},{17,1},{25,9},{2,18},{10... | collective-permute-start | bytes 786440 | tf_op jit(solution)/shard_map/ppermute | solution.py:766
  73.7 9.8 %collective-permute-start.9 = (bf16[4,8,16,256]{3,2,1,0:T(8,128)(2,1)S(1)}, bf16[4,8,16,256]{3,2,1,0:T(8,128)(2,1)S(1)}, u32[]{:S(2)}, u32[]{:S(2)}) collective-permute-start(bf16[4,8,16,256]{3,2,1,0:T(8,128)(2,1)S(1)} %all-to-all-done.2.refs_0_), channel_id=1, source_target_pairs={{0,24},{8,0},{16,8},{24,16},{1,25},{9,1},{17,9},{25,17},{2,26},{10... | collective-permute-start | bytes 786440 | tf_op jit(solution)/shard_map/ppermute | solution.py:766
  75.8 1.0 copy-start.13
  83.5 16.7 %copy-start.15 = (f32[320,256]{1,0:T(8,128)S(1)}, f32[320,256]{1,0:T(8,128)}, u32[]{:S(2)}) copy-start(f32[320,256]{1,0:T(8,128)} %copy-done.14) | copy-start | bytes 983044
  83.5 1.6 %collective-permute-start.14 = (bf16[4,8,16,256]{3,2,1,0:T(8,128)(2,1)S(1)}, bf16[4,8,16,256]{3,2,1,0:T(8,128)(2,1)S(1)}, u32[]{:S(2)}, u32[]{:S(2)}) collective-permute-start(bf16[4,8,16,256]{3,2,1,0:T(8,128)(2,1)S(1)} %all-to-all-done.2.refs_0_), channel_id=1, source_target_pairs={{0,1},{1,0},{2,3},{3,2},{4,5},{5,4},{6,7},{7,6},{8,9},{9,8},{10,11... | collective-permute-start | bytes 786440 | tf_op jit(solution)/shard_map/ppermute | solution.py:775
  83.6 1.9 %collective-permute-start.15 = (bf16[4,8,16,256]{3,2,1,0:T(8,128)(2,1)S(1)}, bf16[4,8,16,256]{3,2,1,0:T(8,128)(2,1)S(1)}, u32[]{:S(2)}, u32[]{:S(2)}) collective-permute-start(bf16[4,8,16,256]{3,2,1,0:T(8,128)(2,1)S(1)} %collective-permute-done.7.refs_2_), channel_id=1, source_target_pairs={{0,1},{1,0},{2,3},{3,2},{4,5},{5,4},{6,7},{7,6},{8,9},{9,8},{10,11... | collective-permute-start | bytes 786440 | tf_op jit(solution)/shard_map/ppermute | solution.py:775
  84.1 1.8 %collective-permute-start.16 = (bf16[4,8,16,256]{3,2,1,0:T(8,128)(2,1)S(1)}, bf16[4,8,16,256]{3,2,1,0:T(8,128)(2,1)S(1)}, u32[]{:S(2)}, u32[]{:S(2)}) collective-permute-start(bf16[4,8,16,256]{3,2,1,0:T(8,128)(2,1)S(1)} %collective-permute-done.8.refs_4_), channel_id=1, source_target_pairs={{0,1},{1,0},{2,3},{3,2},{4,5},{5,4},{6,7},{7,6},{8,9},{9,8},{10,11... | collective-permute-start | bytes 786440 | tf_op jit(solution)/shard_map/ppermute | solution.py:775
  84.2 2.1 %collective-permute-start.17 = (bf16[4,8,16,256]{3,2,1,0:T(8,128)(2,1)S(1)}, bf16[4,8,16,256]{3,2,1,0:T(8,128)(2,1)S(1)}, u32[]{:S(2)}, u32[]{:S(2)}) collective-permute-start(bf16[4,8,16,256]{3,2,1,0:T(8,128)(2,1)S(1)} %collective-permute-done.9.refs_6_), channel_id=1, source_target_pairs={{0,1},{1,0},{2,3},{3,2},{4,5},{5,4},{6,7},{7,6},{8,9},{9,8},{10,11... | collective-permute-start | bytes 786440 | tf_op jit(solution)/shard_map/ppermute | solution.py:775
  99.6 4.6 %collective-permute-start.18 = (f32[9,256,256]{2,1,0:T(8,128)S(1)}, f32[9,256,256]{2,1,0:T(8,128)S(1)}, u32[]{:S(2)}, u32[]{:S(2)}) collective-permute-start(f32[9,256,256]{2,1,0:T(8,128)S(1)} %get-tuple-element.73), channel_id=1, source_target_pairs={{0,1},{1,0},{2,3},{3,2},{4,5},{5,4},{6,7},{7,6},{8,9},{9,8},{10,11... | collective-permute-start | bytes 7077896 | tf_op jit(solution)/shard_map/ppermute | solution.py:814
  99.9 7.8 %collective-permute-start.19 = (f32[9,256,256]{2,1,0:T(8,128)S(1)}, f32[9,256,256]{2,1,0:T(8,128)S(1)}, u32[]{:S(2)}, u32[]{:S(2)}) collective-permute-start(f32[9,256,256]{2,1,0:T(8,128)S(1)} %get-tuple-element.74), channel_id=1, source_target_pairs={{0,1},{1,0},{2,3},{3,2},{4,5},{5,4},{6,7},{7,6},{8,9},{9,8},{10,11... | collective-permute-start | bytes 7077896 | tf_op jit(solution)/shard_map/ppermute | solution.py:814

commit v8 on v7

--- a/solution.py
+++ b/solution.py
@@ -101,7 +101,7 @@
         out_shape=jax.ShapeDtypeStruct((devices, rows, 128), F32),
         in_specs=[vmem()] * 7,
         out_specs=vmem(),
-        compiler_params=params(16),
+        compiler_params=params(60),
         name="route",
     )(
         obs_owner.reshape(1, blocks),
@@ -175,8 +175,12 @@
 
 
 def forward_kernel(slots, bands, group, parts, tile_ref, north_ref, south_ref, west_ref, east_ref,
-                   w1_ref, w2_ref, got_ref, adj_ref, pull_ref, slope_ref, line_ref, shift_ref,
-                   hid_ref, obs_ref, sum_ref):
+                   w1_hbm, w2_hbm, got_ref, adj_ref, pull_ref, slope_ref, line_ref, shift_ref,
+                   hid_ref, obs_ref, sum_ref, w1_ref, w2_ref, sems):
+    w1_copy = pltpu.make_async_copy(w1_hbm, w1_ref, sems.at[0])
+    w2_copy = pltpu.make_async_copy(w2_hbm, w2_ref, sems.at[1])
+    w1_copy.start()
+    w2_copy.start()
     rows, cols, chans = tile_ref.shape
     span = hid_ref.shape[1]
     line_ref[0:2, 2 : 2 + cols, :] = north_ref[...].astype(F32)
@@ -187,6 +191,7 @@
     line_ref[:, cols + 4 :, :] = jnp.zeros(
         (rows + 4, line_ref.shape[1] - cols - 4, chans), F32
     )
+    w1_copy.wait()
     first = jnp.zeros(((rows + 2) * span, chans), F32)
     for b in range(3):
         shift_ref[...] = (
@@ -201,6 +206,7 @@
     hidden = hidden.astype(BF16).astype(F32).reshape(rows + 2, span, chans)
     hidden = jnp.where(inside_grid(rows, hidden.shape, bands), hidden, 0.0)
     hid_ref[...] = hidden
+    w2_copy.wait()
     total = line_ref[2 : 2 + rows, 2 : 2 + cols, :].reshape(rows * cols, chans)
     for b in range(3):
         shift_ref[0 : (rows + 2) * cols, :] = (
@@ -302,7 +308,7 @@
             jax.ShapeDtypeStruct((rows * cols, chans), BF16),
             jax.ShapeDtypeStruct(((rows + 2) * SPAN, chans), F32),
         ],
-        in_specs=[vmem()] * 8,
+        in_specs=[vmem()] * 5 + [anywhere()] * 2 + [vmem()],
         out_specs=[vmem()] * 3,
         scratch_shapes=[
             pltpu.VMEM((rows + 4, SPAN + 8, chans), F32),
@@ -310,14 +316,17 @@
             pltpu.VMEM((rows + 2, SPAN, chans), F32),
             pltpu.VMEM((FIELDS, groups, 128), F32),
             pltpu.VMEM((chans, rows * cols), F32),
+            pltpu.VMEM(w1.shape, BF16),
+            pltpu.VMEM(w2.shape, BF16),
+            pltpu.SemaphoreType.DMA((2,)),
         ],
-        compiler_params=params(24),
+        compiler_params=params(58),
         cost_estimate=cost(4e9, 4e6),
         name="forward",
     )(*pieces, w1, w2, got)
 
 
-def spread_matrix(steps, tiles):
+def spread_matrix(steps, tiles, backwards):
     lons = 16 * steps
     half = tiles // 2
     place = iota(((steps + 2) * 16, lons), 0)
@@ -326,7 +335,11 @@
     column = iota(((steps + 2) * 16, lons), 1)
     chunk = lax.shift_right_logical(column, 4)
     core = lax.shift_right_logical(chunk, half.bit_length() - 1)
-    column = (2 * (chunk & (half - 1)) + core) * 16 + (column & 15)
+    here = lax.shift_right_logical(lax.axis_index("lon"), 1)
+    q = chunk & (half - 1)
+    if backwards:
+        q = (here - q) & (half - 1)
+    column = (2 * q + core) * 16 + (column & 15)
     return jnp.where(column == lon, 1.0, 0.0)
 
 
@@ -365,7 +378,7 @@
     copies = band_copies(bands, piece_refs, all_ref, sems)
     for copy in copies:
         copy.start()
-    matrix = spread_matrix(steps, 2 * half)
+    matrix = spread_matrix(steps, 2 * half, True)
     for tap in range(9):
         w2t_ref[tap] = w2_ref[tap].T
     for copy in copies:
@@ -461,7 +474,7 @@
     hidden_copy.start()
     slope_copy.start()
     state_copy.start()
-    matrix = spread_matrix(steps, 2 * half)
+    matrix = spread_matrix(steps, 2 * half, False)
     for copy in copies:
         copy.wait()
     spread(
@@ -760,6 +773,17 @@
     return lax.all_to_all(copies, "lon", 0, 0, axis_index_groups=same, tiled=True)
 
 
+def gather_line_backwards(x):
+    tiles = lax.axis_size("lon")
+    return jnp.stack(
+        [x]
+        + [
+            lax.ppermute(x, "lon", [(i, (i + step) % tiles) for i in range(tiles)])
+            for step in range(2, tiles, 2)
+        ]
+    )
+
+
 def gather_bands(line):
     bands = lax.axis_size("lat")
     return [line] + [
@@ -793,10 +817,10 @@
         devices, slots, chans, obs_owner, obs_cell, obs_level, obs_count, obs_frac, obs_value,
         obs_weight,
     )
+    outgoing, sent = lax.optimization_barrier((outgoing, state))
     pieces = halo_pieces(state)
     got = lax.all_to_all(outgoing, ("lat", "lon"), split_axis=0, concat_axis=0, tiled=True)
-    pieces, got, sent = lax.optimization_barrier((pieces, got, state))
-    line = gather_line(sent)
+    line = gather_line_backwards(sent)
     line, pieces, got = lax.optimization_barrier((line, pieces, got))
     state_lines = gather_bands(line)
     adjoint, pullback, near_slope = forward(

time: 110 us -> 97.7 us (0.89)
  blocking collectives: 12.1 us -> 0 us
  local copies, waits for them, and re-layouts: 13.8 us -> 5.36 us
  Pallas kernels: 33.2 us -> 37.2 us
  starting transfers between devices: 30.5 us -> 34.5 us
    all_to_all x1 -> x0, blocking collectives: 12.1 us -> none  [gather_line(): lax.all_to_all(copies, 'lon', 0, 0, axis_index_groups=same, tiled=True)]
    unnamed x32 -> x22, local copies, waits for them, and re-layouts: 10.7 us -> 2.17 us
    ppermute x0 -> x3, starting transfers between devices: none -> 6.06 us  [gather_line_backwards(): lax.ppermute(x, 'lon', [(i, (i + step) % tiles) for i in range(tiles)])]
    pallas_call x1, Pallas kernels: 8.22 us -> 11.3 us  [forward(): pl.pallas_call(functools.partial(forward_kernel, slots, bands, 2, 4), out...]
    ppermute x1, starting transfers between devices: 4.83 us -> 3.38 us  [halo_pieces(): lax.ppermute(x[rows - 2:], 'lat', [(i, i + 1) for i in range(bands - 1)])]
    all_to_all x1, waiting for transfers between devices: 1.56 us -> 0.37 us  [per_device(): lax.all_to_all(outgoing, ('lat', 'lon'), split_axis=0, concat_axis=0, til...]
  transfers between devices with their start and end apart: 22 -> 25, of which waited for: 9 -> 10; matrix products, arithmetic and copies ran while one was open for 2% -> 4% of each run, Pallas kernels for 18% -> 22%
where the time goes in v8:
time: 97.7 us; the launch traced here: 97 us
  Pallas kernels  37.2 us (38%)
  starting transfers between devices  34.5 us (35%)
  waiting for transfers between devices  14.7 us (15%)
  local copies, waits for them, and re-layouts  5.36 us (5%)
  other arithmetic  4.34 us (4%)
    pallas_call x1, Pallas kernels, tail(): pl.pallas_call(functools.partial(tail_kernel, 4), out_shape=[jax.ShapeDty...  13.4 us
    pallas_call x1, Pallas kernels, forward(): pl.pallas_call(functools.partial(forward_kernel, slots, bands, 2, 4), out...  11.3 us
    all_to_all x1, waiting for transfers between devices, gather_line(): lax.all_to_all(copies, 'lon', 0, 0, axis_index_groups=same, tiled=True)  7.98 us
    ppermute x6, starting transfers between devices, gather_bands(): lax.ppermute(line, 'lat', [(i, (i + step) % bands) for i in range(bands)])  7.75 us
    pallas_call x1, Pallas kernels, whole(): pl.pallas_call(functools.partial(whole_kernel, 3), out_shape=[jax.ShapeDt...  6.69 us
    all_to_all x1, starting transfers between devices, per_device(): lax.all_to_all(outgoing, ('lat', 'lon'), split_axis=0, concat_axis=0, til...  6.22 us
    ppermute x3, starting transfers between devices, gather_line_backwards(): lax.ppermute(x, 'lon', [(i, (i + step) % tiles) for i in range(tiles)])  6.06 us
    add x2, other arithmetic, per_device(): g1, g2 = [part + their for part, their in zip(sums, theirs)]  3.42 us
  transfers between devices with their start and end apart: 25, of which 10 were waited for; matrix products, arithmetic and copies ran while one was open for 4% of the time, Pallas kernels for 22%

profile of v8, /device:TPU:0, one launch (start us, length us, event | category | flops | bytes accessed | tf_op | source)
XLA Modules:
  0.0 97.0 jit_solution(3389353499857827280)
XLA Ops:
  0.6 2.7 %route.1 = f32[32,8,128]{2,1,0:T(8,128)} custom-call(s32[1,128]{1,0:T(1,128)} %bitcast.23, s32[1,128]{1,0:T(1,128)} %bitcast.24, s32[32,128]{1,0:T(8,128)} %bitcast.19, s32[32,128]{1,0:T(8,128)} %bitcast.20, f32[2,32,128]{2,1,0:T(8,128)} %bitcast.18, f32[32,128]{1,0:T(8,128)} %bitcast.21, f32[32,128]{1,0:T(8,128)} %bitcast.22), custom_call_target="tpu_custom_call" | custom-call | tf_op jit(solution)/shard_map/route/pallas_call | solution.py:99
  3.4 5.0 %collective-permute-start.2 = (bf16[8,16,256]{2,1,0:T(8,128)(2,1)}, bf16[8,16,256]{2,1,0:T(8,128)(2,1)S(1)}, u32[]{:S(2)}, u32[]{:S(2)}) collective-permute-start(bf16[8,16,256]{2,1,0:T(8,128)(2,1)} %tile_ref), channel_id=1, source_target_pairs={{0,6},{1,7},{2,0},{3,1},{4,2},{5,3},{6,4},{7,5},{8,14},{9,15},{10,... | collective-permute-start | bytes 196616 | tf_op jit(solution)/shard_map/ppermute | solution.py:781
  8.4 1.0 %collective-permute-start = (bf16[8,16,256]{2,1,0:T(8,128)(2,1)}, bf16[8,16,256]{2,1,0:T(8,128)(2,1)S(1)}, u32[]{:S(2)}, u32[]{:S(2)}) collective-permute-start(bf16[8,16,256]{2,1,0:T(8,128)(2,1)} %tile_ref), channel_id=1, source_target_pairs={{0,2},{1,3},{2,4},{3,5},{4,6},{5,7},{6,0},{7,1},{8,10},{9,11},{10,... | collective-permute-start | bytes 196616 | tf_op jit(solution)/shard_map/ppermute | solution.py:781
  9.4 0.8 fusion.1
  10.2 3.4 %collective-permute-start.3 = (bf16[2,16,256]{2,1,0:T(8,128)(2,1)S(1)}, bf16[2,16,256]{2,1,0:T(8,128)(2,1)S(1)}, u32[]{:S(2)}, u32[]{:S(2)}) collective-permute-start(bf16[2,16,256]{2,1,0:T(8,128)(2,1)S(1)} %get-tuple-element.68), channel_id=1, source_target_pairs={{0,8},{8,16},{16,24},{1,9},{9,17},{17,25},{2,10},{10,18},{18,26},{... | collective-permute-start | bytes 49160 | tf_op jit(solution)/shard_map/ppermute | solution.py:759
  13.6 1.3 %collective-permute-start.4 = (bf16[2,16,256]{2,1,0:T(8,128)(2,1)S(1)}, bf16[2,16,256]{2,1,0:T(8,128)(2,1)S(1)}, u32[]{:S(2)}, u32[]{:S(2)}) collective-permute-start(bf16[2,16,256]{2,1,0:T(8,128)(2,1)S(1)} %get-tuple-element.67), channel_id=1, source_target_pairs={{8,0},{16,8},{24,16},{9,1},{17,9},{25,17},{10,2},{18,10},{26,18},{... | collective-permute-start | bytes 49160 | tf_op jit(solution)/shard_map/ppermute | solution.py:760
  14.9 6.2 %all-to-all-start = ((f32[32,8,128]{2,1,0:T(8,128)}), f32[32,8,128]{2,1,0:T(8,128)S(1)}, u32[]{:S(2)}, u32[]{:S(2)}) async-start(f32[32,8,128]{2,1,0:T(8,128)} %route.1), calls=%async_computation | async-start | bytes 262144 | tf_op jit(solution)/shard_map/all_to_all | solution.py:822
  21.1 0.8 fusion
  22.0 0.3 collective-permute-start.5
  22.3 3.3 %collective-permute-start.6 = (bf16[12,2,256]{2,1,0:T(2,128)(2,1)S(1)}, bf16[12,2,256]{2,1,0:T(2,128)(2,1)S(1)}, u32[]{:S(2)}, u32[]{:S(2)}) collective-permute-start(bf16[12,2,256]{2,1,0:T(2,128)(2,1)S(1)} %pad_maximum_fusion.2), channel_id=1, source_target_pairs={{1,0},{2,1},{3,2},{4,3},{5,4},{6,5},{7,6},{0,7},{9,8},{10,9},{11,1... | collective-permute-start | bytes 36872 | tf_op jit(solution)/shard_map/ppermute | solution.py:764
  25.7 0.9 pad_maximum_fusion.refs_0_
  26.6 1.1 %collective-permute-done.5.west_ref = bf16[12,2,256]{2,1,0:T(2,128)(2,1)S(1)} collective-permute-done((bf16[12,2,256]{2,1,0:T(2,128)(2,1)S(1)}, bf16[12,2,256]{2,1,0:T(2,128)(2,1)S(1)}, u32[]{:S(2)}, u32[]{:S(2)}) %collective-permute-start.5) | collective-permute-done | bytes 12320 | tf_op jit(solution)/shard_map/ppermute | solution.py:763
  27.7 0.6 copy-done.9
  28.3 0.6 copy-done.10
  28.9 0.4 all-to-all-done.got_ref
  29.3 1.1 %collective-permute-start.7 = (bf16[4,8,16,256]{3,2,1,0:T(8,128)(2,1)S(1)}, bf16[4,8,16,256]{3,2,1,0:T(8,128)(2,1)S(1)}, u32[]{:S(2)}, u32[]{:S(2)}) collective-permute-start(bf16[4,8,16,256]{3,2,1,0:T(8,128)(2,1)S(1)} %pad_maximum_fusion.refs_0_), channel_id=1, source_target_pairs={{0,8},{8,16},{16,24},{24,0},{1,9},{9,17},{17,25},{25,1},{2,10},{10... | collective-permute-start | bytes 786440 | tf_op jit(solution)/shard_map/ppermute | solution.py:790
  30.4 1.5 %collective-permute-start.8 = (bf16[4,8,16,256]{3,2,1,0:T(8,128)(2,1)S(1)}, bf16[4,8,16,256]{3,2,1,0:T(8,128)(2,1)S(1)}, u32[]{:S(2)}, u32[]{:S(2)}) collective-permute-start(bf16[4,8,16,256]{3,2,1,0:T(8,128)(2,1)S(1)} %pad_maximum_fusion.refs_0_), channel_id=1, source_target_pairs={{0,16},{8,24},{16,0},{24,8},{1,17},{9,25},{17,1},{25,9},{2,18},{10... | collective-permute-start | bytes 786440 | tf_op jit(solution)/shard_map/ppermute | solution.py:790
  31.9 1.4 %collective-permute-start.9 = (bf16[4,8,16,256]{3,2,1,0:T(8,128)(2,1)S(1)}, bf16[4,8,16,256]{3,2,1,0:T(8,128)(2,1)S(1)}, u32[]{:S(2)}, u32[]{:S(2)}) collective-permute-start(bf16[4,8,16,256]{3,2,1,0:T(8,128)(2,1)S(1)} %pad_maximum_fusion.refs_0_), channel_id=1, source_target_pairs={{0,24},{8,0},{16,8},{24,16},{1,25},{9,1},{17,9},{25,17},{2,26},{10... | collective-permute-start | bytes 786440 | tf_op jit(solution)/shard_map/ppermute | solution.py:790
  33.3 11.3 %forward.1 = (f32[128,256]{1,0:T(8,128)}, bf16[128,256]{1,0:T(8,128)(2,1)}, f32[320,256]{1,0:T(8,128)}) custom-call(bf16[8,16,256]{2,1,0:T(8,128)(2,1)} %tile_ref, bf16[2,16,256]{2,1,0:T(8,128)(2,1)} %copy-done.7, bf16[2,16,256]{2,1,0:T(8,128)(2,1)} %copy-done.8, bf16[12,2,256]{2,1,0:T(2,128)(2,1)} %copy-done.9, bf16[12,2,256]{2,1,0:T(2,128)(2,1)} %copy-done.10, ...), custom_call_target="tpu_custom_call" | custom-call | flops 4000000000 | bytes 4000000 | tf_op jit(solution)/shard_map/forward/pallas_call | solution.py:304
  44.7 1.6 %broadcast_in_dim.8 = bf16[4,8,16,256]{3,2,1,0:T(8,128)(2,1)} broadcast(bf16[8,16,256]{2,1,0:T(8,128)(2,1)} %bitcast.14), dimensions={1,2,3} | broadcast | bytes 327680 | tf_op jit(solution)/shard_map/broadcast_in_dim | solution.py:772
  46.3 3.4 %all-to-all-start.1 = ((bf16[4,8,16,256]{3,2,1,0:T(8,128)(2,1)}), bf16[4,8,16,256]{3,2,1,0:T(8,128)(2,1)S(1)}, u32[]{:S(2)}, u32[]{:S(2)}) async-start(bf16[4,8,16,256]{3,2,1,0:T(8,128)(2,1)} %broadcast_in_dim.8), calls=%async_computation.1 | async-start | bytes 524288 | tf_op jit(solution)/shard_map/all_to_all | solution.py:773
  49.8 0.1 collective-permute-start.13
  49.8 0.5 collective-permute-start.14
  50.3 0.1 collective-permute-start.15
  50.4 0.4 collective-permute-start.16
  50.8 8.0 %all-to-all-done.1.refs_0_ = bf16[4,8,16,256]{3,2,1,0:T(8,128)(2,1)S(1)} async-done(((bf16[4,8,16,256]{3,2,1,0:T(8,128)(2,1)}), bf16[4,8,16,256]{3,2,1,0:T(8,128)(2,1)S(1)}, u32[]{:S(2)}, u32[]{:S(2)}) %all-to-all-start.1) | async-done | bytes 262176 | tf_op jit(solution)/shard_map/all_to_all | solution.py:773
  58.8 0.8 collective-permute-start.10
  59.6 0.8 collective-permute-start.11
  60.4 2.1 %collective-permute-start.12 = (bf16[4,8,16,256]{3,2,1,0:T(8,128)(2,1)S(1)}, bf16[4,8,16,256]{3,2,1,0:T(8,128)(2,1)S(1)}, u32[]{:S(2)}, u32[]{:S(2)}) collective-permute-start(bf16[4,8,16,256]{3,2,1,0:T(8,128)(2,1)S(1)} %all-to-all-done.1.refs_0_), channel_id=1, source_target_pairs={{0,24},{8,0},{16,8},{24,16},{1,25},{9,1},{17,9},{25,17},{2,26},{10... | collective-permute-start | bytes 786440 | tf_op jit(solution)/shard_map/ppermute | solution.py:790
  62.6 0.9 copy-done.3
  63.5 6.7 %whole.1 = (f32[2304,256]{1,0:T(8,128)S(1)}, bf16[256,2304]{1,0:T(8,128)(2,1)S(1)}, bf16[256,2304]{1,0:T(8,128)(2,1)S(1)}, bf16[9,256,256]{2,1,0:T(8,128)(2,1)S(1)}) custom-call(bf16[4,8,16,256]{3,2,1,0:T(8,128)(2,1)S(1)} %pad_maximum_fusion.refs_0_, bf16[4,8,16,256]{3,2,1,0:T(8,128)(2,1)} %collective-permute-done.13.refs_1_, ...), custom_call_target="tpu_custom_call" | custom-call | flops 6000000000 | bytes 10000000 | tf_op jit(solution)/shard_map/whole/pallas_call | solution.py:415
  70.2 0.9 collective-permute-done.11.refs_4_
  71.2 0.1 collective-permute-start.17
  71.2 0.5 collective-permute-start.18
  71.7 0.1 collective-permute-start.19
  71.8 0.4 collective-permute-start.20
  72.2 0.5 collective-permute-done.17.refs_1_
  72.8 0.4 collective-permute-done.18.refs_3_
  73.1 0.4 collective-permute-done.19.refs_5_
  73.5 0.4 collective-permute-done.20.refs_7_
  73.9 13.4 %tail.1 = (f32[9,256,256]{2,1,0:T(8,128)S(1)}, f32[9,256,256]{2,1,0:T(8,128)S(1)}) custom-call(bf16[4,8,16,256]{3,2,1,0:T(8,128)(2,1)S(1)} %all-to-all-done.1.refs_0_, bf16[4,8,16,256]{3,2,1,0:T(8,128)(2,1)S(1)} %collective-permute-done.17.refs_1_, bf16[4,8,16,256]{3,2,1,0:T(8,128)(2,1)S(1)} %collective-permute-done.10.refs_2_, ...), custom_call_target="tpu_custom_call" | custom-call | flops 10000000000 | bytes 15000000 | tf_op jit(solution)/shard_map/tail/pallas_call | solution.py:516
  87.3 0.2 collective-permute-start.21
  87.5 0.4 collective-permute-start.22
  87.9 3.0 %local_grad.1 = f32[128,256]{1,0:T(8,128)} custom-call(bf16[4,8,16,256]{3,2,1,0:T(8,128)(2,1)S(1)} %all-to-all-done.1.refs_0_, bf16[4,8,16,256]{3,2,1,0:T(8,128)(2,1)S(1)} %collective-permute-done.17.refs_1_, bf16[4,8,16,256]{3,2,1,0:T(8,128)(2,1)S(1)} %collective-permute-done.10.refs_2_, bf16[4,8,16,256]{3,2,1,0:T(8,128)(2,1)S(1)} %collective-permute-done.18.refs_3_, ...), custom_call_target="tpu_custom_call" | custom-call | flops 3000000000 | bytes 4000000 | tf_op jit(solution)/shard_map/local_grad/pallas_call | solution.py:576
  90.9 1.0 %collective-permute-done.21 = f32[9,256,256]{2,1,0:T(8,128)S(1)} collective-permute-done((f32[9,256,256]{2,1,0:T(8,128)S(1)}, f32[9,256,256]{2,1,0:T(8,128)S(1)}, u32[]{:S(2)}, u32[]{:S(2)}) %collective-permute-start.21) | collective-permute-done | bytes 2359328 | tf_op jit(solution)/shard_map/ppermute | solution.py:838
  91.9 1.7 %add.6 = f32[9,256,256]{2,1,0:T(8,128)} add(f32[9,256,256]{2,1,0:T(8,128)S(1)} %get-tuple-element.63, f32[9,256,256]{2,1,0:T(8,128)S(1)} %collective-permute-done.21) | non-fusion elementwise | flops 589824 | bytes 7077888 | tf_op jit(solution)/shard_map/add | solution.py:840
  93.6 1.7 %collective-permute-done.22 = f32[9,256,256]{2,1,0:T(8,128)S(1)} collective-permute-done((f32[9,256,256]{2,1,0:T(8,128)S(1)}, f32[9,256,256]{2,1,0:T(8,128)S(1)}, u32[]{:S(2)}, u32[]{:S(2)}) %collective-permute-start.22) | collective-permute-done | bytes 2359328 | tf_op jit(solution)/shard_map/ppermute | solution.py:838
  95.3 1.7 %add.7 = f32[9,256,256]{2,1,0:T(8,128)} add(f32[9,256,256]{2,1,0:T(8,128)S(1)} %get-tuple-element.64, f32[9,256,256]{2,1,0:T(8,128)S(1)} %collective-permute-done.22) | non-fusion elementwise | flops 589824 | bytes 7077888 | tf_op jit(solution)/shard_map/add | solution.py:840
  (39 shorter events, 0.1 us)
Async XLA Ops:
  3.4 22.3 %collective-permute-start.2 = (bf16[8,16,256]{2,1,0:T(8,128)(2,1)}, bf16[8,16,256]{2,1,0:T(8,128)(2,1)S(1)}, u32[]{:S(2)}, u32[]{:S(2)}) collective-permute-start(bf16[8,16,256]{2,1,0:T(8,128)(2,1)} %tile_ref), channel_id=1, source_target_pairs={{0,6},{1,7},{2,0},{3,1},{4,2},{5,3},{6,4},{7,5},{8,14},{9,15},{10,... | collective-permute-start | bytes 196616 | tf_op jit(solution)/shard_map/ppermute | solution.py:781
  8.4 17.3 %collective-permute-start.1 = (bf16[8,16,256]{2,1,0:T(8,128)(2,1)}, bf16[8,16,256]{2,1,0:T(8,128)(2,1)S(1)}, u32[]{:S(2)}, u32[]{:S(2)}) collective-permute-start(bf16[8,16,256]{2,1,0:T(8,128)(2,1)} %tile_ref), channel_id=1, source_target_pairs={{0,4},{1,5},{2,6},{3,7},{4,0},{5,1},{6,2},{7,3},{8,12},{9,13},{10,... | collective-permute-start | bytes 196616 | tf_op jit(solution)/shard_map/ppermute | solution.py:781
  8.4 17.3 %collective-permute-start = (bf16[8,16,256]{2,1,0:T(8,128)(2,1)}, bf16[8,16,256]{2,1,0:T(8,128)(2,1)S(1)}, u32[]{:S(2)}, u32[]{:S(2)}) collective-permute-start(bf16[8,16,256]{2,1,0:T(8,128)(2,1)} %tile_ref), channel_id=1, source_target_pairs={{0,2},{1,3},{2,4},{3,5},{4,6},{5,7},{6,0},{7,1},{8,10},{9,11},{10,... | collective-permute-start | bytes 196616 | tf_op jit(solution)/shard_map/ppermute | solution.py:781
  10.2 11.8 %collective-permute-start.3 = (bf16[2,16,256]{2,1,0:T(8,128)(2,1)S(1)}, bf16[2,16,256]{2,1,0:T(8,128)(2,1)S(1)}, u32[]{:S(2)}, u32[]{:S(2)}) collective-permute-start(bf16[2,16,256]{2,1,0:T(8,128)(2,1)S(1)} %get-tuple-element.68), channel_id=1, source_target_pairs={{0,8},{8,16},{16,24},{1,9},{9,17},{17,25},{2,10},{10,18},{18,26},{... | collective-permute-start | bytes 49160 | tf_op jit(solution)/shard_map/ppermute | solution.py:759
  13.6 8.3 %collective-permute-start.4 = (bf16[2,16,256]{2,1,0:T(8,128)(2,1)S(1)}, bf16[2,16,256]{2,1,0:T(8,128)(2,1)S(1)}, u32[]{:S(2)}, u32[]{:S(2)}) collective-permute-start(bf16[2,16,256]{2,1,0:T(8,128)(2,1)S(1)} %get-tuple-element.67), channel_id=1, source_target_pairs={{8,0},{16,8},{24,16},{9,1},{17,9},{25,17},{10,2},{18,10},{26,18},{... | collective-permute-start | bytes 49160 | tf_op jit(solution)/shard_map/ppermute | solution.py:760
  14.9 14.4 %all-to-all-start = ((f32[32,8,128]{2,1,0:T(8,128)}), f32[32,8,128]{2,1,0:T(8,128)S(1)}, u32[]{:S(2)}, u32[]{:S(2)}) async-start(f32[32,8,128]{2,1,0:T(8,128)} %route.1), calls=%async_computation | async-start | bytes 262144 | tf_op jit(solution)/shard_map/all_to_all | solution.py:822
  21.9 5.8 %copy-start.8 = (bf16[2,16,256]{2,1,0:T(8,128)(2,1)}, bf16[2,16,256]{2,1,0:T(8,128)(2,1)S(1)}, u32[]{:S(2)}) copy-start(bf16[2,16,256]{2,1,0:T(8,128)(2,1)S(1)} %collective-permute-done.4.south_ref) | copy-start | bytes 49156
  21.9 11.4 %copy-start.7 = (bf16[2,16,256]{2,1,0:T(8,128)(2,1)}, bf16[2,16,256]{2,1,0:T(8,128)(2,1)S(1)}, u32[]{:S(2)}) copy-start(bf16[2,16,256]{2,1,0:T(8,128)(2,1)S(1)} %collective-permute-done.3.north_ref) | copy-start | bytes 49156
  22.0 5.7 %collective-permute-start.5 = (bf16[12,2,256]{2,1,0:T(2,128)(2,1)S(1)}, bf16[12,2,256]{2,1,0:T(2,128)(2,1)S(1)}, u32[]{:S(2)}, u32[]{:S(2)}) collective-permute-start(bf16[12,2,256]{2,1,0:T(2,128)(2,1)S(1)} %pad_maximum_fusion.1), channel_id=1, source_target_pairs={{0,1},{1,2},{2,3},{3,4},{4,5},{5,6},{6,7},{7,0},{8,9},{9,10},{10,1... | collective-permute-start | bytes 36872 | tf_op jit(solution)/shard_map/ppermute | solution.py:763
  22.3 5.4 %collective-permute-start.6 = (bf16[12,2,256]{2,1,0:T(2,128)(2,1)S(1)}, bf16[12,2,256]{2,1,0:T(2,128)(2,1)S(1)}, u32[]{:S(2)}, u32[]{:S(2)}) collective-permute-start(bf16[12,2,256]{2,1,0:T(2,128)(2,1)S(1)} %pad_maximum_fusion.2), channel_id=1, source_target_pairs={{1,0},{2,1},{3,2},{4,3},{5,4},{6,5},{7,6},{0,7},{9,8},{10,9},{11,1... | collective-permute-start | bytes 36872 | tf_op jit(solution)/shard_map/ppermute | solution.py:764
  26.6 36.0 %copy-start = (bf16[9,256,256]{2,1,0:T(8,128)(2,1)S(1)}, bf16[9,256,256]{2,1,0:T(8,128)(2,1)}, u32[]{:S(2)}) copy-start(bf16[9,256,256]{2,1,0:T(8,128)(2,1)} %refs_10_.1) | copy-start | bytes 3538948
  26.6 36.0 %copy-start.1 = (bf16[9,256,256]{2,1,0:T(8,128)(2,1)S(1)}, bf16[9,256,256]{2,1,0:T(8,128)(2,1)}, u32[]{:S(2)}) copy-start(bf16[9,256,256]{2,1,0:T(8,128)(2,1)} %refs_11_.1) | copy-start | bytes 3538948
  27.7 0.6 copy-start.9
  28.3 0.6 copy-start.10
  29.3 4.1 %copy-start.6 = (f32[32,8,128]{2,1,0:T(8,128)}, f32[32,8,128]{2,1,0:T(8,128)S(1)}, u32[]{:S(2)}) copy-start(f32[32,8,128]{2,1,0:T(8,128)S(1)} %all-to-all-done.got_ref) | copy-start | bytes 393220
  29.3 15.4 %collective-permute-start.7 = (bf16[4,8,16,256]{3,2,1,0:T(8,128)(2,1)S(1)}, bf16[4,8,16,256]{3,2,1,0:T(8,128)(2,1)S(1)}, u32[]{:S(2)}, u32[]{:S(2)}) collective-permute-start(bf16[4,8,16,256]{3,2,1,0:T(8,128)(2,1)S(1)} %pad_maximum_fusion.refs_0_), channel_id=1, source_target_pairs={{0,8},{8,16},{16,24},{24,0},{1,9},{9,17},{17,25},{25,1},{2,10},{10... | collective-permute-start | bytes 786440 | tf_op jit(solution)/shard_map/ppermute | solution.py:790
  30.4 14.3 %collective-permute-start.8 = (bf16[4,8,16,256]{3,2,1,0:T(8,128)(2,1)S(1)}, bf16[4,8,16,256]{3,2,1,0:T(8,128)(2,1)S(1)}, u32[]{:S(2)}, u32[]{:S(2)}) collective-permute-start(bf16[4,8,16,256]{3,2,1,0:T(8,128)(2,1)S(1)} %pad_maximum_fusion.refs_0_), channel_id=1, source_target_pairs={{0,16},{8,24},{16,0},{24,8},{1,17},{9,25},{17,1},{25,9},{2,18},{10... | collective-permute-start | bytes 786440 | tf_op jit(solution)/shard_map/ppermute | solution.py:790
  31.9 12.8 %collective-permute-start.9 = (bf16[4,8,16,256]{3,2,1,0:T(8,128)(2,1)S(1)}, bf16[4,8,16,256]{3,2,1,0:T(8,128)(2,1)S(1)}, u32[]{:S(2)}, u32[]{:S(2)}) collective-permute-start(bf16[4,8,16,256]{3,2,1,0:T(8,128)(2,1)S(1)} %pad_maximum_fusion.refs_0_), channel_id=1, source_target_pairs={{0,24},{8,0},{16,8},{24,16},{1,25},{9,1},{17,9},{25,17},{2,26},{10... | collective-permute-start | bytes 786440 | tf_op jit(solution)/shard_map/ppermute | solution.py:790
  44.7 1.6 %copy-start.2 = (bf16[4,8,16,256]{3,2,1,0:T(8,128)(2,1)}, bf16[4,8,16,256]{3,2,1,0:T(8,128)(2,1)S(1)}, u32[]{:S(2)}) copy-start(bf16[4,8,16,256]{3,2,1,0:T(8,128)(2,1)S(1)} %collective-permute-done.9.refs_6_) | copy-start | bytes 786436
  46.3 12.5 %all-to-all-start.1 = ((bf16[4,8,16,256]{3,2,1,0:T(8,128)(2,1)}), bf16[4,8,16,256]{3,2,1,0:T(8,128)(2,1)S(1)}, u32[]{:S(2)}, u32[]{:S(2)}) async-start(bf16[4,8,16,256]{3,2,1,0:T(8,128)(2,1)} %broadcast_in_dim.8), calls=%async_computation.1 | async-start | bytes 524288 | tf_op jit(solution)/shard_map/all_to_all | solution.py:773
  49.8 9.8 %collective-permute-start.13 = (bf16[4,8,16,256]{3,2,1,0:T(8,128)(2,1)S(1)}, bf16[4,8,16,256]{3,2,1,0:T(8,128)(2,1)}, u32[]{:S(2)}, u32[]{:S(2)}) collective-permute-start(bf16[4,8,16,256]{3,2,1,0:T(8,128)(2,1)S(1)} %pad_maximum_fusion.refs_0_), channel_id=1, source_target_pairs={{0,1},{1,0},{2,3},{3,2},{4,5},{5,4},{6,7},{7,6},{8,9},{9,8},{10,11... | collective-permute-start | bytes 786440 | tf_op jit(solution)/shard_map/ppermute | solution.py:799
  49.8 10.6 %collective-permute-start.14 = (bf16[4,8,16,256]{3,2,1,0:T(8,128)(2,1)S(1)}, bf16[4,8,16,256]{3,2,1,0:T(8,128)(2,1)}, u32[]{:S(2)}, u32[]{:S(2)}) collective-permute-start(bf16[4,8,16,256]{3,2,1,0:T(8,128)(2,1)S(1)} %collective-permute-done.7.refs_2_), channel_id=1, source_target_pairs={{0,1},{1,0},{2,3},{3,2},{4,5},{5,4},{6,7},{7,6},{8,9},{9,8},{10,11... | collective-permute-start | bytes 786440 | tf_op jit(solution)/shard_map/ppermute | solution.py:799
  50.3 12.2 %collective-permute-start.15 = (bf16[4,8,16,256]{3,2,1,0:T(8,128)(2,1)S(1)}, bf16[4,8,16,256]{3,2,1,0:T(8,128)(2,1)}, u32[]{:S(2)}, u32[]{:S(2)}) collective-permute-start(bf16[4,8,16,256]{3,2,1,0:T(8,128)(2,1)S(1)} %collective-permute-done.8.refs_4_), channel_id=1, source_target_pairs={{0,1},{1,0},{2,3},{3,2},{4,5},{5,4},{6,7},{7,6},{8,9},{9,8},{10,11... | collective-permute-start | bytes 786440 | tf_op jit(solution)/shard_map/ppermute | solution.py:799
  50.4 12.1 %collective-permute-start.16 = (bf16[4,8,16,256]{3,2,1,0:T(8,128)(2,1)}, bf16[4,8,16,256]{3,2,1,0:T(8,128)(2,1)}, u32[]{:S(2)}, u32[]{:S(2)}) collective-permute-start(bf16[4,8,16,256]{3,2,1,0:T(8,128)(2,1)} %copy-done.2), channel_id=1, source_target_pairs={{0,1},{1,0},{2,3},{3,2},{4,5},{5,4},{6,7},{7,6},{8,9},{9,8},{10,11... | collective-permute-start | bytes 786440 | tf_op jit(solution)/shard_map/ppermute | solution.py:799
  58.8 11.4 %collective-permute-start.10 = (bf16[4,8,16,256]{3,2,1,0:T(8,128)(2,1)S(1)}, bf16[4,8,16,256]{3,2,1,0:T(8,128)(2,1)S(1)}, u32[]{:S(2)}, u32[]{:S(2)}) collective-permute-start(bf16[4,8,16,256]{3,2,1,0:T(8,128)(2,1)S(1)} %all-to-all-done.1.refs_0_), channel_id=1, source_target_pairs={{0,8},{8,16},{16,24},{24,0},{1,9},{9,17},{17,25},{25,1},{2,10},{10... | collective-permute-start | bytes 786440 | tf_op jit(solution)/shard_map/ppermute | solution.py:790
  59.6 11.6 %collective-permute-start.11 = (bf16[4,8,16,256]{3,2,1,0:T(8,128)(2,1)S(1)}, bf16[4,8,16,256]{3,2,1,0:T(8,128)(2,1)S(1)}, u32[]{:S(2)}, u32[]{:S(2)}) collective-permute-start(bf16[4,8,16,256]{3,2,1,0:T(8,128)(2,1)S(1)} %all-to-all-done.1.refs_0_), channel_id=1, source_target_pairs={{0,16},{8,24},{16,0},{24,8},{1,17},{9,25},{17,1},{25,9},{2,18},{10... | collective-permute-start | bytes 786440 | tf_op jit(solution)/shard_map/ppermute | solution.py:790
  60.4 10.8 %collective-permute-start.12 = (bf16[4,8,16,256]{3,2,1,0:T(8,128)(2,1)S(1)}, bf16[4,8,16,256]{3,2,1,0:T(8,128)(2,1)S(1)}, u32[]{:S(2)}, u32[]{:S(2)}) collective-permute-start(bf16[4,8,16,256]{3,2,1,0:T(8,128)(2,1)S(1)} %all-to-all-done.1.refs_0_), channel_id=1, source_target_pairs={{0,24},{8,0},{16,8},{24,16},{1,25},{9,1},{17,9},{25,17},{2,26},{10... | collective-permute-start | bytes 786440 | tf_op jit(solution)/shard_map/ppermute | solution.py:790
  62.6 1.0 copy-start.3
  71.2 16.7 %copy-start.4 = (f32[320,256]{1,0:T(8,128)S(1)}, f32[320,256]{1,0:T(8,128)}, u32[]{:S(2)}) copy-start(f32[320,256]{1,0:T(8,128)} %get-tuple-element.57.refs_8_) | copy-start | bytes 983044
  71.2 16.7 %copy-start.5 = (f32[128,256]{1,0:T(8,128)S(1)}, f32[128,256]{1,0:T(8,128)}, u32[]{:S(2)}) copy-start(f32[128,256]{1,0:T(8,128)} %get-tuple-element.58.refs_9_) | copy-start | bytes 393220
  71.2 1.6 %collective-permute-start.17 = (bf16[4,8,16,256]{3,2,1,0:T(8,128)(2,1)S(1)}, bf16[4,8,16,256]{3,2,1,0:T(8,128)(2,1)S(1)}, u32[]{:S(2)}, u32[]{:S(2)}) collective-permute-start(bf16[4,8,16,256]{3,2,1,0:T(8,128)(2,1)S(1)} %all-to-all-done.1.refs_0_), channel_id=1, source_target_pairs={{0,1},{1,0},{2,3},{3,2},{4,5},{5,4},{6,7},{7,6},{8,9},{9,8},{10,11... | collective-permute-start | bytes 786440 | tf_op jit(solution)/shard_map/ppermute | solution.py:799
  71.2 1.9 %collective-permute-start.18 = (bf16[4,8,16,256]{3,2,1,0:T(8,128)(2,1)S(1)}, bf16[4,8,16,256]{3,2,1,0:T(8,128)(2,1)S(1)}, u32[]{:S(2)}, u32[]{:S(2)}) collective-permute-start(bf16[4,8,16,256]{3,2,1,0:T(8,128)(2,1)S(1)} %collective-permute-done.10.refs_2_), channel_id=1, source_target_pairs={{0,1},{1,0},{2,3},{3,2},{4,5},{5,4},{6,7},{7,6},{8,9},{9,8},{10,11... | collective-permute-start | bytes 786440 | tf_op jit(solution)/shard_map/ppermute | solution.py:799
  71.7 1.8 %collective-permute-start.19 = (bf16[4,8,16,256]{3,2,1,0:T(8,128)(2,1)S(1)}, bf16[4,8,16,256]{3,2,1,0:T(8,128)(2,1)S(1)}, u32[]{:S(2)}, u32[]{:S(2)}) collective-permute-start(bf16[4,8,16,256]{3,2,1,0:T(8,128)(2,1)S(1)} %collective-permute-done.11.refs_4_), channel_id=1, source_target_pairs={{0,1},{1,0},{2,3},{3,2},{4,5},{5,4},{6,7},{7,6},{8,9},{9,8},{10,11... | collective-permute-start | bytes 786440 | tf_op jit(solution)/shard_map/ppermute | solution.py:799
  71.8 2.1 %collective-permute-start.20 = (bf16[4,8,16,256]{3,2,1,0:T(8,128)(2,1)S(1)}, bf16[4,8,16,256]{3,2,1,0:T(8,128)(2,1)S(1)}, u32[]{:S(2)}, u32[]{:S(2)}) collective-permute-start(bf16[4,8,16,256]{3,2,1,0:T(8,128)(2,1)S(1)} %collective-permute-done.12.refs_6_), channel_id=1, source_target_pairs={{0,1},{1,0},{2,3},{3,2},{4,5},{5,4},{6,7},{7,6},{8,9},{9,8},{10,11... | collective-permute-start | bytes 786440 | tf_op jit(solution)/shard_map/ppermute | solution.py:799
  87.3 4.6 %collective-permute-start.21 = (f32[9,256,256]{2,1,0:T(8,128)S(1)}, f32[9,256,256]{2,1,0:T(8,128)S(1)}, u32[]{:S(2)}, u32[]{:S(2)}) collective-permute-start(f32[9,256,256]{2,1,0:T(8,128)S(1)} %get-tuple-element.63), channel_id=1, source_target_pairs={{0,1},{1,0},{2,3},{3,2},{4,5},{5,4},{6,7},{7,6},{8,9},{9,8},{10,11... | collective-permute-start | bytes 7077896 | tf_op jit(solution)/shard_map/ppermute | solution.py:838
  87.5 7.8 %collective-permute-start.22 = (f32[9,256,256]{2,1,0:T(8,128)S(1)}, f32[9,256,256]{2,1,0:T(8,128)S(1)}, u32[]{:S(2)}, u32[]{:S(2)}) collective-permute-start(f32[9,256,256]{2,1,0:T(8,128)S(1)} %get-tuple-element.64), channel_id=1, source_target_pairs={{0,1},{1,0},{2,3},{3,2},{4,5},{5,4},{6,7},{7,6},{8,9},{9,8},{10,11... | collective-permute-start | bytes 7077896 | tf_op jit(solution)/shard_map/ppermute | solution.py:838

commit v9 on v8

--- a/solution.py
+++ b/solution.py
@@ -293,10 +293,11 @@
     lax.fori_loop(0, count, step, 0)
     adjoint = sum_ref[...].T
     adj_ref[...] = adjoint
-    pull_ref[...] = adjoint.astype(BF16)
-
-
-def forward(slots, bands, pieces, w1, w2, got):
+    for copy in range(pull_ref.shape[0]):
+        pull_ref[copy] = adjoint.astype(BF16)
+
+
+def forward(slots, bands, copies, pieces, w1, w2, got):
     rows, cols, chans = pieces[0].shape
     devices = got.shape[0]
     full, rest, _ = slot_layout(slots)
@@ -305,7 +306,7 @@
         functools.partial(forward_kernel, slots, bands, 2, 4),
         out_shape=[
             jax.ShapeDtypeStruct((rows * cols, chans), F32),
-            jax.ShapeDtypeStruct((rows * cols, chans), BF16),
+            jax.ShapeDtypeStruct((copies, rows * cols, chans), BF16),
             jax.ShapeDtypeStruct(((rows + 2) * SPAN, chans), F32),
         ],
         in_specs=[vmem()] * 5 + [anywhere()] * 2 + [vmem()],
@@ -427,7 +428,7 @@
             pltpu.VMEM((2, bands) + pieces[0].shape, BF16),
             pltpu.SemaphoreType.DMA((bands, 2)),
         ],
-        compiler_params=params(28),
+        compiler_params=params(22),
         cost_estimate=cost(6e9, 10e6),
         name="whole",
     )(*pieces, w1, w2)
@@ -449,31 +450,21 @@
     lax.fori_loop(0, 9, step, 0)
 
 
-def tail_kernel(block, *refs):
-    bands = (len(refs) - 18) // 2
+def second_kernel(bands, *refs):
     piece_refs, refs = refs[: 2 * bands], refs[2 * bands :]
-    slope_hbm, hidden_hbm, state_hbm, w2t_ref, g1_hbm, g2_hbm = refs[:6]
-    all_ref, pull_ref, first_ref, slope_ref, hidden_ref, state_ref, g1_ref, g2_ref = refs[6:14]
-    piece_sems, big_sems, g1_sems, g2_sems = refs[14:]
+    hidden_hbm, g2_hbm, pull_ref, all_ref, hidden_ref, g2_ref, piece_sems, sem, g2_sems = refs
     steps = pull_ref.shape[1] - 2
     chans = pull_ref.shape[3]
     lons = steps * 16
-    size = block * lons
-    _, bands, half, rows, cols, _ = all_ref.shape
+    _, _, half, rows, _, _ = all_ref.shape
     lats = bands * rows
     mine = lats // 2
     base = (lax.axis_index("lon") & 1) * mine
     copies = band_copies(bands, piece_refs, all_ref, piece_sems)
-    hidden_copy = pltpu.make_async_copy(hidden_hbm, hidden_ref, big_sems.at[0])
-    slope_copy = pltpu.make_async_copy(
-        slope_hbm.at[pl.ds(lons, mine * lons), :], slope_ref, big_sems.at[1]
-    )
-    state_copy = pltpu.make_async_copy(state_hbm, state_ref, big_sems.at[2])
+    hidden_copy = pltpu.make_async_copy(hidden_hbm, hidden_ref, sem)
     for copy in copies:
         copy.start()
     hidden_copy.start()
-    slope_copy.start()
-    state_copy.start()
     matrix = spread_matrix(steps, 2 * half, False)
     for copy in copies:
         copy.wait()
@@ -483,6 +474,49 @@
     )
     hidden_copy.wait()
     tap_sums(hidden_ref, pull_ref, 1, mine, g2_ref, g2_hbm, g2_sems)
+    for tap in range(9):
+        pltpu.make_async_copy(g2_ref.at[tap], g2_hbm.at[tap], g2_sems.at[tap]).wait()
+
+
+def second_sums(bands, pieces, hidden):
+    half, rows, group, chans = pieces[0].shape
+    lats, lons = bands * rows, 2 * half * group
+    ours = lats // 2
+    return pl.pallas_call(
+        functools.partial(second_kernel, bands),
+        out_shape=[
+            jax.ShapeDtypeStruct((9, chans, chans), F32),
+            jax.ShapeDtypeStruct((ours + 2, lons // 16 + 2, 16, chans), BF16),
+        ],
+        in_specs=[anywhere()] * (len(pieces) + 1),
+        out_specs=[anywhere(), vmem()],
+        scratch_shapes=[
+            pltpu.VMEM((2, bands) + pieces[0].shape, BF16),
+            pltpu.VMEM(hidden.shape, BF16),
+            pltpu.VMEM((9, chans, chans), F32),
+            pltpu.SemaphoreType.DMA((bands, 2)),
+            pltpu.SemaphoreType.DMA,
+            pltpu.SemaphoreType.DMA((9,)),
+        ],
+        compiler_params=params(20),
+        cost_estimate=cost(5e9, 8e6),
+        name="second_sums",
+    )(*pieces, hidden)
+
+
+def first_kernel(block, slope_hbm, state_hbm, pull_ref, w2t_ref, g1_hbm, first_ref, slope_ref,
+                 state_ref, g1_ref, sems, g1_sems):
+    steps = pull_ref.shape[1] - 2
+    chans = pull_ref.shape[3]
+    mine = first_ref.shape[0]
+    lons = steps * 16
+    size = block * lons
+    slope_copy = pltpu.make_async_copy(
+        slope_hbm.at[pl.ds(lons, mine * lons), :], slope_ref, sems.at[0]
+    )
+    state_copy = pltpu.make_async_copy(state_hbm, state_ref, sems.at[1])
+    slope_copy.start()
+    state_copy.start()
     slope_copy.wait()
 
     def step(index, carry):
@@ -504,38 +538,29 @@
     state_copy.wait()
     tap_sums(state_ref, first_ref, 0, mine, g1_ref, g1_hbm, g1_sems)
     for tap in range(9):
-        pltpu.make_async_copy(g2_ref.at[tap], g2_hbm.at[tap], g2_sems.at[tap]).wait()
         pltpu.make_async_copy(g1_ref.at[tap], g1_hbm.at[tap], g1_sems.at[tap]).wait()
 
 
-def tail(bands, pieces, slope, hidden, state, w2t):
-    half, rows, group, chans = pieces[0].shape
-    lats, lons = bands * rows, 2 * half * group
-    steps = lons // 16
-    ours = lats // 2
+def first_sums(slope, state, pull, w2t):
+    ours, wide, group, chans = pull.shape[0] - 2, *pull.shape[1:]
+    lons = (wide - 2) * group
     return pl.pallas_call(
-        functools.partial(tail_kernel, 4),
-        out_shape=[jax.ShapeDtypeStruct((9, chans, chans), F32)] * 2,
-        in_specs=[anywhere()] * (len(pieces) + 3) + [vmem()],
-        out_specs=[anywhere()] * 2,
+        functools.partial(first_kernel, 4),
+        out_shape=jax.ShapeDtypeStruct((9, chans, chans), F32),
+        in_specs=[anywhere()] * 2 + [vmem()] * 2,
+        out_specs=anywhere(),
         scratch_shapes=[
-            pltpu.VMEM((2, bands) + pieces[0].shape, BF16),
-            pltpu.VMEM((ours + 2, steps + 2, 16, chans), BF16),
-            pltpu.VMEM((ours, steps + 2, 16, chans), BF16),
+            pltpu.VMEM((ours, wide, group, chans), BF16),
             pltpu.VMEM((ours * lons, chans), F32),
-            pltpu.VMEM(hidden.shape, BF16),
             pltpu.VMEM(state.shape, BF16),
             pltpu.VMEM((9, chans, chans), F32),
-            pltpu.VMEM((9, chans, chans), F32),
-            pltpu.SemaphoreType.DMA((bands, 2)),
-            pltpu.SemaphoreType.DMA((3,)),
+            pltpu.SemaphoreType.DMA((2,)),
             pltpu.SemaphoreType.DMA((9,)),
-            pltpu.SemaphoreType.DMA((9,)),
-        ],
-        compiler_params=params(36),
-        cost_estimate=cost(10e9, 15e6),
-        name="tail",
-    )(*pieces, slope, hidden, state, w2t)
+        ],
+        compiler_params=params(24),
+        cost_estimate=cost(10e9, 8e6),
+        name="first_sums",
+    )(slope, state, pull, w2t)
 
 
 def local_kernel(bands, *refs):
@@ -765,11 +790,9 @@
     return x, north, south, west, east
 
 
-def gather_line(x):
-    tiles = lax.axis_size("lon")
-    half = tiles // 2
+def gather_line(copies):
+    half = copies.shape[0]
     same = [[2 * q + core for q in range(half)] for core in range(2)]
-    copies = jnp.broadcast_to(x[None], (half,) + x.shape)
     return lax.all_to_all(copies, "lon", 0, 0, axis_index_groups=same, tiled=True)
 
 
@@ -823,21 +846,25 @@
     line = gather_line_backwards(sent)
     line, pieces, got = lax.optimization_barrier((line, pieces, got))
     state_lines = gather_bands(line)
+    half = lax.axis_size("lon") // 2
     adjoint, pullback, near_slope = forward(
-        slots, bands, pieces, weight_first, weight_second, got
+        slots, bands, half, pieces, weight_first, weight_second, got
     )
     state_lines, pullback = lax.optimization_barrier((state_lines, pullback))
     state_pieces = with_other_core(state_lines)
-    pull_lines = gather_bands(gather_line(pullback.reshape(rows, cols, chans)))
+    pull_lines = gather_bands(gather_line(pullback.reshape(half, rows, cols, chans)))
     firsts = whole(bands, state_pieces, weight_first, weight_second)
     pull_lines, firsts = lax.optimization_barrier((pull_lines, firsts))
     slope, hidden, turned, w2t = firsts
     pull_pieces = with_other_core(pull_lines)
-    sums = tail(bands, pull_pieces, slope, hidden, turned, w2t)
-    swap = [(i, i ^ 1) for i in range(lax.axis_size("lon"))]
-    theirs = [lax.ppermute(part, "lon", swap) for part in sums]
+    swap = [(i, i ^ 1) for i in range(2 * half)]
+    g2, pull = second_sums(bands, pull_pieces, hidden)
+    g2_other = lax.ppermute(g2, "lon", swap)
+    g1 = first_sums(slope, turned, pull, w2t)
+    g1, g2_other = lax.optimization_barrier((g1, g2_other))
+    g1_other = lax.ppermute(g1, "lon", swap)
     grad = local_grad(bands, pull_pieces, near_slope, adjoint, weight_first, weight_second)
-    g1, g2 = [part + their for part, their in zip(sums, theirs)]
+    g1, g2 = g1 + g1_other, g2 + g2_other
     return grad.reshape(rows, cols, chans), g1, g2
 
 

time: 97.7 us -> 94.9 us (0.971)
  starting transfers between devices: 34.5 us -> 33.2 us
    ppermute x2, waiting for transfers between devices: 2.63 us -> 0.01 us  [the longest x1 0.01 us: per_device(): g2_other = lax.ppermute(g2, 'lon', swap)]
    ppermute x6, starting transfers between devices: 7.75 us -> 5.96 us  [gather_bands(): lax.ppermute(line, 'lat', [(i, (i + step) % bands) for i in range(bands)])]
    ppermute x6, waiting for transfers between devices: 0.96 us -> 2.63 us  [gather_bands(): lax.ppermute(line, 'lat', [(i, (i + step) % bands) for i in range(bands)])]
    broadcast_in_dim x1 -> x0, local copies, waits for them, and re-layouts: 1.63 us -> none  [gather_line(): copies = jnp.broadcast_to(x[None], (half,) + x.shape)]
    all_to_all x1, starting transfers between devices: 6.22 us -> 5.01 us  [per_device(): lax.all_to_all(outgoing, ('lat', 'lon'), split_axis=0, concat_axis=0, til...]
    ppermute x1, starting transfers between devices: 3.38 us -> 4.55 us  [halo_pieces(): lax.ppermute(x[rows - 2:], 'lat', [(i, i + 1) for i in range(bands - 1)])]
    pallas_call x1 -> x2, Pallas kernels: 13.4 us -> 13.4 us  [the longest x1 7.92 us: first_sums(): pl.pallas_call(functools.partial(first_kernel, 4), out_shape=jax.ShapeDty...]
  transfers between devices with their start and end apart: 25 -> 25, of which waited for: 10 -> 9; matrix products, arithmetic and copies ran while one was open for 4% -> 4% of each run, Pallas kernels for 22% -> 31%
where the time goes in v9:
time: 94.9 us; the launch traced here: 94.2 us
  Pallas kernels  37.3 us (39%)
  starting transfers between devices  33.2 us (35%)
  waiting for transfers between devices  14.1 us (15%)
  local copies, waits for them, and re-layouts  4.44 us (5%)
  other arithmetic  4.35 us (5%)
    pallas_call x1, Pallas kernels, forward(): pl.pallas_call(functools.partial(forward_kernel, slots, bands, 2, 4), out...  11.4 us
    all_to_all x1, waiting for transfers between devices, gather_line(): lax.all_to_all(copies, 'lon', 0, 0, axis_index_groups=same, tiled=True)  8.35 us
    pallas_call x1, Pallas kernels, first_sums(): pl.pallas_call(functools.partial(first_kernel, 4), out_shape=jax.ShapeDty...  7.92 us
    pallas_call x1, Pallas kernels, whole(): pl.pallas_call(functools.partial(whole_kernel, 3), out_shape=[jax.ShapeDt...  6.69 us
    ppermute x3, starting transfers between devices, gather_line_backwards(): lax.ppermute(x, 'lon', [(i, (i + step) % tiles) for i in range(tiles)])  6.06 us
    ppermute x6, starting transfers between devices, gather_bands(): lax.ppermute(line, 'lat', [(i, (i + step) % bands) for i in range(bands)])  5.96 us
    pallas_call x1, Pallas kernels, second_sums(): pl.pallas_call(functools.partial(second_kernel, bands), out_shape=[jax.Sh...  5.48 us
    all_to_all x1, starting transfers between devices, per_device(): lax.all_to_all(outgoing, ('lat', 'lon'), split_axis=0, concat_axis=0, til...  5.01 us
  transfers between devices with their start and end apart: 25, of which 9 were waited for; matrix products, arithmetic and copies ran while one was open for 4% of the time, Pallas kernels for 31%

profile of v9, /device:TPU:0, one launch (start us, length us, event | category | flops | bytes accessed | tf_op | source)
XLA Modules:
  0.0 94.2 jit_solution(12335297356501024301)
XLA Ops:
  0.6 2.7 %route.1 = f32[32,8,128]{2,1,0:T(8,128)} custom-call(s32[1,128]{1,0:T(1,128)} %bitcast.23, s32[1,128]{1,0:T(1,128)} %bitcast.24, s32[32,128]{1,0:T(8,128)} %bitcast.19, s32[32,128]{1,0:T(8,128)} %bitcast.20, f32[2,32,128]{2,1,0:T(8,128)} %bitcast.18, f32[32,128]{1,0:T(8,128)} %bitcast.21, f32[32,128]{1,0:T(8,128)} %bitcast.22), custom_call_target="tpu_custom_call" | custom-call | tf_op jit(solution)/shard_map/route/pallas_call | solution.py:99
  3.4 5.0 %collective-permute-start.2 = (bf16[8,16,256]{2,1,0:T(8,128)(2,1)}, bf16[8,16,256]{2,1,0:T(8,128)(2,1)S(1)}, u32[]{:S(2)}, u32[]{:S(2)}) collective-permute-start(bf16[8,16,256]{2,1,0:T(8,128)(2,1)} %tile_ref), channel_id=1, source_target_pairs={{0,6},{1,7},{2,0},{3,1},{4,2},{5,3},{6,4},{7,5},{8,14},{9,15},{10,... | collective-permute-start | bytes 196616 | tf_op jit(solution)/shard_map/ppermute | solution.py:804
  8.4 1.0 %collective-permute-start = (bf16[8,16,256]{2,1,0:T(8,128)(2,1)}, bf16[8,16,256]{2,1,0:T(8,128)(2,1)S(1)}, u32[]{:S(2)}, u32[]{:S(2)}) collective-permute-start(bf16[8,16,256]{2,1,0:T(8,128)(2,1)} %tile_ref), channel_id=1, source_target_pairs={{0,2},{1,3},{2,4},{3,5},{4,6},{5,7},{6,0},{7,1},{8,10},{9,11},{10,... | collective-permute-start | bytes 196616 | tf_op jit(solution)/shard_map/ppermute | solution.py:804
  9.4 0.8 fusion.1
  10.2 1.3 %collective-permute-start.4 = (bf16[2,16,256]{2,1,0:T(8,128)(2,1)S(1)}, bf16[2,16,256]{2,1,0:T(8,128)(2,1)S(1)}, u32[]{:S(2)}, u32[]{:S(2)}) collective-permute-start(bf16[2,16,256]{2,1,0:T(8,128)(2,1)S(1)} %get-tuple-element.71), channel_id=1, source_target_pairs={{8,0},{16,8},{24,16},{9,1},{17,9},{25,17},{10,2},{18,10},{26,18},{... | collective-permute-start | bytes 49160 | tf_op jit(solution)/shard_map/ppermute | solution.py:785
  11.5 4.5 %collective-permute-start.3 = (bf16[2,16,256]{2,1,0:T(8,128)(2,1)S(1)}, bf16[2,16,256]{2,1,0:T(8,128)(2,1)S(1)}, u32[]{:S(2)}, u32[]{:S(2)}) collective-permute-start(bf16[2,16,256]{2,1,0:T(8,128)(2,1)S(1)} %get-tuple-element.72), channel_id=1, source_target_pairs={{0,8},{8,16},{16,24},{1,9},{9,17},{17,25},{2,10},{10,18},{18,26},{... | collective-permute-start | bytes 49160 | tf_op jit(solution)/shard_map/ppermute | solution.py:784
  16.0 5.0 %all-to-all-start = ((f32[32,8,128]{2,1,0:T(8,128)}), f32[32,8,128]{2,1,0:T(8,128)S(1)}, u32[]{:S(2)}, u32[]{:S(2)}) async-start(f32[32,8,128]{2,1,0:T(8,128)} %route.1), calls=%async_computation | async-start | bytes 262144 | tf_op jit(solution)/shard_map/all_to_all | solution.py:845
  21.0 0.8 fusion
  21.9 0.3 collective-permute-start.5
  22.3 3.3 %collective-permute-start.6 = (bf16[12,2,256]{2,1,0:T(2,128)(2,1)S(1)}, bf16[12,2,256]{2,1,0:T(2,128)(2,1)S(1)}, u32[]{:S(2)}, u32[]{:S(2)}) collective-permute-start(bf16[12,2,256]{2,1,0:T(2,128)(2,1)S(1)} %pad_maximum_fusion.2), channel_id=1, source_target_pairs={{1,0},{2,1},{3,2},{4,3},{5,4},{6,5},{7,6},{0,7},{9,8},{10,9},{11,1... | collective-permute-start | bytes 36872 | tf_op jit(solution)/shard_map/ppermute | solution.py:789
  25.6 0.9 pad_maximum_fusion.refs_0_
  26.5 0.0 copy-start
  26.5 0.0 copy-start.1
  26.5 1.1 %collective-permute-done.5.west_ref = bf16[12,2,256]{2,1,0:T(2,128)(2,1)S(1)} collective-permute-done((bf16[12,2,256]{2,1,0:T(2,128)(2,1)S(1)}, bf16[12,2,256]{2,1,0:T(2,128)(2,1)S(1)}, u32[]{:S(2)}, u32[]{:S(2)}) %collective-permute-start.5) | collective-permute-done | bytes 12320 | tf_op jit(solution)/shard_map/ppermute | solution.py:788
  27.7 0.6 copy-done.9
  28.2 0.6 copy-done.10
  28.8 0.4 all-to-all-done.got_ref
  29.2 2.0 %collective-permute-start.9 = (bf16[4,8,16,256]{3,2,1,0:T(8,128)(2,1)S(1)}, bf16[4,8,16,256]{3,2,1,0:T(8,128)(2,1)S(1)}, u32[]{:S(2)}, u32[]{:S(2)}) collective-permute-start(bf16[4,8,16,256]{3,2,1,0:T(8,128)(2,1)S(1)} %pad_maximum_fusion.refs_0_), channel_id=1, source_target_pairs={{0,24},{8,0},{16,8},{24,16},{1,25},{9,1},{17,9},{25,17},{2,26},{10... | collective-permute-start | bytes 786440 | tf_op jit(solution)/shard_map/ppermute | solution.py:813
  31.3 0.5 collective-permute-start.8
  31.8 0.6 collective-permute-start.7
  32.4 11.4 %forward.1 = (f32[128,256]{1,0:T(8,128)}, bf16[4,128,256]{2,1,0:T(8,128)(2,1)}, f32[320,256]{1,0:T(8,128)}) custom-call(bf16[8,16,256]{2,1,0:T(8,128)(2,1)} %tile_ref, bf16[2,16,256]{2,1,0:T(8,128)(2,1)} %copy-done.8, bf16[2,16,256]{2,1,0:T(8,128)(2,1)} %copy-done.7, bf16[12,2,256]{2,1,0:T(2,128)(2,1)} %copy-done.9, bf16[12,2,256]{2,1,0:T(2,128)(2,1)} %copy-done.10, ...), custom_call_target="tpu_custom_call" | custom-call | flops 4000000000 | bytes 4000000 | tf_op jit(solution)/shard_map/forward/pallas_call | solution.py:305
  43.8 0.1 collective-permute-done.8.refs_4_
  43.9 0.7 copy-done.2
  44.7 4.0 %all-to-all-start.1 = ((bf16[4,8,16,256]{3,2,1,0:T(8,128)(2,1)}), bf16[4,8,16,256]{3,2,1,0:T(8,128)(2,1)S(1)}, u32[]{:S(2)}, u32[]{:S(2)}) async-start(bf16[4,8,16,256]{3,2,1,0:T(8,128)(2,1)} %bitcast.13), calls=%async_computation.1 | async-start | bytes 524288 | tf_op jit(solution)/shard_map/all_to_all | solution.py:796
  48.7 0.1 collective-permute-start.13
  48.7 0.5 collective-permute-start.14
  49.2 0.1 collective-permute-start.15
  49.2 0.5 collective-permute-start.16
  49.7 8.3 %all-to-all-done.1.refs_0_ = bf16[4,8,16,256]{3,2,1,0:T(8,128)(2,1)S(1)} async-done(((bf16[4,8,16,256]{3,2,1,0:T(8,128)(2,1)}), bf16[4,8,16,256]{3,2,1,0:T(8,128)(2,1)S(1)}, u32[]{:S(2)}, u32[]{:S(2)}) %all-to-all-start.1) | async-done | bytes 262176 | tf_op jit(solution)/shard_map/all_to_all | solution.py:796
  58.0 1.3 %collective-permute-start.12 = (bf16[4,8,16,256]{3,2,1,0:T(8,128)(2,1)S(1)}, bf16[4,8,16,256]{3,2,1,0:T(8,128)(2,1)S(1)}, u32[]{:S(2)}, u32[]{:S(2)}) collective-permute-start(bf16[4,8,16,256]{3,2,1,0:T(8,128)(2,1)S(1)} %all-to-all-done.1.refs_0_), channel_id=1, source_target_pairs={{0,24},{8,0},{16,8},{24,16},{1,25},{9,1},{17,9},{25,17},{2,26},{10... | collective-permute-start | bytes 786440 | tf_op jit(solution)/shard_map/ppermute | solution.py:813
  59.4 1.5 %collective-permute-start.11 = (bf16[4,8,16,256]{3,2,1,0:T(8,128)(2,1)S(1)}, bf16[4,8,16,256]{3,2,1,0:T(8,128)(2,1)S(1)}, u32[]{:S(2)}, u32[]{:S(2)}) collective-permute-start(bf16[4,8,16,256]{3,2,1,0:T(8,128)(2,1)S(1)} %all-to-all-done.1.refs_0_), channel_id=1, source_target_pairs={{0,16},{8,24},{16,0},{24,8},{1,17},{9,25},{17,1},{25,9},{2,18},{10... | collective-permute-start | bytes 786440 | tf_op jit(solution)/shard_map/ppermute | solution.py:813
  60.9 0.9 copy-done.3
  61.8 6.7 %whole.1 = (f32[2304,256]{1,0:T(8,128)S(1)}, bf16[256,2304]{1,0:T(8,128)(2,1)S(1)}, bf16[256,2304]{1,0:T(8,128)(2,1)S(1)}, bf16[9,256,256]{2,1,0:T(8,128)(2,1)S(1)}) custom-call(bf16[4,8,16,256]{3,2,1,0:T(8,128)(2,1)S(1)} %pad_maximum_fusion.refs_0_, bf16[4,8,16,256]{3,2,1,0:T(8,128)(2,1)} %collective-permute-done.13.refs_1_, ...), custom_call_target="tpu_custom_call" | custom-call | flops 6000000000 | bytes 10000000 | tf_op jit(solution)/shard_map/whole/pallas_call | solution.py:416
  68.5 2.5 %collective-permute-done.11.refs_4_ = bf16[4,8,16,256]{3,2,1,0:T(8,128)(2,1)S(1)} collective-permute-done((bf16[4,8,16,256]{3,2,1,0:T(8,128)(2,1)S(1)}, bf16[4,8,16,256]{3,2,1,0:T(8,128)(2,1)S(1)}, u32[]{:S(2)}, u32[]{:S(2)}) %collective-permute-start.11) | collective-permute-done | bytes 262176 | tf_op jit(solution)/shard_map/ppermute | solution.py:813
  71.0 0.5 collective-permute-start.18
  71.5 0.0 collective-permute-start.19
  71.5 0.5 collective-permute-start.20
  72.0 0.5 collective-permute-done.17.refs_1_
  72.6 0.4 collective-permute-done.18.refs_3_
  72.9 0.4 collective-permute-done.19.refs_5_
  73.3 0.4 collective-permute-done.20.refs_7_
  73.7 5.5 %second_sums.1 = (f32[9,256,256]{2,1,0:T(8,128)S(1)}, bf16[18,10,16,256]{3,2,1,0:T(8,128)(2,1)S(1)}) custom-call(bf16[4,8,16,256]{3,2,1,0:T(8,128)(2,1)S(1)} %all-to-all-done.1.refs_0_, bf16[4,8,16,256]{3,2,1,0:T(8,128)(2,1)S(1)} %collective-permute-done.17.refs_1_, bf16[4,8,16,256]{3,2,1,0:T(8,128)(2,1)S(1)} %collective-permute-done.10.refs_2_, ...), custom_call_target="tpu_custom_call" | custom-call | flops 5000000000 | bytes 8000000 | tf_op jit(solution)/shard_map/second_sums/pallas_call | solution.py:485
  79.2 0.2 collective-permute-start.21
  79.4 7.9 %first_sums.1 = f32[9,256,256]{2,1,0:T(8,128)S(1)} custom-call(f32[2304,256]{1,0:T(8,128)S(1)} %get-tuple-element.61.slope_hbm, bf16[256,2304]{1,0:T(8,128)(2,1)S(1)} %get-tuple-element.62.state_hbm, bf16[18,10,16,256]{3,2,1,0:T(8,128)(2,1)S(1)} %get-tuple-element.64.pull_ref, bf16[9,256,256]{2,1,0:T(8,128)(2,1)S(1)} %get-tuple-element.65.w2t_ref), custom_call_target="tpu_custom_call" | custom-call | flops 10000000000 | bytes 8000000 | tf_op jit(solution)/shard_map/first_sums/pallas_call | solution.py:547
  87.3 0.4 collective-permute-start.22
  87.8 3.0 %local_grad.1 = f32[128,256]{1,0:T(8,128)} custom-call(bf16[4,8,16,256]{3,2,1,0:T(8,128)(2,1)S(1)} %all-to-all-done.1.refs_0_, bf16[4,8,16,256]{3,2,1,0:T(8,128)(2,1)S(1)} %collective-permute-done.17.refs_1_, bf16[4,8,16,256]{3,2,1,0:T(8,128)(2,1)S(1)} %collective-permute-done.10.refs_2_, bf16[4,8,16,256]{3,2,1,0:T(8,128)(2,1)S(1)} %collective-permute-done.18.refs_3_, ...), custom_call_target="tpu_custom_call" | custom-call | flops 3000000000 | bytes 4000000 | tf_op jit(solution)/shard_map/local_grad/pallas_call | solution.py:601
  90.8 1.7 %add.7 = f32[9,256,256]{2,1,0:T(8,128)} add(f32[9,256,256]{2,1,0:T(8,128)S(1)} %get-tuple-element.66, f32[9,256,256]{2,1,0:T(8,128)S(1)} %collective-permute-done.21) | non-fusion elementwise | flops 589824 | bytes 7077888 | tf_op jit(solution)/shard_map/add | solution.py:867
  92.5 1.7 %add.6 = f32[9,256,256]{2,1,0:T(8,128)} add(f32[9,256,256]{2,1,0:T(8,128)S(1)} %first_sums.1, f32[9,256,256]{2,1,0:T(8,128)S(1)} %collective-permute-done.22) | non-fusion elementwise | flops 589824 | bytes 7077888 | tf_op jit(solution)/shard_map/add | solution.py:867
  (39 shorter events, 0.1 us)
Async XLA Ops:
  3.4 22.3 %collective-permute-start.2 = (bf16[8,16,256]{2,1,0:T(8,128)(2,1)}, bf16[8,16,256]{2,1,0:T(8,128)(2,1)S(1)}, u32[]{:S(2)}, u32[]{:S(2)}) collective-permute-start(bf16[8,16,256]{2,1,0:T(8,128)(2,1)} %tile_ref), channel_id=1, source_target_pairs={{0,6},{1,7},{2,0},{3,1},{4,2},{5,3},{6,4},{7,5},{8,14},{9,15},{10,... | collective-permute-start | bytes 196616 | tf_op jit(solution)/shard_map/ppermute | solution.py:804
  8.4 17.2 %collective-permute-start.1 = (bf16[8,16,256]{2,1,0:T(8,128)(2,1)}, bf16[8,16,256]{2,1,0:T(8,128)(2,1)S(1)}, u32[]{:S(2)}, u32[]{:S(2)}) collective-permute-start(bf16[8,16,256]{2,1,0:T(8,128)(2,1)} %tile_ref), channel_id=1, source_target_pairs={{0,4},{1,5},{2,6},{3,7},{4,0},{5,1},{6,2},{7,3},{8,12},{9,13},{10,... | collective-permute-start | bytes 196616 | tf_op jit(solution)/shard_map/ppermute | solution.py:804
  8.4 17.2 %collective-permute-start = (bf16[8,16,256]{2,1,0:T(8,128)(2,1)}, bf16[8,16,256]{2,1,0:T(8,128)(2,1)S(1)}, u32[]{:S(2)}, u32[]{:S(2)}) collective-permute-start(bf16[8,16,256]{2,1,0:T(8,128)(2,1)} %tile_ref), channel_id=1, source_target_pairs={{0,2},{1,3},{2,4},{3,5},{4,6},{5,7},{6,0},{7,1},{8,10},{9,11},{10,... | collective-permute-start | bytes 196616 | tf_op jit(solution)/shard_map/ppermute | solution.py:804
  10.2 11.7 %collective-permute-start.4 = (bf16[2,16,256]{2,1,0:T(8,128)(2,1)S(1)}, bf16[2,16,256]{2,1,0:T(8,128)(2,1)S(1)}, u32[]{:S(2)}, u32[]{:S(2)}) collective-permute-start(bf16[2,16,256]{2,1,0:T(8,128)(2,1)S(1)} %get-tuple-element.71), channel_id=1, source_target_pairs={{8,0},{16,8},{24,16},{9,1},{17,9},{25,17},{10,2},{18,10},{26,18},{... | collective-permute-start | bytes 49160 | tf_op jit(solution)/shard_map/ppermute | solution.py:785
  11.5 10.4 %collective-permute-start.3 = (bf16[2,16,256]{2,1,0:T(8,128)(2,1)S(1)}, bf16[2,16,256]{2,1,0:T(8,128)(2,1)S(1)}, u32[]{:S(2)}, u32[]{:S(2)}) collective-permute-start(bf16[2,16,256]{2,1,0:T(8,128)(2,1)S(1)} %get-tuple-element.72), channel_id=1, source_target_pairs={{0,8},{8,16},{16,24},{1,9},{9,17},{17,25},{2,10},{10,18},{18,26},{... | collective-permute-start | bytes 49160 | tf_op jit(solution)/shard_map/ppermute | solution.py:784
  16.0 13.2 %all-to-all-start = ((f32[32,8,128]{2,1,0:T(8,128)}), f32[32,8,128]{2,1,0:T(8,128)S(1)}, u32[]{:S(2)}, u32[]{:S(2)}) async-start(f32[32,8,128]{2,1,0:T(8,128)} %route.1), calls=%async_computation | async-start | bytes 262144 | tf_op jit(solution)/shard_map/all_to_all | solution.py:845
  21.8 10.5 %copy-start.7 = (bf16[2,16,256]{2,1,0:T(8,128)(2,1)}, bf16[2,16,256]{2,1,0:T(8,128)(2,1)S(1)}, u32[]{:S(2)}) copy-start(bf16[2,16,256]{2,1,0:T(8,128)(2,1)S(1)} %collective-permute-done.4.south_ref) | copy-start | bytes 49156
  21.9 5.8 %copy-start.8 = (bf16[2,16,256]{2,1,0:T(8,128)(2,1)}, bf16[2,16,256]{2,1,0:T(8,128)(2,1)S(1)}, u32[]{:S(2)}) copy-start(bf16[2,16,256]{2,1,0:T(8,128)(2,1)S(1)} %collective-permute-done.3.north_ref) | copy-start | bytes 49156
  21.9 5.7 %collective-permute-start.5 = (bf16[12,2,256]{2,1,0:T(2,128)(2,1)S(1)}, bf16[12,2,256]{2,1,0:T(2,128)(2,1)S(1)}, u32[]{:S(2)}, u32[]{:S(2)}) collective-permute-start(bf16[12,2,256]{2,1,0:T(2,128)(2,1)S(1)} %pad_maximum_fusion.1), channel_id=1, source_target_pairs={{0,1},{1,2},{2,3},{3,4},{4,5},{5,6},{6,7},{7,0},{8,9},{9,10},{10,1... | collective-permute-start | bytes 36872 | tf_op jit(solution)/shard_map/ppermute | solution.py:788
  22.3 5.4 %collective-permute-start.6 = (bf16[12,2,256]{2,1,0:T(2,128)(2,1)S(1)}, bf16[12,2,256]{2,1,0:T(2,128)(2,1)S(1)}, u32[]{:S(2)}, u32[]{:S(2)}) collective-permute-start(bf16[12,2,256]{2,1,0:T(2,128)(2,1)S(1)} %pad_maximum_fusion.2), channel_id=1, source_target_pairs={{1,0},{2,1},{3,2},{4,3},{5,4},{6,5},{7,6},{0,7},{9,8},{10,9},{11,1... | collective-permute-start | bytes 36872 | tf_op jit(solution)/shard_map/ppermute | solution.py:789
  26.5 34.4 %copy-start = (bf16[9,256,256]{2,1,0:T(8,128)(2,1)S(1)}, bf16[9,256,256]{2,1,0:T(8,128)(2,1)}, u32[]{:S(2)}) copy-start(bf16[9,256,256]{2,1,0:T(8,128)(2,1)} %refs_10_.1) | copy-start | bytes 3538948
  26.5 34.4 %copy-start.1 = (bf16[9,256,256]{2,1,0:T(8,128)(2,1)S(1)}, bf16[9,256,256]{2,1,0:T(8,128)(2,1)}, u32[]{:S(2)}) copy-start(bf16[9,256,256]{2,1,0:T(8,128)(2,1)} %refs_11_.1) | copy-start | bytes 3538948
  27.6 0.6 copy-start.9
  28.2 0.6 copy-start.10
  29.2 3.2 %copy-start.6 = (f32[32,8,128]{2,1,0:T(8,128)}, f32[32,8,128]{2,1,0:T(8,128)S(1)}, u32[]{:S(2)}) copy-start(f32[32,8,128]{2,1,0:T(8,128)S(1)} %all-to-all-done.got_ref) | copy-start | bytes 393220
  29.2 14.6 %collective-permute-start.9 = (bf16[4,8,16,256]{3,2,1,0:T(8,128)(2,1)S(1)}, bf16[4,8,16,256]{3,2,1,0:T(8,128)(2,1)S(1)}, u32[]{:S(2)}, u32[]{:S(2)}) collective-permute-start(bf16[4,8,16,256]{3,2,1,0:T(8,128)(2,1)S(1)} %pad_maximum_fusion.refs_0_), channel_id=1, source_target_pairs={{0,24},{8,0},{16,8},{24,16},{1,25},{9,1},{17,9},{25,17},{2,26},{10... | collective-permute-start | bytes 786440 | tf_op jit(solution)/shard_map/ppermute | solution.py:813
  31.3 12.7 %collective-permute-start.8 = (bf16[4,8,16,256]{3,2,1,0:T(8,128)(2,1)S(1)}, bf16[4,8,16,256]{3,2,1,0:T(8,128)(2,1)S(1)}, u32[]{:S(2)}, u32[]{:S(2)}) collective-permute-start(bf16[4,8,16,256]{3,2,1,0:T(8,128)(2,1)S(1)} %pad_maximum_fusion.refs_0_), channel_id=1, source_target_pairs={{0,16},{8,24},{16,0},{24,8},{1,17},{9,25},{17,1},{25,9},{2,18},{10... | collective-permute-start | bytes 786440 | tf_op jit(solution)/shard_map/ppermute | solution.py:813
  31.8 12.2 %collective-permute-start.7 = (bf16[4,8,16,256]{3,2,1,0:T(8,128)(2,1)S(1)}, bf16[4,8,16,256]{3,2,1,0:T(8,128)(2,1)S(1)}, u32[]{:S(2)}, u32[]{:S(2)}) collective-permute-start(bf16[4,8,16,256]{3,2,1,0:T(8,128)(2,1)S(1)} %pad_maximum_fusion.refs_0_), channel_id=1, source_target_pairs={{0,8},{8,16},{16,24},{24,0},{1,9},{9,17},{17,25},{25,1},{2,10},{10... | collective-permute-start | bytes 786440 | tf_op jit(solution)/shard_map/ppermute | solution.py:813
  43.9 0.7 copy-start.2
  44.7 13.4 %all-to-all-start.1 = ((bf16[4,8,16,256]{3,2,1,0:T(8,128)(2,1)}), bf16[4,8,16,256]{3,2,1,0:T(8,128)(2,1)S(1)}, u32[]{:S(2)}, u32[]{:S(2)}) async-start(bf16[4,8,16,256]{3,2,1,0:T(8,128)(2,1)} %bitcast.13), calls=%async_computation.1 | async-start | bytes 524288 | tf_op jit(solution)/shard_map/all_to_all | solution.py:796
  48.7 10.7 %collective-permute-start.13 = (bf16[4,8,16,256]{3,2,1,0:T(8,128)(2,1)S(1)}, bf16[4,8,16,256]{3,2,1,0:T(8,128)(2,1)}, u32[]{:S(2)}, u32[]{:S(2)}) collective-permute-start(bf16[4,8,16,256]{3,2,1,0:T(8,128)(2,1)S(1)} %pad_maximum_fusion.refs_0_), channel_id=1, source_target_pairs={{0,1},{1,0},{2,3},{3,2},{4,5},{5,4},{6,7},{7,6},{8,9},{9,8},{10,11... | collective-permute-start | bytes 786440 | tf_op jit(solution)/shard_map/ppermute | solution.py:822
  48.7 12.1 %collective-permute-start.14 = (bf16[4,8,16,256]{3,2,1,0:T(8,128)(2,1)}, bf16[4,8,16,256]{3,2,1,0:T(8,128)(2,1)}, u32[]{:S(2)}, u32[]{:S(2)}) collective-permute-start(bf16[4,8,16,256]{3,2,1,0:T(8,128)(2,1)} %copy-done.2), channel_id=1, source_target_pairs={{0,1},{1,0},{2,3},{3,2},{4,5},{5,4},{6,7},{7,6},{8,9},{9,8},{10,11... | collective-permute-start | bytes 786440 | tf_op jit(solution)/shard_map/ppermute | solution.py:822
  49.2 11.7 %collective-permute-start.15 = (bf16[4,8,16,256]{3,2,1,0:T(8,128)(2,1)S(1)}, bf16[4,8,16,256]{3,2,1,0:T(8,128)(2,1)}, u32[]{:S(2)}, u32[]{:S(2)}) collective-permute-start(bf16[4,8,16,256]{3,2,1,0:T(8,128)(2,1)S(1)} %collective-permute-done.8.refs_4_), channel_id=1, source_target_pairs={{0,1},{1,0},{2,3},{3,2},{4,5},{5,4},{6,7},{7,6},{8,9},{9,8},{10,11... | collective-permute-start | bytes 786440 | tf_op jit(solution)/shard_map/ppermute | solution.py:822
  49.2 11.6 %collective-permute-start.16 = (bf16[4,8,16,256]{3,2,1,0:T(8,128)(2,1)S(1)}, bf16[4,8,16,256]{3,2,1,0:T(8,128)(2,1)}, u32[]{:S(2)}, u32[]{:S(2)}) collective-permute-start(bf16[4,8,16,256]{3,2,1,0:T(8,128)(2,1)S(1)} %collective-permute-done.9.refs_6_), channel_id=1, source_target_pairs={{0,1},{1,0},{2,3},{3,2},{4,5},{5,4},{6,7},{7,6},{8,9},{9,8},{10,11... | collective-permute-start | bytes 786440 | tf_op jit(solution)/shard_map/ppermute | solution.py:822
  58.0 10.5 %collective-permute-start.12 = (bf16[4,8,16,256]{3,2,1,0:T(8,128)(2,1)S(1)}, bf16[4,8,16,256]{3,2,1,0:T(8,128)(2,1)S(1)}, u32[]{:S(2)}, u32[]{:S(2)}) collective-permute-start(bf16[4,8,16,256]{3,2,1,0:T(8,128)(2,1)S(1)} %all-to-all-done.1.refs_0_), channel_id=1, source_target_pairs={{0,24},{8,0},{16,8},{24,16},{1,25},{9,1},{17,9},{25,17},{2,26},{10... | collective-permute-start | bytes 786440 | tf_op jit(solution)/shard_map/ppermute | solution.py:813
  59.4 11.6 %collective-permute-start.11 = (bf16[4,8,16,256]{3,2,1,0:T(8,128)(2,1)S(1)}, bf16[4,8,16,256]{3,2,1,0:T(8,128)(2,1)S(1)}, u32[]{:S(2)}, u32[]{:S(2)}) collective-permute-start(bf16[4,8,16,256]{3,2,1,0:T(8,128)(2,1)S(1)} %all-to-all-done.1.refs_0_), channel_id=1, source_target_pairs={{0,16},{8,24},{16,0},{24,8},{1,17},{9,25},{17,1},{25,9},{2,18},{10... | collective-permute-start | bytes 786440 | tf_op jit(solution)/shard_map/ppermute | solution.py:813
  60.8 10.2 %collective-permute-start.10 = (bf16[4,8,16,256]{3,2,1,0:T(8,128)(2,1)S(1)}, bf16[4,8,16,256]{3,2,1,0:T(8,128)(2,1)S(1)}, u32[]{:S(2)}, u32[]{:S(2)}) collective-permute-start(bf16[4,8,16,256]{3,2,1,0:T(8,128)(2,1)S(1)} %all-to-all-done.1.refs_0_), channel_id=1, source_target_pairs={{0,8},{8,16},{16,24},{24,0},{1,9},{9,17},{17,25},{25,1},{2,10},{10... | collective-permute-start | bytes 786440 | tf_op jit(solution)/shard_map/ppermute | solution.py:813
  60.9 1.0 %copy-start.3 = (bf16[4,8,16,256]{3,2,1,0:T(8,128)(2,1)S(1)}, bf16[4,8,16,256]{3,2,1,0:T(8,128)(2,1)}, u32[]{:S(2)}) copy-start(bf16[4,8,16,256]{3,2,1,0:T(8,128)(2,1)} %copy-done.2) | copy-start | bytes 786436
  71.0 1.5 %collective-permute-start.17 = (bf16[4,8,16,256]{3,2,1,0:T(8,128)(2,1)S(1)}, bf16[4,8,16,256]{3,2,1,0:T(8,128)(2,1)S(1)}, u32[]{:S(2)}, u32[]{:S(2)}) collective-permute-start(bf16[4,8,16,256]{3,2,1,0:T(8,128)(2,1)S(1)} %all-to-all-done.1.refs_0_), channel_id=1, source_target_pairs={{0,1},{1,0},{2,3},{3,2},{4,5},{5,4},{6,7},{7,6},{8,9},{9,8},{10,11... | collective-permute-start | bytes 786440 | tf_op jit(solution)/shard_map/ppermute | solution.py:822
  71.0 1.9 %collective-permute-start.18 = (bf16[4,8,16,256]{3,2,1,0:T(8,128)(2,1)S(1)}, bf16[4,8,16,256]{3,2,1,0:T(8,128)(2,1)S(1)}, u32[]{:S(2)}, u32[]{:S(2)}) collective-permute-start(bf16[4,8,16,256]{3,2,1,0:T(8,128)(2,1)S(1)} %collective-permute-done.10.refs_2_), channel_id=1, source_target_pairs={{0,1},{1,0},{2,3},{3,2},{4,5},{5,4},{6,7},{7,6},{8,9},{9,8},{10,11... | collective-permute-start | bytes 786440 | tf_op jit(solution)/shard_map/ppermute | solution.py:822
  71.5 1.8 %collective-permute-start.19 = (bf16[4,8,16,256]{3,2,1,0:T(8,128)(2,1)S(1)}, bf16[4,8,16,256]{3,2,1,0:T(8,128)(2,1)S(1)}, u32[]{:S(2)}, u32[]{:S(2)}) collective-permute-start(bf16[4,8,16,256]{3,2,1,0:T(8,128)(2,1)S(1)} %collective-permute-done.11.refs_4_), channel_id=1, source_target_pairs={{0,1},{1,0},{2,3},{3,2},{4,5},{5,4},{6,7},{7,6},{8,9},{9,8},{10,11... | collective-permute-start | bytes 786440 | tf_op jit(solution)/shard_map/ppermute | solution.py:822
  71.5 2.1 %collective-permute-start.20 = (bf16[4,8,16,256]{3,2,1,0:T(8,128)(2,1)S(1)}, bf16[4,8,16,256]{3,2,1,0:T(8,128)(2,1)S(1)}, u32[]{:S(2)}, u32[]{:S(2)}) collective-permute-start(bf16[4,8,16,256]{3,2,1,0:T(8,128)(2,1)S(1)} %collective-permute-done.12.refs_6_), channel_id=1, source_target_pairs={{0,1},{1,0},{2,3},{3,2},{4,5},{5,4},{6,7},{7,6},{8,9},{9,8},{10,11... | collective-permute-start | bytes 786440 | tf_op jit(solution)/shard_map/ppermute | solution.py:822
  79.2 8.1 %collective-permute-start.21 = (f32[9,256,256]{2,1,0:T(8,128)S(1)}, f32[9,256,256]{2,1,0:T(8,128)S(1)}, u32[]{:S(2)}, u32[]{:S(2)}) collective-permute-start(f32[9,256,256]{2,1,0:T(8,128)S(1)} %get-tuple-element.66), channel_id=1, source_target_pairs={{0,1},{1,0},{2,3},{3,2},{4,5},{5,4},{6,7},{7,6},{8,9},{9,8},{10,11... | collective-permute-start | bytes 7077896 | tf_op jit(solution)/shard_map/ppermute | solution.py:862
  79.4 8.4 %copy-start.4 = (f32[320,256]{1,0:T(8,128)S(1)}, f32[320,256]{1,0:T(8,128)}, u32[]{:S(2)}) copy-start(f32[320,256]{1,0:T(8,128)} %get-tuple-element.59.refs_8_) | copy-start | bytes 983044
  79.4 8.4 %copy-start.5 = (f32[128,256]{1,0:T(8,128)S(1)}, f32[128,256]{1,0:T(8,128)}, u32[]{:S(2)}) copy-start(f32[128,256]{1,0:T(8,128)} %get-tuple-element.60.refs_9_) | copy-start | bytes 393220
  87.3 5.2 %collective-permute-start.22 = (f32[9,256,256]{2,1,0:T(8,128)S(1)}, f32[9,256,256]{2,1,0:T(8,128)S(1)}, u32[]{:S(2)}, u32[]{:S(2)}) collective-permute-start(f32[9,256,256]{2,1,0:T(8,128)S(1)} %first_sums.1), channel_id=1, source_target_pairs={{0,1},{1,0},{2,3},{3,2},{4,5},{5,4},{6,7},{7,6},{8,9},{9,8},{10,11... | collective-permute-start | bytes 7077896 | tf_op jit(solution)/shard_map/ppermute | solution.py:865

commit v10 on v9

--- a/solution.py
+++ b/solution.py
@@ -175,12 +175,8 @@
 
 
 def forward_kernel(slots, bands, group, parts, tile_ref, north_ref, south_ref, west_ref, east_ref,
-                   w1_hbm, w2_hbm, got_ref, adj_ref, pull_ref, slope_ref, line_ref, shift_ref,
-                   hid_ref, obs_ref, sum_ref, w1_ref, w2_ref, sems):
-    w1_copy = pltpu.make_async_copy(w1_hbm, w1_ref, sems.at[0])
-    w2_copy = pltpu.make_async_copy(w2_hbm, w2_ref, sems.at[1])
-    w1_copy.start()
-    w2_copy.start()
+                   w1_ref, w2_ref, got_ref, adj_ref, pull_ref, slope_ref, line_ref, shift_ref,
+                   hid_ref, obs_ref, sum_ref):
     rows, cols, chans = tile_ref.shape
     span = hid_ref.shape[1]
     line_ref[0:2, 2 : 2 + cols, :] = north_ref[...].astype(F32)
@@ -191,7 +187,6 @@
     line_ref[:, cols + 4 :, :] = jnp.zeros(
         (rows + 4, line_ref.shape[1] - cols - 4, chans), F32
     )
-    w1_copy.wait()
     first = jnp.zeros(((rows + 2) * span, chans), F32)
     for b in range(3):
         shift_ref[...] = (
@@ -206,7 +201,6 @@
     hidden = hidden.astype(BF16).astype(F32).reshape(rows + 2, span, chans)
     hidden = jnp.where(inside_grid(rows, hidden.shape, bands), hidden, 0.0)
     hid_ref[...] = hidden
-    w2_copy.wait()
     total = line_ref[2 : 2 + rows, 2 : 2 + cols, :].reshape(rows * cols, chans)
     for b in range(3):
         shift_ref[0 : (rows + 2) * cols, :] = (
@@ -309,7 +303,7 @@
             jax.ShapeDtypeStruct((copies, rows * cols, chans), BF16),
             jax.ShapeDtypeStruct(((rows + 2) * SPAN, chans), F32),
         ],
-        in_specs=[vmem()] * 5 + [anywhere()] * 2 + [vmem()],
+        in_specs=[vmem()] * 8,
         out_specs=[vmem()] * 3,
         scratch_shapes=[
             pltpu.VMEM((rows + 4, SPAN + 8, chans), F32),
@@ -317,11 +311,8 @@
             pltpu.VMEM((rows + 2, SPAN, chans), F32),
             pltpu.VMEM((FIELDS, groups, 128), F32),
             pltpu.VMEM((chans, rows * cols), F32),
-            pltpu.VMEM(w1.shape, BF16),
-            pltpu.VMEM(w2.shape, BF16),
-            pltpu.SemaphoreType.DMA((2,)),
-        ],
-        compiler_params=params(58),
+        ],
+        compiler_params=params(46),
         cost_estimate=cost(4e9, 4e6),
         name="forward",
     )(*pieces, w1, w2, got)
@@ -778,11 +769,15 @@
     return (state_grad, grad_first, grad_second)
 
 
-def halo_pieces(x):
+def halo_rows(x):
+    return x[-2:], x[:2]
+
+
+def halo_pieces(x, sent):
     bands, tiles = lax.axis_size("lat"), lax.axis_size("lon")
     rows, cols, _ = x.shape
-    north = lax.ppermute(x[rows - 2 :], "lat", [(i, i + 1) for i in range(bands - 1)])
-    south = lax.ppermute(x[:2], "lat", [(i + 1, i) for i in range(bands - 1)])
+    north = lax.ppermute(sent[0], "lat", [(i, i + 1) for i in range(bands - 1)])
+    south = lax.ppermute(sent[1], "lat", [(i + 1, i) for i in range(bands - 1)])
     last = jnp.concatenate([p[:, cols - 2 :] for p in (north, x, south)], axis=0)
     first = jnp.concatenate([p[:, :2] for p in (north, x, south)], axis=0)
     west = lax.ppermute(last, "lon", [(i, (i + 1) % tiles) for i in range(tiles)])
@@ -836,12 +831,13 @@
             obs_frac, obs_value, obs_weight,
         )
     slots = max(2, 3 * obs_value.shape[0] // (2 * devices))
+    edges, obs_owner = lax.optimization_barrier((halo_rows(state), obs_owner))
     outgoing = route(
         devices, slots, chans, obs_owner, obs_cell, obs_level, obs_count, obs_frac, obs_value,
         obs_weight,
     )
     outgoing, sent = lax.optimization_barrier((outgoing, state))
-    pieces = halo_pieces(state)
+    pieces = halo_pieces(state, edges)
     got = lax.all_to_all(outgoing, ("lat", "lon"), split_axis=0, concat_axis=0, tiled=True)
     line = gather_line_backwards(sent)
     line, pieces, got = lax.optimization_barrier((line, pieces, got))
@@ -854,9 +850,10 @@
     state_pieces = with_other_core(state_lines)
     pull_lines = gather_bands(gather_line(pullback.reshape(half, rows, cols, chans)))
     firsts = whole(bands, state_pieces, weight_first, weight_second)
-    pull_lines, firsts = lax.optimization_barrier((pull_lines, firsts))
+    pull_pieces = with_other_core(pull_lines[:1])
+    far_lines, firsts = lax.optimization_barrier((pull_lines[1:], firsts))
     slope, hidden, turned, w2t = firsts
-    pull_pieces = with_other_core(pull_lines)
+    pull_pieces += with_other_core(far_lines)
     swap = [(i, i ^ 1) for i in range(2 * half)]
     g2, pull = second_sums(bands, pull_pieces, hidden)
     g2_other = lax.ppermute(g2, "lon", swap)

time: 94.9 us -> 95.7 us (level)
  local copies, waits for them, and re-layouts: 4.44 us -> 7.29 us
  Pallas kernels: 37.3 us -> 34.8 us
    unnamed x22 -> x18, local copies, waits for them, and re-layouts: 2.88 us -> 5.74 us
    pallas_call x1, Pallas kernels: 11.4 us -> 8.93 us  [forward(): pl.pallas_call(functools.partial(forward_kernel, slots, bands, 2, 4), out...]
    all_to_all x1, starting transfers between devices: 5.01 us -> 6.22 us  [per_device(): lax.all_to_all(outgoing, ('lat', 'lon'), split_axis=0, concat_axis=0, til...]
    all_to_all x1, waiting for transfers between devices: 0.37 us -> 1.56 us  [per_device(): lax.all_to_all(outgoing, ('lat', 'lon'), split_axis=0, concat_axis=0, til...]
    ppermute x2, starting transfers between devices: 5.83 us -> 4.68 us  [the longest x1 3.39 us: halo_pieces(): north = lax.ppermute(sent[0], 'lat', [(i, i + 1) for i in range(bands - 1)])]
  transfers between devices with their start and end apart: 25 -> 25, of which waited for: 9 -> 7; matrix products, arithmetic and copies ran while one was open for 4% -> 4% of each run, Pallas kernels for 31% -> 28%
where the time goes in v10:
time: 95.7 us; the launch traced here: 95 us
  Pallas kernels  34.8 us (36%)
  starting transfers between devices  33.1 us (35%)
  waiting for transfers between devices  14.6 us (15%)
  local copies, waits for them, and re-layouts  7.29 us (8%)
  other arithmetic  4.35 us (5%)
    pallas_call x1, Pallas kernels, forward(): pl.pallas_call(functools.partial(forward_kernel, slots, bands, 2, 4), out...  8.93 us
    pallas_call x1, Pallas kernels, first_sums(): pl.pallas_call(functools.partial(first_kernel, 4), out_shape=jax.ShapeDty...  7.92 us
    all_to_all x1, waiting for transfers between devices, gather_line(): lax.all_to_all(copies, 'lon', 0, 0, axis_index_groups=same, tiled=True)  7.46 us
    ppermute x6, starting transfers between devices, gather_bands(): lax.ppermute(line, 'lat', [(i, (i + step) % bands) for i in range(bands)])  6.82 us
    pallas_call x1, Pallas kernels, whole(): pl.pallas_call(functools.partial(whole_kernel, 3), out_shape=[jax.ShapeDt...  6.69 us
    all_to_all x1, starting transfers between devices, per_device(): lax.all_to_all(outgoing, ('lat', 'lon'), split_axis=0, concat_axis=0, til...  6.22 us
    ppermute x3, starting transfers between devices, gather_line_backwards(): lax.ppermute(x, 'lon', [(i, (i + step) % tiles) for i in range(tiles)])  6.06 us
    unnamed x18, local copies, waits for them, and re-layouts  5.74 us
  transfers between devices with their start and end apart: 25, of which 7 were waited for; matrix products, arithmetic and copies ran while one was open for 4% of the time, Pallas kernels for 28%

profile of v10, /device:TPU:0, one launch (start us, length us, event | category | flops | bytes accessed | tf_op | source)
XLA Modules:
  0.0 95.0 jit_solution(2708529621931045153)
XLA Ops:
  0.6 0.7 fusion.1
  1.4 2.7 %route.1 = f32[32,8,128]{2,1,0:T(8,128)} custom-call(s32[1,128]{1,0:T(1,128)} %bitcast.22, s32[1,128]{1,0:T(1,128)} %bitcast.23, s32[32,128]{1,0:T(8,128)} %bitcast.18, s32[32,128]{1,0:T(8,128)} %bitcast.19, f32[2,32,128]{2,1,0:T(8,128)} %bitcast.17, f32[32,128]{1,0:T(8,128)} %bitcast.20, f32[32,128]{1,0:T(8,128)} %bitcast.21), custom_call_target="tpu_custom_call" | custom-call | tf_op jit(solution)/shard_map/route/pallas_call | solution.py:99
  4.1 5.0 %collective-permute-start.2 = (bf16[8,16,256]{2,1,0:T(8,128)(2,1)}, bf16[8,16,256]{2,1,0:T(8,128)(2,1)S(1)}, u32[]{:S(2)}, u32[]{:S(2)}) collective-permute-start(bf16[8,16,256]{2,1,0:T(8,128)(2,1)} %tile_ref), channel_id=1, source_target_pairs={{0,6},{1,7},{2,0},{3,1},{4,2},{5,3},{6,4},{7,5},{8,14},{9,15},{10,... | collective-permute-start | bytes 196616 | tf_op jit(solution)/shard_map/ppermute | solution.py:799
  9.1 0.0 collective-permute-start.1
  9.1 1.0 %collective-permute-start = (bf16[8,16,256]{2,1,0:T(8,128)(2,1)}, bf16[8,16,256]{2,1,0:T(8,128)(2,1)S(1)}, u32[]{:S(2)}, u32[]{:S(2)}) collective-permute-start(bf16[8,16,256]{2,1,0:T(8,128)(2,1)} %tile_ref), channel_id=1, source_target_pairs={{0,2},{1,3},{2,4},{3,5},{4,6},{5,7},{6,0},{7,1},{8,10},{9,11},{10,... | collective-permute-start | bytes 196616 | tf_op jit(solution)/shard_map/ppermute | solution.py:799
  10.2 3.4 %collective-permute-start.3 = (bf16[2,16,256]{2,1,0:T(8,128)(2,1)S(1)}, bf16[2,16,256]{2,1,0:T(8,128)(2,1)S(1)}, u32[]{:S(2)}, u32[]{:S(2)}) collective-permute-start(bf16[2,16,256]{2,1,0:T(8,128)(2,1)S(1)} %get-tuple-element.40), channel_id=1, source_target_pairs={{0,8},{8,16},{16,24},{1,9},{9,17},{17,25},{2,10},{10,18},{18,26},{... | collective-permute-start | bytes 49160 | tf_op jit(solution)/shard_map/ppermute | solution.py:779
  13.5 1.3 %collective-permute-start.4 = (bf16[2,16,256]{2,1,0:T(8,128)(2,1)S(1)}, bf16[2,16,256]{2,1,0:T(8,128)(2,1)S(1)}, u32[]{:S(2)}, u32[]{:S(2)}) collective-permute-start(bf16[2,16,256]{2,1,0:T(8,128)(2,1)S(1)} %get-tuple-element.41), channel_id=1, source_target_pairs={{8,0},{16,8},{24,16},{9,1},{17,9},{25,17},{10,2},{18,10},{26,18},{... | collective-permute-start | bytes 49160 | tf_op jit(solution)/shard_map/ppermute | solution.py:780
  14.8 6.2 %all-to-all-start = ((f32[32,8,128]{2,1,0:T(8,128)}), f32[32,8,128]{2,1,0:T(8,128)S(1)}, u32[]{:S(2)}, u32[]{:S(2)}) async-start(f32[32,8,128]{2,1,0:T(8,128)} %route.1), calls=%async_computation | async-start | bytes 262144 | tf_op jit(solution)/shard_map/all_to_all | solution.py:841
  21.1 0.8 fusion
  21.9 0.0 collective-permute-done.4.south_ref
  22.0 0.3 collective-permute-start.5
  22.3 3.3 %collective-permute-start.6 = (bf16[12,2,256]{2,1,0:T(2,128)(2,1)S(1)}, bf16[12,2,256]{2,1,0:T(2,128)(2,1)S(1)}, u32[]{:S(2)}, u32[]{:S(2)}) collective-permute-start(bf16[12,2,256]{2,1,0:T(2,128)(2,1)S(1)} %pad_maximum_fusion.2), channel_id=1, source_target_pairs={{1,0},{2,1},{3,2},{4,3},{5,4},{6,5},{7,6},{0,7},{9,8},{10,9},{11,1... | collective-permute-start | bytes 36872 | tf_op jit(solution)/shard_map/ppermute | solution.py:784
  25.6 0.9 pad_maximum_fusion.refs_0_
  26.5 1.2 %collective-permute-done.5.west_ref = bf16[12,2,256]{2,1,0:T(2,128)(2,1)S(1)} collective-permute-done((bf16[12,2,256]{2,1,0:T(2,128)(2,1)S(1)}, bf16[12,2,256]{2,1,0:T(2,128)(2,1)S(1)}, u32[]{:S(2)}, u32[]{:S(2)}) %collective-permute-start.5) | collective-permute-done | bytes 12320 | tf_op jit(solution)/shard_map/ppermute | solution.py:783
  27.7 1.6 %all-to-all-done.got_ref = f32[32,8,128]{2,1,0:T(8,128)S(1)} async-done(((f32[32,8,128]{2,1,0:T(8,128)}), f32[32,8,128]{2,1,0:T(8,128)S(1)}, u32[]{:S(2)}, u32[]{:S(2)}) %all-to-all-start) | async-done | bytes 131104 | tf_op jit(solution)/shard_map/all_to_all | solution.py:841
  29.2 1.1 %collective-permute-start.9 = (bf16[4,8,16,256]{3,2,1,0:T(8,128)(2,1)S(1)}, bf16[4,8,16,256]{3,2,1,0:T(8,128)(2,1)S(1)}, u32[]{:S(2)}, u32[]{:S(2)}) collective-permute-start(bf16[4,8,16,256]{3,2,1,0:T(8,128)(2,1)S(1)} %pad_maximum_fusion.refs_0_), channel_id=1, source_target_pairs={{0,24},{8,0},{16,8},{24,16},{1,25},{9,1},{17,9},{25,17},{2,26},{10... | collective-permute-start | bytes 786440 | tf_op jit(solution)/shard_map/ppermute | solution.py:808
  30.3 1.3 %collective-permute-start.8 = (bf16[4,8,16,256]{3,2,1,0:T(8,128)(2,1)S(1)}, bf16[4,8,16,256]{3,2,1,0:T(8,128)(2,1)S(1)}, u32[]{:S(2)}, u32[]{:S(2)}) collective-permute-start(bf16[4,8,16,256]{3,2,1,0:T(8,128)(2,1)S(1)} %pad_maximum_fusion.refs_0_), channel_id=1, source_target_pairs={{0,16},{8,24},{16,0},{24,8},{1,17},{9,25},{17,1},{25,9},{2,18},{10... | collective-permute-start | bytes 786440 | tf_op jit(solution)/shard_map/ppermute | solution.py:808
  31.7 0.6 collective-permute-start.7
  32.2 0.8 copy-done
  33.1 1.3 %copy-done.1 = bf16[9,256,256]{2,1,0:T(8,128)(2,1)S(1)} copy-done((bf16[9,256,256]{2,1,0:T(8,128)(2,1)S(1)}, bf16[9,256,256]{2,1,0:T(8,128)(2,1)}, u32[]{:S(2)}) %copy-start.1) | copy-done | bytes 1179672
  34.4 1.3 %copy-done.3 = bf16[9,256,256]{2,1,0:T(8,128)(2,1)S(1)} copy-done((bf16[9,256,256]{2,1,0:T(8,128)(2,1)S(1)}, bf16[9,256,256]{2,1,0:T(8,128)(2,1)}, u32[]{:S(2)}) %copy-start.3) | copy-done | bytes 1179672
  35.6 8.9 %forward.1 = (f32[128,256]{1,0:T(8,128)S(1)}, bf16[4,128,256]{2,1,0:T(8,128)(2,1)}, f32[320,256]{1,0:T(8,128)S(1)}) custom-call(bf16[8,16,256]{2,1,0:T(8,128)(2,1)S(1)} %copy-done, bf16[2,16,256]{2,1,0:T(8,128)(2,1)S(1)} %collective-permute-done.3.north_ref, bf16[2,16,256]{2,1,0:T(8,128)(2,1)S(1)} %collective-permute-done.4.south_ref, ...), custom_call_target="tpu_custom_call" | custom-call | flops 4000000000 | bytes 4000000 | tf_op jit(solution)/shard_map/forward/pallas_call | solution.py:299
  44.6 0.7 copy-done.7
  45.3 0.7 copy-done.5
  46.0 3.4 %all-to-all-start.1 = ((bf16[4,8,16,256]{3,2,1,0:T(8,128)(2,1)}), bf16[4,8,16,256]{3,2,1,0:T(8,128)(2,1)S(1)}, u32[]{:S(2)}, u32[]{:S(2)}) async-start(bf16[4,8,16,256]{3,2,1,0:T(8,128)(2,1)} %bitcast.11), calls=%async_computation.1 | async-start | bytes 524288 | tf_op jit(solution)/shard_map/all_to_all | solution.py:791
  49.4 0.1 collective-permute-start.14
  49.5 0.5 collective-permute-start.15
  50.0 0.1 collective-permute-start.16
  50.1 0.4 collective-permute-start.17
  50.5 7.5 %all-to-all-done.1.refs_0_ = bf16[4,8,16,256]{3,2,1,0:T(8,128)(2,1)S(1)} async-done(((bf16[4,8,16,256]{3,2,1,0:T(8,128)(2,1)}), bf16[4,8,16,256]{3,2,1,0:T(8,128)(2,1)S(1)}, u32[]{:S(2)}, u32[]{:S(2)}) %all-to-all-start.1) | async-done | bytes 262176 | tf_op jit(solution)/shard_map/all_to_all | solution.py:791
  58.0 2.4 %collective-permute-start.13 = (bf16[4,8,16,256]{3,2,1,0:T(8,128)(2,1)S(1)}, bf16[4,8,16,256]{3,2,1,0:T(8,128)(2,1)S(1)}, u32[]{:S(2)}, u32[]{:S(2)}) collective-permute-start(bf16[4,8,16,256]{3,2,1,0:T(8,128)(2,1)S(1)} %all-to-all-done.1.refs_0_), channel_id=1, source_target_pairs={{0,24},{8,0},{16,8},{24,16},{1,25},{9,1},{17,9},{25,17},{2,26},{10... | collective-permute-start | bytes 786440 | tf_op jit(solution)/shard_map/ppermute | solution.py:808
  60.3 1.5 %collective-permute-start.12 = (bf16[4,8,16,256]{3,2,1,0:T(8,128)(2,1)S(1)}, bf16[4,8,16,256]{3,2,1,0:T(8,128)(2,1)S(1)}, u32[]{:S(2)}, u32[]{:S(2)}) collective-permute-start(bf16[4,8,16,256]{3,2,1,0:T(8,128)(2,1)S(1)} %all-to-all-done.1.refs_0_), channel_id=1, source_target_pairs={{0,16},{8,24},{16,0},{24,8},{1,17},{9,25},{17,1},{25,9},{2,18},{10... | collective-permute-start | bytes 786440 | tf_op jit(solution)/shard_map/ppermute | solution.py:808
  61.8 0.9 copy-done.6
  62.8 6.7 %whole.1 = (f32[2304,256]{1,0:T(8,128)S(1)}, bf16[256,2304]{1,0:T(8,128)(2,1)S(1)}, bf16[256,2304]{1,0:T(8,128)(2,1)S(1)}, bf16[9,256,256]{2,1,0:T(8,128)(2,1)S(1)}) custom-call(bf16[4,8,16,256]{3,2,1,0:T(8,128)(2,1)S(1)} %pad_maximum_fusion.refs_0_, bf16[4,8,16,256]{3,2,1,0:T(8,128)(2,1)} %collective-permute-done.14.refs_1_, ...), custom_call_target="tpu_custom_call" | custom-call | flops 6000000000 | bytes 10000000 | tf_op jit(solution)/shard_map/whole/pallas_call | solution.py:407
  69.5 0.1 collective-permute-start.10
  69.6 2.6 %collective-permute-done.12.refs_4_ = bf16[4,8,16,256]{3,2,1,0:T(8,128)(2,1)S(1)} collective-permute-done((bf16[4,8,16,256]{3,2,1,0:T(8,128)(2,1)S(1)}, bf16[4,8,16,256]{3,2,1,0:T(8,128)(2,1)S(1)}, u32[]{:S(2)}, u32[]{:S(2)}) %collective-permute-start.12) | collective-permute-done | bytes 262176 | tf_op jit(solution)/shard_map/ppermute | solution.py:808
  72.1 0.5 collective-permute-start.19
  72.6 0.0 collective-permute-start.20
  72.6 1.0 %collective-permute-done.18.refs_3_ = bf16[4,8,16,256]{3,2,1,0:T(8,128)(2,1)S(1)} collective-permute-done((bf16[4,8,16,256]{3,2,1,0:T(8,128)(2,1)S(1)}, bf16[4,8,16,256]{3,2,1,0:T(8,128)(2,1)S(1)}, u32[]{:S(2)}, u32[]{:S(2)}) %collective-permute-start.18) | collective-permute-done | bytes 262176 | tf_op jit(solution)/shard_map/ppermute | solution.py:817
  73.7 0.4 collective-permute-done.19.refs_5_
  74.0 0.4 collective-permute-done.20.refs_7_
  74.4 5.5 %second_sums.1 = (f32[9,256,256]{2,1,0:T(8,128)S(1)}, bf16[18,10,16,256]{3,2,1,0:T(8,128)(2,1)S(1)}) custom-call(bf16[4,8,16,256]{3,2,1,0:T(8,128)(2,1)S(1)} %all-to-all-done.1.refs_0_, bf16[4,8,16,256]{3,2,1,0:T(8,128)(2,1)S(1)} %collective-permute-done.10.refs_1_, bf16[4,8,16,256]{3,2,1,0:T(8,128)(2,1)S(1)} %collective-permute-done.11.refs_2_, ...), custom_call_target="tpu_custom_call" | custom-call | flops 5000000000 | bytes 8000000 | tf_op jit(solution)/shard_map/second_sums/pallas_call | solution.py:476
  79.9 0.2 collective-permute-start.21
  80.1 7.9 %first_sums.1 = f32[9,256,256]{2,1,0:T(8,128)S(1)} custom-call(f32[2304,256]{1,0:T(8,128)S(1)} %get-tuple-element.65.slope_hbm, bf16[256,2304]{1,0:T(8,128)(2,1)S(1)} %get-tuple-element.66.state_hbm, bf16[18,10,16,256]{3,2,1,0:T(8,128)(2,1)S(1)} %get-tuple-element.68.pull_ref, bf16[9,256,256]{2,1,0:T(8,128)(2,1)S(1)} %get-tuple-element.69.w2t_ref), custom_call_target="tpu_custom_call" | custom-call | flops 10000000000 | bytes 8000000 | tf_op jit(solution)/shard_map/first_sums/pallas_call | solution.py:538
  88.0 0.4 collective-permute-start.22
  88.5 3.0 %local_grad.1 = f32[128,256]{1,0:T(8,128)} custom-call(bf16[4,8,16,256]{3,2,1,0:T(8,128)(2,1)S(1)} %all-to-all-done.1.refs_0_, bf16[4,8,16,256]{3,2,1,0:T(8,128)(2,1)S(1)} %collective-permute-done.10.refs_1_, bf16[4,8,16,256]{3,2,1,0:T(8,128)(2,1)S(1)} %collective-permute-done.11.refs_2_, bf16[4,8,16,256]{3,2,1,0:T(8,128)(2,1)S(1)} %collective-permute-done.18.refs_3_, ...), custom_call_target="tpu_custom_call" | custom-call | flops 3000000000 | bytes 4000000 | tf_op jit(solution)/shard_map/local_grad/pallas_call | solution.py:592
  91.5 1.7 %add.7 = f32[9,256,256]{2,1,0:T(8,128)} add(f32[9,256,256]{2,1,0:T(8,128)S(1)} %get-tuple-element.70, f32[9,256,256]{2,1,0:T(8,128)S(1)} %collective-permute-done.21) | non-fusion elementwise | flops 589824 | bytes 7077888 | tf_op jit(solution)/shard_map/add | solution.py:864
  93.2 1.7 %add.6 = f32[9,256,256]{2,1,0:T(8,128)} add(f32[9,256,256]{2,1,0:T(8,128)S(1)} %first_sums.1, f32[9,256,256]{2,1,0:T(8,128)S(1)} %collective-permute-done.22) | non-fusion elementwise | flops 589824 | bytes 7077888 | tf_op jit(solution)/shard_map/add | solution.py:864
  (35 shorter events, 0.1 us)
Async XLA Ops:
  4.1 21.5 %collective-permute-start.2 = (bf16[8,16,256]{2,1,0:T(8,128)(2,1)}, bf16[8,16,256]{2,1,0:T(8,128)(2,1)S(1)}, u32[]{:S(2)}, u32[]{:S(2)}) collective-permute-start(bf16[8,16,256]{2,1,0:T(8,128)(2,1)} %tile_ref), channel_id=1, source_target_pairs={{0,6},{1,7},{2,0},{3,1},{4,2},{5,3},{6,4},{7,5},{8,14},{9,15},{10,... | collective-permute-start | bytes 196616 | tf_op jit(solution)/shard_map/ppermute | solution.py:799
  9.1 16.5 %collective-permute-start.1 = (bf16[8,16,256]{2,1,0:T(8,128)(2,1)}, bf16[8,16,256]{2,1,0:T(8,128)(2,1)S(1)}, u32[]{:S(2)}, u32[]{:S(2)}) collective-permute-start(bf16[8,16,256]{2,1,0:T(8,128)(2,1)} %tile_ref), channel_id=1, source_target_pairs={{0,4},{1,5},{2,6},{3,7},{4,0},{5,1},{6,2},{7,3},{8,12},{9,13},{10,... | collective-permute-start | bytes 196616 | tf_op jit(solution)/shard_map/ppermute | solution.py:799
  9.1 16.5 %collective-permute-start = (bf16[8,16,256]{2,1,0:T(8,128)(2,1)}, bf16[8,16,256]{2,1,0:T(8,128)(2,1)S(1)}, u32[]{:S(2)}, u32[]{:S(2)}) collective-permute-start(bf16[8,16,256]{2,1,0:T(8,128)(2,1)} %tile_ref), channel_id=1, source_target_pairs={{0,2},{1,3},{2,4},{3,5},{4,6},{5,7},{6,0},{7,1},{8,10},{9,11},{10,... | collective-permute-start | bytes 196616 | tf_op jit(solution)/shard_map/ppermute | solution.py:799
  10.2 11.7 %collective-permute-start.3 = (bf16[2,16,256]{2,1,0:T(8,128)(2,1)S(1)}, bf16[2,16,256]{2,1,0:T(8,128)(2,1)S(1)}, u32[]{:S(2)}, u32[]{:S(2)}) collective-permute-start(bf16[2,16,256]{2,1,0:T(8,128)(2,1)S(1)} %get-tuple-element.40), channel_id=1, source_target_pairs={{0,8},{8,16},{16,24},{1,9},{9,17},{17,25},{2,10},{10,18},{18,26},{... | collective-permute-start | bytes 49160 | tf_op jit(solution)/shard_map/ppermute | solution.py:779
  13.5 8.4 %collective-permute-start.4 = (bf16[2,16,256]{2,1,0:T(8,128)(2,1)S(1)}, bf16[2,16,256]{2,1,0:T(8,128)(2,1)S(1)}, u32[]{:S(2)}, u32[]{:S(2)}) collective-permute-start(bf16[2,16,256]{2,1,0:T(8,128)(2,1)S(1)} %get-tuple-element.41), channel_id=1, source_target_pairs={{8,0},{16,8},{24,16},{9,1},{17,9},{25,17},{10,2},{18,10},{26,18},{... | collective-permute-start | bytes 49160 | tf_op jit(solution)/shard_map/ppermute | solution.py:780
  14.8 14.4 %all-to-all-start = ((f32[32,8,128]{2,1,0:T(8,128)}), f32[32,8,128]{2,1,0:T(8,128)S(1)}, u32[]{:S(2)}, u32[]{:S(2)}) async-start(f32[32,8,128]{2,1,0:T(8,128)} %route.1), calls=%async_computation | async-start | bytes 262144 | tf_op jit(solution)/shard_map/all_to_all | solution.py:841
  22.0 5.7 %collective-permute-start.5 = (bf16[12,2,256]{2,1,0:T(2,128)(2,1)S(1)}, bf16[12,2,256]{2,1,0:T(2,128)(2,1)S(1)}, u32[]{:S(2)}, u32[]{:S(2)}) collective-permute-start(bf16[12,2,256]{2,1,0:T(2,128)(2,1)S(1)} %pad_maximum_fusion.1), channel_id=1, source_target_pairs={{0,1},{1,2},{2,3},{3,4},{4,5},{5,6},{6,7},{7,0},{8,9},{9,10},{10,1... | collective-permute-start | bytes 36872 | tf_op jit(solution)/shard_map/ppermute | solution.py:783
  22.3 5.4 %collective-permute-start.6 = (bf16[12,2,256]{2,1,0:T(2,128)(2,1)S(1)}, bf16[12,2,256]{2,1,0:T(2,128)(2,1)S(1)}, u32[]{:S(2)}, u32[]{:S(2)}) collective-permute-start(bf16[12,2,256]{2,1,0:T(2,128)(2,1)S(1)} %pad_maximum_fusion.2), channel_id=1, source_target_pairs={{1,0},{2,1},{3,2},{4,3},{5,4},{6,5},{7,6},{0,7},{9,8},{10,9},{11,1... | collective-permute-start | bytes 36872 | tf_op jit(solution)/shard_map/ppermute | solution.py:784
  29.2 16.0 %collective-permute-start.9 = (bf16[4,8,16,256]{3,2,1,0:T(8,128)(2,1)S(1)}, bf16[4,8,16,256]{3,2,1,0:T(8,128)(2,1)S(1)}, u32[]{:S(2)}, u32[]{:S(2)}) collective-permute-start(bf16[4,8,16,256]{3,2,1,0:T(8,128)(2,1)S(1)} %pad_maximum_fusion.refs_0_), channel_id=1, source_target_pairs={{0,24},{8,0},{16,8},{24,16},{1,25},{9,1},{17,9},{25,17},{2,26},{10... | collective-permute-start | bytes 786440 | tf_op jit(solution)/shard_map/ppermute | solution.py:808
  30.3 14.9 %collective-permute-start.8 = (bf16[4,8,16,256]{3,2,1,0:T(8,128)(2,1)S(1)}, bf16[4,8,16,256]{3,2,1,0:T(8,128)(2,1)S(1)}, u32[]{:S(2)}, u32[]{:S(2)}) collective-permute-start(bf16[4,8,16,256]{3,2,1,0:T(8,128)(2,1)S(1)} %pad_maximum_fusion.refs_0_), channel_id=1, source_target_pairs={{0,16},{8,24},{16,0},{24,8},{1,17},{9,25},{17,1},{25,9},{2,18},{10... | collective-permute-start | bytes 786440 | tf_op jit(solution)/shard_map/ppermute | solution.py:808
  31.7 13.6 %collective-permute-start.7 = (bf16[4,8,16,256]{3,2,1,0:T(8,128)(2,1)S(1)}, bf16[4,8,16,256]{3,2,1,0:T(8,128)(2,1)S(1)}, u32[]{:S(2)}, u32[]{:S(2)}) collective-permute-start(bf16[4,8,16,256]{3,2,1,0:T(8,128)(2,1)S(1)} %pad_maximum_fusion.refs_0_), channel_id=1, source_target_pairs={{0,8},{8,16},{16,24},{24,0},{1,9},{9,17},{17,25},{25,1},{2,10},{10... | collective-permute-start | bytes 786440 | tf_op jit(solution)/shard_map/ppermute | solution.py:808
  32.2 0.8 copy-start
  33.1 1.3 %copy-start.1 = (bf16[9,256,256]{2,1,0:T(8,128)(2,1)S(1)}, bf16[9,256,256]{2,1,0:T(8,128)(2,1)}, u32[]{:S(2)}) copy-start(bf16[9,256,256]{2,1,0:T(8,128)(2,1)} %refs_10_.1) | copy-start | bytes 3538948
  34.4 1.3 %copy-start.3 = (bf16[9,256,256]{2,1,0:T(8,128)(2,1)S(1)}, bf16[9,256,256]{2,1,0:T(8,128)(2,1)}, u32[]{:S(2)}) copy-start(bf16[9,256,256]{2,1,0:T(8,128)(2,1)} %refs_11_.1) | copy-start | bytes 3538948
  35.6 26.2 %copy-start.2 = (bf16[9,256,256]{2,1,0:T(8,128)(2,1)S(1)}, bf16[9,256,256]{2,1,0:T(8,128)(2,1)}, u32[]{:S(2)}) copy-start(bf16[9,256,256]{2,1,0:T(8,128)(2,1)} %refs_10_.1) | copy-start | bytes 3538948
  35.6 26.2 %copy-start.4 = (bf16[9,256,256]{2,1,0:T(8,128)(2,1)S(1)}, bf16[9,256,256]{2,1,0:T(8,128)(2,1)}, u32[]{:S(2)}) copy-start(bf16[9,256,256]{2,1,0:T(8,128)(2,1)} %refs_11_.1) | copy-start | bytes 3538948
  44.6 0.7 copy-start.7
  45.3 0.7 copy-start.5
  46.0 12.0 %all-to-all-start.1 = ((bf16[4,8,16,256]{3,2,1,0:T(8,128)(2,1)}), bf16[4,8,16,256]{3,2,1,0:T(8,128)(2,1)S(1)}, u32[]{:S(2)}, u32[]{:S(2)}) async-start(bf16[4,8,16,256]{3,2,1,0:T(8,128)(2,1)} %bitcast.11), calls=%async_computation.1 | async-start | bytes 524288 | tf_op jit(solution)/shard_map/all_to_all | solution.py:791
  49.4 10.9 %collective-permute-start.14 = (bf16[4,8,16,256]{3,2,1,0:T(8,128)(2,1)S(1)}, bf16[4,8,16,256]{3,2,1,0:T(8,128)(2,1)}, u32[]{:S(2)}, u32[]{:S(2)}) collective-permute-start(bf16[4,8,16,256]{3,2,1,0:T(8,128)(2,1)S(1)} %pad_maximum_fusion.refs_0_), channel_id=1, source_target_pairs={{0,1},{1,0},{2,3},{3,2},{4,5},{5,4},{6,7},{7,6},{8,9},{9,8},{10,11... | collective-permute-start | bytes 786440 | tf_op jit(solution)/shard_map/ppermute | solution.py:817
  49.5 12.3 %collective-permute-start.15 = (bf16[4,8,16,256]{3,2,1,0:T(8,128)(2,1)}, bf16[4,8,16,256]{3,2,1,0:T(8,128)(2,1)}, u32[]{:S(2)}, u32[]{:S(2)}) collective-permute-start(bf16[4,8,16,256]{3,2,1,0:T(8,128)(2,1)} %copy-done.5), channel_id=1, source_target_pairs={{0,1},{1,0},{2,3},{3,2},{4,5},{5,4},{6,7},{7,6},{8,9},{9,8},{10,11... | collective-permute-start | bytes 786440 | tf_op jit(solution)/shard_map/ppermute | solution.py:817
  50.0 11.8 %collective-permute-start.16 = (bf16[4,8,16,256]{3,2,1,0:T(8,128)(2,1)S(1)}, bf16[4,8,16,256]{3,2,1,0:T(8,128)(2,1)}, u32[]{:S(2)}, u32[]{:S(2)}) collective-permute-start(bf16[4,8,16,256]{3,2,1,0:T(8,128)(2,1)S(1)} %collective-permute-done.8.refs_4_), channel_id=1, source_target_pairs={{0,1},{1,0},{2,3},{3,2},{4,5},{5,4},{6,7},{7,6},{8,9},{9,8},{10,11... | collective-permute-start | bytes 786440 | tf_op jit(solution)/shard_map/ppermute | solution.py:817
  50.1 11.7 %collective-permute-start.17 = (bf16[4,8,16,256]{3,2,1,0:T(8,128)(2,1)S(1)}, bf16[4,8,16,256]{3,2,1,0:T(8,128)(2,1)}, u32[]{:S(2)}, u32[]{:S(2)}) collective-permute-start(bf16[4,8,16,256]{3,2,1,0:T(8,128)(2,1)S(1)} %collective-permute-done.9.refs_6_), channel_id=1, source_target_pairs={{0,1},{1,0},{2,3},{3,2},{4,5},{5,4},{6,7},{7,6},{8,9},{9,8},{10,11... | collective-permute-start | bytes 786440 | tf_op jit(solution)/shard_map/ppermute | solution.py:817
  58.0 11.6 %collective-permute-start.13 = (bf16[4,8,16,256]{3,2,1,0:T(8,128)(2,1)S(1)}, bf16[4,8,16,256]{3,2,1,0:T(8,128)(2,1)S(1)}, u32[]{:S(2)}, u32[]{:S(2)}) collective-permute-start(bf16[4,8,16,256]{3,2,1,0:T(8,128)(2,1)S(1)} %all-to-all-done.1.refs_0_), channel_id=1, source_target_pairs={{0,24},{8,0},{16,8},{24,16},{1,25},{9,1},{17,9},{25,17},{2,26},{10... | collective-permute-start | bytes 786440 | tf_op jit(solution)/shard_map/ppermute | solution.py:808
  60.3 11.8 %collective-permute-start.12 = (bf16[4,8,16,256]{3,2,1,0:T(8,128)(2,1)S(1)}, bf16[4,8,16,256]{3,2,1,0:T(8,128)(2,1)S(1)}, u32[]{:S(2)}, u32[]{:S(2)}) collective-permute-start(bf16[4,8,16,256]{3,2,1,0:T(8,128)(2,1)S(1)} %all-to-all-done.1.refs_0_), channel_id=1, source_target_pairs={{0,16},{8,24},{16,0},{24,8},{1,17},{9,25},{17,1},{25,9},{2,18},{10... | collective-permute-start | bytes 786440 | tf_op jit(solution)/shard_map/ppermute | solution.py:808
  61.8 10.3 %collective-permute-start.11 = (bf16[4,8,16,256]{3,2,1,0:T(8,128)(2,1)S(1)}, bf16[4,8,16,256]{3,2,1,0:T(8,128)(2,1)S(1)}, u32[]{:S(2)}, u32[]{:S(2)}) collective-permute-start(bf16[4,8,16,256]{3,2,1,0:T(8,128)(2,1)S(1)} %all-to-all-done.1.refs_0_), channel_id=1, source_target_pairs={{0,8},{8,16},{16,24},{24,0},{1,9},{9,17},{17,25},{25,1},{2,10},{10... | collective-permute-start | bytes 786440 | tf_op jit(solution)/shard_map/ppermute | solution.py:808
  61.8 1.0 %copy-start.6 = (bf16[4,8,16,256]{3,2,1,0:T(8,128)(2,1)S(1)}, bf16[4,8,16,256]{3,2,1,0:T(8,128)(2,1)}, u32[]{:S(2)}) copy-start(bf16[4,8,16,256]{3,2,1,0:T(8,128)(2,1)} %copy-done.5) | copy-start | bytes 786436
  69.5 3.2 %collective-permute-start.10 = (bf16[4,8,16,256]{3,2,1,0:T(8,128)(2,1)S(1)}, bf16[4,8,16,256]{3,2,1,0:T(8,128)(2,1)S(1)}, u32[]{:S(2)}, u32[]{:S(2)}) collective-permute-start(bf16[4,8,16,256]{3,2,1,0:T(8,128)(2,1)S(1)} %all-to-all-done.1.refs_0_), channel_id=1, source_target_pairs={{0,1},{1,0},{2,3},{3,2},{4,5},{5,4},{6,7},{7,6},{8,9},{9,8},{10,11... | collective-permute-start | bytes 786440 | tf_op jit(solution)/shard_map/ppermute | solution.py:817
  72.1 1.5 %collective-permute-start.18 = (bf16[4,8,16,256]{3,2,1,0:T(8,128)(2,1)S(1)}, bf16[4,8,16,256]{3,2,1,0:T(8,128)(2,1)S(1)}, u32[]{:S(2)}, u32[]{:S(2)}) collective-permute-start(bf16[4,8,16,256]{3,2,1,0:T(8,128)(2,1)S(1)} %collective-permute-done.11.refs_2_), channel_id=1, source_target_pairs={{0,1},{1,0},{2,3},{3,2},{4,5},{5,4},{6,7},{7,6},{8,9},{9,8},{10,11... | collective-permute-start | bytes 786440 | tf_op jit(solution)/shard_map/ppermute | solution.py:817
  72.1 1.9 %collective-permute-start.19 = (bf16[4,8,16,256]{3,2,1,0:T(8,128)(2,1)S(1)}, bf16[4,8,16,256]{3,2,1,0:T(8,128)(2,1)S(1)}, u32[]{:S(2)}, u32[]{:S(2)}) collective-permute-start(bf16[4,8,16,256]{3,2,1,0:T(8,128)(2,1)S(1)} %collective-permute-done.12.refs_4_), channel_id=1, source_target_pairs={{0,1},{1,0},{2,3},{3,2},{4,5},{5,4},{6,7},{7,6},{8,9},{9,8},{10,11... | collective-permute-start | bytes 786440 | tf_op jit(solution)/shard_map/ppermute | solution.py:817
  72.6 1.8 %collective-permute-start.20 = (bf16[4,8,16,256]{3,2,1,0:T(8,128)(2,1)S(1)}, bf16[4,8,16,256]{3,2,1,0:T(8,128)(2,1)S(1)}, u32[]{:S(2)}, u32[]{:S(2)}) collective-permute-start(bf16[4,8,16,256]{3,2,1,0:T(8,128)(2,1)S(1)} %collective-permute-done.13.refs_6_), channel_id=1, source_target_pairs={{0,1},{1,0},{2,3},{3,2},{4,5},{5,4},{6,7},{7,6},{8,9},{9,8},{10,11... | collective-permute-start | bytes 786440 | tf_op jit(solution)/shard_map/ppermute | solution.py:817
  79.9 8.1 %collective-permute-start.21 = (f32[9,256,256]{2,1,0:T(8,128)S(1)}, f32[9,256,256]{2,1,0:T(8,128)S(1)}, u32[]{:S(2)}, u32[]{:S(2)}) collective-permute-start(f32[9,256,256]{2,1,0:T(8,128)S(1)} %get-tuple-element.70), channel_id=1, source_target_pairs={{0,1},{1,0},{2,3},{3,2},{4,5},{5,4},{6,7},{7,6},{8,9},{9,8},{10,11... | collective-permute-start | bytes 7077896 | tf_op jit(solution)/shard_map/ppermute | solution.py:859
  80.1 8.4 %copy-start.8 = (f32[320,256]{1,0:T(8,128)S(1)}, f32[320,256]{1,0:T(8,128)}, u32[]{:S(2)}) copy-start(f32[320,256]{1,0:T(8,128)} %copy-done.7) | copy-start | bytes 983044
  88.0 5.2 %collective-permute-start.22 = (f32[9,256,256]{2,1,0:T(8,128)S(1)}, f32[9,256,256]{2,1,0:T(8,128)S(1)}, u32[]{:S(2)}, u32[]{:S(2)}) collective-permute-start(f32[9,256,256]{2,1,0:T(8,128)S(1)} %first_sums.1), channel_id=1, source_target_pairs={{0,1},{1,0},{2,3},{3,2},{4,5},{5,4},{6,7},{7,6},{8,9},{9,8},{10,11... | collective-permute-start | bytes 7077896 | tf_op jit(solution)/shard_map/ppermute | solution.py:862

commit v11 on v9

--- a/solution.py
+++ b/solution.py
@@ -191,37 +191,6 @@
     line_ref[:, cols + 4 :, :] = jnp.zeros(
         (rows + 4, line_ref.shape[1] - cols - 4, chans), F32
     )
-    w1_copy.wait()
-    first = jnp.zeros(((rows + 2) * span, chans), F32)
-    for b in range(3):
-        shift_ref[...] = (
-            line_ref[:, b : b + span, :].astype(BF16).reshape((rows + 4) * span, chans)
-        )
-        for a in range(3):
-            first = first + dot(
-                shift_ref[a * span : a * span + (rows + 2) * span, :], w1_ref[3 * a + b]
-            )
-    sig, hidden = silu_parts(first)
-    slope_ref[...] = sig * (1.0 + first * (1.0 - sig))
-    hidden = hidden.astype(BF16).astype(F32).reshape(rows + 2, span, chans)
-    hidden = jnp.where(inside_grid(rows, hidden.shape, bands), hidden, 0.0)
-    hid_ref[...] = hidden
-    w2_copy.wait()
-    total = line_ref[2 : 2 + rows, 2 : 2 + cols, :].reshape(rows * cols, chans)
-    for b in range(3):
-        shift_ref[0 : (rows + 2) * cols, :] = (
-            hid_ref[:, b : b + cols, :].astype(BF16).reshape((rows + 2) * cols, chans)
-        )
-        for a in range(3):
-            total = total + dot(
-                shift_ref[a * cols : a * cols + rows * cols, :], w2_ref[3 * a + b]
-            )
-    cells = rows * cols
-    turned = total.T
-    grid_high = turned.astype(BF16)
-    grid_low = (turned - grid_high.astype(F32)).astype(BF16)
-    grid_both = jnp.concatenate([grid_high, grid_low], axis=1)
-
     devices = got_ref.shape[0]
     full, rest, _ = slot_layout(slots)
     half = devices // 2
@@ -246,6 +215,37 @@
     obs_ref[4] = (code & (chans - 1)).astype(F32)
     obs_ref[0] = obs_ref[0] + lax.shift_right_logical(cell, 4).astype(F32)
     obs_ref[1] = obs_ref[1] + (cell & (cols - 1)).astype(F32)
+
+    w1_copy.wait()
+    first = jnp.zeros(((rows + 2) * span, chans), F32)
+    for b in range(3):
+        shift_ref[...] = (
+            line_ref[:, b : b + span, :].astype(BF16).reshape((rows + 4) * span, chans)
+        )
+        for a in range(3):
+            first = first + dot(
+                shift_ref[a * span : a * span + (rows + 2) * span, :], w1_ref[3 * a + b]
+            )
+    sig, hidden = silu_parts(first)
+    slope_ref[...] = sig * (1.0 + first * (1.0 - sig))
+    hidden = hidden.astype(BF16).astype(F32).reshape(rows + 2, span, chans)
+    hidden = jnp.where(inside_grid(rows, hidden.shape, bands), hidden, 0.0)
+    hid_ref[...] = hidden
+    w2_copy.wait()
+    total = line_ref[2 : 2 + rows, 2 : 2 + cols, :].reshape(rows * cols, chans)
+    for b in range(3):
+        shift_ref[0 : (rows + 2) * cols, :] = (
+            hid_ref[:, b : b + cols, :].astype(BF16).reshape((rows + 2) * cols, chans)
+        )
+        for a in range(3):
+            total = total + dot(
+                shift_ref[a * cols : a * cols + rows * cols, :], w2_ref[3 * a + b]
+            )
+    cells = rows * cols
+    turned = total.T
+    grid_high = turned.astype(BF16)
+    grid_low = (turned - grid_high.astype(F32)).astype(BF16)
+    grid_both = jnp.concatenate([grid_high, grid_low], axis=1)
 
     sum_ref[...] = jnp.zeros(sum_ref.shape, F32)
     count = obs_ref.shape[1] // (group * parts)
@@ -303,7 +303,7 @@
     full, rest, _ = slot_layout(slots)
     groups = full * devices + (devices // 2 if rest else 0)
     return pl.pallas_call(
-        functools.partial(forward_kernel, slots, bands, 2, 4),
+        functools.partial(forward_kernel, slots, bands, 2, 8),
         out_shape=[
             jax.ShapeDtypeStruct((rows * cols, chans), F32),
             jax.ShapeDtypeStruct((copies, rows * cols, chans), BF16),

time: 94.9 us -> 94 us (level)
  Pallas kernels: 37.3 us -> 35.5 us
  waiting for transfers between devices: 14.1 us -> 15.3 us
    pallas_call x1, Pallas kernels: 11.4 us -> 9.67 us  [forward(): pl.pallas_call(functools.partial(forward_kernel, slots, bands, 2, 8), out...]
    ppermute x6, waiting for transfers between devices: 2.63 us -> 3.77 us  [gather_bands(): lax.ppermute(line, 'lat', [(i, (i + step) % bands) for i in range(bands)])]
  transfers between devices with their start and end apart: 25 -> 25, of which waited for: 9 -> 9; matrix products, arithmetic and copies ran while one was open for 4% -> 4% of each run, Pallas kernels for 31% -> 29%
where the time goes in v11:
time: 94 us; the launch traced here: 93.4 us
  Pallas kernels  35.5 us (38%)
  starting transfers between devices  32.9 us (35%)
  waiting for transfers between devices  15.3 us (16%)
  local copies, waits for them, and re-layouts  4.44 us (5%)
  other arithmetic  4.35 us (5%)
    pallas_call x1, Pallas kernels, forward(): pl.pallas_call(functools.partial(forward_kernel, slots, bands, 2, 8), out...  9.67 us
    all_to_all x1, waiting for transfers between devices, gather_line(): lax.all_to_all(copies, 'lon', 0, 0, axis_index_groups=same, tiled=True)  8.35 us
    pallas_call x1, Pallas kernels, first_sums(): pl.pallas_call(functools.partial(first_kernel, 4), out_shape=jax.ShapeDty...  7.92 us
    pallas_call x1, Pallas kernels, whole(): pl.pallas_call(functools.partial(whole_kernel, 3), out_shape=[jax.ShapeDt...  6.69 us
    ppermute x3, starting transfers between devices, gather_line_backwards(): lax.ppermute(x, 'lon', [(i, (i + step) % tiles) for i in range(tiles)])  6.06 us
    ppermute x6, starting transfers between devices, gather_bands(): lax.ppermute(line, 'lat', [(i, (i + step) % bands) for i in range(bands)])  5.71 us
    pallas_call x1, Pallas kernels, second_sums(): pl.pallas_call(functools.partial(second_kernel, bands), out_shape=[jax.Sh...  5.49 us
    all_to_all x1, starting transfers between devices, per_device(): lax.all_to_all(outgoing, ('lat', 'lon'), split_axis=0, concat_axis=0, til...  5.01 us
  transfers between devices with their start and end apart: 25, of which 9 were waited for; matrix products, arithmetic and copies ran while one was open for 4% of the time, Pallas kernels for 29%

profile of v11, /device:TPU:0, one launch (start us, length us, event | category | flops | bytes accessed | tf_op | source)
XLA Modules:
  0.0 93.4 jit_solution(9860093756463346959)
XLA Ops:
  0.6 2.7 %route.1 = f32[32,8,128]{2,1,0:T(8,128)} custom-call(s32[1,128]{1,0:T(1,128)} %bitcast.23, s32[1,128]{1,0:T(1,128)} %bitcast.24, s32[32,128]{1,0:T(8,128)} %bitcast.19, s32[32,128]{1,0:T(8,128)} %bitcast.20, f32[2,32,128]{2,1,0:T(8,128)} %bitcast.18, f32[32,128]{1,0:T(8,128)} %bitcast.21, f32[32,128]{1,0:T(8,128)} %bitcast.22), custom_call_target="tpu_custom_call" | custom-call | tf_op jit(solution)/shard_map/route/pallas_call | solution.py:99
  3.4 5.0 %collective-permute-start.2 = (bf16[8,16,256]{2,1,0:T(8,128)(2,1)}, bf16[8,16,256]{2,1,0:T(8,128)(2,1)S(1)}, u32[]{:S(2)}, u32[]{:S(2)}) collective-permute-start(bf16[8,16,256]{2,1,0:T(8,128)(2,1)} %tile_ref), channel_id=1, source_target_pairs={{0,6},{1,7},{2,0},{3,1},{4,2},{5,3},{6,4},{7,5},{8,14},{9,15},{10,... | collective-permute-start | bytes 196616 | tf_op jit(solution)/shard_map/ppermute | solution.py:804
  8.4 1.0 %collective-permute-start = (bf16[8,16,256]{2,1,0:T(8,128)(2,1)}, bf16[8,16,256]{2,1,0:T(8,128)(2,1)S(1)}, u32[]{:S(2)}, u32[]{:S(2)}) collective-permute-start(bf16[8,16,256]{2,1,0:T(8,128)(2,1)} %tile_ref), channel_id=1, source_target_pairs={{0,2},{1,3},{2,4},{3,5},{4,6},{5,7},{6,0},{7,1},{8,10},{9,11},{10,... | collective-permute-start | bytes 196616 | tf_op jit(solution)/shard_map/ppermute | solution.py:804
  9.4 0.8 fusion.1
  10.2 1.3 %collective-permute-start.4 = (bf16[2,16,256]{2,1,0:T(8,128)(2,1)S(1)}, bf16[2,16,256]{2,1,0:T(8,128)(2,1)S(1)}, u32[]{:S(2)}, u32[]{:S(2)}) collective-permute-start(bf16[2,16,256]{2,1,0:T(8,128)(2,1)S(1)} %get-tuple-element.71), channel_id=1, source_target_pairs={{8,0},{16,8},{24,16},{9,1},{17,9},{25,17},{10,2},{18,10},{26,18},{... | collective-permute-start | bytes 49160 | tf_op jit(solution)/shard_map/ppermute | solution.py:785
  11.5 4.5 %collective-permute-start.3 = (bf16[2,16,256]{2,1,0:T(8,128)(2,1)S(1)}, bf16[2,16,256]{2,1,0:T(8,128)(2,1)S(1)}, u32[]{:S(2)}, u32[]{:S(2)}) collective-permute-start(bf16[2,16,256]{2,1,0:T(8,128)(2,1)S(1)} %get-tuple-element.72), channel_id=1, source_target_pairs={{0,8},{8,16},{16,24},{1,9},{9,17},{17,25},{2,10},{10,18},{18,26},{... | collective-permute-start | bytes 49160 | tf_op jit(solution)/shard_map/ppermute | solution.py:784
  16.0 5.0 %all-to-all-start = ((f32[32,8,128]{2,1,0:T(8,128)}), f32[32,8,128]{2,1,0:T(8,128)S(1)}, u32[]{:S(2)}, u32[]{:S(2)}) async-start(f32[32,8,128]{2,1,0:T(8,128)} %route.1), calls=%async_computation | async-start | bytes 262144 | tf_op jit(solution)/shard_map/all_to_all | solution.py:845
  21.0 0.8 fusion
  21.9 0.3 collective-permute-start.5
  22.3 3.3 %collective-permute-start.6 = (bf16[12,2,256]{2,1,0:T(2,128)(2,1)S(1)}, bf16[12,2,256]{2,1,0:T(2,128)(2,1)S(1)}, u32[]{:S(2)}, u32[]{:S(2)}) collective-permute-start(bf16[12,2,256]{2,1,0:T(2,128)(2,1)S(1)} %pad_maximum_fusion.2), channel_id=1, source_target_pairs={{1,0},{2,1},{3,2},{4,3},{5,4},{6,5},{7,6},{0,7},{9,8},{10,9},{11,1... | collective-permute-start | bytes 36872 | tf_op jit(solution)/shard_map/ppermute | solution.py:789
  25.6 0.9 pad_maximum_fusion.refs_0_
  26.5 0.0 copy-start
  26.5 0.0 copy-start.1
  26.5 1.1 %collective-permute-done.5.west_ref = bf16[12,2,256]{2,1,0:T(2,128)(2,1)S(1)} collective-permute-done((bf16[12,2,256]{2,1,0:T(2,128)(2,1)S(1)}, bf16[12,2,256]{2,1,0:T(2,128)(2,1)S(1)}, u32[]{:S(2)}, u32[]{:S(2)}) %collective-permute-start.5) | collective-permute-done | bytes 12320 | tf_op jit(solution)/shard_map/ppermute | solution.py:788
  27.7 0.6 copy-done.9
  28.2 0.6 copy-done.10
  28.8 0.4 all-to-all-done.got_ref
  29.2 2.0 %collective-permute-start.9 = (bf16[4,8,16,256]{3,2,1,0:T(8,128)(2,1)S(1)}, bf16[4,8,16,256]{3,2,1,0:T(8,128)(2,1)S(1)}, u32[]{:S(2)}, u32[]{:S(2)}) collective-permute-start(bf16[4,8,16,256]{3,2,1,0:T(8,128)(2,1)S(1)} %pad_maximum_fusion.refs_0_), channel_id=1, source_target_pairs={{0,24},{8,0},{16,8},{24,16},{1,25},{9,1},{17,9},{25,17},{2,26},{10... | collective-permute-start | bytes 786440 | tf_op jit(solution)/shard_map/ppermute | solution.py:813
  31.3 0.5 collective-permute-start.8
  31.8 0.6 collective-permute-start.7
  32.4 9.7 %forward.1 = (f32[128,256]{1,0:T(8,128)}, bf16[4,128,256]{2,1,0:T(8,128)(2,1)}, f32[320,256]{1,0:T(8,128)}) custom-call(bf16[8,16,256]{2,1,0:T(8,128)(2,1)} %tile_ref, bf16[2,16,256]{2,1,0:T(8,128)(2,1)} %copy-done.8, bf16[2,16,256]{2,1,0:T(8,128)(2,1)} %copy-done.7, bf16[12,2,256]{2,1,0:T(2,128)(2,1)} %copy-done.9, bf16[12,2,256]{2,1,0:T(2,128)(2,1)} %copy-done.10, ...), custom_call_target="tpu_custom_call" | custom-call | flops 4000000000 | bytes 4000000 | tf_op jit(solution)/shard_map/forward/pallas_call | solution.py:305
  42.1 1.9 %collective-permute-done.8.refs_4_ = bf16[4,8,16,256]{3,2,1,0:T(8,128)(2,1)S(1)} collective-permute-done((bf16[4,8,16,256]{3,2,1,0:T(8,128)(2,1)S(1)}, bf16[4,8,16,256]{3,2,1,0:T(8,128)(2,1)S(1)}, u32[]{:S(2)}, u32[]{:S(2)}) %collective-permute-start.8) | collective-permute-done | bytes 262176 | tf_op jit(solution)/shard_map/ppermute | solution.py:813
  43.9 0.7 copy-done.2
  44.7 4.0 %all-to-all-start.1 = ((bf16[4,8,16,256]{3,2,1,0:T(8,128)(2,1)}), bf16[4,8,16,256]{3,2,1,0:T(8,128)(2,1)S(1)}, u32[]{:S(2)}, u32[]{:S(2)}) async-start(bf16[4,8,16,256]{3,2,1,0:T(8,128)(2,1)} %bitcast.13), calls=%async_computation.1 | async-start | bytes 524288 | tf_op jit(solution)/shard_map/all_to_all | solution.py:796
  48.7 0.1 collective-permute-start.13
  48.7 0.5 collective-permute-start.14
  49.2 0.1 collective-permute-start.15
  49.2 0.5 collective-permute-start.16
  49.7 8.3 %all-to-all-done.1.refs_0_ = bf16[4,8,16,256]{3,2,1,0:T(8,128)(2,1)S(1)} async-done(((bf16[4,8,16,256]{3,2,1,0:T(8,128)(2,1)}), bf16[4,8,16,256]{3,2,1,0:T(8,128)(2,1)S(1)}, u32[]{:S(2)}, u32[]{:S(2)}) %all-to-all-start.1) | async-done | bytes 262176 | tf_op jit(solution)/shard_map/all_to_all | solution.py:796
  58.0 0.6 collective-permute-start.12
  58.6 0.9 collective-permute-start.11
  59.5 1.1 %collective-permute-start.10 = (bf16[4,8,16,256]{3,2,1,0:T(8,128)(2,1)S(1)}, bf16[4,8,16,256]{3,2,1,0:T(8,128)(2,1)S(1)}, u32[]{:S(2)}, u32[]{:S(2)}) collective-permute-start(bf16[4,8,16,256]{3,2,1,0:T(8,128)(2,1)S(1)} %all-to-all-done.1.refs_0_), channel_id=1, source_target_pairs={{0,8},{8,16},{16,24},{24,0},{1,9},{9,17},{17,25},{25,1},{2,10},{10... | collective-permute-start | bytes 786440 | tf_op jit(solution)/shard_map/ppermute | solution.py:813
  60.6 0.9 %copy-done.3 = bf16[4,8,16,256]{3,2,1,0:T(8,128)(2,1)S(1)} copy-done((bf16[4,8,16,256]{3,2,1,0:T(8,128)(2,1)S(1)}, bf16[4,8,16,256]{3,2,1,0:T(8,128)(2,1)}, u32[]{:S(2)}) %copy-start.3) | copy-done | bytes 262168
  61.6 6.7 %whole.1 = (f32[2304,256]{1,0:T(8,128)S(1)}, bf16[256,2304]{1,0:T(8,128)(2,1)S(1)}, bf16[256,2304]{1,0:T(8,128)(2,1)S(1)}, bf16[9,256,256]{2,1,0:T(8,128)(2,1)S(1)}) custom-call(bf16[4,8,16,256]{3,2,1,0:T(8,128)(2,1)S(1)} %pad_maximum_fusion.refs_0_, bf16[4,8,16,256]{3,2,1,0:T(8,128)(2,1)} %collective-permute-done.13.refs_1_, ...), custom_call_target="tpu_custom_call" | custom-call | flops 6000000000 | bytes 10000000 | tf_op jit(solution)/shard_map/whole/pallas_call | solution.py:416
  68.3 1.9 %collective-permute-done.11.refs_4_ = bf16[4,8,16,256]{3,2,1,0:T(8,128)(2,1)S(1)} collective-permute-done((bf16[4,8,16,256]{3,2,1,0:T(8,128)(2,1)S(1)}, bf16[4,8,16,256]{3,2,1,0:T(8,128)(2,1)S(1)}, u32[]{:S(2)}, u32[]{:S(2)}) %collective-permute-start.11) | collective-permute-done | bytes 262176 | tf_op jit(solution)/shard_map/ppermute | solution.py:813
  70.2 0.5 collective-permute-start.18
  70.7 0.5 collective-permute-start.20
  71.2 0.5 collective-permute-done.17.refs_1_
  71.7 0.4 collective-permute-done.18.refs_3_
  72.1 0.4 collective-permute-done.19.refs_5_
  72.5 0.4 collective-permute-done.20.refs_7_
  72.8 5.5 %second_sums.1 = (f32[9,256,256]{2,1,0:T(8,128)S(1)}, bf16[18,10,16,256]{3,2,1,0:T(8,128)(2,1)S(1)}) custom-call(bf16[4,8,16,256]{3,2,1,0:T(8,128)(2,1)S(1)} %all-to-all-done.1.refs_0_, bf16[4,8,16,256]{3,2,1,0:T(8,128)(2,1)S(1)} %collective-permute-done.17.refs_1_, bf16[4,8,16,256]{3,2,1,0:T(8,128)(2,1)S(1)} %collective-permute-done.10.refs_2_, ...), custom_call_target="tpu_custom_call" | custom-call | flops 5000000000 | bytes 8000000 | tf_op jit(solution)/shard_map/second_sums/pallas_call | solution.py:485
  78.3 0.2 collective-permute-start.21
  78.5 7.9 %first_sums.1 = f32[9,256,256]{2,1,0:T(8,128)S(1)} custom-call(f32[2304,256]{1,0:T(8,128)S(1)} %get-tuple-element.61.slope_hbm, bf16[256,2304]{1,0:T(8,128)(2,1)S(1)} %get-tuple-element.62.state_hbm, bf16[18,10,16,256]{3,2,1,0:T(8,128)(2,1)S(1)} %get-tuple-element.64.pull_ref, bf16[9,256,256]{2,1,0:T(8,128)(2,1)S(1)} %get-tuple-element.65.w2t_ref), custom_call_target="tpu_custom_call" | custom-call | flops 10000000000 | bytes 8000000 | tf_op jit(solution)/shard_map/first_sums/pallas_call | solution.py:547
  86.5 0.4 collective-permute-start.22
  86.9 3.0 %local_grad.1 = f32[128,256]{1,0:T(8,128)} custom-call(bf16[4,8,16,256]{3,2,1,0:T(8,128)(2,1)S(1)} %all-to-all-done.1.refs_0_, bf16[4,8,16,256]{3,2,1,0:T(8,128)(2,1)S(1)} %collective-permute-done.17.refs_1_, bf16[4,8,16,256]{3,2,1,0:T(8,128)(2,1)S(1)} %collective-permute-done.10.refs_2_, bf16[4,8,16,256]{3,2,1,0:T(8,128)(2,1)S(1)} %collective-permute-done.18.refs_3_, ...), custom_call_target="tpu_custom_call" | custom-call | flops 3000000000 | bytes 4000000 | tf_op jit(solution)/shard_map/local_grad/pallas_call | solution.py:601
  90.0 1.7 %add.7 = f32[9,256,256]{2,1,0:T(8,128)} add(f32[9,256,256]{2,1,0:T(8,128)S(1)} %get-tuple-element.66, f32[9,256,256]{2,1,0:T(8,128)S(1)} %collective-permute-done.21) | non-fusion elementwise | flops 589824 | bytes 7077888 | tf_op jit(solution)/shard_map/add | solution.py:867
  91.7 1.7 %add.6 = f32[9,256,256]{2,1,0:T(8,128)} add(f32[9,256,256]{2,1,0:T(8,128)S(1)} %first_sums.1, f32[9,256,256]{2,1,0:T(8,128)S(1)} %collective-permute-done.22) | non-fusion elementwise | flops 589824 | bytes 7077888 | tf_op jit(solution)/shard_map/add | solution.py:867
  (39 shorter events, 0.1 us)
Async XLA Ops:
  3.4 22.3 %collective-permute-start.2 = (bf16[8,16,256]{2,1,0:T(8,128)(2,1)}, bf16[8,16,256]{2,1,0:T(8,128)(2,1)S(1)}, u32[]{:S(2)}, u32[]{:S(2)}) collective-permute-start(bf16[8,16,256]{2,1,0:T(8,128)(2,1)} %tile_ref), channel_id=1, source_target_pairs={{0,6},{1,7},{2,0},{3,1},{4,2},{5,3},{6,4},{7,5},{8,14},{9,15},{10,... | collective-permute-start | bytes 196616 | tf_op jit(solution)/shard_map/ppermute | solution.py:804
  8.4 17.2 %collective-permute-start.1 = (bf16[8,16,256]{2,1,0:T(8,128)(2,1)}, bf16[8,16,256]{2,1,0:T(8,128)(2,1)S(1)}, u32[]{:S(2)}, u32[]{:S(2)}) collective-permute-start(bf16[8,16,256]{2,1,0:T(8,128)(2,1)} %tile_ref), channel_id=1, source_target_pairs={{0,4},{1,5},{2,6},{3,7},{4,0},{5,1},{6,2},{7,3},{8,12},{9,13},{10,... | collective-permute-start | bytes 196616 | tf_op jit(solution)/shard_map/ppermute | solution.py:804
  8.4 17.2 %collective-permute-start = (bf16[8,16,256]{2,1,0:T(8,128)(2,1)}, bf16[8,16,256]{2,1,0:T(8,128)(2,1)S(1)}, u32[]{:S(2)}, u32[]{:S(2)}) collective-permute-start(bf16[8,16,256]{2,1,0:T(8,128)(2,1)} %tile_ref), channel_id=1, source_target_pairs={{0,2},{1,3},{2,4},{3,5},{4,6},{5,7},{6,0},{7,1},{8,10},{9,11},{10,... | collective-permute-start | bytes 196616 | tf_op jit(solution)/shard_map/ppermute | solution.py:804
  10.2 11.7 %collective-permute-start.4 = (bf16[2,16,256]{2,1,0:T(8,128)(2,1)S(1)}, bf16[2,16,256]{2,1,0:T(8,128)(2,1)S(1)}, u32[]{:S(2)}, u32[]{:S(2)}) collective-permute-start(bf16[2,16,256]{2,1,0:T(8,128)(2,1)S(1)} %get-tuple-element.71), channel_id=1, source_target_pairs={{8,0},{16,8},{24,16},{9,1},{17,9},{25,17},{10,2},{18,10},{26,18},{... | collective-permute-start | bytes 49160 | tf_op jit(solution)/shard_map/ppermute | solution.py:785
  11.5 10.4 %collective-permute-start.3 = (bf16[2,16,256]{2,1,0:T(8,128)(2,1)S(1)}, bf16[2,16,256]{2,1,0:T(8,128)(2,1)S(1)}, u32[]{:S(2)}, u32[]{:S(2)}) collective-permute-start(bf16[2,16,256]{2,1,0:T(8,128)(2,1)S(1)} %get-tuple-element.72), channel_id=1, source_target_pairs={{0,8},{8,16},{16,24},{1,9},{9,17},{17,25},{2,10},{10,18},{18,26},{... | collective-permute-start | bytes 49160 | tf_op jit(solution)/shard_map/ppermute | solution.py:784
  16.0 13.2 %all-to-all-start = ((f32[32,8,128]{2,1,0:T(8,128)}), f32[32,8,128]{2,1,0:T(8,128)S(1)}, u32[]{:S(2)}, u32[]{:S(2)}) async-start(f32[32,8,128]{2,1,0:T(8,128)} %route.1), calls=%async_computation | async-start | bytes 262144 | tf_op jit(solution)/shard_map/all_to_all | solution.py:845
  21.8 10.5 %copy-start.7 = (bf16[2,16,256]{2,1,0:T(8,128)(2,1)}, bf16[2,16,256]{2,1,0:T(8,128)(2,1)S(1)}, u32[]{:S(2)}) copy-start(bf16[2,16,256]{2,1,0:T(8,128)(2,1)S(1)} %collective-permute-done.4.south_ref) | copy-start | bytes 49156
  21.9 5.8 %copy-start.8 = (bf16[2,16,256]{2,1,0:T(8,128)(2,1)}, bf16[2,16,256]{2,1,0:T(8,128)(2,1)S(1)}, u32[]{:S(2)}) copy-start(bf16[2,16,256]{2,1,0:T(8,128)(2,1)S(1)} %collective-permute-done.3.north_ref) | copy-start | bytes 49156
  21.9 5.7 %collective-permute-start.5 = (bf16[12,2,256]{2,1,0:T(2,128)(2,1)S(1)}, bf16[12,2,256]{2,1,0:T(2,128)(2,1)S(1)}, u32[]{:S(2)}, u32[]{:S(2)}) collective-permute-start(bf16[12,2,256]{2,1,0:T(2,128)(2,1)S(1)} %pad_maximum_fusion.1), channel_id=1, source_target_pairs={{0,1},{1,2},{2,3},{3,4},{4,5},{5,6},{6,7},{7,0},{8,9},{9,10},{10,1... | collective-permute-start | bytes 36872 | tf_op jit(solution)/shard_map/ppermute | solution.py:788
  22.3 5.4 %collective-permute-start.6 = (bf16[12,2,256]{2,1,0:T(2,128)(2,1)S(1)}, bf16[12,2,256]{2,1,0:T(2,128)(2,1)S(1)}, u32[]{:S(2)}, u32[]{:S(2)}) collective-permute-start(bf16[12,2,256]{2,1,0:T(2,128)(2,1)S(1)} %pad_maximum_fusion.2), channel_id=1, source_target_pairs={{1,0},{2,1},{3,2},{4,3},{5,4},{6,5},{7,6},{0,7},{9,8},{10,9},{11,1... | collective-permute-start | bytes 36872 | tf_op jit(solution)/shard_map/ppermute | solution.py:789
  26.5 34.1 %copy-start = (bf16[9,256,256]{2,1,0:T(8,128)(2,1)S(1)}, bf16[9,256,256]{2,1,0:T(8,128)(2,1)}, u32[]{:S(2)}) copy-start(bf16[9,256,256]{2,1,0:T(8,128)(2,1)} %refs_10_.1) | copy-start | bytes 3538948
  26.5 34.1 %copy-start.1 = (bf16[9,256,256]{2,1,0:T(8,128)(2,1)S(1)}, bf16[9,256,256]{2,1,0:T(8,128)(2,1)}, u32[]{:S(2)}) copy-start(bf16[9,256,256]{2,1,0:T(8,128)(2,1)} %refs_11_.1) | copy-start | bytes 3538948
  27.6 0.6 copy-start.9
  28.2 0.6 copy-start.10
  29.2 3.2 %copy-start.6 = (f32[32,8,128]{2,1,0:T(8,128)}, f32[32,8,128]{2,1,0:T(8,128)S(1)}, u32[]{:S(2)}) copy-start(f32[32,8,128]{2,1,0:T(8,128)S(1)} %all-to-all-done.got_ref) | copy-start | bytes 393220
  29.2 12.8 %collective-permute-start.9 = (bf16[4,8,16,256]{3,2,1,0:T(8,128)(2,1)S(1)}, bf16[4,8,16,256]{3,2,1,0:T(8,128)(2,1)S(1)}, u32[]{:S(2)}, u32[]{:S(2)}) collective-permute-start(bf16[4,8,16,256]{3,2,1,0:T(8,128)(2,1)S(1)} %pad_maximum_fusion.refs_0_), channel_id=1, source_target_pairs={{0,24},{8,0},{16,8},{24,16},{1,25},{9,1},{17,9},{25,17},{2,26},{10... | collective-permute-start | bytes 786440 | tf_op jit(solution)/shard_map/ppermute | solution.py:813
  31.3 12.7 %collective-permute-start.8 = (bf16[4,8,16,256]{3,2,1,0:T(8,128)(2,1)S(1)}, bf16[4,8,16,256]{3,2,1,0:T(8,128)(2,1)S(1)}, u32[]{:S(2)}, u32[]{:S(2)}) collective-permute-start(bf16[4,8,16,256]{3,2,1,0:T(8,128)(2,1)S(1)} %pad_maximum_fusion.refs_0_), channel_id=1, source_target_pairs={{0,16},{8,24},{16,0},{24,8},{1,17},{9,25},{17,1},{25,9},{2,18},{10... | collective-permute-start | bytes 786440 | tf_op jit(solution)/shard_map/ppermute | solution.py:813
  31.8 12.2 %collective-permute-start.7 = (bf16[4,8,16,256]{3,2,1,0:T(8,128)(2,1)S(1)}, bf16[4,8,16,256]{3,2,1,0:T(8,128)(2,1)S(1)}, u32[]{:S(2)}, u32[]{:S(2)}) collective-permute-start(bf16[4,8,16,256]{3,2,1,0:T(8,128)(2,1)S(1)} %pad_maximum_fusion.refs_0_), channel_id=1, source_target_pairs={{0,8},{8,16},{16,24},{24,0},{1,9},{9,17},{17,25},{25,1},{2,10},{10... | collective-permute-start | bytes 786440 | tf_op jit(solution)/shard_map/ppermute | solution.py:813
  43.9 0.7 copy-start.2
  44.7 13.4 %all-to-all-start.1 = ((bf16[4,8,16,256]{3,2,1,0:T(8,128)(2,1)}), bf16[4,8,16,256]{3,2,1,0:T(8,128)(2,1)S(1)}, u32[]{:S(2)}, u32[]{:S(2)}) async-start(bf16[4,8,16,256]{3,2,1,0:T(8,128)(2,1)} %bitcast.13), calls=%async_computation.1 | async-start | bytes 524288 | tf_op jit(solution)/shard_map/all_to_all | solution.py:796
  48.7 10.0 %collective-permute-start.13 = (bf16[4,8,16,256]{3,2,1,0:T(8,128)(2,1)S(1)}, bf16[4,8,16,256]{3,2,1,0:T(8,128)(2,1)}, u32[]{:S(2)}, u32[]{:S(2)}) collective-permute-start(bf16[4,8,16,256]{3,2,1,0:T(8,128)(2,1)S(1)} %pad_maximum_fusion.refs_0_), channel_id=1, source_target_pairs={{0,1},{1,0},{2,3},{3,2},{4,5},{5,4},{6,7},{7,6},{8,9},{9,8},{10,11... | collective-permute-start | bytes 786440 | tf_op jit(solution)/shard_map/ppermute | solution.py:822
  48.7 10.8 %collective-permute-start.14 = (bf16[4,8,16,256]{3,2,1,0:T(8,128)(2,1)}, bf16[4,8,16,256]{3,2,1,0:T(8,128)(2,1)}, u32[]{:S(2)}, u32[]{:S(2)}) collective-permute-start(bf16[4,8,16,256]{3,2,1,0:T(8,128)(2,1)} %copy-done.2), channel_id=1, source_target_pairs={{0,1},{1,0},{2,3},{3,2},{4,5},{5,4},{6,7},{7,6},{8,9},{9,8},{10,11... | collective-permute-start | bytes 786440 | tf_op jit(solution)/shard_map/ppermute | solution.py:822
  49.2 11.4 %collective-permute-start.15 = (bf16[4,8,16,256]{3,2,1,0:T(8,128)(2,1)S(1)}, bf16[4,8,16,256]{3,2,1,0:T(8,128)(2,1)}, u32[]{:S(2)}, u32[]{:S(2)}) collective-permute-start(bf16[4,8,16,256]{3,2,1,0:T(8,128)(2,1)S(1)} %collective-permute-done.8.refs_4_), channel_id=1, source_target_pairs={{0,1},{1,0},{2,3},{3,2},{4,5},{5,4},{6,7},{7,6},{8,9},{9,8},{10,11... | collective-permute-start | bytes 786440 | tf_op jit(solution)/shard_map/ppermute | solution.py:822
  49.2 11.4 %collective-permute-start.16 = (bf16[4,8,16,256]{3,2,1,0:T(8,128)(2,1)S(1)}, bf16[4,8,16,256]{3,2,1,0:T(8,128)(2,1)}, u32[]{:S(2)}, u32[]{:S(2)}) collective-permute-start(bf16[4,8,16,256]{3,2,1,0:T(8,128)(2,1)S(1)} %collective-permute-done.9.refs_6_), channel_id=1, source_target_pairs={{0,1},{1,0},{2,3},{3,2},{4,5},{5,4},{6,7},{7,6},{8,9},{9,8},{10,11... | collective-permute-start | bytes 786440 | tf_op jit(solution)/shard_map/ppermute | solution.py:822
  58.0 10.2 %collective-permute-start.12 = (bf16[4,8,16,256]{3,2,1,0:T(8,128)(2,1)S(1)}, bf16[4,8,16,256]{3,2,1,0:T(8,128)(2,1)S(1)}, u32[]{:S(2)}, u32[]{:S(2)}) collective-permute-start(bf16[4,8,16,256]{3,2,1,0:T(8,128)(2,1)S(1)} %all-to-all-done.1.refs_0_), channel_id=1, source_target_pairs={{0,24},{8,0},{16,8},{24,16},{1,25},{9,1},{17,9},{25,17},{2,26},{10... | collective-permute-start | bytes 786440 | tf_op jit(solution)/shard_map/ppermute | solution.py:813
  58.6 11.5 %collective-permute-start.11 = (bf16[4,8,16,256]{3,2,1,0:T(8,128)(2,1)S(1)}, bf16[4,8,16,256]{3,2,1,0:T(8,128)(2,1)S(1)}, u32[]{:S(2)}, u32[]{:S(2)}) collective-permute-start(bf16[4,8,16,256]{3,2,1,0:T(8,128)(2,1)S(1)} %all-to-all-done.1.refs_0_), channel_id=1, source_target_pairs={{0,16},{8,24},{16,0},{24,8},{1,17},{9,25},{17,1},{25,9},{2,18},{10... | collective-permute-start | bytes 786440 | tf_op jit(solution)/shard_map/ppermute | solution.py:813
  59.5 10.6 %collective-permute-start.10 = (bf16[4,8,16,256]{3,2,1,0:T(8,128)(2,1)S(1)}, bf16[4,8,16,256]{3,2,1,0:T(8,128)(2,1)S(1)}, u32[]{:S(2)}, u32[]{:S(2)}) collective-permute-start(bf16[4,8,16,256]{3,2,1,0:T(8,128)(2,1)S(1)} %all-to-all-done.1.refs_0_), channel_id=1, source_target_pairs={{0,8},{8,16},{16,24},{24,0},{1,9},{9,17},{17,25},{25,1},{2,10},{10... | collective-permute-start | bytes 786440 | tf_op jit(solution)/shard_map/ppermute | solution.py:813
  60.6 1.0 %copy-start.3 = (bf16[4,8,16,256]{3,2,1,0:T(8,128)(2,1)S(1)}, bf16[4,8,16,256]{3,2,1,0:T(8,128)(2,1)}, u32[]{:S(2)}) copy-start(bf16[4,8,16,256]{3,2,1,0:T(8,128)(2,1)} %copy-done.2) | copy-start | bytes 786436
  70.2 1.5 %collective-permute-start.17 = (bf16[4,8,16,256]{3,2,1,0:T(8,128)(2,1)S(1)}, bf16[4,8,16,256]{3,2,1,0:T(8,128)(2,1)S(1)}, u32[]{:S(2)}, u32[]{:S(2)}) collective-permute-start(bf16[4,8,16,256]{3,2,1,0:T(8,128)(2,1)S(1)} %all-to-all-done.1.refs_0_), channel_id=1, source_target_pairs={{0,1},{1,0},{2,3},{3,2},{4,5},{5,4},{6,7},{7,6},{8,9},{9,8},{10,11... | collective-permute-start | bytes 786440 | tf_op jit(solution)/shard_map/ppermute | solution.py:822
  70.2 1.9 %collective-permute-start.18 = (bf16[4,8,16,256]{3,2,1,0:T(8,128)(2,1)S(1)}, bf16[4,8,16,256]{3,2,1,0:T(8,128)(2,1)S(1)}, u32[]{:S(2)}, u32[]{:S(2)}) collective-permute-start(bf16[4,8,16,256]{3,2,1,0:T(8,128)(2,1)S(1)} %collective-permute-done.10.refs_2_), channel_id=1, source_target_pairs={{0,1},{1,0},{2,3},{3,2},{4,5},{5,4},{6,7},{7,6},{8,9},{9,8},{10,11... | collective-permute-start | bytes 786440 | tf_op jit(solution)/shard_map/ppermute | solution.py:822
  70.7 1.8 %collective-permute-start.19 = (bf16[4,8,16,256]{3,2,1,0:T(8,128)(2,1)S(1)}, bf16[4,8,16,256]{3,2,1,0:T(8,128)(2,1)S(1)}, u32[]{:S(2)}, u32[]{:S(2)}) collective-permute-start(bf16[4,8,16,256]{3,2,1,0:T(8,128)(2,1)S(1)} %collective-permute-done.11.refs_4_), channel_id=1, source_target_pairs={{0,1},{1,0},{2,3},{3,2},{4,5},{5,4},{6,7},{7,6},{8,9},{9,8},{10,11... | collective-permute-start | bytes 786440 | tf_op jit(solution)/shard_map/ppermute | solution.py:822
  70.7 2.1 %collective-permute-start.20 = (bf16[4,8,16,256]{3,2,1,0:T(8,128)(2,1)S(1)}, bf16[4,8,16,256]{3,2,1,0:T(8,128)(2,1)S(1)}, u32[]{:S(2)}, u32[]{:S(2)}) collective-permute-start(bf16[4,8,16,256]{3,2,1,0:T(8,128)(2,1)S(1)} %collective-permute-done.12.refs_6_), channel_id=1, source_target_pairs={{0,1},{1,0},{2,3},{3,2},{4,5},{5,4},{6,7},{7,6},{8,9},{9,8},{10,11... | collective-permute-start | bytes 786440 | tf_op jit(solution)/shard_map/ppermute | solution.py:822
  78.3 8.1 %collective-permute-start.21 = (f32[9,256,256]{2,1,0:T(8,128)S(1)}, f32[9,256,256]{2,1,0:T(8,128)S(1)}, u32[]{:S(2)}, u32[]{:S(2)}) collective-permute-start(f32[9,256,256]{2,1,0:T(8,128)S(1)} %get-tuple-element.66), channel_id=1, source_target_pairs={{0,1},{1,0},{2,3},{3,2},{4,5},{5,4},{6,7},{7,6},{8,9},{9,8},{10,11... | collective-permute-start | bytes 7077896 | tf_op jit(solution)/shard_map/ppermute | solution.py:862
  78.5 8.4 %copy-start.4 = (f32[320,256]{1,0:T(8,128)S(1)}, f32[320,256]{1,0:T(8,128)}, u32[]{:S(2)}) copy-start(f32[320,256]{1,0:T(8,128)} %get-tuple-element.59.refs_8_) | copy-start | bytes 983044
  78.5 8.4 %copy-start.5 = (f32[128,256]{1,0:T(8,128)S(1)}, f32[128,256]{1,0:T(8,128)}, u32[]{:S(2)}) copy-start(f32[128,256]{1,0:T(8,128)} %get-tuple-element.60.refs_9_) | copy-start | bytes 393220
  86.5 5.2 %collective-permute-start.22 = (f32[9,256,256]{2,1,0:T(8,128)S(1)}, f32[9,256,256]{2,1,0:T(8,128)S(1)}, u32[]{:S(2)}, u32[]{:S(2)}) collective-permute-start(f32[9,256,256]{2,1,0:T(8,128)S(1)} %first_sums.1), channel_id=1, source_target_pairs={{0,1},{1,0},{2,3},{3,2},{4,5},{5,4},{6,7},{7,6},{8,9},{9,8},{10,11... | collective-permute-start | bytes 7077896 | tf_op jit(solution)/shard_map/ppermute | solution.py:865
